TPU v7x, 128 devices: a whole 4x4x4 slice. The times are simulated.
128 devices in a mesh: section: 2 (over core), seq: 16 (over z, y), head: 4 (over x).
Axes of the slice: x: 4, y: 4, z: 4, core: 2. Of those that a mesh axis runs over, the one named last changes fastest.
Arguments:
- tokens_in: bfloat16 [2, 8192, 1536], P(None, ('seq', 'head')), may hold values from -6 to 6
- cotangent: bfloat16 [2, 8192, 1536], P(None, ('seq', 'head')), may hold values from -6 to 6
- input_gain: bfloat16 [2, 1536], P('section', ('seq', 'head')), may hold values from 0.25 to 1.75
- gate_inner: bfloat16 [2, 1536, 6144], P('section', ('seq', 'head')), may hold values from -0.15625 to 0.15625
- shared_bc: bfloat16 [2, 1536, 256], P('section', ('seq', 'head')), may hold values from -0.15625 to 0.15625
- step_proj: bfloat16 [2, 1536, 48], P('section', ('seq', 'head')), may hold values from -0.15625 to 0.15625
- conv_weight: bfloat16 [2, 4, 3328], P('section', None, ('seq', 'head')), may hold values from -3 to 3
- conv_bias: bfloat16 [2, 3328], P('section', ('seq', 'head')), may hold values from -0.5 to 0.5
- step_bias: float32 [2, 48], P('section'), may hold values from -9 to -3
- decay_log: float32 [2, 48], P('section'), may hold values from -1 to 0.5
- skip_gain: float32 [2, 48], P('section'), may hold values from 0.5 to 1.5
- output_gain: bfloat16 [2, 3072], P('section', ('seq', 'head')), may hold values from 0.25 to 1.75
- out_proj: bfloat16 [2, 3072, 1536], P('section', ('seq', 'head')), may hold values from -0.109375 to 0.109375
Outputs:
- layer_out: bfloat16 [2, 2, 8192, 1536], P('section', None, ('seq', 'head'))
- grad_in: bfloat16 [2, 2, 8192, 1536], P('section', None, ('seq', 'head'))
- grad_input_gain: float32 [2, 1536], P('section', ('seq', 'head'))
- grad_gate_inner: float32 [2, 1536, 6144], P('section', ('seq', 'head'))
- grad_shared_bc: float32 [2, 1536, 256], P('section', ('seq', 'head'))
- grad_step_proj: float32 [2, 1536, 48], P('section', ('seq', 'head'))
- grad_conv_weight: float32 [2, 4, 3328], P('section', None, ('seq', 'head'))
- grad_conv_bias: float32 [2, 3328], P('section', ('seq', 'head'))
- grad_step_bias: float32 [2, 48], P('section')
- grad_decay_log: float32 [2, 48], P('section')
- grad_skip_gain: float32 [2, 48], P('section')
- grad_output_gain: float32 [2, 3072], P('section', ('seq', 'head'))
- grad_out_proj: float32 [2, 3072, 1536], P('section', ('seq', 'head'))
All inputs are finite; a program needn't handle non-finite values.
Results may differ from a plain program's by a relative error of at most 0.025.
Values may be sent and summed in bfloat16 or wider, within the bound.
No kernel may reach another device: no remote copies, remote signals or barrier semaphores. Data moves between devices by JAX's collectives and lax.ppermute only.
A program may use at most 320 MiB of HBM per device.

v0:
```python
import jax
import jax.numpy as jnp
from jax import lax
from jax.sharding import PartitionSpec as P

P_SIZE = 64
N = 128
BLOCK = 256


epsilon = 1e-05
highest = lax.Precision.HIGHEST


def shifted(array, axis, by):
    count = lax.axis_size(axis)
    pairs = [(i, i + by) for i in range(count) if 0 <= i + by < count]
    return lax.ppermute(array, axis, pairs)


def carried_in(array, axis, join, neutral):
    place = lax.axis_index(axis)
    gathered = jax.tree.map(
        lambda a, kind: lax.all_gather(a.astype(kind), axis), array, (jnp.bfloat16, jnp.bfloat16)
    )
    state = jax.tree.map(lambda a, e: jnp.zeros_like(a) + jnp.asarray(e, a.dtype), array, neutral)

    def carried_one(lap, state):
        return join(
            state,
            jax.tree.map(
                lambda a, own: lax.dynamic_index_in_dim(a, lap, 0, False).astype(own.dtype),
                gathered,
                array,
            ),
        )

    return lax.fori_loop(0, place, carried_one, state)


def prefix(array, axis, join, neutral):
    count = lax.axis_size(axis)
    place = lax.axis_index(axis)
    ahead = count - 1 - place
    gathered = jax.tree.map(
        lambda a, kind: lax.all_gather(a.astype(kind), axis),
        array,
        jax.tree.map(lambda a: jnp.bfloat16 if a.dtype == jnp.float32 else a.dtype, array),
    )
    state = jax.tree.map(lambda a, e: jnp.zeros_like(a) + jnp.asarray(e, a.dtype), array, neutral)

    def prefix_one(lap, state):
        source = count - 1 - lap
        return join(
            state,
            jax.tree.map(
                lambda a, own: lax.dynamic_index_in_dim(a, source, 0, False).astype(own.dtype),
                gathered,
                array,
            ),
        )

    return lax.fori_loop(0, ahead, prefix_one, state)


def rms_scale(values):
    return lax.rsqrt(jnp.mean(values * values, axis=-1, keepdims=True) + epsilon)


def conv_causal(padded, weight, bias):
    width = weight.shape[0]
    length = padded.shape[0] - width + 1
    total = jnp.zeros((length, padded.shape[1]), jnp.float32) + bias[None, :]
    for offset in range(width):
        total = total + weight[offset][None, :] * padded[offset : offset + length]
    return total


def piece_step(carry_state, pieces):
    inner_heads, step_sizes, key_rows, queries, log_decay = pieces
    length = step_sizes.shape[0]
    running = jnp.cumsum(log_decay, axis=0)
    row_index = lax.broadcasted_iota(jnp.int32, (length, length), 0)
    col_index = lax.broadcasted_iota(jnp.int32, (length, length), 1)
    causal = (row_index >= col_index)[:, :, None]
    spread_log = jnp.where(causal, running[:, None, :] - running[None, :, :], 0.0)
    affinity = jnp.dot(queries, key_rows.T, precision=highest)
    weights = (
        jnp.where(causal, jnp.exp(spread_log), 0.0) * affinity[:, :, None] * step_sizes[None, :, :]
    )
    result = jnp.einsum("tsh,shp->thp", weights, inner_heads, precision=highest)
    result = result + jnp.exp(running)[:, :, None] * jnp.einsum(
        "tn,hpn->thp", queries, carry_state, precision=highest
    )
    carried = jnp.exp(running[-1][None, :] - running) * step_sizes
    carry_state = jnp.exp(running[-1])[:, None, None] * carry_state + jnp.einsum(
        "sh,shp,sn->hpn", carried, inner_heads, key_rows, precision=highest
    )
    return (carry_state, result)


def scan_heads(inner_act, step_sizes, key_rows, queries, log_decay, start_state, piece_len):
    length, head_count = step_sizes.shape
    pieces_count = length // piece_len

    def to_pieces(values):
        return values.reshape((pieces_count, piece_len) + values.shape[1:])

    inner_heads = inner_act.reshape(length, head_count, -1)
    final_state, outputs = lax.scan(
        jax.checkpoint(piece_step),
        start_state,
        (
            to_pieces(inner_heads),
            to_pieces(step_sizes),
            to_pieces(key_rows),
            to_pieces(queries),
            to_pieces(log_decay),
        ),
    )
    return (outputs.reshape(length, -1), final_state)


def head_prepare(block_in, rim_rows, conv_group, bias_group, step_raw, step_bias, decay_log):
    head_count = step_raw.shape[1]
    group_width = head_count * P_SIZE
    padded = jnp.concatenate([rim_rows, block_in], axis=0)
    active = jax.nn.silu(conv_causal(padded, conv_group, bias_group))
    inner_act = active[:, :group_width]
    key_rows = active[:, group_width : group_width + N]
    queries = active[:, group_width + N :]
    step_sizes = jax.nn.softplus(step_raw + step_bias[None, :])
    log_decay = -jnp.exp(decay_log)[None, :] * step_sizes
    running = jnp.cumsum(log_decay, axis=0)
    carried = jnp.exp(running[-1][None, :] - running) * step_sizes
    length = inner_act.shape[0]
    local_state = jnp.einsum(
        "sh,shp,sn->hpn",
        carried,
        inner_act.reshape(length, head_count, P_SIZE),
        key_rows,
        precision=highest,
    )
    return (inner_act, step_sizes, key_rows, queries, log_decay, running, local_state)


def head_finish(inner_act, step_sizes, key_rows, queries, log_decay, skip_gain, state_in):
    mixed = scan_heads(inner_act, step_sizes, key_rows, queries, log_decay, state_in, BLOCK)[0]
    return mixed + jnp.repeat(skip_gain, P_SIZE)[None, :] * inner_act


def head_mix(
    block_in, rim_rows, conv_group, bias_group, step_raw, step_bias, decay_log, skip_gain, state_in
):
    inner_act, step_sizes, key_rows, queries, log_decay, running, local_state = head_prepare(
        block_in, rim_rows, conv_group, bias_group, step_raw, step_bias, decay_log
    )
    mixed = head_finish(inner_act, step_sizes, key_rows, queries, log_decay, skip_gain, state_in)
    return ((mixed, local_state, running[-1]), (running, queries))


def combine_states(earlier, later):
    return (earlier[0] * later[0], earlier[1] * later[0][:, None, None] + later[1])


def group_params(conv_weight, conv_bias, head_params, group_width, head_count):
    group_index = lax.axis_index("head")
    inner_width = conv_weight.shape[1] - 2 * N
    conv_float = conv_weight.astype(jnp.float32)
    bias_float = conv_bias.astype(jnp.float32)
    conv_group = jnp.concatenate(
        [
            lax.dynamic_slice_in_dim(conv_float, group_index * group_width, group_width, 1),
            conv_float[:, inner_width:],
        ],
        axis=1,
    )
    bias_group = jnp.concatenate(
        [
            lax.dynamic_slice_in_dim(bias_float, group_index * group_width, group_width, 0),
            bias_float[inner_width:],
        ]
    )
    head_group = tuple(
        (
            lax.dynamic_slice_in_dim(values, group_index * head_count, head_count, 0)
            for values in head_params
        )
    )
    return (group_index, conv_group, bias_group, head_group)


def fetch_weights(packed):
    gathered = (
        lax.all_gather(packed[0], ("seq", "head"), axis=1, tiled=True),
        lax.all_gather(packed[1], ("seq", "head"), axis=1, tiled=True),
        lax.all_gather(packed[2], ("seq", "head"), axis=1, tiled=True),
        lax.all_gather(packed[3], ("seq", "head"), axis=1, tiled=True),
        lax.all_gather(packed[4], ("seq", "head"), axis=2, tiled=True),
        lax.all_gather(packed[5], ("seq", "head"), axis=1, tiled=True),
        lax.all_gather(packed[6], ("seq", "head"), axis=1, tiled=True),
        lax.all_gather(packed[7], ("seq", "head"), axis=1, tiled=True),
    )
    return tuple((values[0] for values in gathered))


def reduce_grads(grads):
    return (
        lax.psum_scatter(grads[0], ("seq", "head"), scatter_dimension=0, tiled=True),
        lax.psum_scatter(grads[1], ("seq", "head"), scatter_dimension=0, tiled=True),
        lax.psum_scatter(grads[2], ("seq", "head"), scatter_dimension=0, tiled=True),
        lax.psum_scatter(grads[3], ("seq", "head"), scatter_dimension=0, tiled=True),
        lax.psum_scatter(grads[4], ("seq", "head"), scatter_dimension=1, tiled=True),
        lax.psum_scatter(grads[5], ("seq", "head"), scatter_dimension=0, tiled=True),
        lax.psum_scatter(grads[6], ("seq", "head"), scatter_dimension=0, tiled=True),
        lax.psum_scatter(grads[7], ("seq", "head"), scatter_dimension=0, tiled=True),
    )


def contract_rows(left, right):
    return lax.dot_general(
        left, right, (((0,), (0,)), ((), ())), preferred_element_type=jnp.float32
    )


def contract_cols(left, right):
    return lax.dot_general(
        left, right, (((1,), (1,)), ((), ())), preferred_element_type=jnp.float32
    )


def layer_forward(feed, whole, head_params):
    input_gain, gate_inner, shared_bc, step_proj, conv_weight, conv_bias, output_gain, out_proj = (
        whole
    )
    residual = feed.astype(jnp.float32)
    normed = (residual * rms_scale(residual) * input_gain.astype(jnp.float32)[None, :]).astype(
        jnp.bfloat16
    )
    projected = jnp.dot(normed, gate_inner, preferred_element_type=jnp.float32)
    inner_width = projected.shape[1] // 2
    gate_pre = projected[:, :inner_width]
    inner_low = projected[:, inner_width:].astype(jnp.bfloat16)
    shared_low = jnp.dot(normed, shared_bc, preferred_element_type=jnp.float32).astype(jnp.bfloat16)
    step_low = jnp.dot(normed, step_proj, preferred_element_type=jnp.float32).astype(jnp.bfloat16)
    tiled = jnp.tile(shared_low, (1, lax.axis_size("head")))
    inner_head, step_head, shared_head = (
        lax.all_to_all(inner_low, "head", split_axis=1, concat_axis=0, tiled=True),
        lax.all_to_all(step_low, "head", split_axis=1, concat_axis=0, tiled=True),
        lax.all_to_all(tiled, "head", split_axis=1, concat_axis=0, tiled=True),
    )
    block_in = jnp.concatenate([inner_head, shared_head], axis=1)
    width = conv_weight.shape[0]
    rim_rows = shifted(block_in[block_in.shape[0] - (width - 1) :], "seq", 1)
    group_width = inner_head.shape[1]
    head_count = step_head.shape[1]
    group_index, conv_group, bias_group, head_group = group_params(
        conv_weight, conv_bias, head_params, group_width, head_count
    )
    inner_act, step_sizes, key_rows, queries, log_decay, running, local_state = head_prepare(
        block_in.astype(jnp.float32),
        rim_rows.astype(jnp.float32),
        conv_group,
        bias_group,
        step_head.astype(jnp.float32),
        head_group[0],
        head_group[1],
    )
    decay_total = jnp.exp(running[-1])
    identity = (jnp.ones_like(decay_total), jnp.zeros_like(local_state))
    state_in = carried_in((decay_total, local_state), "seq", combine_states, identity)[1]
    mixed = head_finish(
        inner_act, step_sizes, key_rows, queries, log_decay, head_group[2], state_in
    )
    scan_out = lax.all_to_all(
        mixed.astype(jnp.bfloat16), "head", split_axis=0, concat_axis=1, tiled=True
    )
    gated = scan_out.astype(jnp.float32) * jax.nn.silu(gate_pre)
    normed_out = (gated * rms_scale(gated) * output_gain.astype(jnp.float32)[None, :]).astype(
        jnp.bfloat16
    )
    branch = jnp.dot(normed_out, out_proj, preferred_element_type=jnp.float32)
    result = (residual + branch).astype(jnp.bfloat16)
    kept = (
        feed,
        normed,
        gate_pre,
        block_in,
        rim_rows,
        step_head,
        state_in,
        decay_total,
        scan_out,
        normed_out,
    )
    return (result, kept)


def layer_backward(incoming, kept, whole, head_params):
    (
        feed,
        normed,
        gate_pre,
        block_in,
        rim_rows,
        step_head,
        state_in,
        decay_total,
        scan_out,
        normed_out,
    ) = kept
    input_gain, gate_inner, shared_bc, step_proj, conv_weight, conv_bias, output_gain, out_proj = (
        whole
    )
    grad_out_proj = contract_rows(normed_out, incoming)
    grad_normed_out = contract_cols(incoming, out_proj)
    scan_float = scan_out.astype(jnp.float32)
    gate_sig = jax.nn.sigmoid(gate_pre)
    gate_act = gate_pre * gate_sig
    gated = scan_float * gate_act
    scale_out = rms_scale(gated)
    unit_out = gated * scale_out
    grad_output_gain = jnp.sum(grad_normed_out * unit_out, axis=0)
    grad_unit = grad_normed_out * output_gain.astype(jnp.float32)[None, :]
    grad_gated = scale_out * (
        grad_unit - unit_out * jnp.mean(unit_out * grad_unit, axis=-1, keepdims=True)
    )
    grad_scan = (grad_gated * gate_act).astype(jnp.bfloat16)
    grad_gate = (grad_gated * scan_float * gate_sig * (1.0 + gate_pre * (1.0 - gate_sig))).astype(
        jnp.bfloat16
    )
    grad_head = lax.all_to_all(grad_scan, "head", split_axis=1, concat_axis=0, tiled=True)
    group_width = grad_head.shape[1]
    head_count = step_head.shape[1]
    inner_width = gate_inner.shape[1] // 2
    group_index, conv_group, bias_group, head_group = group_params(
        conv_weight, conv_bias, head_params, group_width, head_count
    )
    primals = (
        block_in.astype(jnp.float32),
        rim_rows.astype(jnp.float32),
        conv_group,
        bias_group,
        step_head.astype(jnp.float32),
        head_group[0],
        head_group[1],
        head_group[2],
        state_in,
    )
    outputs, pull, auxiliary = jax.vjp(head_mix, *primals, has_aux=True)
    running, queries = auxiliary
    grad_mixed = grad_head.astype(jnp.float32)
    length = grad_mixed.shape[0]
    local_grad = jnp.einsum(
        "th,thp,tn->hpn",
        jnp.exp(running),
        grad_mixed.reshape(length, head_count, P_SIZE),
        queries,
        precision=highest,
    )
    identity = (jnp.ones_like(decay_total), jnp.zeros_like(local_grad))
    later_grad = prefix((decay_total, local_grad), "seq", combine_states, identity)[1]
    grad_running = decay_total * jnp.sum(state_in * later_grad, axis=(1, 2))
    (
        grad_block,
        grad_rim,
        grad_conv_group,
        grad_bias_group,
        grad_step_raw,
        grad_bias_heads,
        grad_decay_heads,
        grad_skip_heads,
        unused_grad,
    ) = pull((grad_mixed, later_grad, grad_running))
    rim_grad = shifted(grad_rim, "seq", -1)
    rim_width = rim_grad.shape[0]
    grad_block = jnp.concatenate(
        [grad_block[: length - rim_width], grad_block[length - rim_width :] + rim_grad], axis=0
    )
    back_inner = grad_block[:, :group_width].astype(jnp.bfloat16)
    back_shared = grad_block[:, group_width:].astype(jnp.bfloat16)
    back_step = grad_step_raw.astype(jnp.bfloat16)
    token_inner, token_step, token_shared = (
        lax.all_to_all(back_inner, "head", split_axis=0, concat_axis=1, tiled=True),
        lax.all_to_all(back_step, "head", split_axis=0, concat_axis=1, tiled=True),
        lax.all_to_all(back_shared, "head", split_axis=0, concat_axis=1, tiled=True),
    )
    token_count = token_inner.shape[0]
    grad_shared = jnp.sum(
        token_shared.astype(jnp.float32).reshape(token_count, lax.axis_size("head"), -1), axis=1
    ).astype(jnp.bfloat16)
    grad_proj = jnp.concatenate([grad_gate, token_inner], axis=1)
    grad_gate_inner = contract_rows(normed, grad_proj)
    grad_shared_bc = contract_rows(normed, grad_shared)
    grad_step_proj = contract_rows(normed, token_step)
    grad_normed = (
        contract_cols(grad_proj, gate_inner)
        + contract_cols(grad_shared, shared_bc)
        + contract_cols(token_step, step_proj)
    )
    residual = feed.astype(jnp.float32)
    scale_in = rms_scale(residual)
    unit_in = residual * scale_in
    grad_input_gain = jnp.sum(grad_normed * unit_in, axis=0)
    grad_unit_in = grad_normed * input_gain.astype(jnp.float32)[None, :]
    grad_residual = incoming.astype(jnp.float32) + scale_in * (
        grad_unit_in - unit_in * jnp.mean(unit_in * grad_unit_in, axis=-1, keepdims=True)
    )
    width = conv_weight.shape[0]
    conv_inner = lax.dynamic_update_slice_in_dim(
        jnp.zeros((width, inner_width), jnp.float32),
        grad_conv_group[:, :group_width],
        group_index * group_width,
        1,
    )
    grad_conv_weight = jnp.concatenate([conv_inner, grad_conv_group[:, group_width:]], axis=1)
    bias_inner = lax.dynamic_update_slice_in_dim(
        jnp.zeros((inner_width,), jnp.float32),
        grad_bias_group[:group_width],
        group_index * group_width,
        0,
    )
    grad_conv_bias = jnp.concatenate([bias_inner, grad_bias_group[group_width:]])
    total_heads = head_params[0].shape[0]
    head_grads = tuple(
        (
            lax.dynamic_update_slice_in_dim(
                jnp.zeros((total_heads,), jnp.float32), values, group_index * head_count, 0
            )
            for values in (grad_bias_heads, grad_decay_heads, grad_skip_heads)
        )
    )
    weight_grads = (
        grad_input_gain,
        grad_gate_inner,
        grad_shared_bc,
        grad_step_proj,
        grad_conv_weight,
        grad_conv_bias,
        grad_output_gain,
        grad_out_proj,
    )
    return (grad_residual.astype(jnp.bfloat16), weight_grads, head_grads)


def add_trees(total, extra):
    if total is None:
        return extra
    return jax.tree.map(lambda left, right: left + right, total, extra)


def guarded(usable, compute):
    computed = compute()
    return jax.tree.map(lambda values: jnp.where(usable, values, jnp.zeros_like(values)), computed)


def per_device(
    tokens_in,
    cotangent,
    input_gain,
    gate_inner,
    shared_bc,
    step_proj,
    conv_weight,
    conv_bias,
    step_bias,
    decay_log,
    skip_gain,
    output_gain,
    out_proj,
):
    packed = (
        input_gain,
        gate_inner,
        shared_bc,
        step_proj,
        conv_weight,
        conv_bias,
        output_gain,
        out_proj,
    )
    head_params = (step_bias[0], decay_log[0], skip_gain[0])
    whole = fetch_weights(packed)
    section_index = lax.axis_index("section")
    micro = tokens_in.shape[0]
    received = jnp.zeros(tokens_in.shape[1:], jnp.bfloat16)
    results = []
    keeps = []
    for moment in range(micro + 1):
        feed = jnp.where(section_index == 0, tokens_in[min(moment, micro - 1)], received)
        forward_batch = moment - section_index
        forward_usable = jnp.logical_and(forward_batch >= 0, forward_batch < micro)
        result, kept = guarded(forward_usable, lambda: layer_forward(feed, whole, head_params))
        results.append(result)
        keeps.append(kept)
        if moment < micro:
            received = shifted(result, "section", 1)
    stacked = jax.tree.map(lambda *values: jnp.stack(values), *keeps)
    sent_back = jnp.zeros(tokens_in.shape[1:], jnp.bfloat16)
    grad_feeds = []
    shard_sum = None
    head_sum = None
    for moment in range(micro + 1):
        batch_index = moment - 1 + section_index
        usable = jnp.logical_and(batch_index >= 0, batch_index < micro)
        forward_moment = jnp.clip(moment - 1 + 2 * section_index, 0, micro)
        kept = jax.tree.map(
            lambda values: lax.dynamic_index_in_dim(values, forward_moment, 0, keepdims=False),
            stacked,
        )
        incoming = jnp.where(section_index == 1, cotangent[min(moment, micro - 1)], sent_back)
        back_weights = fetch_weights(packed)
        grad_feed, weight_grads, head_grads = guarded(
            usable, lambda: layer_backward(incoming, kept, back_weights, head_params)
        )
        grad_feeds.append(grad_feed)
        if moment < micro:
            sent_back = shifted(grad_feed, "section", -1)
        head_sum = add_trees(head_sum, head_grads)
        shard_sum = add_trees(shard_sum, reduce_grads(weight_grads))
    head_total = lax.psum(head_sum, ("seq", "head"))
    layer_out = lax.dynamic_slice_in_dim(jnp.stack(results), section_index, micro, 0)
    grad_in = lax.dynamic_slice_in_dim(jnp.stack(grad_feeds), 1 - section_index, micro, 0)
    return (
        layer_out[None],
        grad_in[None],
        shard_sum[0][None],
        shard_sum[1][None],
        shard_sum[2][None],
        shard_sum[3][None],
        shard_sum[4][None],
        shard_sum[5][None],
        head_total[0][None],
        head_total[1][None],
        head_total[2][None],
        shard_sum[6][None],
        shard_sum[7][None],
    )


def solution(mesh):
    placed = (
        P(None, ("seq", "head"), None),
        P(None, ("seq", "head"), None),
        P("section", ("seq", "head")),
        P("section", ("seq", "head"), None),
        P("section", ("seq", "head"), None),
        P("section", ("seq", "head"), None),
        P("section", None, ("seq", "head")),
        P("section", ("seq", "head")),
        P("section", None),
        P("section", None),
        P("section", None),
        P("section", ("seq", "head")),
        P("section", ("seq", "head"), None),
    )
    return jax.shard_map(
        per_device,
        mesh=mesh,
        in_specs=placed,
        out_specs=(
            P("section", None, ("seq", "head"), None),
            P("section", None, ("seq", "head"), None),
            P("section", ("seq", "head")),
            P("section", ("seq", "head"), None),
            P("section", ("seq", "head"), None),
            P("section", ("seq", "head"), None),
            P("section", None, ("seq", "head")),
            P("section", ("seq", "head")),
            P("section", None),
            P("section", None),
            P("section", None),
            P("section", ("seq", "head")),
            P("section", ("seq", "head"), None),
        ),
        check_vma=False,
    )
```

profile of v0, /device:TPU:103, one launch (start us, length us, event | category | flops | bytes accessed | tf_op | source)
XLA Modules:
  0.0 3635.2 jit_solution(11803016138533142955)
XLA Ops:
  13.8 260.4 %all-reduce.54 = (bf16[1536]{0:T(1024)(128)(2,1)S(1)}, bf16[3328]{0:T(1024)(128)(2,1)S(1)}, bf16[3072]{0:T(1024)(128)(2,1)}) all-reduce(bf16[1536]{0:T(1024)(128)(2,1)S(1)} %dynamic-update-slice.15, bf16[3328]{0:T(1024)(128)(2,1)S(1)} %dynamic-update-slice.16, ...), channel_id=1, replica_groups=mesh['section'=2,'seq'=16,'head'=4] {'seq','head'}, use_global_device_ids=true, to_apply=%add.45 | all-reduce | flops 7936 | bytes 31744
  274.1 145.9 %all_gather.53 = bf16[1,1536,48]{2,1,0:T(8,128)(2,1)S(1)} all-gather(bf16[1,24,48]{2,1,0:T(8,128)(2,1)} %param.49), channel_id=1, replica_groups=mesh['section'=2,'seq'=16,'head'=4] {'seq','head'}, dimensions={1}, use_global_device_ids=true | all-gather | bytes 149760 | tf_op jit(solution)/shard_map/all_gather | solution.py:198
  427.4 151.5 %all_gather.112 = bf16[1,4,3328]{1,0,2:T(2,128)(2,1)S(1)} all-gather(bf16[1,4,52]{1,0,2:T(2,128)(2,1)S(1)} %copy.955), channel_id=1, replica_groups=mesh['section'=2,'seq'=16,'head'=4] {'seq','head'}, dimensions={2}, use_global_device_ids=true | all-gather | bytes 27040 | tf_op jit(solution)/shard_map/all_gather | solution.py:199
  581.4 148.4 %all_gather.114 = bf16[1,1536,256]{2,1,0:T(8,128)(2,1)S(1)} all-gather(bf16[1,24,256]{2,1,0:T(8,128)(2,1)S(1)} %copy-done.322), channel_id=1, replica_groups=mesh['section'=2,'seq'=16,'head'=4] {'seq','head'}, dimensions={1}, use_global_device_ids=true | all-gather | bytes 798720 | tf_op jit(solution)/shard_map/all_gather | solution.py:197
  737.0 7.9 fusion.253
  758.5 12.5 collective-permute-start
  782.9 35.2 all-gather.6
  823.0 165.2 %all-gather.25.cloned.1.call-done = bf16[192,64,128]{2,1,0:T(8,128)(2,1)} async-done(((bf16[12,64,128]{2,1,0:T(8,128)(2,1)}), bf16[192,64,128]{2,1,0:T(8,128)(2,1)}) %all-gather.25.cloned.1.call-update) | async-done | bytes 3145744 | tf_op jit(solution)/shard_map/all_gather | solution.py:24
  988.2 13.5 while.225
  1003.6 58.1 %while.226 = (s32[]{:T(128)}, f32[12,64,128]{2,1,0:T(8,128)S(1)}, f32[2,256,12,64]{1,0,3,2:T(2,128)}, f32[2,256,12]{1,0,2:T(2,128)}, f32[2,256,12]{1,0,2:T(2,128...) while((s32[]{:T(128)}, f32[12,64,128]{2,1,0:T(8,128)S(1)}, ...), condition=%wide.region_8.9_spmd, body=%wide.region_5.8_spmd.sunk | while | flops 1313806336 | bytes 11393157 | solution.py:110
  1016.0 16.7 dynamic_update_slice.238
  1045.0 16.7 dynamic_update_slice.238
  1074.6 8.4 all-to-all-done.3
  1136.3 9.0 all-to-all-done.5
  1162.0 16.0 all-gather.7
  1182.2 28.8 all-gather.27.cloned.1.call-done
  1211.0 13.5 while.227
  1226.3 54.7 %while.228 = (s32[]{:T(128)}, f32[12,64,128]{2,1,0:T(8,128)S(1)}, f32[2,256,12,64]{1,0,3,2:T(2,128)}, f32[2,256,12]{1,0,2:T(2,128)S(1)}, f32[2,256,12]{1,0,2:T(2...) while((s32[]{:T(128)}, f32[12,64,128]{2,1,0:T(8,128)S(1)}, ...), condition=%wide.region_18.19_spmd, body=%wide.region_15.18_spmd.sunk | while | flops 1313806336 | bytes 11397253 | solution.py:110
  1236.9 16.7 dynamic_update_slice.239
  1264.3 16.7 dynamic_update_slice.239
  1292.4 8.4 all-to-all-done.7
  1324.2 7.9 fusion.249
  1383.7 15.5 all-gather.8
  1404.1 28.1 all-gather.29.cloned.1.call-done
  1432.2 13.7 while.229
  1447.7 71.3 %while.230 = (s32[]{:T(128)}, f32[12,64,128]{2,1,0:T(8,128)S(1)}, f32[2,256,12,64]{1,0,3,2:T(2,128)}, f32[2,256,12]{1,0,2:T(2,128)}, f32[2,256,12]{1,0,2:T(2,128...) while((s32[]{:T(128)}, f32[12,64,128]{2,1,0:T(8,128)S(1)}, ...), condition=%wide.region_28.29_spmd, body=%wide.region_25.28_spmd.sunk | while | flops 1313806336 | bytes 14280893 | solution.py:110
  1466.7 16.7 dynamic_update_slice.240
  1502.3 16.7 dynamic_update_slice.240
  1571.4 9.7 fusion.341
  1590.9 18.6 all-gather.9
  1628.5 13.5 all-gather.31.cloned.1.call-done
  1655.0 10.8 while.231
  1670.2 110.1 %while.237 = (s32[]{:T(128)}, f32[12,64,128]{2,1,0:T(8,128)}, f32[2,256,12,64]{1,0,3,2:T(2,128)}, f32[2,256,12]{1,0,2:T(2,128)}, f32[2,256,128]{2,1,0:T(8,128)},...) while((s32[]{:T(128)}, f32[12,64,128]{2,1,0:T(8,128)}, ...), condition=%wide.region_49.51_spmd.clone, body=%wide.region_37.50_spmd.clone.sunk | while | flops 3038771200 | bytes 30768016 | solution.py:110
  1699.0 16.7 dynamic_update_slice.246
  1754.3 16.7 dynamic_update_slice.246
  1844.7 13.9 fusion.247
  1870.2 8.1 multiply_reduce_fusion.25
  1888.4 10.0 all-to-all-done.16
  1905.0 31.8 all-gather.10
  1952.1 16.2 all-gather.33.cloned.1.call-done
  1983.9 10.9 while.233
  1999.2 110.1 %while.238 = (s32[]{:T(128)}, f32[12,64,128]{2,1,0:T(8,128)}, f32[2,256,12,64]{1,0,3,2:T(2,128)}, f32[2,256,12]{1,0,2:T(2,128)}, f32[2,256,128]{2,1,0:T(8,128)},...) while((s32[]{:T(128)}, f32[12,64,128]{2,1,0:T(8,128)}, ...), condition=%wide.region_79.81_spmd.clone, body=%wide.region_67.80_spmd.clone.sunk | while | flops 3038771200 | bytes 30768016 | solution.py:110
  2027.9 16.7 dynamic_update_slice.251
  2083.2 16.7 dynamic_update_slice.251
  2171.4 13.0 fusion.245
  2213.5 9.8 all-to-all-done.20
  2232.3 31.8 all-gather.11
  2283.3 12.4 all-gather.35.cloned.1.call-done
  2313.3 10.8 while.235
  2328.5 106.6 %while.239 = (s32[]{:T(128)}, f32[12,64,128]{2,1,0:T(8,128)}, f32[2,256,12,64]{1,0,3,2:T(2,128)}, f32[2,256,12]{1,0,2:T(2,128)}, f32[2,256,128]{2,1,0:T(8,128)},...) while((s32[]{:T(128)}, f32[12,64,128]{2,1,0:T(8,128)}, ...), condition=%wide.region_109.111_spmd.clone, body=%wide.region_97.110_spmd.clone.sunk | while | flops 3038771200 | bytes 30768016 | solution.py:110
  2355.5 16.7 dynamic_update_slice.256
  2409.0 16.7 dynamic_update_slice.256
  2501.5 13.7 fusion.243
  2529.7 10.4 fusion.481
  2540.1 9.4 fusion.479
  2549.5 21.1 add_add_fusion.1
  2570.7 16.3 fusion.430
  2587.0 14.9 fusion.431
  2601.9 38.5 %add_add_fusion = f32[1536,6144]{1,0:T(8,128)} fusion(f32[1536,6144]{1,0:T(8,128)} %fusion.430, f32[1536,6144]{1,0:T(8,128)} %fusion.431, pred[]{:T(512)S(6)} %and.26, pred[]{:T(512)S(6)} %and.25, pred[]{:T(512)S(6)} %and.24, bf16[128,3072]{1,0:T(8,128)(2,1)S(1)} %bitcast.1923, bf16[128,3072]{1,0:T(8,128)(2,1)S(1)} %copy-done.93, ...), kind=kOutput, calls=%fused_computation.396 | convolution fusion | flops 2466250752 | bytes 115212296 | tf_op jit(solution)/shard_map/dot_general | solution.py:221
  2650.6 14.6 all-reduce.57.cloned.1.call-done
  2670.3 215.9 %reduce-scatter.14.cloned.1.call-done = f32[24,48]{1,0:T(8,128)} async-done(((f32[1536,48]{1,0:T(8,128)}), f32[24,48]{1,0:T(8,128)}) %reduce-scatter.14.cloned.1.call-update) | async-done | bytes 4624
  2886.2 221.3 %reduce-scatter.10.cloned.1.call-done = f32[24,256]{1,0:T(8,128)} async-done(((f32[1536,256]{1,0:T(8,128)}), f32[24,256]{1,0:T(8,128)}) %reduce-scatter.10.cloned.1.call-update) | async-done | bytes 24592 | tf_op jit(solution)/shard_map/reduce_scatter | solution.py:211
  3107.5 241.2 %reduce-scatter.12.cloned.1.call-done = f32[48,1536]{1,0:T(8,128)} async-done(((f32[3072,1536]{1,0:T(8,128)}), f32[48,1536]{1,0:T(8,128)}) %reduce-scatter.12.cloned.1.call-update) | async-done | bytes 294928 | tf_op jit(solution)/shard_map/reduce_scatter | solution.py:216
  3348.7 276.4 %reduce-scatter.8.cloned.1.call-done = f32[24,6144]{1,0:T(8,128)} async-done(((f32[1536,6144]{1,0:T(8,128)}), f32[24,6144]{1,0:T(8,128)}) %reduce-scatter.8.cloned.1.call-update) | async-done | bytes 589840 | tf_op jit(solution)/shard_map/reduce_scatter | solution.py:210
  (2089 shorter events, 1089.8 us)
Async XLA Ops:
  7.2 722.9 %copy-start = (f32[1,48]{1,0:T(1,128)S(1)}, f32[1,48]{1,0:T(1,128)}, u32[]{:S(2)}) copy-start(f32[1,48]{1,0:T(1,128)} %param.52) | copy-start | bytes 580
  7.2 420.1 %copy-start.372 = (bf16[1,4,52]{2,1,0:T(4,128)(2,1)S(1)}, bf16[1,4,52]{2,1,0:T(4,128)(2,1)}, u32[]{:S(2)}) copy-start(bf16[1,4,52]{2,1,0:T(4,128)(2,1)} %param.50) | copy-start | bytes 1252
  7.2 729.8 %all-gather.21.cloned.1.call-start = ((), (), s32[]{:S(2)}) async-start(), calls=%async_computation.28 | async-start | bytes 19169280 | tf_op jit(solution)/shard_map/all_gather | solution.py:196
  274.1 462.9 %copy-start.142 = (f32[1536]{0:T(1024)}, f32[1536]{0:T(1024)S(1)}, u32[]{:S(2)}) copy-start(f32[1536]{0:T(1024)S(1)} %mul.2122) | copy-start | bytes 18436
  421.4 315.7 %copy-start.333 = (f32[128]{0:T(128)}, f32[128]{0:T(128)S(1)}, u32[]{:S(2)}) copy-start(f32[128]{0:T(128)S(1)} %add_rsqrt_fusion.11) | copy-start | bytes 1540
  422.7 158.0 %copy-start.373 = (f32[1,48]{1,0:T(1,128)S(1)}, f32[1,48]{1,0:T(1,128)}, u32[]{:S(2)}) copy-start(f32[1,48]{1,0:T(1,128)} %param.53) | copy-start | bytes 580
  422.7 158.6 %copy-start.322 = (bf16[1,24,256]{2,1,0:T(8,128)(2,1)S(1)}, bf16[1,24,256]{2,1,0:T(8,128)(2,1)}, u32[]{:S(2)}) copy-start(bf16[1,24,256]{2,1,0:T(8,128)(2,1)} %param.48) | copy-start | bytes 36868
  423.3 306.9 %all-to-all-start = ((bf16[128,4,12]{0,2,1:T(8,128)(2,1)}), bf16[128,4,12]{0,2,1:T(8,128)(2,1)S(1)}, u32[]{:S(2)}, u32[]{:S(2)}) async-start(bf16[128,4,12]{0,2,1:T(8,128)(2,1)} %all_to_all.282), calls=%async_computation | async-start | bytes 32768 | tf_op jit(solution)/shard_map/all_to_all | solution.py:249
  427.4 302.4 %copy-start.89 = (bf16[2,128,1536]{2,1,0:T(8,128)(2,1)S(1)}, bf16[2,128,1536]{2,1,0:T(8,128)(2,1)}, u32[]{:S(2)}) copy-start(bf16[2,128,1536]{2,1,0:T(8,128)(2,1)} %param.44) | copy-start | bytes 2359300
  581.3 236.8 %copy-start.291 = (f32[12]{0:T(128)}, f32[12]{0:T(128)S(1)}, u32[]{:S(2)}) copy-start(f32[12]{0:T(128)S(1)} %get-tuple-element.2645) | copy-start | bytes 148
  581.3 191.1 %copy-start.264 = (f32[1024]{0:T(1024)}, f32[1024]{0:T(1024)S(1)}, u32[]{:S(2)}) copy-start(f32[1024]{0:T(1024)S(1)} %pad_maximum_fusion.27) | copy-start | bytes 12292
  581.4 191.0 %copy-start.204 = (f32[1,1024]{1,0:T(1,128)}, f32[1,1024]{1,0:T(1,128)S(1)}, u32[]{:S(2)}) copy-start(f32[1,1024]{1,0:T(1,128)S(1)} %get-tuple-element.2788) | copy-start | bytes 12292
  581.4 191.0 %copy-start.206 = (f32[1,1024]{1,0:T(1,128)}, f32[1,1024]{1,0:T(1,128)S(1)}, u32[]{:S(2)}) copy-start(f32[1,1024]{1,0:T(1,128)S(1)} %get-tuple-element.2789) | copy-start | bytes 12292
  581.4 191.0 %copy-start.213 = (f32[1,1024]{1,0:T(1,128)}, f32[1,1024]{1,0:T(1,128)S(1)}, u32[]{:S(2)}) copy-start(f32[1,1024]{1,0:T(1,128)S(1)} %get-tuple-element.2790) | copy-start | bytes 12292
  581.4 191.0 %copy-start.220 = (f32[1,1024]{1,0:T(1,128)}, f32[1,1024]{1,0:T(1,128)S(1)}, u32[]{:S(2)}) copy-start(f32[1,1024]{1,0:T(1,128)S(1)} %get-tuple-element.2791) | copy-start | bytes 12292
  729.8 387.3 %copy-start.68 = (bf16[1,1536,256]{2,1,0:T(8,128)(2,1)}, bf16[1,1536,256]{2,1,0:T(8,128)(2,1)S(1)}, u32[]{:S(2)}) copy-start(bf16[1,1536,256]{2,1,0:T(8,128)(2,1)S(1)} %all_gather.114) | copy-start | bytes 2359300
  730.9 16.8 all-to-all-start.2
  747.7 10.8 all-to-all-start.1
  752.0 236.2 %all-gather.25.cloned.1.call-start = ((), (), s32[]{:S(2)}) async-start(), calls=%async_computation.30 | async-start | bytes 3342336 | tf_op jit(solution)/shard_map/all_gather | solution.py:24
  758.5 13.2 collective-permute-start
  781.7 305.9 %all-gather.23.cloned.1.call-start = ((), (), s32[]{:S(2)}) async-start(), calls=%async_computation.29 | async-start | bytes 9584640 | tf_op jit(solution)/shard_map/all_gather | solution.py:202
  782.7 285.0 %copy-start.231 = (f32[768]{0:T(1024)}, f32[768]{0:T(1024)S(1)}, u32[]{:S(2)}) copy-start(f32[768]{0:T(1024)S(1)} %mul.1903) | copy-start | bytes 9220
  1070.3 12.6 all-to-all-start.3
  1074.6 230.9 %copy-start.133 = (f32[3072]{0:T(1024)}, f32[3072]{0:T(1024)S(1)}, u32[]{:S(2)}) copy-start(f32[3072]{0:T(1024)S(1)} %mul.2123) | copy-start | bytes 36868
  1094.2 5.9 collective-permute-start.1
  1103.7 16.1 all-to-all-start.4
  1120.5 9.5 all-to-all-start.6
  1130.0 15.3 all-to-all-start.5
  1135.3 75.7 %all-gather.27.cloned.1.call-start = ((), (), s32[]{:S(2)}) async-start(), calls=%async_computation.31 | async-start | bytes 3342336 | tf_op jit(solution)/shard_map/all_gather | solution.py:24
  1145.4 6.5 collective-permute-start.2
  1288.2 12.6 all-to-all-start.7
  1311.4 5.7 collective-permute-start.3
  1319.0 16.0 all-to-all-start.8
  1335.7 8.0 all-to-all-start.10
  1343.8 12.6 all-to-all-start.9
  1349.1 83.1 %all-gather.29.cloned.1.call-start = ((), (), s32[]{:S(2)}) async-start(), calls=%async_computation.32 | async-start | bytes 3342336 | tf_op jit(solution)/shard_map/all_gather | solution.py:24
  1361.2 6.6 collective-permute-start.4
  1526.3 13.4 all-to-all-start.11
  1565.7 15.5 all-to-all-start.12
  1571.0 71.1 %all-gather.31.cloned.1.call-start = ((), (), s32[]{:S(2)}) async-start(), calls=%async_computation.33 | async-start | bytes 3342336 | tf_op jit(solution)/shard_map/all_gather | solution.py:46
  1799.0 21.9 collective-permute-start.5
  1816.7 6.7 all-to-all-start.15
  1823.3 8.9 all-to-all-start.14
  1832.3 12.3 all-to-all-start.13
  1861.8 8.3 collective-permute-start.6
  1883.0 15.5 all-to-all-start.16
  1888.2 80.1 %all-gather.33.cloned.1.call-start = ((), (), s32[]{:S(2)}) async-start(), calls=%async_computation.34 | async-start | bytes 3342336 | tf_op jit(solution)/shard_map/all_gather | solution.py:46
  2125.8 22.0 collective-permute-start.7
  2143.6 6.7 all-to-all-start.19
  2150.3 8.9 all-to-all-start.18
  2159.2 12.1 all-to-all-start.17
  2187.1 8.3 collective-permute-start.8
  2207.8 15.5 all-to-all-start.20
  2213.1 82.6 %all-gather.35.cloned.1.call-start = ((), (), s32[]{:S(2)}) async-start(), calls=%async_computation.35 | async-start | bytes 3342336 | tf_op jit(solution)/shard_map/all_gather | solution.py:46
  2457.9 21.5 collective-permute-start.9
  2470.1 10.9 all-to-all-start.23
  2481.0 8.0 all-to-all-start.22
  2489.0 12.3 all-to-all-start.21
  2494.3 170.9 %all-reduce.57.cloned.1.call-start = ((), (), s32[]{:S(2)}) async-start(), calls=%async_computation.40 | async-start | bytes 183296
  2523.3 362.8 %reduce-scatter.14.cloned.1.call-start = ((), (), s32[]{:S(2)}) async-start(), calls=%async_computation.39 | async-start | bytes 798720
  2525.8 581.7 %reduce-scatter.10.cloned.1.call-start = ((), (), s32[]{:S(2)}) async-start(), calls=%async_computation.37 | async-start | bytes 1597440 | tf_op jit(solution)/shard_map/reduce_scatter | solution.py:211
  2529.6 819.1 %reduce-scatter.12.cloned.1.call-start = ((), (), s32[]{:S(2)}) async-start(), calls=%async_computation.38 | async-start | bytes 19169280 | tf_op jit(solution)/shard_map/reduce_scatter | solution.py:216
  2570.6 1054.5 %reduce-scatter.8.cloned.1.call-start = ((), (), s32[]{:S(2)}) async-start(), calls=%async_computation.36 | async-start | bytes 38338560 | tf_op jit(solution)/shard_map/reduce_scatter | solution.py:210
  2642.6 985.9 %copy-start.1 = (f32[1,48]{1,0:T(1,128)S(1)}, f32[1,48]{1,0:T(1,128)}, u32[]{:S(2)}) copy-start(f32[1,48]{1,0:T(1,128)} %param.52) | copy-start | bytes 580
  (399 other events, 3144.9 us)
Sparse Core Ops, SparseCore 0:
  10.8 111.4 all-gather.20
  781.8 206.3 all-gather.24
  991.0 81.9 all-gather.22
  1161.9 49.0 all-gather.26
  1380.4 51.7 all-gather.28
  1590.0 51.9 all-gather.30
  1905.0 63.2 all-gather.32
  2232.3 63.2 all-gather.34
  2523.5 141.6 all-reduce.56
  2670.5 215.5 reduce-scatter.13
  2891.7 215.7 reduce-scatter.9
  3113.4 235.3 reduce-scatter.11
  3354.4 270.6 reduce-scatter.7
where the time goes:
time: 3670 us; the launch traced here: 3640 us
  waiting for transfers between devices  1330 us (36%)
  blocking collectives  855 us (23%)
  local copies, waits for them, and re-layouts  512 us (14%)
  matrix products  452 us (12%)
  other arithmetic  285 us (8%)
  starting transfers between devices  168 us (5%)
    reduce_scatter x1, waiting for transfers between devices, reduce_grads(): lax.psum_scatter(grads[1], ('seq', 'head'), scatter_dimension=0, tiled=True)  276 us
    unnamed x1, blocking collectives  260 us
    reduce_scatter x1, waiting for transfers between devices, reduce_grads(): lax.psum_scatter(grads[7], ('seq', 'head'), scatter_dimension=0, tiled=True)  241 us
    unnamed x15, waiting for transfers between devices  232 us
    all_gather x3, waiting for transfers between devices, carried_in(): lax.all_gather(a.astype(kind), axis)  222 us
    reduce_scatter x1, waiting for transfers between devices, reduce_grads(): lax.psum_scatter(grads[2], ('seq', 'head'), scatter_dimension=0, tiled=True)  221 us
    dynamic_update_slice x54, local copies, waits for them, and re-layouts, scan_heads(): lax.scan(jax.checkpoint(piece_step), start_state, (to_pieces(inner_heads)...  216 us
    all_gather x1, blocking collectives, fetch_weights(): lax.all_gather(packed[4], ('seq', 'head'), axis=2, tiled=True)  151 us
  transfers between devices with their start and end apart: 47, of which 34 were waited for; matrix products, arithmetic and copies ran while one was open for 11% of the time, Pallas kernels for 0%

commit v1 on v0

v1 whole, which is shorter than its diff:
```python
import jax
import jax.numpy as jnp
from jax import lax
from jax.experimental import pallas as pl
from jax.experimental.pallas import tpu as pltpu
from jax.sharding import PartitionSpec as P

bf16 = jnp.bfloat16
f32 = jnp.float32
HIGHEST = lax.Precision.HIGHEST

D = 1536
DI = 3072
N = 128
GROUP = 768
HALF = 384
HEADS = 12
PIECE = 128
PAIRS = 6
EXTRA = 256
ACT = GROUP + 2 * N
STEP_AT, SMALL_AT, SMALL = 0, 19, 13
VMEM = 40 * 1024 * 1024
epsilon = 1e-05


def from_head(a, k):
    return lax.ppermute(a, "head", [(i, (i - k) % 4) for i in range(4)])


def from_seq(a, dz, dy, wrap):
    pairs = []
    for z in range(4):
        for y in range(4):
            sz, sy = z + dz, y + dy
            if wrap:
                sz, sy = sz % 4, sy % 4
            if 0 <= sz < 4 and 0 <= sy < 4:
                pairs.append((sz * 4 + sy, z * 4 + y))
    return lax.ppermute(a, "seq", pairs)


def swap(a):
    return lax.ppermute(a, "section", [(0, 1), (1, 0)])


def gather_head(a):
    two = from_head(a, 2)
    one, three = from_head(a, 1), from_head(a, 3)
    return [a, one, two, three]


def scatter_head(parts):
    two = from_head(parts[2].astype(bf16), 2)
    one, three = from_head(parts[1].astype(bf16), 3), from_head(parts[3].astype(bf16), 1)
    return parts[0] + one.astype(f32) + two.astype(f32) + three.astype(f32)


def exchange_head(parts, place):
    got = [lax.dynamic_index_in_dim(parts, place, 0, False)]
    for k in (1, 2, 3):
        sent = lax.dynamic_index_in_dim(parts, lax.rem(place + 4 - k, 4), 0, False)
        got.append(from_head(sent, k))
    twice = jnp.stack(got + got)
    return lax.dynamic_slice_in_dim(twice, lax.rem(4 - place, 4), 4, 0)


def unpack_state(a):
    decay = a[N : N + 1].astype(f32) + a[N + 1 : N + 2].astype(f32)
    return decay, a[:N].astype(f32)


def join(earlier, later):
    return earlier[0] * later[0], earlier[1] * later[0] + later[1]


def carried(packed, sign):
    seq = lax.axis_index("seq")
    y = lax.rem(seq, 4)
    ahead = y if sign < 0 else 3 - y
    near = {k: unpack_state(from_seq(packed, 0, sign * k, True)) for k in (2, 1, 3)}
    own = unpack_state(packed)
    before = (jnp.ones_like(own[0]), jnp.zeros_like(own[1]))
    after = own
    for k in (3, 2, 1):
        decay, state = near[k]
        use = k <= ahead
        before = join(before, (jnp.where(use, decay, 1.0), jnp.where(use, state, 0.0)))
        after = join(after, (jnp.where(use, 1.0, decay), jnp.where(use, 0.0, state)))
    whole = join(before, after)
    packed_whole = pack_state(whole[0], whole[1])
    far = {k: unpack_state(from_seq(packed_whole, sign * k, 0, False)) for k in (2, 1, 3)}
    total = jnp.zeros_like(own[1])
    for k in (3, 2, 1):
        decay, state = far[k]
        total = total * decay + state
    return total * before[0] + before[1]


def pack_state(decay, state):
    high = decay.astype(bf16)
    low = (decay - high.astype(f32)).astype(bf16)
    fill = jnp.zeros((14, state.shape[1]), bf16)
    return jnp.concatenate([state.astype(bf16), high, low, fill], axis=0)


def dot(a, b):
    return jnp.dot(a.astype(bf16), b.astype(bf16), preferred_element_type=f32)


def dot_nt(a, b):
    return lax.dot_general(
        a.astype(bf16), b.astype(bf16), (((1,), (1,)), ((), ())), preferred_element_type=f32
    )


def dot_tn(a, b):
    return lax.dot_general(
        a.astype(bf16), b.astype(bf16), (((0,), (0,)), ((), ())), preferred_element_type=f32
    )


def dot_split(a, b):
    high = a.astype(bf16)
    low = (a - high.astype(f32)).astype(bf16)
    return dot(high, b) + dot(low, b)


def lanes(shape):
    return lax.broadcasted_iota(jnp.int32, shape, 1)


def rows(shape):
    return lax.broadcasted_iota(jnp.int32, shape, 0)


def spread(values, j, first):
    return jnp.where(first, values[:, 2 * j : 2 * j + 1], values[:, 2 * j + 1 : 2 * j + 2])


def step_parts(step, hp):
    raw = step + hp[0:1]
    live = lanes(raw.shape) < HEADS
    sizes = jnp.maximum(raw, 0.0) + jnp.log1p(jnp.exp(-jnp.abs(raw)))
    sizes = jnp.where(live, sizes, 0.0)
    return raw, sizes, -jnp.exp(hp[1:2]) * sizes


def scan_kernel(
    place, conv_in, step, rim, taps, hp, skip, pre_out, mixed, query, run, starts, last, packed,
    padded, act, state, carry
):
    k = pl.program_id(0)

    @pl.when(k == 0)
    def _():
        state[...] = jnp.zeros_like(state)
        carry[...] = jnp.zeros_like(carry)
        padded[0:8] = rim[...].astype(f32)

    @pl.when(k > 0)
    def _():
        padded[0:8] = padded[PIECE : PIECE + 8]

    padded[8 : PIECE + 8] = conv_in[...].astype(f32)
    for j in range(ACT // 128):
        cols = slice(128 * j, 128 * j + 128)
        pre = taps[4:5, cols] + taps[0:1, cols] * padded[5 : PIECE + 5, cols]
        for t in range(1, 4):
            pre = pre + taps[t : t + 1, cols] * padded[5 + t : PIECE + 5 + t, cols]
        pre_out[:, cols] = pre
        act[:, cols] = pre * jax.nn.sigmoid(pre)
    raw, sizes, log_decay = step_parts(step[...], hp[...])
    lower = rows((PIECE, PIECE)) >= lanes((PIECE, PIECE))
    start = carry[0:1]
    running = start + jnp.dot(
        lower.astype(f32), log_decay, precision=HIGHEST, preferred_element_type=f32
    )
    run[...] = running
    end = running[PIECE - 1 : PIECE]
    carry[...] = jnp.broadcast_to(end, carry.shape)
    running_t = running.T
    keys = act[:, GROUP : GROUP + N]
    queries = act[:, GROUP + N :].astype(bf16)
    query[...] = queries
    affinity = jnp.where(lower, dot_nt(queries, keys), 0.0)
    keys_t = keys.T.astype(bf16)
    from_start = jnp.exp(running - start)
    to_end = jnp.exp(end - running)
    whole = jnp.exp(end - start)
    total = jnp.exp(end)
    first = lanes((PIECE, 128)) < 64
    first_row = lanes((1, 128)) < 64
    row16 = rows((16, 128))
    for j in range(PAIRS):
        cols = slice(128 * j, 128 * j + 128)
        x = act[:, cols]
        scaled = x * spread(sizes, j, first)
        y = jnp.zeros((PIECE, 128), f32)
        for side in range(2):
            h = 2 * j + side
            gap = jnp.exp(jnp.minimum(running[:, h : h + 1] - running_t[h : h + 1, :], 0.0))
            mine = jnp.where(first if side == 0 else ~first, scaled, 0.0)
            y = y + dot(gap * affinity, mine)
        before = state[:, cols]
        starts[0, :, cols] = before
        y = y + spread(from_start, j, first) * dot(queries, before)
        mixed[:, cols] = y + skip[0:1, cols] * x
        after = spread(whole, j, first_row) * before + dot(
            keys_t, scaled * spread(to_end, j, first)
        )
        state[:, cols] = after
        last[:, cols] = after
        packed[0:N, cols] = after.astype(bf16)
        decay = jnp.broadcast_to(spread(total, j, first_row), (16, 128))
        high = decay.astype(bf16).astype(f32)
        packed[N : N + 16, cols] = jnp.where(
            row16 == 0, high, jnp.where(row16 == 1, decay - high, 0.0)
        ).astype(bf16)


def turned(k, place):
    return lax.rem(k + 4 - place[0], 4)


def scan_local(place, conv_in, step, rim, taps, hp, skip):
    tokens = conv_in.shape[0]

    def whole(shape):
        return pl.BlockSpec(shape, lambda k, place: (0,) * len(shape))

    def piece(width):
        return pl.BlockSpec((PIECE, width), lambda k, place: (turned(k, place), 0))

    return pl.pallas_call(
        scan_kernel,
        grid_spec=pltpu.PrefetchScalarGridSpec(
            num_scalar_prefetch=1,
            grid=(tokens // PIECE,),
            in_specs=[
                piece(ACT),
                piece(128),
                whole((8, ACT)),
                whole((8, ACT)),
                whole((8, 128)),
                whole((8, GROUP)),
            ],
            out_specs=[
                piece(ACT),
                piece(GROUP),
                piece(N),
                piece(128),
                pl.BlockSpec((1, N, GROUP), lambda k, place: (k, 0, 0)),
                whole((N, GROUP)),
                whole((N + 16, GROUP)),
            ],
            scratch_shapes=[
                pltpu.VMEM((PIECE + 8, ACT), f32),
                pltpu.VMEM((PIECE, ACT), f32),
                pltpu.VMEM((N, GROUP), f32),
                pltpu.VMEM((8, 128), f32),
            ],
        ),
        out_shape=[
            jax.ShapeDtypeStruct((tokens, ACT), f32),
            jax.ShapeDtypeStruct((tokens, GROUP), f32),
            jax.ShapeDtypeStruct((tokens, N), bf16),
            jax.ShapeDtypeStruct((tokens, 128), f32),
            jax.ShapeDtypeStruct((tokens // PIECE, N, GROUP), f32),
            jax.ShapeDtypeStruct((N, GROUP), f32),
            jax.ShapeDtypeStruct((N + 16, GROUP), bf16),
        ],
        compiler_params=pltpu.CompilerParams(vmem_limit_bytes=VMEM),
        cost_estimate=pl.CostEstimate(
            flops=1_000_000_000, bytes_accessed=8_000_000, transcendentals=1_500_000
        ),
        name="scan_local",
    )(place, conv_in, step, rim, taps, hp, skip)


def gate_kernel(mixed, run, query, entering, gate, gain, mixed_out, normed, square):
    decay = jnp.exp(run[...])
    queries = query[...]
    first = lanes((PIECE, 128)) < 64
    total = jnp.zeros((PIECE, 1), f32)
    for j in range(PAIRS):
        cols = slice(128 * j, 128 * j + 128)
        y = mixed[:, cols] + spread(decay, j, first) * dot(queries, entering[:, cols])
        mixed_out[:, cols] = y
        pre = gate[:, cols]
        gated = y.astype(bf16).astype(f32) * (pre * jax.nn.sigmoid(pre))
        total = total + jnp.sum(gated * gated, axis=1, keepdims=True)
        normed[:, cols] = (gated * gain[0:1, cols]).astype(bf16)
    square[...] = jnp.broadcast_to(total, square.shape)


def gate_out(mixed, run, query, entering, gate, gain):
    tokens = mixed.shape[0]

    def whole(shape):
        return pl.BlockSpec(shape, lambda k: (0, 0))

    def piece(width):
        return pl.BlockSpec((PIECE, width), lambda k: (k, 0))

    return pl.pallas_call(
        gate_kernel,
        grid=(tokens // PIECE,),
        in_specs=[
            piece(GROUP),
            piece(128),
            piece(N),
            whole((N, GROUP)),
            piece(GROUP),
            whole((8, GROUP)),
        ],
        out_specs=[piece(GROUP), piece(GROUP), piece(128)],
        out_shape=[
            jax.ShapeDtypeStruct((tokens, GROUP), f32),
            jax.ShapeDtypeStruct((tokens, GROUP), bf16),
            jax.ShapeDtypeStruct((tokens, 128), f32),
        ],
        compiler_params=pltpu.CompilerParams(vmem_limit_bytes=VMEM),
        cost_estimate=pl.CostEstimate(
            flops=110_000_000, bytes_accessed=6_500_000, transcendentals=400_000
        ),
        name="gate_out",
    )(mixed, run, query, entering, gate, gain)


def gate_back_kernel(
    grad, gate, mixed, scale, run, query, gain, decay, grad_scan, grad_gate, normed, packed, state
):
    k = pl.program_id(0)

    @pl.when(k == 0)
    def _():
        state[...] = jnp.zeros_like(state)

    grown = jnp.exp(run[...])
    queries_t = query[...].astype(f32).T.astype(bf16)
    first = lanes((PIECE, 128)) < 64
    s_out, mean = scale[:, 0:1], scale[:, 1:2]
    row16 = rows((16, 128))
    for j in range(PAIRS):
        cols = slice(128 * j, 128 * j + 128)
        pre = gate[:, cols]
        sig = jax.nn.sigmoid(pre)
        out = mixed[:, cols].astype(bf16).astype(f32)
        unit = out * (pre * sig) * s_out
        gain_j = gain[0:1, cols]
        gated = s_out * (grad[:, cols] * gain_j - unit * mean)
        scan = (gated * (pre * sig)).astype(bf16)
        grad_scan[:, cols] = scan
        grad_gate[:, cols] = (gated * out * sig * (1.0 + pre * (1.0 - sig))).astype(bf16)
        normed[:, cols] = (unit * gain_j).astype(bf16)
        total = state[:, cols] + dot(queries_t, spread(grown, j, first) * scan.astype(f32))
        state[:, cols] = total
        packed[0:N, cols] = total.astype(bf16)
        fall = jnp.broadcast_to(decay[0:1, cols], (16, 128))
        high = fall.astype(bf16).astype(f32)
        packed[N : N + 16, cols] = jnp.where(
            row16 == 0, high, jnp.where(row16 == 1, fall - high, 0.0)
        ).astype(bf16)


def gate_back(grad, gate, mixed, scale, run, query, gain, decay):
    tokens = mixed.shape[0]

    def whole(shape):
        return pl.BlockSpec(shape, lambda k: (0, 0))

    def piece(width):
        return pl.BlockSpec((PIECE, width), lambda k: (k, 0))

    return pl.pallas_call(
        gate_back_kernel,
        grid=(tokens // PIECE,),
        in_specs=[
            piece(GROUP),
            piece(GROUP),
            piece(GROUP),
            piece(128),
            piece(128),
            piece(N),
            whole((8, GROUP)),
            whole((8, GROUP)),
        ],
        out_specs=[piece(GROUP), piece(GROUP), piece(GROUP), whole((N + 16, GROUP))],
        out_shape=[
            jax.ShapeDtypeStruct((tokens, GROUP), bf16),
            jax.ShapeDtypeStruct((tokens, GROUP), bf16),
            jax.ShapeDtypeStruct((tokens, GROUP), bf16),
            jax.ShapeDtypeStruct((N + 16, GROUP), bf16),
        ],
        scratch_shapes=[pltpu.VMEM((N, GROUP), f32)],
        compiler_params=pltpu.CompilerParams(vmem_limit_bytes=VMEM),
        cost_estimate=pl.CostEstimate(
            flops=120_000_000, bytes_accessed=8_000_000, transcendentals=400_000
        ),
        name="gate_back",
    )(grad, gate, mixed, scale, run, query, gain, decay)


def scan_back_kernel(
    place, conv_in, pre_in, step, run, grad, mixed, starts, last, entering, leaving, rim, taps, hp,
    skip, grad_in, tail, grad_step, rim_grad, grad_taps, grad_hp, act, delta, state, after, skip_sum
):
    k = pl.program_id(0)
    count = pl.num_programs(0)
    first = lanes((PIECE, 128)) < 64
    first_row = lanes((1, 128)) < 64
    raw, sizes, log_decay = step_parts(step[...], hp[...])
    running = run[...]
    start = running[0:1] - log_decay[0:1]
    end = running[PIECE - 1 : PIECE]
    from_start = jnp.exp(running - start)
    to_end = jnp.exp(end - running)
    whole = jnp.exp(end - start)
    before_all = jnp.exp(start)
    until_end = jnp.exp(end)

    @pl.when(k == 0)
    def _():
        delta[PIECE : PIECE + 8] = jnp.zeros((8, ACT), f32)
        grad_taps[...] = jnp.zeros_like(grad_taps)
        grad_hp[...] = jnp.zeros_like(grad_hp)
        skip_sum[...] = jnp.zeros_like(skip_sum)
        for j in range(PAIRS):
            cols = slice(128 * j, 128 * j + 128)
            state[:, cols] = leaving[:, cols]
            after[:, cols] = spread(until_end, j, first_row) * entering[:, cols] + last[:, cols]

    @pl.when(k > 0)
    def _():
        delta[PIECE : PIECE + 8] = delta[0:8]

    for j in range(ACT // 128):
        cols = slice(128 * j, 128 * j + 128)
        pre = pre_in[:, cols]
        act[:, cols] = pre * jax.nn.sigmoid(pre)

    upper = rows((PIECE, PIECE)) <= lanes((PIECE, PIECE))
    keys = act[:, GROUP : GROUP + N].astype(bf16)
    queries32 = act[:, GROUP + N :]
    queries = queries32.astype(bf16)
    queries_t = queries32.T.astype(bf16)
    affinity = jnp.where(upper, dot_nt(keys, queries), 0.0)
    running_t = running.T
    grad_affinity = jnp.zeros((PIECE, PIECE), f32)
    grad_keys = jnp.zeros((PIECE, N), f32)
    grad_queries = jnp.zeros((PIECE, N), f32)
    inner_sum = jnp.zeros((PIECE, 128), f32)
    outer_sum = jnp.zeros((PIECE, 128), f32)
    bound = jnp.zeros((8, 128), f32)
    for j in range(PAIRS):
        cols = slice(128 * j, 128 * j + 128)
        x = act[:, cols]
        sizes_j = spread(sizes, j, first)
        scaled = x * sizes_j
        dm = grad[:, cols]
        dm32 = dm.astype(f32)
        to_end_j = spread(to_end, j, first)
        back = state[:, cols]
        z = to_end_j * dot(keys, back)
        for side in range(2):
            h = 2 * j + side
            half = first if side == 0 else ~first
            gap = jnp.exp(jnp.minimum(running_t[h : h + 1, :] - running[:, h : h + 1], 0.0))
            mine = jnp.where(half, dm32, 0.0)
            z = z + dot(gap * affinity, mine)
            grad_affinity = grad_affinity + gap * dot_nt(jnp.where(half, scaled, 0.0), dm)
        skip_j = skip[0:1, cols]
        delta[0:PIECE, cols] = sizes_j * z + skip_j * dm32
        skip_sum[0:1, cols] += jnp.sum(dm32 * x, axis=0, keepdims=True)
        heads = (lanes((128, 128)) == 2 * j + (rows((128, 128)) >= 64)).astype(bf16)
        inner_sum = inner_sum + dot_split(x * z, heads)
        outer_sum = outer_sum + dot_split(dm32 * (mixed[:, cols] - skip_j * x), heads)
        after_j = after[:, cols]
        inside = jnp.sum(back * after_j, axis=0, keepdims=True)
        bound = bound + dot_split(jnp.broadcast_to(inside, (8, 128)), heads)
        before = spread(before_all, j, first_row) * entering[:, cols] + starts[0, :, cols]
        after[:, cols] = before
        weighted = spread(from_start, j, first) * dm32
        grad_queries = grad_queries + dot_nt(weighted, before)
        grad_keys = grad_keys + dot_nt(scaled * to_end_j, back)
        state[:, cols] = spread(whole, j, first_row) * back + dot(queries_t, weighted)
    grad_affinity = jnp.where(upper, grad_affinity, 0.0)
    delta[0:PIECE, GROUP : GROUP + N] = grad_keys + dot(grad_affinity, queries)
    delta[0:PIECE, GROUP + N :] = grad_queries + dot(grad_affinity.T, keys)

    flow = outer_sum - sizes * inner_sum
    grad_log = bound[0:1] + jnp.dot(
        upper.astype(f32), flow, precision=HIGHEST, preferred_element_type=f32
    )
    rate = jnp.exp(hp[1:2])
    live = lanes((PIECE, 128)) < HEADS
    grad_raw = jnp.where(live, (inner_sum - rate * grad_log) * jax.nn.sigmoid(raw), 0.0)
    grad_step[...] = grad_raw.astype(bf16)
    grad_hp[0:1] += jnp.sum(grad_raw, axis=0, keepdims=True)
    grad_hp[1:2] += jnp.sum(jnp.where(live, grad_log * log_decay, 0.0), axis=0, keepdims=True)

    for j in range(ACT // 128):
        cols = slice(128 * j, 128 * j + 128)
        pre = pre_in[:, cols]
        sig = jax.nn.sigmoid(pre)
        grown = delta[0:PIECE, cols] * sig * (1.0 + pre * (1.0 - sig))
        delta[0:PIECE, cols] = grown
        grad_taps[4:5, cols] += jnp.sum(grown, axis=0, keepdims=True)
        taken = conv_in[:, cols].astype(f32)
        total = jnp.zeros((PIECE, 128), f32)
        for t in range(4):
            moved = delta[3 - t : 3 - t + PIECE, cols]
            total = total + taps[t : t + 1, cols] * moved
            grad_taps[t : t + 1, cols] += jnp.sum(taken * moved, axis=0, keepdims=True)
        grad_in[:, cols] = total.astype(bf16)

        @pl.when(k == 0)
        def _():
            tail[:, cols] = total[PIECE - 8 :]

    @pl.when(k == count - 1)
    def _():
        for j in range(PAIRS):
            cols = slice(128 * j, 128 * j + 128)
            heads = (lanes((128, 128)) == 2 * j + (rows((128, 128)) >= 64)).astype(bf16)
            sums = dot_split(jnp.broadcast_to(skip_sum[0:1, cols], (8, 128)), heads)
            grad_hp[2:3] += sums[0:1]
        for j in range(ACT // 128):
            cols = slice(128 * j, 128 * j + 128)
            edge = jnp.concatenate([jnp.zeros((8, 128), f32), delta[0:8, cols]], axis=0)
            taken = rim[:, cols].astype(f32)
            total = jnp.zeros((8, 128), f32)
            for t in range(4):
                moved = edge[3 - t : 11 - t]
                total = total + taps[t : t + 1, cols] * moved
                grad_taps[t : t + 1, cols] += jnp.sum(taken * moved, axis=0, keepdims=True)
            rim_grad[:, cols] = total


def scan_back(
    place, conv_in, pre, step, run, grad, mixed, starts, last, entering, leaving, rim, taps, hp, skip
):
    tokens = conv_in.shape[0]
    count = tokens // PIECE

    def whole(shape):
        return pl.BlockSpec(shape, lambda k, place: (0,) * len(shape))

    def piece(width):
        return pl.BlockSpec((PIECE, width), lambda k, place: (turned(count - 1 - k, place), 0))

    return pl.pallas_call(
        scan_back_kernel,
        grid_spec=pltpu.PrefetchScalarGridSpec(
            num_scalar_prefetch=1,
            grid=(count,),
            in_specs=[
                piece(ACT),
                piece(ACT),
                piece(128),
                piece(128),
                piece(GROUP),
                piece(GROUP),
                pl.BlockSpec((1, N, GROUP), lambda k, place: (count - 1 - k, 0, 0)),
                whole((N, GROUP)),
                whole((N, GROUP)),
                whole((N, GROUP)),
                whole((8, ACT)),
                whole((8, ACT)),
                whole((8, 128)),
                whole((8, GROUP)),
            ],
            out_specs=[
                piece(ACT),
                whole((8, ACT)),
                piece(128),
                whole((8, ACT)),
                whole((8, ACT)),
                whole((8, 128)),
            ],
            scratch_shapes=[
                pltpu.VMEM((PIECE, ACT), f32),
                pltpu.VMEM((PIECE + 8, ACT), f32),
                pltpu.VMEM((N, GROUP), f32),
                pltpu.VMEM((N, GROUP), f32),
                pltpu.VMEM((8, GROUP), f32),
            ],
        ),
        out_shape=[
            jax.ShapeDtypeStruct((tokens, ACT), bf16),
            jax.ShapeDtypeStruct((8, ACT), f32),
            jax.ShapeDtypeStruct((tokens, 128), bf16),
            jax.ShapeDtypeStruct((8, ACT), f32),
            jax.ShapeDtypeStruct((8, ACT), f32),
            jax.ShapeDtypeStruct((8, 128), f32),
        ],
        compiler_params=pltpu.CompilerParams(vmem_limit_bytes=VMEM),
        cost_estimate=pl.CostEstimate(
            flops=2_000_000_000, bytes_accessed=9_000_000, transcendentals=2_500_000
        ),
        name="scan_back",
    )(place, conv_in, pre, step, run, grad, mixed, starts, last, entering, leaving, rim, taps, hp,
      skip)


def pick(core, first, second):
    return jnp.where(core == 0, first, second)


def spread_weights(core, head, gate_inner, shared_bc, step_proj, input_gain, small):
    gate = gate_inner[:, :DI].reshape(24, 4, 2, HALF)
    inner = gate_inner[:, DI:].reshape(24, 4, 2, HALF)
    heads = step_proj.reshape(24, 4, HEADS)
    slots = []
    for g in range(4):
        own = heads[:, g]
        slots.append(
            jnp.concatenate(
                [own, own[:, :6], input_gain[:, None], small, jnp.zeros((24, EXTRA - 32), bf16)],
                axis=1,
            )
        )
    halves = []
    for q in range(2):
        pieces = [
            jnp.concatenate(
                [inner[:, g, q], shared_bc if q == 0 else slots[g], gate[:, g, q]], axis=1
            )
            for g in range(4)
        ]
        halves.append(jnp.stack(pieces))
    kept = pick(core, halves[0], halves[1])
    got = swap(pick(core, halves[1], halves[0]))
    layers = [pick(core, kept, got), pick(core, got, kept)]
    return [exchange_head(values, head).reshape(96, HALF + EXTRA + HALF) for values in layers]


def out_pairs():
    pairs = []
    for layer in range(2):
        for z in range(4):
            for y in range(4):
                for x in range(4):
                    source = (layer * 16 + z * 4 + y) * 4 + x
                    place = layer * 8 + (y % 2) * 4 + x
                    pairs.append((source, ((y // 2) * 16 + place) * 4 + z))
    return pairs


def out_back_pairs(layer, part):
    pairs = []
    for core in range(2):
        for j in range(8):
            for group in range(4):
                source = (core * 16 + 2 * j + part) * 4 + group
                target = (layer * 16 + group * 4 + 2 * core + j // 4) * 4 + j % 4
                pairs.append((source, target))
    return pairs


EVERY = ("section", "seq", "head")


def gather_seq(a):
    return lax.all_gather(a, "seq", axis=0, tiled=True)


def layer_params(core, head, slot, step_bias, decay_log, skip_gain):
    small = slot[:, SMALL_AT : SMALL_AT + SMALL].reshape(64, 24 * SMALL).astype(f32)
    conv = small[:, :208].reshape(64, 4, 52).transpose(1, 0, 2).reshape(4, DI + 2 * N)
    bias = small[:, 208:260].reshape(1, DI + 2 * N)
    gain = small[:, 260:308].reshape(1, DI)
    taps = jnp.concatenate([conv, bias, jnp.zeros((3, DI + 2 * N), f32)], axis=0)

    def grouped(values, width):
        own = lax.dynamic_slice_in_dim(values, (2 * head + core) * width, width, 1)
        other = lax.dynamic_slice_in_dim(values, (2 * head + 1 - core) * width, width, 1)
        return [own, other]

    taps = jnp.concatenate(grouped(taps, HALF) + [taps[:, DI:]], axis=1)
    gain = jnp.broadcast_to(jnp.concatenate(grouped(gain, HALF), axis=1), (8, GROUP))
    per_head = jnp.concatenate([step_bias, decay_log, skip_gain], axis=0)
    per_head = jnp.concatenate(grouped(per_head, 6), axis=1)
    hp = jnp.pad(per_head, ((0, 5), (0, 128 - HEADS)))
    skip = jnp.broadcast_to(jnp.repeat(per_head[2:3], 64, axis=1), (8, GROUP))
    return dict(taps=taps, gain=gain, hp=hp, skip=skip)


def rms_scale(values):
    return lax.rsqrt(jnp.mean(values * values, axis=-1, keepdims=True) + epsilon)


def piece_rows(values, k):
    return values[PIECE * k : PIECE * (k + 1)]


def layer_forward(core, head, feed, normed, weights):
    place = head.reshape(1)
    own = dot(normed, weights["x_own"]).astype(bf16)
    other = dot(normed, weights["x_other"]).astype(bf16)
    shared = pick(core, own[:, HALF:], other[:, HALF:])
    conv_in = jnp.concatenate([own[:, :HALF], other[:, :HALF], shared], axis=1)
    slot = pick(core, other[:, HALF : HALF + 128], own[:, HALF + 6 : HALF + 134]).astype(f32)
    last_row = PIECE * lax.rem(7 - head, 4) + PIECE - 8
    rim = lax.ppermute(
        lax.dynamic_slice_in_dim(conv_in, last_row, 8, 0), "seq", [(i, i + 1) for i in range(15)]
    )
    pre, mixed0, query, run, starts, last, packed = scan_local(
        place, conv_in, slot, rim, weights["taps"], weights["hp"], weights["skip"]
    )
    entering = carried(packed, -1)
    gate = jnp.concatenate([dot(normed, weights["g_own"]), dot(normed, weights["g_other"])], axis=1)
    mixed, normed_out, square = gate_out(mixed0, run, query, entering, gate, weights["gain"])
    square = square[:, 0].reshape(4, PIECE)
    total = square
    for k in (2, 1, 3):
        total = total + from_head(jnp.roll(square, k, axis=0), k)
    s_out = lax.rsqrt(total / DI + epsilon)
    parts = {}
    for k in (2, 1, 3, 0):
        piece = piece_rows(normed_out, k)
        parts[k] = dot(piece[:, :HALF], weights["o_own"]) + dot(piece[:, HALF:], weights["o_other"])
    branch = s_out[0][:, None] * scatter_head(parts)
    result = (feed.astype(f32) + branch).astype(bf16)
    kept = dict(
        feed=feed, normed=normed, gate=gate, conv_in=conv_in, rim=rim, step=slot, pre=pre,
        mixed=mixed, query=query, run=run, starts=starts, last=last, entering=entering,
        s_out=s_out, branch=branch, packed=packed,
    )
    return result, kept


def layer_backward(core, head, incoming, gathered, kept, weights):
    place = head.reshape(1)
    grad_new = incoming.astype(f32)
    mean_own = jnp.sum(kept["branch"] * grad_new, axis=1) / DI
    mean = jnp.stack(gather_head(mean_own))
    scale = jnp.stack([kept["s_out"].reshape(-1), mean.reshape(-1)], axis=1)
    scale = jnp.pad(scale, ((0, 0), (0, 126)))
    grad_normed_out = jnp.concatenate(
        [dot_nt(gathered, weights["o_own"]), dot_nt(gathered, weights["o_other"])], axis=1
    )
    decay = jnp.broadcast_to(
        kept["packed"][N : N + 1].astype(f32) + kept["packed"][N + 1 : N + 2].astype(f32),
        (8, GROUP),
    )
    grad_scan, grad_gate, normed_out, packed = gate_back(
        grad_normed_out, kept["gate"], kept["mixed"], scale, kept["run"], kept["query"],
        weights["gain"], decay,
    )
    leaving = carried(packed, 1)
    grad_out = (dot_tn(normed_out[:, :HALF], gathered), dot_tn(normed_out[:, HALF:], gathered))
    normed = kept["normed"]
    grad_g = (dot_tn(normed, grad_gate[:, :HALF]), dot_tn(normed, grad_gate[:, HALF:]))
    grad_conv, tail, grad_step, rim_grad, grad_taps, grad_hp = scan_back(
        place, kept["conv_in"], kept["pre"], kept["step"], kept["run"], grad_scan, kept["mixed"],
        kept["starts"], kept["last"], kept["entering"], leaving, kept["rim"], weights["taps"],
        weights["hp"], weights["skip"],
    )
    from_next = lax.ppermute(rim_grad, "seq", [(i + 1, i) for i in range(15)])
    last_row = PIECE * lax.rem(7 - head, 4) + PIECE - 8
    grad_conv = lax.dynamic_update_slice_in_dim(
        grad_conv, (tail + from_next).astype(bf16), last_row, 0
    )
    shared = grad_conv[:, GROUP:]
    first, second = grad_step[:, :6], grad_step[:, 6:12]
    step = jnp.concatenate(
        [
            pick(core, first, second),
            pick(core, second, first),
            jnp.zeros((grad_step.shape[0], EXTRA - HEADS), bf16),
        ],
        axis=1,
    )
    use_own = jnp.concatenate([grad_conv[:, :HALF], pick(core, shared, step)], axis=1)
    use_other = jnp.concatenate([grad_conv[:, HALF:GROUP], pick(core, step, shared)], axis=1)
    parts = {}
    for k in (2, 1, 3, 0):
        parts[k] = (
            dot_nt(piece_rows(use_own, k), weights["x_own"])
            + dot_nt(piece_rows(use_other, k), weights["x_other"])
            + dot_nt(piece_rows(grad_gate, k)[:, :HALF], weights["g_own"])
            + dot_nt(piece_rows(grad_gate, k)[:, HALF:], weights["g_other"])
        )
    grad_normed = scatter_head(parts)
    grad_x = (dot_tn(normed, use_own), dot_tn(normed, use_other))
    feed = kept["feed"].astype(f32)
    s_in = rms_scale(feed)
    unit = feed * s_in
    grad_unit = grad_normed * weights["input_gain"]
    grad_feed = grad_new + s_in * (
        grad_unit - unit * jnp.mean(unit * grad_unit, axis=-1, keepdims=True)
    )
    return grad_feed.astype(bf16), (grad_x, grad_g, grad_out, grad_taps, grad_hp)


def small_columns(core, head, grad_taps, grad_hp):
    taps = grad_taps[:5]
    full = jnp.zeros((5, DI), f32)
    full = lax.dynamic_update_slice_in_dim(full, taps[:, :HALF], (2 * head + core) * HALF, 1)
    full = lax.dynamic_update_slice_in_dim(
        full, taps[:, HALF:GROUP], (2 * head + 1 - core) * HALF, 1
    )
    full = jnp.concatenate([full, taps[:, GROUP:]], axis=1)
    full = full.reshape(5, 64, 52).transpose(1, 0, 2).reshape(64, 260)
    first, second = grad_hp[:3, :6], grad_hp[:3, 6:HEADS]
    sums = jnp.concatenate([pick(core, first, second), pick(core, second, first)], axis=1)
    sums = jnp.broadcast_to(sums.reshape(1, 36), (64, 36))
    return jnp.concatenate([full, sums, jnp.zeros((64, 16), f32)], axis=1).reshape(D, SMALL)


def summed(own, other):
    return own + swap(other.astype(bf16)).astype(f32)


def scatter_seq(a):
    return lax.psum_scatter(a, "seq", scatter_dimension=0, tiled=True)


def reduce_layer(core, head, layer, grads):
    grad_x, grad_g, grad_out, grad_taps, grad_hp = grads
    out = scatter_seq(summed(*grad_out))
    gate = scatter_seq(summed(*grad_g))
    small = small_columns(core, head, grad_taps, grad_hp)
    small = jnp.pad(small, ((0, 0), (HALF + SMALL_AT, EXTRA - SMALL_AT - SMALL)))
    own = grad_x[0] + jnp.where(core == 1, small, 0.0)
    other = grad_x[1] + jnp.where(core == 0, small, 0.0)
    x = scatter_seq(summed(own, other))
    both = jnp.concatenate([x, gate], axis=1).reshape(4, 24, HALF + EXTRA + HALF)
    mine = exchange_head(both, head)
    theirs = lax.ppermute(mine, "section", [(1 - layer, layer)])
    rows_out = [lax.ppermute(out, EVERY, out_back_pairs(layer, part)) for part in range(2)]
    return mine, theirs, rows_out


def per_device(
    tokens_in, cotangent, input_gain, gate_inner, shared_bc, step_proj, conv_weight, conv_bias,
    step_bias, decay_log, skip_gain, output_gain, out_proj
):
    core = lax.axis_index("section")
    head = lax.axis_index("head")
    tokens = lax.dynamic_index_in_dim(tokens_in, core, 0, False)
    grad_top = lax.dynamic_index_in_dim(cotangent, core, 0, False)

    small = jnp.concatenate(
        [conv_weight[0].reshape(208), conv_bias[0], output_gain[0], jnp.zeros((4,), bf16)]
    ).reshape(24, SMALL)
    pieces = spread_weights(
        core, head, gate_inner[0], shared_bc[0], step_proj[0], input_gain[0], small
    )
    out_piece = lax.ppermute(out_proj[0], EVERY, out_pairs())
    per_head = jnp.concatenate([step_bias, decay_log, skip_gain], axis=0)
    other_head = swap(per_head)
    head_values = [pick(core, per_head, other_head), pick(core, other_head, per_head)]

    feed_all = jnp.concatenate(gather_head(tokens), axis=0)
    weights = [{}, {}]
    for layer in range(2):
        own = gather_seq(pieces[layer][:, : HALF + EXTRA])
        weights[layer].update(x_own=own, x_other=swap(own))
        gate = gather_seq(pieces[layer][:, HALF + EXTRA :])
        weights[layer].update(g_own=gate, g_other=swap(gate))
        if layer == 0:
            out = gather_seq(out_piece)
            out_other = swap(out)
        weights[layer].update(
            o_own=out[HALF * layer : HALF * (layer + 1)],
            o_other=out_other[HALF * layer : HALF * (layer + 1)],
        )
        slot = pick(core, weights[layer]["x_other"], own)[:, HALF : HALF + 128]
        values = head_values[layer]
        weights[layer].update(
            layer_params(core, head, slot, values[0:1], values[1:2], values[2:3])
        )
        weights[layer]["input_gain"] = slot[:, 18].astype(f32)[None, :]

    def normalised(feed, gain):
        values = feed.astype(f32)
        return (values * rms_scale(values) * gain).astype(bf16)

    normed = normalised(feed_all, weights[0]["input_gain"])
    hidden, kept0 = layer_forward(core, head, tokens, normed, weights[0])
    normed_own = normalised(hidden, weights[1]["input_gain"])
    normed = jnp.concatenate(gather_head(normed_own), axis=0)
    result, kept1 = layer_forward(core, head, hidden, normed, weights[1])
    got = swap(pick(core, result, hidden))
    layer_out = jnp.stack([pick(core, hidden, got), pick(core, got, result)])

    grad_all = jnp.concatenate(gather_head(grad_top), axis=0)
    grad_hidden, grads1 = layer_backward(core, head, grad_top, grad_all, kept1, weights[1])
    grad_all = jnp.concatenate(gather_head(grad_hidden), axis=0)
    mine1, theirs1, out1 = reduce_layer(core, head, 1, grads1)
    grad_feed, grads0 = layer_backward(core, head, grad_hidden, grad_all, kept0, weights[0])
    mine0, theirs0, out0 = reduce_layer(core, head, 0, grads0)
    got = swap(pick(core, grad_hidden, grad_feed))
    grad_in = jnp.stack([pick(core, grad_feed, got), pick(core, got, grad_hidden)])

    mine = pick(core, mine0, mine1)
    theirs = theirs0 + theirs1
    low, high = pick(core, mine, theirs), pick(core, theirs, mine)
    columns = []
    for start in (HALF + EXTRA, 0):
        for g in range(4):
            for half in (low, high):
                columns.append(half[g, :, start : start + HALF])
    grad_gate_inner = jnp.concatenate(columns, axis=1)
    grad_shared = jnp.sum(low[:, :, HALF : HALF + EXTRA], axis=0)
    slot = high[:, :, HALF : HALF + 128]
    grad_step = jnp.concatenate([slot[g, :, :HEADS] for g in range(4)], axis=1)
    small = slot[:, :, SMALL_AT : SMALL_AT + SMALL].reshape(4, 24 * SMALL)
    taps = jnp.sum(small[:, :260], axis=0)
    sums = small[:, 260:296].reshape(4, 3, HEADS).transpose(1, 0, 2).reshape(3, 48)
    grad_out = jnp.concatenate([out0[0] + out1[0], out0[1] + out1[1]], axis=0)
    grad_output_gain = jnp.sum(grad_out * out_proj[0].astype(f32), axis=1) / output_gain[0].astype(
        f32
    )
    grad_input_gain = (
        jnp.sum(grad_gate_inner * gate_inner[0].astype(f32), axis=1)
        + jnp.sum(grad_shared * shared_bc[0].astype(f32), axis=1)
        + jnp.sum(grad_step * step_proj[0].astype(f32), axis=1)
    ) / input_gain[0].astype(f32)
    return (
        layer_out[None],
        grad_in[None],
        grad_input_gain[None],
        grad_gate_inner[None],
        grad_shared[None],
        grad_step[None],
        taps[:208].reshape(1, 4, 52),
        taps[208:260][None],
        sums[0:1],
        sums[1:2],
        sums[2:3],
        grad_output_gain[None],
        grad_out[None],
    )


def solution(mesh):
    both = ("seq", "head")
    return jax.shard_map(
        per_device,
        mesh=mesh,
        in_specs=(
            P(None, both, None),
            P(None, both, None),
            P("section", both),
            P("section", both, None),
            P("section", both, None),
            P("section", both, None),
            P("section", None, both),
            P("section", both),
            P("section", None),
            P("section", None),
            P("section", None),
            P("section", both),
            P("section", both, None),
        ),
        out_specs=(
            P("section", None, both, None),
            P("section", None, both, None),
            P("section", both),
            P("section", both, None),
            P("section", both, None),
            P("section", both, None),
            P("section", None, both),
            P("section", both),
            P("section", None),
            P("section", None),
            P("section", None),
            P("section", both),
            P("section", both, None),
        ),
        check_vma=False,
    )
```

time: 3670 us -> 1060 us (0.29)
  blocking collectives: 855 us -> 0 us
  waiting for transfers between devices: 1330 us -> 595 us
  local copies, waits for them, and re-layouts: 512 us -> 67.2 us
  matrix products: 452 us -> 123 us
  other arithmetic: 285 us -> 41 us
  Pallas kernels: 0 us -> 49.2 us
    all_gather x9 -> x0, blocking collectives: 595 us -> none  [the longest x1 151 us: fetch_weights(): lax.all_gather(packed[4], ('seq', 'head'), axis=2, tiled=True)]
    reduce_scatter x3 -> x4, waiting for transfers between devices: 739 us -> 260 us  [scatter_seq(): return lax.psum_scatter(a, 'seq', scatter_dimension=0, tiled=True)]
    dot_general x138 -> x72, matrix products: 452 us -> 123 us  [the longest x36 48.5 us: dot_nt(): lax.dot_general(a.astype(bf16), b.astype(bf16), (((1,), (1,)), ((), ())),...]
    unnamed x1 -> x0, blocking collectives: 260 us -> none
    unnamed x15 -> x13, waiting for transfers between devices: 232 us -> 0.26 us
    dynamic_update_slice x60 -> x4, local copies, waits for them, and re-layouts: 217 us -> 1.44 us  [the longest x2 0.73 us: small_columns(): lax.dynamic_update_slice_in_dim(full, taps[:, :HALF], (2 * head + core) *...]
    ppermute x10 -> x98, waiting for transfers between devices: 15.1 us -> 197 us  [the longest x48 99.2 us: from_head(): return lax.ppermute(a, 'head', [(i, (i - k) % 4) for i in range(4)])]
    all_gather x8 -> x5, waiting for transfers between devices: 264 us -> 138 us  [gather_seq(): return lax.all_gather(a, 'seq', axis=0, tiled=True)]
  transfers between devices with their start and end apart: 47 -> 109, of which waited for: 34 -> 65; matrix products, arithmetic and copies ran while one was open for 11% -> 17% of each run, Pallas kernels for 0% -> 4%
where the time goes in v1:
time: 1060 us; the launch traced here: 1050 us
  waiting for transfers between devices  595 us (56%)
  starting transfers between devices  156 us (15%)
  matrix products  123 us (12%)
  local copies, waits for them, and re-layouts  67.2 us (6%)
  Pallas kernels  49.2 us (5%)
  other arithmetic  41 us (4%)
  between operations  18.1 us (2%)
    reduce_scatter x4, waiting for transfers between devices, scatter_seq(): return lax.psum_scatter(a, 'seq', scatter_dimension=0, tiled=True)  260 us
    all_gather x5, waiting for transfers between devices, gather_seq(): return lax.all_gather(a, 'seq', axis=0, tiled=True)  138 us
    ppermute x48, waiting for transfers between devices, from_head(): return lax.ppermute(a, 'head', [(i, (i - k) % 4) for i in range(4)])  99.2 us
    ppermute x24, waiting for transfers between devices, from_seq(): return lax.ppermute(a, 'seq', pairs)  69.5 us
    ppermute x48, starting transfers between devices, from_head(): return lax.ppermute(a, 'head', [(i, (i - k) % 4) for i in range(4)])  52.5 us
    dot_general x36, matrix products, dot_nt(): lax.dot_general(a.astype(bf16), b.astype(bf16), (((1,), (1,)), ((), ())),...  48.5 us
    ppermute x24, starting transfers between devices, from_seq(): return lax.ppermute(a, 'seq', pairs)  41 us
    dot_general x24, matrix products, dot(): return jnp.dot(a.astype(bf16), b.astype(bf16), preferred_element_type=f32)  38.3 us
  transfers between devices with their start and end apart: 109, of which 65 were waited for; matrix products, arithmetic and copies ran while one was open for 17% of the time, Pallas kernels for 4%

profile of v1, /device:TPU:103, one launch (start us, length us, event | category | flops | bytes accessed | tf_op | source)
XLA Modules:
  0.0 1049.6 jit_solution(1617349942613895715)
XLA Ops:
  30.7 7.7 collective-permute-start.20
  38.4 7.2 collective-permute-done.20
  46.3 27.8 %all-gather.6.cloned.1.call-done = bf16[1536,640]{1,0:T(8,128)(2,1)} async-done(((bf16[96,640]{1,0:T(8,128)(2,1)}), bf16[1536,640]{1,0:T(8,128)(2,1)}) %all-gather.6.cloned.1.call-update) | async-done | bytes 1966096 | tf_op jit(solution)/shard_map/all_gather | solution.py:666
  88.4 9.0 collective-permute-done
  98.4 20.2 %all-gather.8.cloned.1.call-done = bf16[1536,384]{1,0:T(8,128)(2,1)} async-done(((bf16[96,384]{1,0:T(8,128)(2,1)}), bf16[1536,384]{1,0:T(8,128)(2,1)}) %all-gather.8.cloned.1.call-update) | async-done | bytes 1179664 | tf_op jit(solution)/shard_map/all_gather | solution.py:666
  120.1 44.7 %all-gather.12.cloned.1.call-done = bf16[1536,640]{1,0:T(8,128)(2,1)} async-done(((bf16[96,640]{1,0:T(8,128)(2,1)}), bf16[1536,640]{1,0:T(8,128)(2,1)}) %all-gather.12.cloned.1.call-update) | async-done | bytes 1966096 | tf_op jit(solution)/shard_map/all_gather | solution.py:666
  166.3 45.4 %all-gather.10.cloned.1.call-done = bf16[768,1536]{1,0:T(8,128)(2,1)} async-done(((bf16[48,1536]{1,0:T(8,128)(2,1)}), bf16[768,1536]{1,0:T(8,128)(2,1)}) %all-gather.10.cloned.1.call-update) | async-done | bytes 2359312 | tf_op jit(solution)/shard_map/all_gather | solution.py:666
  214.9 3.5 convolution_convert_fusion.6
  243.0 5.9 scan_local.2
  253.9 3.9 collective-permute-done.12
  269.1 2.9 collective-permute-done.14
  272.0 7.2 collective-permute-done.13
  279.5 3.2 gate_out.2
  300.1 6.9 collective-permute-done.23
  307.0 4.6 collective-permute-done.22
  313.3 3.5 collective-permute-start.31
  326.5 10.7 %collective-permute-done.29 = bf16[128,1536]{1,0:T(8,128)(2,1)} collective-permute-done((bf16[128,1536]{1,0:T(8,128)(2,1)S(1)}, bf16[128,1536]{1,0:T(8,128)(2,1)}, u32[]{:S(2)}, u32[]{:S(2)}) %collective-permute-start.29) | collective-permute-done | bytes 393248 | tf_op jit(solution)/shard_map/ppermute | solution.py:28
  337.2 3.3 convolution_convert_fusion.4
  343.4 3.9 collective-permute-start.32
  350.0 5.9 scan_local.3
  361.0 6.9 collective-permute-done.35
  376.0 5.0 collective-permute-done.37
  381.0 6.8 collective-permute-done.36
  388.2 3.1 gate_out.3
  407.9 5.8 collective-permute-done.41
  425.2 9.4 collective-permute-done.52
  434.6 3.1 collective-permute-done.51
  437.8 3.6 collective-permute-done.50
  443.3 2.9 fusion.59
  450.0 3.2 gate_back.2
  455.9 5.1 collective-permute-start.55
  461.7 7.8 collective-permute-done.55
  469.5 3.9 collective-permute-done.53
  477.0 3.0 collective-permute-start.57
  486.4 4.8 collective-permute-done.56
  491.6 12.7 %scan_back.2 = (bf16[512,1024]{1,0:T(8,128)(2,1)S(1)}, f32[8,1024]{1,0:T(8,128)S(1)}, bf16[512,128]{1,0:T(8,128)(2,1)S(1)}, f32[8,1024]{1,0:T(8,128)S(1)}, f32[8,1024]{1,0:T(8,128)S(1)}, /*index=5*/f32[8,128]{1,0:T(8,128)S(1)}) custom-call(s32[1]{0:T(128)} %bitcast.1.place, bf16[512,1024]{1,0:T(8,128)(2,1)S(1)} %copy-done.8, f32[512,1024]{1,0:T(8,128)S(1)} %copy-done.20, ...), custom_call_target="tpu_custom_call" | custom-call | flops 2000000000 | bytes 9000000 | tf_op jit(solution)/shard_map/scan_back/pallas_call | solution.py:553
  527.8 3.5 convolution_add_fusion
  536.8 2.9 collective-permute-done.60
  543.2 3.7 collective-permute-start.65
  551.4 8.9 collective-permute-done.68
  560.2 5.3 collective-permute-done.67
  583.8 3.2 convolution_add_fusion.1
  588.2 3.3 convolution_convert_fusion.2
  595.8 3.4 collective-permute-done.71
  600.8 6.7 collective-permute-done.69
  611.1 4.7 collective-permute-start.74
  615.8 6.4 collective-permute-start.73
  622.2 4.2 convolution_add_fusion.2
  630.1 3.5 collective-permute-done.72
  641.2 12.7 %scan_back.3 = (bf16[512,1024]{1,0:T(8,128)(2,1)S(1)}, f32[8,1024]{1,0:T(8,128)S(1)}, bf16[512,128]{1,0:T(8,128)(2,1)S(1)}, f32[8,1024]{1,0:T(8,128)S(1)}, f32[8,1024]{1,0:T(8,128)S(1)}, /*index=5*/f32[8,128]{1,0:T(8,128)S(1)}) custom-call(s32[1]{0:T(128)} %bitcast.1.place, bf16[512,1024]{1,0:T(8,128)(2,1)S(1)} %copy-done.6, f32[512,1024]{1,0:T(8,128)S(1)} %copy-done.18, ...), custom_call_target="tpu_custom_call" | custom-call | flops 2000000000 | bytes 9000000 | tf_op jit(solution)/shard_map/scan_back/pallas_call | solution.py:553
  662.5 4.0 fusion.7
  668.8 3.9 collective-permute-done.85
  672.8 5.3 fusion.5
  697.1 3.6 collective-permute-done.80
  700.7 3.4 fusion.1
  725.7 5.1 collective-permute-done.77
  730.9 4.4 collective-permute-done.76
  740.8 4.8 collective-permute-start.95
  746.2 8.6 collective-permute-start.93
  758.1 27.3 %reduce-scatter.17.cloned.1.call-done = f32[96,384]{1,0:T(8,128)} async-done(((f32[1536,384]{1,0:T(8,128)}), f32[96,384]{1,0:T(8,128)}) %reduce-scatter.17.cloned.1.call-update) | async-done | bytes 147472 | tf_op jit(solution)/shard_map/reduce_scatter | solution.py:818
  785.4 80.1 %reduce-scatter.15.cloned.1.call-done = f32[96,640]{1,0:T(8,128)} async-done(((f32[1536,640]{1,0:T(8,128)}), f32[96,640]{1,0:T(8,128)}) %reduce-scatter.15.cloned.1.call-update) | async-done | bytes 245776 | tf_op jit(solution)/shard_map/reduce_scatter | solution.py:818
  869.9 72.6 %reduce-scatter.13.cloned.1.call-done = f32[96,384]{1,0:T(8,128)} async-done(((f32[1536,384]{1,0:T(8,128)}), f32[96,384]{1,0:T(8,128)}) %reduce-scatter.13.cloned.1.call-update) | async-done | bytes 147472 | tf_op jit(solution)/shard_map/reduce_scatter | solution.py:818
  942.5 80.0 %reduce-scatter.11.cloned.1.call-done = f32[96,640]{1,0:T(8,128)} async-done(((f32[1536,640]{1,0:T(8,128)}), f32[96,640]{1,0:T(8,128)}) %reduce-scatter.11.cloned.1.call-update) | async-done | bytes 245776 | tf_op jit(solution)/shard_map/reduce_scatter | solution.py:818
  1030.1 5.9 collective-permute-start.90
  (936 shorter events, 335.8 us)
Async XLA Ops:
  7.2 66.9 %all-gather.6.cloned.1.call-start = ((), (), s32[]{:S(2)}) async-start(), calls=%async_computation.6 | async-start | bytes 2088960 | tf_op jit(solution)/shard_map/all_gather | solution.py:666
  21.8 96.7 %all-gather.8.cloned.1.call-start = ((), (), s32[]{:S(2)}) async-start(), calls=%async_computation.7 | async-start | bytes 1253376 | tf_op jit(solution)/shard_map/all_gather | solution.py:666
  22.6 142.2 %all-gather.12.cloned.1.call-start = ((), (), s32[]{:S(2)}) async-start(), calls=%async_computation.9 | async-start | bytes 2088960 | tf_op jit(solution)/shard_map/all_gather | solution.py:666
  30.6 181.0 %all-gather.10.cloned.1.call-start = ((), (), s32[]{:S(2)}) async-start(), calls=%async_computation.8 | async-start | bytes 2506752 | tf_op jit(solution)/shard_map/all_gather | solution.py:666
  30.7 14.8 %collective-permute-start.20 = (bf16[48,1536]{1,0:T(8,128)(2,1)S(1)}, bf16[48,1536]{1,0:T(8,128)(2,1)S(1)}, u32[]{:S(2)}, u32[]{:S(2)}) collective-permute-start(bf16[48,1536]{1,0:T(8,128)(2,1)S(1)} %bitcast.370), channel_id=1, source_target_pairs={{0,0},{1,4},{2,8},{3,12},{4,16},{5,20},{6,24},{7,28},{8,64},{9,68}... | collective-permute-start | bytes 442376 | tf_op jit(solution)/shard_map/ppermute | solution.py:852
  46.2 272.0 %all-gather.14.cloned.1.call-start = ((), (), s32[]{:S(2)}) async-start(), calls=%async_computation.10 | async-start | bytes 1253376 | tf_op jit(solution)/shard_map/all_gather | solution.py:666
  74.0 139.8 %collective-permute-start.7 = (bf16[1536,640]{1,0:T(8,128)(2,1)}, bf16[1536,640]{1,0:T(8,128)(2,1)}, u32[]{:S(2)}, u32[]{:S(2)}) collective-permute-start(bf16[1536,640]{1,0:T(8,128)(2,1)} %all-gather.6.cloned.1.call-done), channel_id=1, source_target_pairs={{0,64},{64,0},{1,65},{65,1},{2,66},{66,2},{3,67},{67,3},{4,68},{68... | collective-permute-start | bytes 5898248 | tf_op jit(solution)/shard_map/ppermute | solution.py:44
  76.2 10.7 %collective-permute-start.2 = (bf16[128,1536]{1,0:T(8,128)(2,1)S(1)}, bf16[128,1536]{1,0:T(8,128)(2,1)S(1)}, u32[]{:S(2)}, u32[]{:S(2)}) collective-permute-start(bf16[128,1536]{1,0:T(8,128)(2,1)S(1)} %get-tuple-element.137), channel_id=1, source_target_pairs={{0,1},{1,2},{2,3},{3,0},{4,5},{5,6},{6,7},{7,4},{8,9},{9,10},{10,1... | collective-permute-start | bytes 1179656 | tf_op jit(solution)/shard_map/ppermute | solution.py:28
  76.4 12.0 %collective-permute-start.1 = (bf16[128,1536]{1,0:T(8,128)(2,1)S(1)}, bf16[128,1536]{1,0:T(8,128)(2,1)S(1)}, u32[]{:S(2)}, u32[]{:S(2)}) collective-permute-start(bf16[128,1536]{1,0:T(8,128)(2,1)S(1)} %get-tuple-element.137), channel_id=1, source_target_pairs={{0,2},{1,3},{2,0},{3,1},{4,6},{5,7},{6,4},{7,5},{8,10},{9,11},{10,... | collective-permute-start | bytes 1179656 | tf_op jit(solution)/shard_map/ppermute | solution.py:28
  78.5 18.9 %collective-permute-start = (bf16[128,1536]{1,0:T(8,128)(2,1)S(1)}, bf16[128,1536]{1,0:T(8,128)(2,1)S(1)}, u32[]{:S(2)}, u32[]{:S(2)}) collective-permute-start(bf16[128,1536]{1,0:T(8,128)(2,1)S(1)} %get-tuple-element.137), channel_id=1, source_target_pairs={{0,3},{1,0},{2,1},{3,2},{4,7},{5,4},{6,5},{7,6},{8,11},{9,8},{10,9... | collective-permute-start | bytes 1179656 | tf_op jit(solution)/shard_map/ppermute | solution.py:28
  84.3 655.2 %reduce-scatter.21.cloned.1.call-start = ((), (), s32[]{:S(2)}) async-start(), calls=%async_computation.16 | async-start | bytes 2506752
  118.6 134.3 %collective-permute-start.16 = (bf16[1536,384]{1,0:T(8,128)(2,1)}, bf16[1536,384]{1,0:T(8,128)(2,1)S(1)}, u32[]{:S(2)}, u32[]{:S(2)}) collective-permute-start(bf16[1536,384]{1,0:T(8,128)(2,1)} %all-gather.8.cloned.1.call-done), channel_id=1, source_target_pairs={{0,64},{64,0},{1,65},{65,1},{2,66},{66,2},{3,67},{67,3},{4,68},{68... | collective-permute-start | bytes 3538952 | tf_op jit(solution)/shard_map/ppermute | solution.py:44
  164.8 57.5 %collective-permute-start.28 = (bf16[1536,640]{1,0:T(8,128)(2,1)}, bf16[1536,640]{1,0:T(8,128)(2,1)}, u32[]{:S(2)}, u32[]{:S(2)}) collective-permute-start(bf16[1536,640]{1,0:T(8,128)(2,1)} %all-gather.12.cloned.1.call-done), channel_id=1, source_target_pairs={{0,64},{64,0},{1,65},{65,1},{2,66},{66,2},{3,67},{67,3},{4,68},{68... | collective-permute-start | bytes 5898248 | tf_op jit(solution)/shard_map/ppermute | solution.py:44
  211.7 77.3 %collective-permute-start.21 = (bf16[768,1536]{1,0:T(8,128)(2,1)}, bf16[768,1536]{1,0:T(8,128)(2,1)}, u32[]{:S(2)}, u32[]{:S(2)}) collective-permute-start(bf16[768,1536]{1,0:T(8,128)(2,1)} %all-gather.10.cloned.1.call-done), channel_id=1, source_target_pairs={{0,64},{64,0},{1,65},{65,1},{2,66},{66,2},{3,67},{67,3},{4,68},{68... | collective-permute-start | bytes 7077896 | tf_op jit(solution)/shard_map/ppermute | solution.py:44
  249.9 10.7 %collective-permute-start.11 = (bf16[144,768]{1,0:T(8,128)(2,1)S(1)}, bf16[144,768]{1,0:T(8,128)(2,1)S(1)}, u32[]{:S(2)}, u32[]{:S(2)}) collective-permute-start(bf16[144,768]{1,0:T(8,128)(2,1)S(1)} %get-tuple-element.56), channel_id=1, source_target_pairs={{8,0},{12,4},{0,8},{4,12},{24,16},{28,20},{16,24},{20,28},{40,32},... | collective-permute-start | bytes 663560 | tf_op jit(solution)/shard_map/ppermute | solution.py:40
  266.4 12.8 %collective-permute-start.13 = (bf16[144,768]{1,0:T(8,128)(2,1)S(1)}, bf16[144,768]{1,0:T(8,128)(2,1)S(1)}, u32[]{:S(2)}, u32[]{:S(2)}) collective-permute-start(bf16[144,768]{1,0:T(8,128)(2,1)S(1)} %maximum_maximum_fusion.2), channel_id=1, source_target_pairs={{0,48},{4,52},{8,56},{12,60},{1,49},{5,53},{9,57},{13,61},{2,50},{... | collective-permute-start | bytes 663560 | tf_op jit(solution)/shard_map/ppermute | solution.py:40
  293.6 13.4 %collective-permute-start.23 = (bf16[128,1536]{1,0:T(8,128)(2,1)S(1)}, bf16[128,1536]{1,0:T(8,128)(2,1)S(1)}, u32[]{:S(2)}, u32[]{:S(2)}) collective-permute-start(bf16[128,1536]{1,0:T(8,128)(2,1)S(1)} %fusion.28), channel_id=1, source_target_pairs={{0,2},{1,3},{2,0},{3,1},{4,6},{5,7},{6,4},{7,5},{8,10},{9,11},{10,... | collective-permute-start | bytes 1179656 | tf_op jit(solution)/shard_map/ppermute | solution.py:28
  297.8 13.8 %collective-permute-start.22 = (bf16[128,1536]{1,0:T(8,128)(2,1)S(1)}, bf16[128,1536]{1,0:T(8,128)(2,1)S(1)}, u32[]{:S(2)}, u32[]{:S(2)}) collective-permute-start(bf16[128,1536]{1,0:T(8,128)(2,1)S(1)} %fusion.27), channel_id=1, source_target_pairs={{0,1},{1,2},{2,3},{3,0},{4,5},{5,6},{6,7},{7,4},{8,9},{9,10},{10,1... | collective-permute-start | bytes 1179656 | tf_op jit(solution)/shard_map/ppermute | solution.py:28
  313.3 12.8 %collective-permute-start.31 = (bf16[128,1536]{1,0:T(8,128)(2,1)S(1)}, bf16[128,1536]{1,0:T(8,128)(2,1)}, u32[]{:S(2)}, u32[]{:S(2)}) collective-permute-start(bf16[128,1536]{1,0:T(8,128)(2,1)S(1)} %fusion.51), channel_id=1, source_target_pairs={{0,1},{1,2},{2,3},{3,0},{4,5},{5,6},{6,7},{7,4},{8,9},{9,10},{10,1... | collective-permute-start | bytes 1179656 | tf_op jit(solution)/shard_map/ppermute | solution.py:28
  316.7 20.4 %collective-permute-start.29 = (bf16[128,1536]{1,0:T(8,128)(2,1)S(1)}, bf16[128,1536]{1,0:T(8,128)(2,1)}, u32[]{:S(2)}, u32[]{:S(2)}) collective-permute-start(bf16[128,1536]{1,0:T(8,128)(2,1)S(1)} %fusion.51), channel_id=1, source_target_pairs={{0,3},{1,0},{2,1},{3,2},{4,7},{5,4},{6,5},{7,6},{8,11},{9,8},{10,9... | collective-permute-start | bytes 1179656 | tf_op jit(solution)/shard_map/ppermute | solution.py:28
  318.2 52.0 %collective-permute-start.39 = (bf16[1536,384]{1,0:T(8,128)(2,1)}, bf16[1536,384]{1,0:T(8,128)(2,1)S(1)}, u32[]{:S(2)}, u32[]{:S(2)}) collective-permute-start(bf16[1536,384]{1,0:T(8,128)(2,1)} %all-gather.14.cloned.1.call-done), channel_id=1, source_target_pairs={{0,64},{64,0},{1,65},{65,1},{2,66},{66,2},{3,67},{67,3},{4,68},{68... | collective-permute-start | bytes 3538952 | tf_op jit(solution)/shard_map/ppermute | solution.py:44
  356.0 12.0 %collective-permute-start.35 = (bf16[144,768]{1,0:T(8,128)(2,1)S(1)}, bf16[144,768]{1,0:T(8,128)(2,1)S(1)}, u32[]{:S(2)}, u32[]{:S(2)}) collective-permute-start(bf16[144,768]{1,0:T(8,128)(2,1)S(1)} %get-tuple-element.62), channel_id=1, source_target_pairs={{12,0},{0,4},{4,8},{8,12},{28,16},{16,20},{20,24},{24,28},{44,32},... | collective-permute-start | bytes 663560 | tf_op jit(solution)/shard_map/ppermute | solution.py:40
  356.1 11.9 %collective-permute-start.34 = (bf16[144,768]{1,0:T(8,128)(2,1)S(1)}, bf16[144,768]{1,0:T(8,128)(2,1)S(1)}, u32[]{:S(2)}, u32[]{:S(2)}) collective-permute-start(bf16[144,768]{1,0:T(8,128)(2,1)S(1)} %get-tuple-element.62), channel_id=1, source_target_pairs={{8,0},{12,4},{0,8},{4,12},{24,16},{28,20},{16,24},{20,28},{40,32},... | collective-permute-start | bytes 663560 | tf_op jit(solution)/shard_map/ppermute | solution.py:40
  356.6 11.7 %collective-permute-start.33 = (bf16[144,768]{1,0:T(8,128)(2,1)S(1)}, bf16[144,768]{1,0:T(8,128)(2,1)S(1)}, u32[]{:S(2)}, u32[]{:S(2)}) collective-permute-start(bf16[144,768]{1,0:T(8,128)(2,1)S(1)} %get-tuple-element.62), channel_id=1, source_target_pairs={{4,0},{8,4},{12,8},{0,12},{20,16},{24,20},{28,24},{16,28},{36,32},... | collective-permute-start | bytes 663560 | tf_op jit(solution)/shard_map/ppermute | solution.py:40
  374.3 13.5 %collective-permute-start.36 = (bf16[144,768]{1,0:T(8,128)(2,1)S(1)}, bf16[144,768]{1,0:T(8,128)(2,1)S(1)}, u32[]{:S(2)}, u32[]{:S(2)}) collective-permute-start(bf16[144,768]{1,0:T(8,128)(2,1)S(1)} %maximum_maximum_fusion.3), channel_id=1, source_target_pairs={{0,48},{4,52},{8,56},{12,60},{1,49},{5,53},{9,57},{13,61},{2,50},{... | collective-permute-start | bytes 663560 | tf_op jit(solution)/shard_map/ppermute | solution.py:40
  394.6 19.1 %collective-permute-start.45 = (bf16[128,1536]{1,0:T(8,128)(2,1)S(1)}, bf16[128,1536]{1,0:T(8,128)(2,1)S(1)}, u32[]{:S(2)}, u32[]{:S(2)}) collective-permute-start(bf16[128,1536]{1,0:T(8,128)(2,1)S(1)} %fusion.32), channel_id=1, source_target_pairs={{0,3},{1,0},{2,1},{3,2},{4,7},{5,4},{6,5},{7,6},{8,11},{9,8},{10,9... | collective-permute-start | bytes 1179656 | tf_op jit(solution)/shard_map/ppermute | solution.py:28
  396.7 17.0 %collective-permute-start.44 = (bf16[128,1536]{1,0:T(8,128)(2,1)S(1)}, bf16[128,1536]{1,0:T(8,128)(2,1)S(1)}, u32[]{:S(2)}, u32[]{:S(2)}) collective-permute-start(bf16[128,1536]{1,0:T(8,128)(2,1)S(1)} %fusion.31), channel_id=1, source_target_pairs={{0,2},{1,3},{2,0},{3,1},{4,6},{5,7},{6,4},{7,5},{8,10},{9,11},{10,... | collective-permute-start | bytes 1179656 | tf_op jit(solution)/shard_map/ppermute | solution.py:28
  399.6 14.1 %collective-permute-start.41 = (f32[4,128]{1,0:T(4,128)S(1)}, f32[4,128]{1,0:T(4,128)S(1)}, u32[]{:S(2)}, u32[]{:S(2)}) collective-permute-start(f32[4,128]{1,0:T(4,128)S(1)} %pad_maximum_fusion.41), channel_id=1, source_target_pairs={{0,3},{1,0},{2,1},{3,2},{4,7},{5,4},{6,5},{7,6},{8,11},{9,8},{10,9... | collective-permute-start | bytes 6152 | tf_op jit(solution)/shard_map/ppermute | solution.py:28
  400.2 13.5 %collective-permute-start.40 = (f32[4,128]{1,0:T(4,128)S(1)}, f32[4,128]{1,0:T(4,128)S(1)}, u32[]{:S(2)}, u32[]{:S(2)}) collective-permute-start(f32[4,128]{1,0:T(4,128)S(1)} %pad_maximum_fusion.40), channel_id=1, source_target_pairs={{0,2},{1,3},{2,0},{3,1},{4,6},{5,7},{6,4},{7,5},{8,10},{9,11},{10,... | collective-permute-start | bytes 6152 | tf_op jit(solution)/shard_map/ppermute | solution.py:28
  418.7 24.5 %collective-permute-start.49 = (bf16[128,1536]{1,0:T(8,128)(2,1)}, bf16[128,1536]{1,0:T(8,128)(2,1)}, u32[]{:S(2)}, u32[]{:S(2)}) collective-permute-start(bf16[128,1536]{1,0:T(8,128)(2,1)} %get-tuple-element.155), channel_id=1, source_target_pairs={{0,1},{1,2},{2,3},{3,0},{4,5},{5,6},{6,7},{7,4},{8,9},{9,10},{10,1... | collective-permute-start | bytes 1179656 | tf_op jit(solution)/shard_map/ppermute | solution.py:28
  420.8 22.5 %collective-permute-start.48 = (bf16[128,1536]{1,0:T(8,128)(2,1)}, bf16[128,1536]{1,0:T(8,128)(2,1)}, u32[]{:S(2)}, u32[]{:S(2)}) collective-permute-start(bf16[128,1536]{1,0:T(8,128)(2,1)} %get-tuple-element.155), channel_id=1, source_target_pairs={{0,2},{1,3},{2,0},{3,1},{4,6},{5,7},{6,4},{7,5},{8,10},{9,11},{10,... | collective-permute-start | bytes 1179656 | tf_op jit(solution)/shard_map/ppermute | solution.py:28
  420.8 22.5 %collective-permute-start.47 = (bf16[128,1536]{1,0:T(8,128)(2,1)}, bf16[128,1536]{1,0:T(8,128)(2,1)}, u32[]{:S(2)}, u32[]{:S(2)}) collective-permute-start(bf16[128,1536]{1,0:T(8,128)(2,1)} %get-tuple-element.155), channel_id=1, source_target_pairs={{0,3},{1,0},{2,1},{3,2},{4,7},{5,4},{6,5},{7,6},{8,11},{9,8},{10,9... | collective-permute-start | bytes 1179656 | tf_op jit(solution)/shard_map/ppermute | solution.py:28
  421.3 13.3 %collective-permute-start.52 = (f32[128]{0:T(128)S(1)}, f32[128]{0:T(128)S(1)}, u32[]{:S(2)}, u32[]{:S(2)}) collective-permute-start(f32[128]{0:T(128)S(1)} %get-tuple-element.297), channel_id=1, source_target_pairs={{0,1},{1,2},{2,3},{3,0},{4,5},{5,6},{6,7},{7,4},{8,9},{9,10},{10,1... | collective-permute-start | bytes 1544 | tf_op jit(solution)/shard_map/ppermute | solution.py:28
  423.4 14.3 %collective-permute-start.51 = (f32[128]{0:T(128)S(1)}, f32[128]{0:T(128)S(1)}, u32[]{:S(2)}, u32[]{:S(2)}) collective-permute-start(f32[128]{0:T(128)S(1)} %get-tuple-element.297), channel_id=1, source_target_pairs={{0,2},{1,3},{2,0},{3,1},{4,6},{5,7},{6,4},{7,5},{8,10},{9,11},{10,... | collective-permute-start | bytes 1544 | tf_op jit(solution)/shard_map/ppermute | solution.py:28
  455.9 13.5 %collective-permute-start.55 = (bf16[144,768]{1,0:T(8,128)(2,1)}, bf16[144,768]{1,0:T(8,128)(2,1)S(1)}, u32[]{:S(2)}, u32[]{:S(2)}) collective-permute-start(bf16[144,768]{1,0:T(8,128)(2,1)} %get-tuple-element.70), channel_id=1, source_target_pairs={{4,0},{8,4},{12,8},{0,12},{20,16},{24,20},{28,24},{16,28},{36,32},... | collective-permute-start | bytes 663560 | tf_op jit(solution)/shard_map/ppermute | solution.py:40
  461.1 12.4 %collective-permute-start.53 = (bf16[144,768]{1,0:T(8,128)(2,1)}, bf16[144,768]{1,0:T(8,128)(2,1)S(1)}, u32[]{:S(2)}, u32[]{:S(2)}) collective-permute-start(bf16[144,768]{1,0:T(8,128)(2,1)} %get-tuple-element.70), channel_id=1, source_target_pairs={{12,0},{0,4},{4,8},{8,12},{28,16},{16,20},{20,24},{24,28},{44,32},... | collective-permute-start | bytes 663560 | tf_op jit(solution)/shard_map/ppermute | solution.py:40
  482.5 45.3 %collective-permute-start.94 = (bf16[384,1536]{1,0:T(8,128)(2,1)S(1)}, bf16[384,1536]{1,0:T(8,128)(2,1)S(1)}, u32[]{:S(2)}, u32[]{:S(2)}) collective-permute-start(bf16[384,1536]{1,0:T(8,128)(2,1)S(1)} %convolution_convert_fusion), channel_id=1, source_target_pairs={{0,64},{64,0},{1,65},{65,1},{2,66},{66,2},{3,67},{67,3},{4,68},{68... | collective-permute-start | bytes 3538952 | tf_op jit(solution)/shard_map/ppermute | solution.py:44
  515.3 21.5 %collective-permute-start.62 = (bf16[128,1536]{1,0:T(8,128)(2,1)}, bf16[128,1536]{1,0:T(8,128)(2,1)}, u32[]{:S(2)}, u32[]{:S(2)}) collective-permute-start(bf16[128,1536]{1,0:T(8,128)(2,1)} %fusion.35), channel_id=1, source_target_pairs={{0,3},{1,0},{2,1},{3,2},{4,7},{5,4},{6,5},{7,6},{8,11},{9,8},{10,9... | collective-permute-start | bytes 1179656 | tf_op jit(solution)/shard_map/ppermute | solution.py:28
  520.1 16.7 %collective-permute-start.61 = (bf16[128,1536]{1,0:T(8,128)(2,1)}, bf16[128,1536]{1,0:T(8,128)(2,1)}, u32[]{:S(2)}, u32[]{:S(2)}) collective-permute-start(bf16[128,1536]{1,0:T(8,128)(2,1)} %fusion.34), channel_id=1, source_target_pairs={{0,2},{1,3},{2,0},{3,1},{4,6},{5,7},{6,4},{7,5},{8,10},{9,11},{10,... | collective-permute-start | bytes 1179656 | tf_op jit(solution)/shard_map/ppermute | solution.py:28
  526.6 13.2 %collective-permute-start.60 = (bf16[128,1536]{1,0:T(8,128)(2,1)}, bf16[128,1536]{1,0:T(8,128)(2,1)}, u32[]{:S(2)}, u32[]{:S(2)}) collective-permute-start(bf16[128,1536]{1,0:T(8,128)(2,1)} %fusion.33), channel_id=1, source_target_pairs={{0,1},{1,2},{2,3},{3,0},{4,5},{5,6},{6,7},{7,4},{8,9},{9,10},{10,1... | collective-permute-start | bytes 1179656 | tf_op jit(solution)/shard_map/ppermute | solution.py:28
  531.3 214.2 %reduce-scatter.19.cloned.1.call-start = ((), (), s32[]{:S(2)}) async-start(), calls=%async_computation.15 | async-start | bytes 2506752
  543.2 24.4 %collective-permute-start.65 = (bf16[128,1536]{1,0:T(8,128)(2,1)S(1)}, bf16[128,1536]{1,0:T(8,128)(2,1)S(1)}, u32[]{:S(2)}, u32[]{:S(2)}) collective-permute-start(bf16[128,1536]{1,0:T(8,128)(2,1)S(1)} %get-tuple-element.146), channel_id=1, source_target_pairs={{0,1},{1,2},{2,3},{3,0},{4,5},{5,6},{6,7},{7,4},{8,9},{9,10},{10,1... | collective-permute-start | bytes 1179656 | tf_op jit(solution)/shard_map/ppermute | solution.py:28
  546.9 20.7 %collective-permute-start.64 = (bf16[128,1536]{1,0:T(8,128)(2,1)S(1)}, bf16[128,1536]{1,0:T(8,128)(2,1)S(1)}, u32[]{:S(2)}, u32[]{:S(2)}) collective-permute-start(bf16[128,1536]{1,0:T(8,128)(2,1)S(1)} %get-tuple-element.146), channel_id=1, source_target_pairs={{0,2},{1,3},{2,0},{3,1},{4,6},{5,7},{6,4},{7,5},{8,10},{9,11},{10,... | collective-permute-start | bytes 1179656 | tf_op jit(solution)/shard_map/ppermute | solution.py:28
  546.9 20.7 %collective-permute-start.63 = (bf16[128,1536]{1,0:T(8,128)(2,1)S(1)}, bf16[128,1536]{1,0:T(8,128)(2,1)}, u32[]{:S(2)}, u32[]{:S(2)}) collective-permute-start(bf16[128,1536]{1,0:T(8,128)(2,1)S(1)} %get-tuple-element.146), channel_id=1, source_target_pairs={{0,3},{1,0},{2,1},{3,2},{4,7},{5,4},{6,5},{7,6},{8,11},{9,8},{10,9... | collective-permute-start | bytes 1179656 | tf_op jit(solution)/shard_map/ppermute | solution.py:28
  547.6 12.7 %collective-permute-start.68 = (f32[128]{0:T(128)S(1)}, f32[128]{0:T(128)S(1)}, u32[]{:S(2)}, u32[]{:S(2)}) collective-permute-start(f32[128]{0:T(128)S(1)} %get-tuple-element.295), channel_id=1, source_target_pairs={{0,1},{1,2},{2,3},{3,0},{4,5},{5,6},{6,7},{7,4},{8,9},{9,10},{10,1... | collective-permute-start | bytes 1544 | tf_op jit(solution)/shard_map/ppermute | solution.py:28
  549.6 15.9 %collective-permute-start.67 = (f32[128]{0:T(128)S(1)}, f32[128]{0:T(128)S(1)}, u32[]{:S(2)}, u32[]{:S(2)}) collective-permute-start(f32[128]{0:T(128)S(1)} %get-tuple-element.295), channel_id=1, source_target_pairs={{0,2},{1,3},{2,0},{3,1},{4,6},{5,7},{6,4},{7,5},{8,10},{9,11},{10,... | collective-permute-start | bytes 1544 | tf_op jit(solution)/shard_map/ppermute | solution.py:28
  587.0 198.4 %reduce-scatter.17.cloned.1.call-start = ((), (), s32[]{:S(2)}) async-start(), calls=%async_computation.14 | async-start | bytes 2506752 | tf_op jit(solution)/shard_map/reduce_scatter | solution.py:818
  591.5 30.7 %collective-permute-start.86 = (bf16[1536,384]{1,0:T(8,128)(2,1)}, bf16[1536,384]{1,0:T(8,128)(2,1)}, u32[]{:S(2)}, u32[]{:S(2)}) collective-permute-start(bf16[1536,384]{1,0:T(8,128)(2,1)} %convolution_convert_fusion.2), channel_id=1, source_target_pairs={{0,64},{64,0},{1,65},{65,1},{2,66},{66,2},{3,67},{67,3},{4,68},{68... | collective-permute-start | bytes 3538952 | tf_op jit(solution)/shard_map/ppermute | solution.py:44
  593.9 13.6 %collective-permute-start.69 = (bf16[144,768]{1,0:T(8,128)(2,1)S(1)}, bf16[144,768]{1,0:T(8,128)(2,1)}, u32[]{:S(2)}, u32[]{:S(2)}) collective-permute-start(bf16[144,768]{1,0:T(8,128)(2,1)S(1)} %copy-done.55), channel_id=1, source_target_pairs={{12,0},{0,4},{4,8},{8,12},{28,16},{16,20},{20,24},{24,28},{44,32},... | collective-permute-start | bytes 663560 | tf_op jit(solution)/shard_map/ppermute | solution.py:40
  611.1 17.4 %collective-permute-start.74 = (bf16[144,768]{1,0:T(8,128)(2,1)}, bf16[144,768]{1,0:T(8,128)(2,1)}, u32[]{:S(2)}, u32[]{:S(2)}) collective-permute-start(bf16[144,768]{1,0:T(8,128)(2,1)} %maximum_maximum_fusion.5), channel_id=1, source_target_pairs={{16,0},{20,4},{24,8},{28,12},{32,16},{36,20},{40,24},{44,28},{48,3... | collective-permute-start | bytes 663560 | tf_op jit(solution)/shard_map/ppermute | solution.py:40
  615.8 13.5 %collective-permute-start.73 = (bf16[144,768]{1,0:T(8,128)(2,1)}, bf16[144,768]{1,0:T(8,128)(2,1)}, u32[]{:S(2)}, u32[]{:S(2)}) collective-permute-start(bf16[144,768]{1,0:T(8,128)(2,1)} %maximum_maximum_fusion.5), channel_id=1, source_target_pairs={{32,0},{36,4},{40,8},{44,12},{48,16},{52,20},{56,24},{60,28},{33,1... | collective-permute-start | bytes 663560 | tf_op jit(solution)/shard_map/ppermute | solution.py:40
  626.5 239.0 %reduce-scatter.15.cloned.1.call-start = ((), (), s32[]{:S(2)}) async-start(), calls=%async_computation.13 | async-start | bytes 4177920 | tf_op jit(solution)/shard_map/reduce_scatter | solution.py:818
  678.1 264.4 %reduce-scatter.13.cloned.1.call-start = ((), (), s32[]{:S(2)}) async-start(), calls=%async_computation.12 | async-start | bytes 2506752 | tf_op jit(solution)/shard_map/reduce_scatter | solution.py:818
  686.2 336.3 %reduce-scatter.11.cloned.1.call-start = ((), (), s32[]{:S(2)}) async-start(), calls=%async_computation.11 | async-start | bytes 4177920 | tf_op jit(solution)/shard_map/reduce_scatter | solution.py:818
  704.7 33.3 %collective-permute-start.46 = (bf16[128,1536]{1,0:T(8,128)(2,1)}, bf16[128,1536]{1,0:T(8,128)(2,1)S(1)}, u32[]{:S(2)}, u32[]{:S(2)}) collective-permute-start(bf16[128,1536]{1,0:T(8,128)(2,1)} %get-tuple-element.301), channel_id=1, source_target_pairs={{0,64},{64,0},{1,65},{65,1},{2,66},{66,2},{3,67},{67,3},{4,68},{68... | collective-permute-start | bytes 1179656 | tf_op jit(solution)/shard_map/ppermute | solution.py:44
  710.7 15.0 %collective-permute-start.78 = (bf16[128,1536]{1,0:T(8,128)(2,1)S(1)}, bf16[128,1536]{1,0:T(8,128)(2,1)S(1)}, u32[]{:S(2)}, u32[]{:S(2)}) collective-permute-start(bf16[128,1536]{1,0:T(8,128)(2,1)S(1)} %fusion.38), channel_id=1, source_target_pairs={{0,3},{1,0},{2,1},{3,2},{4,7},{5,4},{6,5},{7,6},{8,11},{9,8},{10,9... | collective-permute-start | bytes 1179656 | tf_op jit(solution)/shard_map/ppermute | solution.py:28
  715.0 15.9 %collective-permute-start.77 = (bf16[128,1536]{1,0:T(8,128)(2,1)S(1)}, bf16[128,1536]{1,0:T(8,128)(2,1)S(1)}, u32[]{:S(2)}, u32[]{:S(2)}) collective-permute-start(bf16[128,1536]{1,0:T(8,128)(2,1)S(1)} %fusion.37), channel_id=1, source_target_pairs={{0,2},{1,3},{2,0},{3,1},{4,6},{5,7},{6,4},{7,5},{8,10},{9,11},{10,... | collective-permute-start | bytes 1179656 | tf_op jit(solution)/shard_map/ppermute | solution.py:28
  722.0 13.3 %collective-permute-start.76 = (bf16[128,1536]{1,0:T(8,128)(2,1)S(1)}, bf16[128,1536]{1,0:T(8,128)(2,1)S(1)}, u32[]{:S(2)}, u32[]{:S(2)}) collective-permute-start(bf16[128,1536]{1,0:T(8,128)(2,1)S(1)} %fusion.36), channel_id=1, source_target_pairs={{0,1},{1,2},{2,3},{3,0},{4,5},{5,6},{6,7},{7,4},{8,9},{9,10},{10,1... | collective-permute-start | bytes 1179656 | tf_op jit(solution)/shard_map/ppermute | solution.py:28
  739.5 16.4 %collective-permute-start.97 = (f32[24,1536]{1,0:T(8,128)}, f32[24,1536]{1,0:T(8,128)S(1)}, u32[]{:S(2)}, u32[]{:S(2)}) collective-permute-start(f32[24,1536]{1,0:T(8,128)} %reduce-scatter.21.cloned.1.call-done), channel_id=1, source_target_pairs={{4,64},{5,80},{6,96},{7,112},{12,65},{13,81},{14,97},{15,113},{20,... | collective-permute-start | bytes 442376 | tf_op jit(solution)/shard_map/ppermute | solution.py:833
  740.8 15.1 %collective-permute-start.95 = (f32[24,1536]{1,0:T(8,128)}, f32[24,1536]{1,0:T(8,128)S(1)}, u32[]{:S(2)}, u32[]{:S(2)}) collective-permute-start(f32[24,1536]{1,0:T(8,128)} %reduce-scatter.21.cloned.1.call-done), channel_id=1, source_target_pairs={{0,64},{1,80},{2,96},{3,112},{8,65},{9,81},{10,97},{11,113},{16,66... | collective-permute-start | bytes 442376 | tf_op jit(solution)/shard_map/ppermute | solution.py:833
  746.2 11.8 %collective-permute-start.93 = (f32[24,1536]{1,0:T(8,128)}, f32[24,1536]{1,0:T(8,128)S(1)}, u32[]{:S(2)}, u32[]{:S(2)}) collective-permute-start(f32[24,1536]{1,0:T(8,128)} %reduce-scatter.19.cloned.1.call-done), channel_id=1, source_target_pairs={{0,0},{1,16},{2,32},{3,48},{8,1},{9,17},{10,33},{11,49},{16,2},{17... | collective-permute-start | bytes 442376 | tf_op jit(solution)/shard_map/ppermute | solution.py:833
  866.6 158.5 %collective-permute-start.87 = (f32[24,1024]{1,0:T(8,128)S(1)}, f32[24,1024]{1,0:T(8,128)S(1)}, u32[]{:S(2)}, u32[]{:S(2)}) collective-permute-start(f32[24,1024]{1,0:T(8,128)S(1)} %get-tuple-element.193), channel_id=1, source_target_pairs={{0,3},{1,0},{2,1},{3,2},{4,7},{5,4},{6,5},{7,6},{8,11},{9,8},{10,9... | collective-permute-start | bytes 294920 | tf_op jit(solution)/shard_map/ppermute | solution.py:28
  867.2 159.7 %collective-permute-start.88 = (f32[24,1024]{1,0:T(8,128)S(1)}, f32[24,1024]{1,0:T(8,128)S(1)}, u32[]{:S(2)}, u32[]{:S(2)}) collective-permute-start(f32[24,1024]{1,0:T(8,128)S(1)} %get-tuple-element.192), channel_id=1, source_target_pairs={{0,2},{1,3},{2,0},{3,1},{4,6},{5,7},{6,4},{7,5},{8,10},{9,11},{10,... | collective-permute-start | bytes 294920 | tf_op jit(solution)/shard_map/ppermute | solution.py:28
  868.1 158.9 %collective-permute-start.89 = (f32[24,1024]{1,0:T(8,128)S(1)}, f32[24,1024]{1,0:T(8,128)S(1)}, u32[]{:S(2)}, u32[]{:S(2)}) collective-permute-start(f32[24,1024]{1,0:T(8,128)S(1)} %get-tuple-element.190), channel_id=1, source_target_pairs={{0,1},{1,2},{2,3},{3,0},{4,5},{5,6},{6,7},{7,4},{8,9},{9,10},{10,1... | collective-permute-start | bytes 294920 | tf_op jit(solution)/shard_map/ppermute | solution.py:28
  (233 other events, 2338.1 us)
Sparse Core Ops, SparseCore 0:
  22.0 52.0 all-gather.5
  76.2 42.3 all-gather.7
  120.7 44.0 all-gather.11
  166.8 44.7 all-gather.9
  213.6 43.8 all-gather.13
  531.5 79.5 reduce-scatter.20
  614.3 74.1 reduce-scatter.18
  691.8 93.5 reduce-scatter.16
  788.8 76.6 reduce-scatter.14
  868.7 73.7 reduce-scatter.12
  945.9 76.5 reduce-scatter.10

commit v2 on v1

--- a/solution.py
+++ b/solution.py
@@ -19,8 +19,9 @@
 PAIRS = 6
 EXTRA = 256
 ACT = GROUP + 2 * N
-STEP_AT, SMALL_AT, SMALL = 0, 19, 13
-VMEM = 40 * 1024 * 1024
+SMALL_AT, SMALL = 19, 13
+WIDE = HALF + EXTRA + HALF
+VMEM = 24 * 1024 * 1024
 epsilon = 1e-05
 
 
@@ -45,22 +46,23 @@
 
 
 def gather_head(a):
+    one, three = from_head(a, 1), from_head(a, 3)
     two = from_head(a, 2)
-    one, three = from_head(a, 1), from_head(a, 3)
     return [a, one, two, three]
 
 
 def scatter_head(parts):
-    two = from_head(parts[2].astype(bf16), 2)
-    one, three = from_head(parts[1].astype(bf16), 3), from_head(parts[3].astype(bf16), 1)
-    return parts[0] + one.astype(f32) + two.astype(f32) + three.astype(f32)
+    one, three = from_head(parts[1], 3), from_head(parts[3], 1)
+    two = from_head(parts[2], 2)
+    return [parts[0], one, two, three]
 
 
 def exchange_head(parts, place):
     got = [lax.dynamic_index_in_dim(parts, place, 0, False)]
-    for k in (1, 2, 3):
+    for k in (1, 3, 2):
         sent = lax.dynamic_index_in_dim(parts, lax.rem(place + 4 - k, 4), 0, False)
         got.append(from_head(sent, k))
+    got = [got[0], got[1], got[3], got[2]]
     twice = jnp.stack(got + got)
     return lax.dynamic_slice_in_dim(twice, lax.rem(4 - place, 4), 4, 0)
 
@@ -78,7 +80,7 @@
     seq = lax.axis_index("seq")
     y = lax.rem(seq, 4)
     ahead = y if sign < 0 else 3 - y
-    near = {k: unpack_state(from_seq(packed, 0, sign * k, True)) for k in (2, 1, 3)}
+    near = {k: unpack_state(from_seq(packed, 0, sign * k, True)) for k in (1, 3, 2)}
     own = unpack_state(packed)
     before = (jnp.ones_like(own[0]), jnp.zeros_like(own[1]))
     after = own
@@ -89,7 +91,7 @@
         after = join(after, (jnp.where(use, 1.0, decay), jnp.where(use, 0.0, state)))
     whole = join(before, after)
     packed_whole = pack_state(whole[0], whole[1])
-    far = {k: unpack_state(from_seq(packed_whole, sign * k, 0, False)) for k in (2, 1, 3)}
+    far = {k: unpack_state(from_seq(packed_whole, sign * k, 0, False)) for k in (1, 3, 2)}
     total = jnp.zeros_like(own[1])
     for k in (3, 2, 1):
         decay, state = far[k]
@@ -278,11 +280,64 @@
     )(place, conv_in, step, rim, taps, hp, skip)
 
 
-def gate_kernel(mixed, run, query, entering, gate, gain, mixed_out, normed, square):
+def project_kernel(core, feed, gain, own, other, normed, conv_in, step, gate):
+    values = feed[...].astype(f32)
+    scale = lax.rsqrt(jnp.mean(values * values, axis=1, keepdims=True) + epsilon)
+    low = (values * scale * gain[0:1]).astype(bf16)
+    normed[...] = low
+    mine = dot(low, own[...])
+    theirs = dot(low, other[...])
+    is_first = core[0] == 0
+    edge = HALF + EXTRA
+    conv_in[:, :HALF] = mine[:, :HALF].astype(bf16)
+    conv_in[:, HALF:GROUP] = theirs[:, :HALF].astype(bf16)
+    conv_in[:, GROUP:] = jnp.where(is_first, mine[:, HALF:edge], theirs[:, HALF:edge]).astype(bf16)
+    slot = jnp.where(is_first, theirs[:, HALF : HALF + 128], mine[:, HALF + 128 : edge])
+    step[...] = slot.astype(bf16).astype(f32)
+    gate[:, :HALF] = mine[:, edge:]
+    gate[:, HALF:] = theirs[:, edge:]
+
+
+def project(core, feed, gain, own, other):
+    tokens = feed.shape[0]
+
+    def whole(shape):
+        return pl.BlockSpec(shape, lambda k, core: (0, 0))
+
+    def piece(width):
+        return pl.BlockSpec((2 * PIECE, width), lambda k, core: (k, 0))
+
+    return pl.pallas_call(
+        project_kernel,
+        grid_spec=pltpu.PrefetchScalarGridSpec(
+            num_scalar_prefetch=1,
+            grid=(tokens // (2 * PIECE),),
+            in_specs=[piece(D), whole((8, D)), whole((D, WIDE)), whole((D, WIDE))],
+            out_specs=[piece(D), piece(ACT), piece(128), piece(GROUP)],
+        ),
+        out_shape=[
+            jax.ShapeDtypeStruct((tokens, D), bf16),
+            jax.ShapeDtypeStruct((tokens, ACT), bf16),
+            jax.ShapeDtypeStruct((tokens, 128), f32),
+            jax.ShapeDtypeStruct((tokens, GROUP), f32),
+        ],
+        compiler_params=pltpu.CompilerParams(vmem_limit_bytes=VMEM),
+        cost_estimate=pl.CostEstimate(
+            flops=3_200_000_000, bytes_accessed=12_000_000, transcendentals=1000
+        ),
+        name="project",
+    )(core, feed, gain, own, other)
+
+
+def gate_kernel(
+    mixed, run, query, entering, gate, gain, out_own, out_other, mixed_out, sent0, sent1, sent2, sent3
+):
+    k = pl.program_id(0)
     decay = jnp.exp(run[...])
     queries = query[...]
     first = lanes((PIECE, 128)) < 64
     total = jnp.zeros((PIECE, 1), f32)
+    normed = []
     for j in range(PAIRS):
         cols = slice(128 * j, 128 * j + 128)
         y = mixed[:, cols] + spread(decay, j, first) * dot(queries, entering[:, cols])
@@ -290,11 +345,21 @@
         pre = gate[:, cols]
         gated = y.astype(bf16).astype(f32) * (pre * jax.nn.sigmoid(pre))
         total = total + jnp.sum(gated * gated, axis=1, keepdims=True)
-        normed[:, cols] = (gated * gain[0:1, cols]).astype(bf16)
-    square[...] = jnp.broadcast_to(total, square.shape)
-
-
-def gate_out(mixed, run, query, entering, gate, gain):
+        normed.append((gated * gain[0:1, cols]).astype(bf16))
+    part = dot(jnp.concatenate(normed[:3], axis=1), out_own[...])
+    part = part + dot(jnp.concatenate(normed[3:], axis=1), out_other[...])
+    lane = lanes((PIECE, 128))
+    high = total.astype(bf16).astype(f32)
+    split = jnp.where(lane == 0, high, jnp.where(lane == 1, total - high, 0.0))
+    for index, sent in enumerate((sent0, sent1, sent2, sent3)):
+
+        @pl.when(k == index)
+        def _():
+            sent[:, :D] = part.astype(sent.dtype)
+            sent[:, D:] = split.astype(sent.dtype)
+
+
+def gate_out(mixed, run, query, entering, gate, gain, out_own, out_other):
     tokens = mixed.shape[0]
 
     def whole(shape):
@@ -313,43 +378,48 @@
             whole((N, GROUP)),
             piece(GROUP),
             whole((8, GROUP)),
+            whole((HALF, D)),
+            whole((HALF, D)),
         ],
-        out_specs=[piece(GROUP), piece(GROUP), piece(128)],
-        out_shape=[
-            jax.ShapeDtypeStruct((tokens, GROUP), f32),
-            jax.ShapeDtypeStruct((tokens, GROUP), bf16),
-            jax.ShapeDtypeStruct((tokens, 128), f32),
-        ],
+        out_specs=[piece(GROUP)] + [whole((PIECE, D + 128))] * 4,
+        out_shape=[jax.ShapeDtypeStruct((tokens, GROUP), f32)]
+        + [jax.ShapeDtypeStruct((PIECE, D + 128), f32 if k == 0 else bf16) for k in range(4)],
         compiler_params=pltpu.CompilerParams(vmem_limit_bytes=VMEM),
         cost_estimate=pl.CostEstimate(
-            flops=110_000_000, bytes_accessed=6_500_000, transcendentals=400_000
+            flops=1_300_000_000, bytes_accessed=9_000_000, transcendentals=400_000
         ),
         name="gate_out",
-    )(mixed, run, query, entering, gate, gain)
+    )(mixed, run, query, entering, gate, gain, out_own, out_other)
 
 
 def gate_back_kernel(
-    grad, gate, mixed, scale, run, query, gain, decay, grad_scan, grad_gate, normed, packed, state
+    grad_new, out_own, out_other, gate, mixed, scale, run, query, gain, decay,
+    grad_scan, grad_gate, normed, packed, state, product
 ):
     k = pl.program_id(0)
 
     @pl.when(k == 0)
     def _():
         state[...] = jnp.zeros_like(state)
-
+        product[:, :HALF] = dot_nt(grad_new[...], out_own[...])
+        product[:, HALF:] = dot_nt(grad_new[...], out_other[...])
+
+    token = pl.ds(pl.multiple_of(k * PIECE, PIECE), PIECE)
     grown = jnp.exp(run[...])
     queries_t = query[...].astype(f32).T.astype(bf16)
     first = lanes((PIECE, 128)) < 64
-    s_out, mean = scale[:, 0:1], scale[:, 1:2]
+    parts = scale[...].astype(f32)
+    s_out, mean = parts[:, 0:1] + parts[:, 1:2], parts[:, 2:3] + parts[:, 3:4]
     row16 = rows((16, 128))
     for j in range(PAIRS):
         cols = slice(128 * j, 128 * j + 128)
+        grad = product[token, cols]
         pre = gate[:, cols]
         sig = jax.nn.sigmoid(pre)
         out = mixed[:, cols].astype(bf16).astype(f32)
         unit = out * (pre * sig) * s_out
         gain_j = gain[0:1, cols]
-        gated = s_out * (grad[:, cols] * gain_j - unit * mean)
+        gated = s_out * (grad * gain_j - unit * mean)
         scan = (gated * (pre * sig)).astype(bf16)
         grad_scan[:, cols] = scan
         grad_gate[:, cols] = (gated * out * sig * (1.0 + pre * (1.0 - sig))).astype(bf16)
@@ -364,7 +434,7 @@
         ).astype(bf16)
 
 
-def gate_back(grad, gate, mixed, scale, run, query, gain, decay):
+def gate_back(grad_new, out_own, out_other, gate, mixed, scale, run, query, gain, decay):
     tokens = mixed.shape[0]
 
     def whole(shape):
@@ -377,7 +447,9 @@
         gate_back_kernel,
         grid=(tokens // PIECE,),
         in_specs=[
-            piece(GROUP),
+            whole((tokens, D)),
+            whole((HALF, D)),
+            whole((HALF, D)),
             piece(GROUP),
             piece(GROUP),
             piece(128),
@@ -393,18 +465,19 @@
             jax.ShapeDtypeStruct((tokens, GROUP), bf16),
             jax.ShapeDtypeStruct((N + 16, GROUP), bf16),
         ],
-        scratch_shapes=[pltpu.VMEM((N, GROUP), f32)],
+        scratch_shapes=[pltpu.VMEM((N, GROUP), f32), pltpu.VMEM((tokens, GROUP), f32)],
         compiler_params=pltpu.CompilerParams(vmem_limit_bytes=VMEM),
         cost_estimate=pl.CostEstimate(
-            flops=120_000_000, bytes_accessed=8_000_000, transcendentals=400_000
+            flops=1_400_000_000, bytes_accessed=12_000_000, transcendentals=400_000
         ),
         name="gate_back",
-    )(grad, gate, mixed, scale, run, query, gain, decay)
+    )(grad_new, out_own, out_other, gate, mixed, scale, run, query, gain, decay)
 
 
 def scan_back_kernel(
-    place, conv_in, pre_in, step, run, grad, mixed, starts, last, entering, leaving, rim, taps, hp,
-    skip, grad_in, tail, grad_step, rim_grad, grad_taps, grad_hp, act, delta, state, after, skip_sum
+    place, conv_in, pre_in, step, run, grad, grad_gate, mixed, starts, last, entering, leaving, rim,
+    taps, hp, skip, use_own, use_other, tail, rim_grad, grad_taps, grad_hp, act, delta, state, after,
+    skip_sum
 ):
     k = pl.program_id(0)
     count = pl.num_programs(0)
@@ -496,7 +569,19 @@
     rate = jnp.exp(hp[1:2])
     live = lanes((PIECE, 128)) < HEADS
     grad_raw = jnp.where(live, (inner_sum - rate * grad_log) * jax.nn.sigmoid(raw), 0.0)
-    grad_step[...] = grad_raw.astype(bf16)
+    is_first = place[1] == 0
+    edge = HALF + EXTRA
+    step_first = jnp.where(is_first, grad_raw, 0.0)
+    step_second = jnp.where(is_first, 0.0, grad_raw)
+    for use, gate_cols in ((use_own, slice(0, HALF)), (use_other, slice(HALF, GROUP))):
+        use[:, edge:] = grad_gate[:, gate_cols]
+
+    @pl.when(k == 0)
+    def _():
+        for side, gate_cols in ((0, slice(0, HALF)), (1, slice(HALF, GROUP))):
+            tail[:, WIDE * side + edge : WIDE * side + WIDE] = grad_gate[
+                PIECE - 16 :, gate_cols
+            ].astype(f32)[8:]
     grad_hp[0:1] += jnp.sum(grad_raw, axis=0, keepdims=True)
     grad_hp[1:2] += jnp.sum(jnp.where(live, grad_log * log_decay, 0.0), axis=0, keepdims=True)
 
@@ -513,11 +598,24 @@
             moved = delta[3 - t : 3 - t + PIECE, cols]
             total = total + taps[t : t + 1, cols] * moved
             grad_taps[t : t + 1, cols] += jnp.sum(taken * moved, axis=0, keepdims=True)
-        grad_in[:, cols] = total.astype(bf16)
+        if j < PAIRS:
+            use = use_own if j < 3 else use_other
+            at = 128 * (j % 3)
+            use[:, at : at + 128] = total.astype(bf16)
+            targets = [(WIDE * (j // 3) + at, total)]
+        else:
+            at = HALF + 128 * (j - PAIRS)
+            slot = step_first if j == PAIRS else step_second
+            first_use = jnp.where(is_first, total, slot)
+            second_use = jnp.where(is_first, slot, total)
+            use_own[:, at : at + 128] = first_use.astype(bf16)
+            use_other[:, at : at + 128] = second_use.astype(bf16)
+            targets = [(at, first_use), (WIDE + at, second_use)]
 
         @pl.when(k == 0)
         def _():
-            tail[:, cols] = total[PIECE - 8 :]
+            for at, values in targets:
+                tail[:, at : at + 128] = values[PIECE - 8 :]
 
     @pl.when(k == count - 1)
     def _():
@@ -528,18 +626,27 @@
             grad_hp[2:3] += sums[0:1]
         for j in range(ACT // 128):
             cols = slice(128 * j, 128 * j + 128)
-            edge = jnp.concatenate([jnp.zeros((8, 128), f32), delta[0:8, cols]], axis=0)
+            border = jnp.concatenate([jnp.zeros((8, 128), f32), delta[0:8, cols]], axis=0)
             taken = rim[:, cols].astype(f32)
             total = jnp.zeros((8, 128), f32)
             for t in range(4):
-                moved = edge[3 - t : 11 - t]
+                moved = border[3 - t : 11 - t]
                 total = total + taps[t : t + 1, cols] * moved
                 grad_taps[t : t + 1, cols] += jnp.sum(taken * moved, axis=0, keepdims=True)
-            rim_grad[:, cols] = total
+            if j < PAIRS:
+                at = WIDE * (j // 3) + 128 * (j % 3)
+                rim_grad[:, at : at + 128] = total
+            else:
+                at = HALF + 128 * (j - PAIRS)
+                rim_grad[:, at : at + 128] = jnp.where(is_first, total, 0.0)
+                rim_grad[:, WIDE + at : WIDE + at + 128] = jnp.where(is_first, 0.0, total)
+        for side in range(2):
+            rim_grad[:, WIDE * side + edge : WIDE * side + WIDE] = jnp.zeros((8, HALF), f32)
 
 
 def scan_back(
-    place, conv_in, pre, step, run, grad, mixed, starts, last, entering, leaving, rim, taps, hp, skip
+    place, conv_in, pre, step, run, grad, grad_gate, mixed, starts, last, entering, leaving, rim,
+    taps, hp, skip
 ):
     tokens = conv_in.shape[0]
     count = tokens // PIECE
@@ -562,6 +669,7 @@
                 piece(128),
                 piece(GROUP),
                 piece(GROUP),
+                piece(GROUP),
                 pl.BlockSpec((1, N, GROUP), lambda k, place: (count - 1 - k, 0, 0)),
                 whole((N, GROUP)),
                 whole((N, GROUP)),
@@ -572,10 +680,10 @@
                 whole((8, GROUP)),
             ],
             out_specs=[
-                piece(ACT),
-                whole((8, ACT)),
-                piece(128),
-                whole((8, ACT)),
+                piece(WIDE),
+                piece(WIDE),
+                whole((8, 2 * WIDE)),
+                whole((8, 2 * WIDE)),
                 whole((8, ACT)),
                 whole((8, 128)),
             ],
@@ -588,10 +696,10 @@
             ],
         ),
         out_shape=[
-            jax.ShapeDtypeStruct((tokens, ACT), bf16),
-            jax.ShapeDtypeStruct((8, ACT), f32),
-            jax.ShapeDtypeStruct((tokens, 128), bf16),
-            jax.ShapeDtypeStruct((8, ACT), f32),
+            jax.ShapeDtypeStruct((tokens, WIDE), bf16),
+            jax.ShapeDtypeStruct((tokens, WIDE), bf16),
+            jax.ShapeDtypeStruct((8, 2 * WIDE), f32),
+            jax.ShapeDtypeStruct((8, 2 * WIDE), f32),
             jax.ShapeDtypeStruct((8, ACT), f32),
             jax.ShapeDtypeStruct((8, 128), f32),
         ],
@@ -600,40 +708,169 @@
             flops=2_000_000_000, bytes_accessed=9_000_000, transcendentals=2_500_000
         ),
         name="scan_back",
-    )(place, conv_in, pre, step, run, grad, mixed, starts, last, entering, leaving, rim, taps, hp,
-      skip)
+    )(place, conv_in, pre, step, run, grad, grad_gate, mixed, starts, last, entering, leaving, rim,
+      taps, hp, skip)
+
+
+def parts_kernel(use_own, use_other, own, other, sent0, sent1, sent2, sent3):
+    part = dot_nt(use_own[...], own[...]) + dot_nt(use_other[...], other[...])
+    for index, sent in enumerate((sent0, sent1, sent2, sent3)):
+        sent[...] = part[PIECE * index : PIECE * index + PIECE].astype(sent.dtype)
+
+
+def project_back(use_own, use_other, own, other):
+    tokens = use_own.shape[0]
+    width = 256
+
+    def whole(shape):
+        return pl.BlockSpec(shape, lambda k: (0, 0))
+
+    return pl.pallas_call(
+        parts_kernel,
+        grid=(D // width,),
+        in_specs=[whole((tokens, WIDE))] * 2 + [pl.BlockSpec((width, WIDE), lambda k: (k, 0))] * 2,
+        out_specs=[pl.BlockSpec((PIECE, width), lambda k: (0, k))] * 4,
+        out_shape=[jax.ShapeDtypeStruct((PIECE, D), f32 if k == 0 else bf16) for k in range(4)],
+        compiler_params=pltpu.CompilerParams(vmem_limit_bytes=VMEM),
+        cost_estimate=pl.CostEstimate(
+            flops=3_200_000_000, bytes_accessed=9_000_000, transcendentals=0
+        ),
+        name="project_back",
+    )(use_own, use_other, own, other)
+
+
+def early_kernel(normed, grad_gate, normed_out, grad_new, own, other, sums):
+    i = pl.program_id(0)
+
+    @pl.when(i == 0)
+    def _():
+        sums[0] = dot_tn(normed_out[:, :HALF], grad_new[...])
+        sums[1] = dot_tn(normed_out[:, HALF:], grad_new[...])
+
+    block = dot_tn(normed[...], grad_gate[...])
+    for side, sent in enumerate((own, other)):
+        sent[:, :HALF] = block[:, HALF * side : HALF * side + HALF].astype(bf16)
+        for s in range(4):
+            row = pl.ds(pl.multiple_of(96 * i + 24 * s, 8), 24)
+            pieces = [sums[side, row, HALF * q : HALF * q + HALF] for q in range(4)]
+            sent[96 * s : 96 * s + 96, HALF:] = jnp.concatenate(pieces, axis=0).astype(bf16)
+
+
+def early_grads(normed, grad_gate, normed_out, grad_new):
+    tokens = normed.shape[0]
+
+    def whole(shape):
+        return pl.BlockSpec(shape, lambda i: (0, 0))
+
+    return pl.pallas_call(
+        early_kernel,
+        grid=(4,),
+        in_specs=[
+            pl.BlockSpec((tokens, HALF), lambda i: (0, i)),
+            whole((tokens, GROUP)),
+            whole((tokens, GROUP)),
+            whole((tokens, D)),
+        ],
+        out_specs=[pl.BlockSpec((HALF, GROUP), lambda i: (i, 0))] * 2,
+        out_shape=[jax.ShapeDtypeStruct((D, GROUP), bf16)] * 2,
+        scratch_shapes=[pltpu.VMEM((2, HALF, D), f32)],
+        compiler_params=pltpu.CompilerParams(vmem_limit_bytes=VMEM),
+        cost_estimate=pl.CostEstimate(
+            flops=2_400_000_000, bytes_accessed=9_000_000, transcendentals=0
+        ),
+        name="early_grads",
+    )(normed, grad_gate, normed_out, grad_new)
+
+
+def split_pair(values, lane, at):
+    high = values.astype(bf16).astype(f32)
+    return jnp.where(lane == at, high, jnp.where(lane == at + 1, values - high, 0.0))
+
+
+def receive_kernel(part, one, two, three, feed, target, branch_out, result, scale):
+    total = part[...] + one[...].astype(f32) + two[...].astype(f32) + three[...].astype(f32)
+    square = total[:, D : D + 1] + total[:, D + 1 : D + 2]
+    s_out = lax.rsqrt(square / DI + epsilon)
+    branch = s_out * total[:, :D]
+    branch_out[...] = branch
+    result[...] = (feed[...].astype(f32) + branch).astype(bf16)
+    mean = jnp.sum(branch * target[...].astype(f32), axis=1, keepdims=True) / DI
+    lane = lanes((PIECE, 128))
+    scale[...] = (split_pair(s_out, lane, 0) + split_pair(mean, lane, 2)).astype(bf16)
+
+
+def receive(parts, feed, target):
+    return pl.pallas_call(
+        receive_kernel,
+        out_shape=[
+            jax.ShapeDtypeStruct((PIECE, D), f32),
+            jax.ShapeDtypeStruct((PIECE, D), bf16),
+            jax.ShapeDtypeStruct((PIECE, 128), bf16),
+        ],
+        compiler_params=pltpu.CompilerParams(vmem_limit_bytes=VMEM),
+        cost_estimate=pl.CostEstimate(
+            flops=3_000_000, bytes_accessed=4_500_000, transcendentals=1000
+        ),
+        name="receive",
+    )(*parts, feed, target)
+
+
+def receive_back_kernel(
+    part, one, two, three, feed, grad_new, gain, branch, scale_in, grad_out, scale_out
+):
+    total = part[...] + one[...].astype(f32) + two[...].astype(f32) + three[...].astype(f32)
+    values = feed[...].astype(f32)
+    s_in = lax.rsqrt(jnp.mean(values * values, axis=1, keepdims=True) + epsilon)
+    unit = values * s_in
+    grad_unit = total * gain[0:1]
+    grad = grad_new[...].astype(f32) + s_in * (
+        grad_unit - unit * jnp.mean(unit * grad_unit, axis=1, keepdims=True)
+    )
+    low = grad.astype(bf16)
+    grad_out[...] = low
+    mean = jnp.sum(branch[...] * low.astype(f32), axis=1, keepdims=True) / DI
+    lane = lanes((PIECE, 128))
+    kept = jnp.where(lane < 2, scale_in[...].astype(f32), 0.0)
+    scale_out[...] = (kept + split_pair(mean, lane, 2)).astype(bf16)
+
+
+def receive_back(parts, feed, grad_new, gain, branch, scale):
+    return pl.pallas_call(
+        receive_back_kernel,
+        out_shape=[
+            jax.ShapeDtypeStruct((PIECE, D), bf16),
+            jax.ShapeDtypeStruct((PIECE, 128), bf16),
+        ],
+        compiler_params=pltpu.CompilerParams(vmem_limit_bytes=VMEM),
+        cost_estimate=pl.CostEstimate(
+            flops=4_000_000, bytes_accessed=4_500_000, transcendentals=1000
+        ),
+        name="receive_back",
+    )(*parts, feed, grad_new, gain, branch, scale)
 
 
 def pick(core, first, second):
     return jnp.where(core == 0, first, second)
 
 
-def spread_weights(core, head, gate_inner, shared_bc, step_proj, input_gain, small):
+def spread_weights(core, head, gate_inner, shared_bc, step_proj):
     gate = gate_inner[:, :DI].reshape(24, 4, 2, HALF)
     inner = gate_inner[:, DI:].reshape(24, 4, 2, HALF)
     heads = step_proj.reshape(24, 4, HEADS)
-    slots = []
-    for g in range(4):
-        own = heads[:, g]
-        slots.append(
-            jnp.concatenate(
-                [own, own[:, :6], input_gain[:, None], small, jnp.zeros((24, EXTRA - 32), bf16)],
-                axis=1,
-            )
-        )
+    fill = jnp.zeros((24, 128 - HEADS), bf16)
     halves = []
     for q in range(2):
-        pieces = [
-            jnp.concatenate(
-                [inner[:, g, q], shared_bc if q == 0 else slots[g], gate[:, g, q]], axis=1
-            )
-            for g in range(4)
-        ]
+        pieces = []
+        for g in range(4):
+            own = heads[:, g]
+            slot = [own, fill, own[:, 6:], own[:, :6], fill]
+            extra = [shared_bc] if q == 0 else slot
+            pieces.append(jnp.concatenate([inner[:, g, q]] + extra + [gate[:, g, q]], axis=1))
         halves.append(jnp.stack(pieces))
     kept = pick(core, halves[0], halves[1])
     got = swap(pick(core, halves[1], halves[0]))
     layers = [pick(core, kept, got), pick(core, got, kept)]
-    return [exchange_head(values, head).reshape(96, HALF + EXTRA + HALF) for values in layers]
+    return [exchange_head(values, head).reshape(96, WIDE) for values in layers]
 
 
 def out_pairs():
@@ -648,14 +885,15 @@
     return pairs
 
 
-def out_back_pairs(layer, part):
+def out_back_pairs(part):
     pairs = []
     for core in range(2):
-        for j in range(8):
+        for place in range(16):
+            layer = (place + part) % 2
             for group in range(4):
-                source = (core * 16 + 2 * j + part) * 4 + group
+                j = place // 2
                 target = (layer * 16 + group * 4 + 2 * core + j // 4) * 4 + j % 4
-                pairs.append((source, target))
+                pairs.append(((core * 16 + place) * 4 + group, target))
     return pairs
 
 
@@ -666,11 +904,21 @@
     return lax.all_gather(a, "seq", axis=0, tiled=True)
 
 
-def layer_params(core, head, slot, step_bias, decay_log, skip_gain):
-    small = slot[:, SMALL_AT : SMALL_AT + SMALL].reshape(64, 24 * SMALL).astype(f32)
-    conv = small[:, :208].reshape(64, 4, 52).transpose(1, 0, 2).reshape(4, DI + 2 * N)
-    bias = small[:, 208:260].reshape(1, DI + 2 * N)
-    gain = small[:, 260:308].reshape(1, DI)
+def gather_small(core, a):
+    other = swap(a)
+    both = jnp.concatenate([pick(core, a, other), pick(core, other, a)], axis=1)
+    width = a.shape[1]
+    both = jnp.pad(both.reshape(2 * width // 128, 128), ((0, 8 - 2 * width // 128), (0, 0)))
+    sent = jnp.broadcast_to(both[None], (64, 8, 128)).reshape(512, 128)
+    got = lax.all_to_all(sent, ("seq", "head"), 0, 0, tiled=True).reshape(64, 1024)
+    return got[:, :width], got[:, width : 2 * width]
+
+
+def layer_params(core, head, small, per_head):
+    gain_in = small[:, :24].reshape(1, D)
+    conv = small[:, 24:232].reshape(64, 4, 52).transpose(1, 0, 2).reshape(4, DI + 2 * N)
+    bias = small[:, 232:284].reshape(1, DI + 2 * N)
+    gain = small[:, 284:332].reshape(1, DI)
     taps = jnp.concatenate([conv, bias, jnp.zeros((3, DI + 2 * N), f32)], axis=0)
 
     def grouped(values, width):
@@ -680,119 +928,83 @@
 
     taps = jnp.concatenate(grouped(taps, HALF) + [taps[:, DI:]], axis=1)
     gain = jnp.broadcast_to(jnp.concatenate(grouped(gain, HALF), axis=1), (8, GROUP))
-    per_head = jnp.concatenate([step_bias, decay_log, skip_gain], axis=0)
     per_head = jnp.concatenate(grouped(per_head, 6), axis=1)
     hp = jnp.pad(per_head, ((0, 5), (0, 128 - HEADS)))
     skip = jnp.broadcast_to(jnp.repeat(per_head[2:3], 64, axis=1), (8, GROUP))
-    return dict(taps=taps, gain=gain, hp=hp, skip=skip)
-
-
-def rms_scale(values):
-    return lax.rsqrt(jnp.mean(values * values, axis=-1, keepdims=True) + epsilon)
-
-
-def piece_rows(values, k):
-    return values[PIECE * k : PIECE * (k + 1)]
-
-
-def layer_forward(core, head, feed, normed, weights):
-    place = head.reshape(1)
-    own = dot(normed, weights["x_own"]).astype(bf16)
-    other = dot(normed, weights["x_other"]).astype(bf16)
-    shared = pick(core, own[:, HALF:], other[:, HALF:])
-    conv_in = jnp.concatenate([own[:, :HALF], other[:, :HALF], shared], axis=1)
-    slot = pick(core, other[:, HALF : HALF + 128], own[:, HALF + 6 : HALF + 134]).astype(f32)
+    return dict(
+        taps=taps, gain=gain, hp=hp, skip=skip, gain_in=jnp.broadcast_to(gain_in, (8, D))
+    )
+
+
+def tied(values, anchor):
+    return lax.optimization_barrier((values, anchor))[0]
+
+
+def layer_forward(core, head, feed, feed_all, target, weights, out_weights):
+    place = jnp.stack([head, core])
+    own, other = weights["own"], weights["other"]
+    normed, conv_in, step, gate = project(core.reshape(1), feed_all, weights["gain_in"], own, other)
     last_row = PIECE * lax.rem(7 - head, 4) + PIECE - 8
     rim = lax.ppermute(
         lax.dynamic_slice_in_dim(conv_in, last_row, 8, 0), "seq", [(i, i + 1) for i in range(15)]
     )
     pre, mixed0, query, run, starts, last, packed = scan_local(
-        place, conv_in, slot, rim, weights["taps"], weights["hp"], weights["skip"]
+        place, conv_in, step, rim, weights["taps"], weights["hp"], weights["skip"]
     )
     entering = carried(packed, -1)
-    gate = jnp.concatenate([dot(normed, weights["g_own"]), dot(normed, weights["g_other"])], axis=1)
-    mixed, normed_out, square = gate_out(mixed0, run, query, entering, gate, weights["gain"])
-    square = square[:, 0].reshape(4, PIECE)
-    total = square
-    for k in (2, 1, 3):
-        total = total + from_head(jnp.roll(square, k, axis=0), k)
-    s_out = lax.rsqrt(total / DI + epsilon)
-    parts = {}
-    for k in (2, 1, 3, 0):
-        piece = piece_rows(normed_out, k)
-        parts[k] = dot(piece[:, :HALF], weights["o_own"]) + dot(piece[:, HALF:], weights["o_other"])
-    branch = s_out[0][:, None] * scatter_head(parts)
-    result = (feed.astype(f32) + branch).astype(bf16)
+    entering, out_own, out_other = out_weights(packed, entering)
+    mixed, *sent = gate_out(
+        mixed0, run, query, entering, gate, weights["gain"], out_own, out_other
+    )
+    branch, result, scale = receive(scatter_head(sent), feed, target)
     kept = dict(
-        feed=feed, normed=normed, gate=gate, conv_in=conv_in, rim=rim, step=slot, pre=pre,
+        feed=feed, normed=normed, gate=gate, conv_in=conv_in, rim=rim, step=step, pre=pre,
         mixed=mixed, query=query, run=run, starts=starts, last=last, entering=entering,
-        s_out=s_out, branch=branch, packed=packed,
+        scale=scale, branch=branch, packed=packed, out_own=out_own, out_other=out_other,
     )
     return result, kept
 
 
-def layer_backward(core, head, incoming, gathered, kept, weights):
-    place = head.reshape(1)
-    grad_new = incoming.astype(f32)
-    mean_own = jnp.sum(kept["branch"] * grad_new, axis=1) / DI
-    mean = jnp.stack(gather_head(mean_own))
-    scale = jnp.stack([kept["s_out"].reshape(-1), mean.reshape(-1)], axis=1)
-    scale = jnp.pad(scale, ((0, 0), (0, 126)))
-    grad_normed_out = jnp.concatenate(
-        [dot_nt(gathered, weights["o_own"]), dot_nt(gathered, weights["o_other"])], axis=1
-    )
+def layer_backward(
+    core, head, incoming, gathered, scale, kept, below, weights, after_gate, before_receive
+):
+    place = jnp.stack([head, core])
+    own, other = weights["own"], weights["other"]
     decay = jnp.broadcast_to(
         kept["packed"][N : N + 1].astype(f32) + kept["packed"][N + 1 : N + 2].astype(f32),
         (8, GROUP),
     )
     grad_scan, grad_gate, normed_out, packed = gate_back(
-        grad_normed_out, kept["gate"], kept["mixed"], scale, kept["run"], kept["query"],
-        weights["gain"], decay,
+        gathered, kept["out_own"], kept["out_other"], kept["gate"], kept["mixed"], scale,
+        kept["run"], kept["query"], weights["gain"], decay,
     )
     leaving = carried(packed, 1)
-    grad_out = (dot_tn(normed_out[:, :HALF], gathered), dot_tn(normed_out[:, HALF:], gathered))
     normed = kept["normed"]
-    grad_g = (dot_tn(normed, grad_gate[:, :HALF]), dot_tn(normed, grad_gate[:, HALF:]))
-    grad_conv, tail, grad_step, rim_grad, grad_taps, grad_hp = scan_back(
-        place, kept["conv_in"], kept["pre"], kept["step"], kept["run"], grad_scan, kept["mixed"],
-        kept["starts"], kept["last"], kept["entering"], leaving, kept["rim"], weights["taps"],
-        weights["hp"], weights["skip"],
+    early, leaving = after_gate(early_grads(normed, grad_gate, normed_out, gathered), leaving)
+    use_own, use_other, tail, rim_grad, grad_taps, grad_hp = scan_back(
+        place, kept["conv_in"], kept["pre"], kept["step"], kept["run"], grad_scan, grad_gate,
+        kept["mixed"], kept["starts"], kept["last"], kept["entering"], leaving, kept["rim"],
+        weights["taps"], weights["hp"], weights["skip"],
     )
     from_next = lax.ppermute(rim_grad, "seq", [(i + 1, i) for i in range(15)])
     last_row = PIECE * lax.rem(7 - head, 4) + PIECE - 8
-    grad_conv = lax.dynamic_update_slice_in_dim(
-        grad_conv, (tail + from_next).astype(bf16), last_row, 0
-    )
-    shared = grad_conv[:, GROUP:]
-    first, second = grad_step[:, :6], grad_step[:, 6:12]
-    step = jnp.concatenate(
-        [
-            pick(core, first, second),
-            pick(core, second, first),
-            jnp.zeros((grad_step.shape[0], EXTRA - HEADS), bf16),
-        ],
-        axis=1,
-    )
-    use_own = jnp.concatenate([grad_conv[:, :HALF], pick(core, shared, step)], axis=1)
-    use_other = jnp.concatenate([grad_conv[:, HALF:GROUP], pick(core, step, shared)], axis=1)
-    parts = {}
-    for k in (2, 1, 3, 0):
-        parts[k] = (
-            dot_nt(piece_rows(use_own, k), weights["x_own"])
-            + dot_nt(piece_rows(use_other, k), weights["x_other"])
-            + dot_nt(piece_rows(grad_gate, k)[:, :HALF], weights["g_own"])
-            + dot_nt(piece_rows(grad_gate, k)[:, HALF:], weights["g_other"])
-        )
-    grad_normed = scatter_head(parts)
-    grad_x = (dot_tn(normed, use_own), dot_tn(normed, use_other))
-    feed = kept["feed"].astype(f32)
-    s_in = rms_scale(feed)
-    unit = feed * s_in
-    grad_unit = grad_normed * weights["input_gain"]
-    grad_feed = grad_new + s_in * (
-        grad_unit - unit * jnp.mean(unit * grad_unit, axis=-1, keepdims=True)
-    )
-    return grad_feed.astype(bf16), (grad_x, grad_g, grad_out, grad_taps, grad_hp)
+    tail = (tail + from_next).astype(bf16)
+    use_own = lax.dynamic_update_slice_in_dim(use_own, tail[:, :WIDE], last_row, 0)
+    use_other = lax.dynamic_update_slice_in_dim(use_other, tail[:, WIDE:], last_row, 0)
+    sent = project_back(use_own, use_other, own, other)
+    edge = HALF + EXTRA
+    use_own, use_other = tied((use_own, use_other), sent[1])
+    small = small_columns(core, head, grad_taps, grad_hp)
+    small = jnp.pad(small, ((0, 0), (HALF + SMALL_AT, EXTRA - SMALL_AT - SMALL)))
+    grad_x = (
+        (dot_tn(normed, use_own[:, :edge]) + jnp.where(core == 1, small, 0.0)).astype(bf16),
+        (dot_tn(normed, use_other[:, :edge]) + jnp.where(core == 0, small, 0.0)).astype(bf16),
+    )
+    grad_feed, scale_below = receive_back(
+        before_receive(scatter_head(sent), grad_x), kept["feed"], incoming, weights["gain_in"], below["branch"],
+        below["scale"],
+    )
+    return grad_feed, scale_below, grad_x, early
 
 
 def small_columns(core, head, grad_taps, grad_hp):
@@ -811,27 +1023,16 @@
 
 
 def summed(own, other):
-    return own + swap(other.astype(bf16)).astype(f32)
+    return (own.astype(f32) + swap(other).astype(f32)).astype(bf16)
 
 
 def scatter_seq(a):
     return lax.psum_scatter(a, "seq", scatter_dimension=0, tiled=True)
 
 
-def reduce_layer(core, head, layer, grads):
-    grad_x, grad_g, grad_out, grad_taps, grad_hp = grads
-    out = scatter_seq(summed(*grad_out))
-    gate = scatter_seq(summed(*grad_g))
-    small = small_columns(core, head, grad_taps, grad_hp)
-    small = jnp.pad(small, ((0, 0), (HALF + SMALL_AT, EXTRA - SMALL_AT - SMALL)))
-    own = grad_x[0] + jnp.where(core == 1, small, 0.0)
-    other = grad_x[1] + jnp.where(core == 0, small, 0.0)
-    x = scatter_seq(summed(own, other))
-    both = jnp.concatenate([x, gate], axis=1).reshape(4, 24, HALF + EXTRA + HALF)
-    mine = exchange_head(both, head)
-    theirs = lax.ppermute(mine, "section", [(1 - layer, layer)])
-    rows_out = [lax.ppermute(out, EVERY, out_back_pairs(layer, part)) for part in range(2)]
-    return mine, theirs, rows_out
+def scatter_seq_now(a):
+    got = lax.all_to_all(a, "seq", 0, 0, tiled=True).astype(f32)
+    return jnp.sum(got.reshape(16, 96, a.shape[1]), axis=0).astype(bf16)
 
 
 def per_device(
@@ -842,76 +1043,114 @@
     head = lax.axis_index("head")
     tokens = lax.dynamic_index_in_dim(tokens_in, core, 0, False)
     grad_top = lax.dynamic_index_in_dim(cotangent, core, 0, False)
-
+    edge = HALF + EXTRA
+
+    pieces = spread_weights(core, head, gate_inner[0], shared_bc[0], step_proj[0])
+    own0 = gather_seq(pieces[0])
+    out_piece = lax.ppermute(out_proj[0], EVERY, out_pairs())
     small = jnp.concatenate(
-        [conv_weight[0].reshape(208), conv_bias[0], output_gain[0], jnp.zeros((4,), bf16)]
-    ).reshape(24, SMALL)
-    pieces = spread_weights(
-        core, head, gate_inner[0], shared_bc[0], step_proj[0], input_gain[0], small
-    )
-    out_piece = lax.ppermute(out_proj[0], EVERY, out_pairs())
+        [input_gain, conv_weight[0].reshape(1, 208), conv_bias, output_gain], axis=1
+    ).astype(f32)
+    small = gather_small(core, tied(jnp.pad(small, ((0, 0), (0, 52))), pieces[0]))
     per_head = jnp.concatenate([step_bias, decay_log, skip_gain], axis=0)
-    other_head = swap(per_head)
+    other_head = swap(tied(per_head, pieces[0]))
     head_values = [pick(core, per_head, other_head), pick(core, other_head, per_head)]
-
-    feed_all = jnp.concatenate(gather_head(tokens), axis=0)
-    weights = [{}, {}]
-    for layer in range(2):
-        own = gather_seq(pieces[layer][:, : HALF + EXTRA])
-        weights[layer].update(x_own=own, x_other=swap(own))
-        gate = gather_seq(pieces[layer][:, HALF + EXTRA :])
-        weights[layer].update(g_own=gate, g_other=swap(gate))
-        if layer == 0:
-            out = gather_seq(out_piece)
-            out_other = swap(out)
-        weights[layer].update(
-            o_own=out[HALF * layer : HALF * (layer + 1)],
-            o_other=out_other[HALF * layer : HALF * (layer + 1)],
-        )
-        slot = pick(core, weights[layer]["x_other"], own)[:, HALF : HALF + 128]
-        values = head_values[layer]
-        weights[layer].update(
-            layer_params(core, head, slot, values[0:1], values[1:2], values[2:3])
-        )
-        weights[layer]["input_gain"] = slot[:, 18].astype(f32)[None, :]
-
-    def normalised(feed, gain):
-        values = feed.astype(f32)
-        return (values * rms_scale(values) * gain).astype(bf16)
-
-    normed = normalised(feed_all, weights[0]["input_gain"])
-    hidden, kept0 = layer_forward(core, head, tokens, normed, weights[0])
-    normed_own = normalised(hidden, weights[1]["input_gain"])
-    normed = jnp.concatenate(gather_head(normed_own), axis=0)
-    result, kept1 = layer_forward(core, head, hidden, normed, weights[1])
+    weights = [layer_params(core, head, small[l], head_values[l]) for l in range(2)]
+    feed_all = jnp.concatenate(gather_head(tied(tokens, pieces[0])), axis=0)
+    feed_all, weights, own0, out_piece = lax.optimization_barrier(
+        (feed_all, weights, own0, out_piece)
+    )
+    weights[0].update(own=own0, other=swap(own0))
+    out = gather_seq(out_piece)
+    own1 = gather_seq(tied(pieces[1], weights[0]["other"]))
+
+    later = {}
+
+    def out_first(packed, entering):
+        mine = tied(out, packed)
+        later["out"] = (mine, swap(mine))
+        grad_all = jnp.concatenate(gather_head(tied(grad_top, packed)), axis=0)
+        entering, later["grad_all"] = lax.optimization_barrier((entering, grad_all))
+        return [entering] + [a[:HALF] for a in later["out"]]
+
+    def out_second(packed, entering):
+        return [entering] + [a[HALF:] for a in later["out"]]
+
+    hidden, kept0 = layer_forward(core, head, tokens, feed_all, tokens, weights[0], out_first)
+    feed_all = jnp.concatenate(gather_head(hidden), axis=0)
+    own1 = tied(own1, hidden)
+    weights[1].update(own=own1, other=swap(own1))
+    result, kept1 = layer_forward(core, head, hidden, feed_all, grad_top, weights[1], out_second)
+    scale = jnp.concatenate(gather_head(kept1["scale"]), axis=0)
+
+    def after_gate1(values, leaving):
+        later["sum"] = summed(*values)
+        return later["sum"], leaving
+
+    def before_receive1(sent, grad_x):
+        return tied(sent, later["sum"])
+
+    grad_hidden, scale, grad_x1, early1 = layer_backward(
+        core, head, grad_top, later["grad_all"], scale, kept1, kept0, weights[1], after_gate1, before_receive1
+    )
+    chunks = gather_head(jnp.concatenate([grad_hidden, scale], axis=1))
+    early1 = scatter_seq_now(tied(early1, grad_hidden))
+    chunks, grad_x1, early1 = lax.optimization_barrier((chunks, grad_x1, early1))
+    grad_all = jnp.concatenate([a[:, :D] for a in chunks], axis=0)
+    scale = jnp.concatenate([a[:, D:] for a in chunks], axis=0)
+
+    def after_gate0(values, leaving):
+        values = [jnp.concatenate([grad_x1[i], values[i]], axis=1) for i in range(2)]
+        later["sum"] = summed(*values)
+        return scatter_seq(later["sum"]), leaving
+
+    def before_receive0(sent, grad_x):
+        return tied(sent, later["sum"])
+
+    grad_feed, _, grad_x0, early0 = layer_backward(
+        core, head, grad_hidden, grad_all, scale, kept0, kept0, weights[0], after_gate0, before_receive0
+    )
+    x0 = scatter_seq_now(summed(*grad_x0))
     got = swap(pick(core, result, hidden))
     layer_out = jnp.stack([pick(core, hidden, got), pick(core, got, result)])
-
-    grad_all = jnp.concatenate(gather_head(grad_top), axis=0)
-    grad_hidden, grads1 = layer_backward(core, head, grad_top, grad_all, kept1, weights[1])
-    grad_all = jnp.concatenate(gather_head(grad_hidden), axis=0)
-    mine1, theirs1, out1 = reduce_layer(core, head, 1, grads1)
-    grad_feed, grads0 = layer_backward(core, head, grad_hidden, grad_all, kept0, weights[0])
-    mine0, theirs0, out0 = reduce_layer(core, head, 0, grads0)
     got = swap(pick(core, grad_hidden, grad_feed))
     grad_in = jnp.stack([pick(core, grad_feed, got), pick(core, got, grad_hidden)])
 
-    mine = pick(core, mine0, mine1)
-    theirs = theirs0 + theirs1
-    low, high = pick(core, mine, theirs), pick(core, theirs, mine)
+    def out_rows(a):
+        return a.reshape(4, 24, HALF).transpose(1, 0, 2).reshape(24, D)
+
+    out0, out1 = out_rows(early0[:, WIDE:]), out_rows(early1[:, HALF:])
+    even = lax.rem(lax.axis_index("seq"), 2)
+    rows_out = [
+        lax.ppermute(pick(even, out0, out1), EVERY, out_back_pairs(0)),
+        lax.ppermute(pick(even, out1, out0), EVERY, out_back_pairs(1)),
+    ]
+    grad_out = jnp.concatenate(
+        [pick(core, rows_out[0], rows_out[1]), pick(core, rows_out[1], rows_out[0])], axis=0
+    ).astype(f32)
+    both = jnp.concatenate(
+        [x0, early0[:, edge:WIDE], early0[:, :edge], early1[:, :HALF]], axis=1
+    ).reshape(4, 24, 2 * WIDE)
+    both = exchange_head(both, head)
+    first, second = both[:, :, :WIDE], both[:, :, WIDE:]
+    mine = pick(core, first, second)
+    theirs = swap(pick(core, second, first))
+    low, high = pick(core, mine, theirs).astype(f32), pick(core, theirs, mine).astype(f32)
     columns = []
-    for start in (HALF + EXTRA, 0):
+    for start in (edge, 0):
         for g in range(4):
             for half in (low, high):
                 columns.append(half[g, :, start : start + HALF])
     grad_gate_inner = jnp.concatenate(columns, axis=1)
-    grad_shared = jnp.sum(low[:, :, HALF : HALF + EXTRA], axis=0)
-    slot = high[:, :, HALF : HALF + 128]
-    grad_step = jnp.concatenate([slot[g, :, :HEADS] for g in range(4)], axis=1)
+    grad_shared = jnp.sum(low[:, :, HALF:edge], axis=0)
+    slot, turned_slot = high[:, :, HALF : HALF + 128], high[:, :, HALF + 128 : edge]
+    steps = slot[:, :, :HEADS] + jnp.concatenate(
+        [turned_slot[:, :, 6:HEADS], turned_slot[:, :, :6]], axis=2
+    )
+    grad_step = jnp.concatenate([steps[g] for g in range(4)], axis=1)
     small = slot[:, :, SMALL_AT : SMALL_AT + SMALL].reshape(4, 24 * SMALL)
     taps = jnp.sum(small[:, :260], axis=0)
     sums = small[:, 260:296].reshape(4, 3, HEADS).transpose(1, 0, 2).reshape(3, 48)
-    grad_out = jnp.concatenate([out0[0] + out1[0], out0[1] + out1[1]], axis=0)
     grad_output_gain = jnp.sum(grad_out * out_proj[0].astype(f32), axis=1) / output_gain[0].astype(
         f32
     )

time: 1060 us -> 638 us (0.60)
  waiting for transfers between devices: 595 us -> 231 us
  matrix products: 123 us -> 10.1 us
  Pallas kernels: 49.2 us -> 86.9 us
  local copies, waits for them, and re-layouts: 67.2 us -> 102 us
  starting transfers between devices: 156 us -> 138 us
    reduce_scatter x4 -> x1, waiting for transfers between devices: 260 us -> 0.01 us  [scatter_seq(): return lax.psum_scatter(a, 'seq', scatter_dimension=0, tiled=True)]
    all_gather x5 -> x3, waiting for transfers between devices: 138 us -> 12.8 us  [gather_seq(): return lax.all_gather(a, 'seq', axis=0, tiled=True)]
    dot_general x60 -> x0, matrix products: 86.8 us -> none  [the longest x36 48.5 us: dot_nt(): lax.dot_general(a.astype(bf16), b.astype(bf16), (((1,), (1,)), ((), ())),...]
    unnamed x412 -> x384, local copies, waits for them, and re-layouts: 24.4 us -> 67.3 us
    pallas_call x2 -> x12, Pallas kernels: 5.73 us -> 39.5 us  [the longest x2 9.86 us: project_back(): pl.pallas_call(parts_kernel, grid=(D // width,), in_specs=[whole((tokens,...]
    all_to_all x0 -> x3, waiting for transfers between devices: none -> 33.6 us  [the longest x2 23.5 us: scatter_seq_now(): got = lax.all_to_all(a, 'seq', 0, 0, tiled=True).astype(f32)]
    all_to_all x0 -> x3, starting transfers between devices: none -> 30 us  [the longest x2 20.9 us: scatter_seq_now(): got = lax.all_to_all(a, 'seq', 0, 0, tiled=True).astype(f32)]
    dot_general x12 -> x4, matrix products: 36.3 us -> 10.1 us  [dot_tn(): lax.dot_general(a.astype(bf16), b.astype(bf16), (((0,), (0,)), ((), ())),...]
  transfers between devices with their start and end apart: 109 -> 86, of which waited for: 65 -> 51; matrix products, arithmetic and copies ran while one was open for 17% -> 10% of each run, Pallas kernels for 4% -> 9%
where the time goes in v2:
time: 638 us; the launch traced here: 627 us
  waiting for transfers between devices  231 us (36%)
  starting transfers between devices  138 us (22%)
  local copies, waits for them, and re-layouts  102 us (16%)
  Pallas kernels  86.9 us (14%)
  other arithmetic  42.1 us (7%)
  between operations  17.1 us (3%)
  matrix products  10.1 us (2%)
    ppermute x36, waiting for transfers between devices, from_head(): return lax.ppermute(a, 'head', [(i, (i - k) % 4) for i in range(4)])  102 us
    unnamed x384, local copies, waits for them, and re-layouts  67.3 us
    ppermute x24, waiting for transfers between devices, from_seq(): return lax.ppermute(a, 'seq', pairs)  57.6 us
    ppermute x36, starting transfers between devices, from_head(): return lax.ppermute(a, 'head', [(i, (i - k) % 4) for i in range(4)])  42.7 us
    ppermute x24, starting transfers between devices, from_seq(): return lax.ppermute(a, 'seq', pairs)  31.3 us
    pallas_call x2, Pallas kernels, scan_back(): pl.pallas_call(scan_back_kernel, grid_spec=pltpu.PrefetchScalarGridSpec(n...  27.7 us
    all_to_all x2, waiting for transfers between devices, scatter_seq_now(): got = lax.all_to_all(a, 'seq', 0, 0, tiled=True).astype(f32)  23.5 us
    all_to_all x2, starting transfers between devices, scatter_seq_now(): got = lax.all_to_all(a, 'seq', 0, 0, tiled=True).astype(f32)  20.9 us
  transfers between devices with their start and end apart: 86, of which 51 were waited for; matrix products, arithmetic and copies ran while one was open for 10% of the time, Pallas kernels for 9%

profile of v2, /device:TPU:103, one launch (start us, length us, event | category | flops | bytes accessed | tf_op | source)
XLA Modules:
  0.0 627.1 jit_solution(8780330034222934552)
XLA Ops:
  20.0 5.9 collective-permute-start.9
  27.7 2.5 collective-permute-start.6
  32.8 9.1 %all-to-all-start = ((f32[64,8,128]{2,1,0:T(8,128)}), f32[64,8,128]{2,1,0:T(8,128)S(1)}, u32[]{:S(2)}, u32[]{:S(2)}) async-start(f32[64,8,128]{2,1,0:T(8,128)} %broadcast_in_dim.168), calls=%async_computation | async-start | bytes 524288 | tf_op jit(solution)/shard_map/all_to_all | solution.py:913
  42.9 10.1 %all-to-all-done = f32[64,8,128]{2,1,0:T(8,128)S(1)} async-done(((f32[64,8,128]{2,1,0:T(8,128)}), f32[64,8,128]{2,1,0:T(8,128)S(1)}, u32[]{:S(2)}, u32[]{:S(2)}) %all-to-all-start) | async-done | bytes 262176 | tf_op jit(solution)/shard_map/all_to_all | solution.py:913
  57.4 12.7 %all-gather.4.cloned.1.call-done.own = bf16[1536,1024]{1,0:T(8,128)(2,1)} async-done(((bf16[96,1024]{1,0:T(8,128)(2,1)}), bf16[1536,1024]{1,0:T(8,128)(2,1)}) %all-gather.4.cloned.1.call-update) | async-done | bytes 3145744 | tf_op jit(solution)/shard_map/all_gather | solution.py:904
  86.6 4.1 project.2
  93.0 2.3 collective-permute-start.11
  95.4 4.3 collective-permute-done.11.rim
  99.7 6.4 %scan_local.2 = (f32[512,1024]{1,0:T(8,128)S(1)}, f32[512,768]{1,0:T(8,128)S(1)}, bf16[512,128]{1,0:T(8,128)(2,1)S(1)}, f32[512,128]{1,0:T(8,128)S(1)}, f32[4,12...) custom-call(s32[2]{0:T(128)S(1)} %pad_add_fusion.place, ...), custom_call_target="tpu_custom_call" | custom-call | flops 1000000000 | bytes 8000000 | tf_op jit(solution)/shard_map/scan_local/pallas_call | solution.py:237
  112.3 2.9 collective-permute-start.19
  115.2 4.9 collective-permute-done.12
  120.9 5.1 collective-permute-done.14
  133.4 5.1 collective-permute-done.17
  139.1 5.2 collective-permute-done.15
  147.3 3.4 gate_out.2
  154.5 7.2 %collective-permute-done.22.one = bf16[128,1664]{1,0:T(8,128)(2,1)S(1)} collective-permute-done((bf16[128,1664]{1,0:T(8,128)(2,1)S(1)}, bf16[128,1664]{1,0:T(8,128)(2,1)S(1)}, u32[]{:S(2)}, u32[]{:S(2)}) %collective-permute-start.22) | collective-permute-done | bytes 426016 | tf_op jit(solution)/shard_map/ppermute | solution.py:29
  161.7 2.5 collective-permute-done.23.two
  164.2 11.4 %collective-permute-done.24.three = bf16[128,1664]{1,0:T(8,128)(2,1)S(1)} collective-permute-done((bf16[128,1664]{1,0:T(8,128)(2,1)S(1)}, bf16[128,1664]{1,0:T(8,128)(2,1)S(1)}, u32[]{:S(2)}, u32[]{:S(2)}) %collective-permute-start.24) | collective-permute-done | bytes 426016 | tf_op jit(solution)/shard_map/ppermute | solution.py:29
  182.2 17.1 %collective-permute-done.25 = bf16[128,1536]{1,0:T(8,128)(2,1)S(1)} collective-permute-done((bf16[128,1536]{1,0:T(8,128)(2,1)}, bf16[128,1536]{1,0:T(8,128)(2,1)S(1)}, u32[]{:S(2)}, u32[]{:S(2)}) %collective-permute-start.25) | collective-permute-done | bytes 393248 | tf_op jit(solution)/shard_map/ppermute | solution.py:29
  202.6 4.0 project.3
  207.8 2.3 collective-permute-start.32
  210.2 5.8 collective-permute-done.32.rim
  216.0 6.4 %scan_local.3 = (f32[512,1024]{1,0:T(8,128)S(1)}, f32[512,768]{1,0:T(8,128)S(1)}, bf16[512,128]{1,0:T(8,128)(2,1)S(1)}, f32[512,128]{1,0:T(8,128)S(1)}, f32[4,12...) custom-call(s32[2]{0:T(128)S(1)} %copy-done.109, ...), custom_call_target="tpu_custom_call" | custom-call | flops 1000000000 | bytes 8000000 | tf_op jit(solution)/shard_map/scan_local/pallas_call | solution.py:237
  225.2 3.3 collective-permute-done.33
  230.2 6.6 %collective-permute-done.35 = bf16[144,768]{1,0:T(8,128)(2,1)S(1)} collective-permute-done((bf16[144,768]{1,0:T(8,128)(2,1)S(1)}, bf16[144,768]{1,0:T(8,128)(2,1)S(1)}, u32[]{:S(2)}, u32[]{:S(2)}) %collective-permute-start.35) | collective-permute-done | bytes 221216 | tf_op jit(solution)/shard_map/ppermute | solution.py:41
  241.8 3.8 collective-permute-done.38
  245.6 7.2 %collective-permute-done.36 = bf16[144,768]{1,0:T(8,128)(2,1)S(1)} collective-permute-done((bf16[144,768]{1,0:T(8,128)(2,1)S(1)}, bf16[144,768]{1,0:T(8,128)(2,1)S(1)}, u32[]{:S(2)}, u32[]{:S(2)}) %collective-permute-start.36) | collective-permute-done | bytes 221216 | tf_op jit(solution)/shard_map/ppermute | solution.py:41
  253.3 3.4 gate_out.3
  258.0 4.3 collective-permute-start.39
  262.8 8.2 %collective-permute-done.39.one = bf16[128,1664]{1,0:T(8,128)(2,1)S(1)} collective-permute-done((bf16[128,1664]{1,0:T(8,128)(2,1)S(1)}, bf16[128,1664]{1,0:T(8,128)(2,1)S(1)}, u32[]{:S(2)}, u32[]{:S(2)}) %collective-permute-start.39) | collective-permute-done | bytes 426016 | tf_op jit(solution)/shard_map/ppermute | solution.py:29
  271.1 2.5 collective-permute-done.40.two
  273.5 11.0 %collective-permute-done.41.three = bf16[128,1664]{1,0:T(8,128)(2,1)S(1)} collective-permute-done((bf16[128,1664]{1,0:T(8,128)(2,1)S(1)}, bf16[128,1664]{1,0:T(8,128)(2,1)S(1)}, u32[]{:S(2)}, u32[]{:S(2)}) %collective-permute-start.41) | collective-permute-done | bytes 426016 | tf_op jit(solution)/shard_map/ppermute | solution.py:29
  301.7 4.5 gate_back.2
  307.1 2.7 collective-permute-start.48
  309.8 4.8 early_grads.2
  316.1 2.5 collective-permute-start.56
  322.6 3.0 collective-permute-start.50
  342.3 13.9 %scan_back.2 = (bf16[512,1024]{1,0:T(8,128)(2,1)S(1)}, bf16[512,1024]{1,0:T(8,128)(2,1)S(1)}, f32[8,2048]{1,0:T(8,128)S(1)}, f32[8,2048]{1,0:T(8,128)}, f32[8,1024]{1,0:T(8,128)S(1)}, /*index=5*/f32[8,128]{1,0:T(8,128)S(1)}) custom-call(s32[2]{0:T(128)S(1)} %copy-done.110, bf16[512,1024]{1,0:T(8,128)(2,1)S(1)} %copy-done.56, f32[512,1024]{1,0:T(8,128)S(1)} %copy-done.44, ...), custom_call_target="tpu_custom_call" | custom-call | flops 2000000000 | bytes 9000000 | tf_op jit(solution)/shard_map/scan_back/pallas_call | solution.py:660
  357.9 3.4 collective-permute-start.52
  369.9 4.6 project_back.2
  377.3 3.7 add_convert_fusion.1
  381.8 2.9 collective-permute-done.54.two
  384.7 12.1 %collective-permute-done.55.three = bf16[128,1536]{1,0:T(8,128)(2,1)S(1)} collective-permute-done((bf16[128,1536]{1,0:T(8,128)(2,1)S(1)}, bf16[128,1536]{1,0:T(8,128)(2,1)S(1)}, u32[]{:S(2)}, u32[]{:S(2)}) %collective-permute-start.55) | collective-permute-done | bytes 393248 | tf_op jit(solution)/shard_map/ppermute | solution.py:29
  397.6 11.6 %all-to-all-start.1 = ((bf16[16,96,768]{2,1,0:T(8,128)(2,1)}), bf16[16,96,768]{2,1,0:T(8,128)(2,1)}, u32[]{:S(2)}, u32[]{:S(2)}) async-start(bf16[16,96,768]{2,1,0:T(8,128)(2,1)} %bitcast.246), calls=%async_computation.1 | async-start | bytes 4718592 | tf_op jit(solution)/shard_map/all_to_all | solution.py:1034
  417.6 2.4 collective-permute-start.59
  420.0 4.5 fusion.3
  424.6 2.8 fusion.1
  427.3 16.2 %all-to-all-done.1 = bf16[16,96,768]{2,1,0:T(8,128)(2,1)} async-done(((bf16[16,96,768]{2,1,0:T(8,128)(2,1)}), bf16[16,96,768]{2,1,0:T(8,128)(2,1)}, u32[]{:S(2)}, u32[]{:S(2)}) %all-to-all-start.1) | async-done | bytes 2359328 | tf_op jit(solution)/shard_map/all_to_all | solution.py:1034
  443.6 2.7 reduce_sum.80
  453.8 4.6 gate_back.3
  458.4 3.7 early_grads.3
  467.0 10.3 %collective-permute-done.60 = bf16[144,768]{1,0:T(8,128)(2,1)S(1)} collective-permute-done((bf16[144,768]{1,0:T(8,128)(2,1)S(1)}, bf16[144,768]{1,0:T(8,128)(2,1)S(1)}, u32[]{:S(2)}, u32[]{:S(2)}) %collective-permute-start.60) | collective-permute-done | bytes 221216 | tf_op jit(solution)/shard_map/ppermute | solution.py:41
  480.1 4.1 collective-permute-start.63
  484.2 3.4 collective-permute-start.64
  488.3 2.7 add_convert_fusion
  501.3 13.9 %scan_back.3 = (bf16[512,1024]{1,0:T(8,128)(2,1)S(1)}, bf16[512,1024]{1,0:T(8,128)(2,1)S(1)}, f32[8,2048]{1,0:T(8,128)S(1)}, f32[8,2048]{1,0:T(8,128)}, f32[8,1024]{1,0:T(8,128)S(1)}, /*index=5*/f32[8,128]{1,0:T(8,128)S(1)}) custom-call(s32[2]{0:T(128)S(1)} %copy-done.111, bf16[512,1024]{1,0:T(8,128)(2,1)S(1)} %copy-done.54, f32[512,1024]{1,0:T(8,128)S(1)} %copy-done.42, ...), custom_call_target="tpu_custom_call" | custom-call | flops 2000000000 | bytes 9000000 | tf_op jit(solution)/shard_map/scan_back/pallas_call | solution.py:660
  517.8 3.8 collective-permute-start.66
  530.1 5.2 project_back.3
  543.9 9.3 %all-to-all-start.2 = ((bf16[16,96,640]{2,1,0:T(8,128)(2,1)}), bf16[16,96,640]{2,1,0:T(8,128)(2,1)}, u32[]{:S(2)}, u32[]{:S(2)}) async-start(bf16[16,96,640]{2,1,0:T(8,128)(2,1)} %bitcast.247), calls=%async_computation.2 | async-start | bytes 3932160 | tf_op jit(solution)/shard_map/all_to_all | solution.py:1034
  556.4 6.9 %collective-permute-done.67.one = bf16[128,1536]{1,0:T(8,128)(2,1)S(1)} collective-permute-done((bf16[128,1536]{1,0:T(8,128)(2,1)}, bf16[128,1536]{1,0:T(8,128)(2,1)S(1)}, u32[]{:S(2)}, u32[]{:S(2)}) %collective-permute-start.67) | collective-permute-done | bytes 393248 | tf_op jit(solution)/shard_map/ppermute | solution.py:29
  564.9 9.7 %collective-permute-done.69.three = bf16[128,1536]{1,0:T(8,128)(2,1)S(1)} collective-permute-done((bf16[128,1536]{1,0:T(8,128)(2,1)S(1)}, bf16[128,1536]{1,0:T(8,128)(2,1)S(1)}, u32[]{:S(2)}, u32[]{:S(2)}) %collective-permute-start.69) | collective-permute-done | bytes 393248 | tf_op jit(solution)/shard_map/ppermute | solution.py:29
  578.9 7.3 %all-to-all-done.2 = bf16[16,96,640]{2,1,0:T(8,128)(2,1)} async-done(((bf16[16,96,640]{2,1,0:T(8,128)(2,1)}), bf16[16,96,640]{2,1,0:T(8,128)(2,1)}, u32[]{:S(2)}, u32[]{:S(2)}) %all-to-all-start.2) | async-done | bytes 1966112 | tf_op jit(solution)/shard_map/all_to_all | solution.py:1034
  593.2 6.0 collective-permute-start.74
  600.3 9.4 %collective-permute-done.77 = bf16[24,1536]{1,0:T(8,128)(2,1)S(1)} collective-permute-done((bf16[24,1536]{1,0:T(8,128)(2,1)S(1)}, bf16[24,1536]{1,0:T(8,128)(2,1)S(1)}, u32[]{:S(2)}, u32[]{:S(2)}) %collective-permute-start.77) | collective-permute-done | bytes 73760 | tf_op jit(solution)/shard_map/ppermute | solution.py:1125
  (760 shorter events, 220.4 us)
Async XLA Ops:
  7.2 63.0 %all-gather.4.cloned.1.call-start = ((), (), s32[]{:S(2)}) async-start(), calls=%async_computation.4 | async-start | bytes 3342336 | tf_op jit(solution)/shard_map/all_gather | solution.py:904
  20.0 37.4 %collective-permute-start.9 = (bf16[48,1536]{1,0:T(8,128)(2,1)}, bf16[48,1536]{1,0:T(8,128)(2,1)}, u32[]{:S(2)}, u32[]{:S(2)}) collective-permute-start(bf16[48,1536]{1,0:T(8,128)(2,1)} %bitcast.44), channel_id=1, source_target_pairs={{0,0},{1,4},{2,8},{3,12},{4,16},{5,20},{6,24},{7,28},{8,64},{9,68}... | collective-permute-start | bytes 442376 | tf_op jit(solution)/shard_map/ppermute | solution.py:1050
  26.3 29.1 %collective-permute-start.4 = (bf16[128,1536]{1,0:T(8,128)(2,1)S(1)}, bf16[128,1536]{1,0:T(8,128)(2,1)S(1)}, u32[]{:S(2)}, u32[]{:S(2)}) collective-permute-start(bf16[128,1536]{1,0:T(8,128)(2,1)S(1)} %dynamic-slice_bitcast_fusion.1.feed.target), channel_id=1, source_target_pairs={{0,3},{1,0},{2,1},{3,2},{4,7},{5,4},{6,5},{7,6},{8,11},{9,8},{10,9... | collective-permute-start | bytes 1179656 | tf_op jit(solution)/shard_map/ppermute | solution.py:29
  27.7 27.7 %collective-permute-start.5 = (bf16[128,1536]{1,0:T(8,128)(2,1)S(1)}, bf16[128,1536]{1,0:T(8,128)(2,1)S(1)}, u32[]{:S(2)}, u32[]{:S(2)}) collective-permute-start(bf16[128,1536]{1,0:T(8,128)(2,1)S(1)} %dynamic-slice_bitcast_fusion.1.feed.target), channel_id=1, source_target_pairs={{0,2},{1,3},{2,0},{3,1},{4,6},{5,7},{6,4},{7,5},{8,10},{9,11},{10,... | collective-permute-start | bytes 1179656 | tf_op jit(solution)/shard_map/ppermute | solution.py:29
  27.7 28.5 %collective-permute-start.6 = (bf16[128,1536]{1,0:T(8,128)(2,1)S(1)}, bf16[128,1536]{1,0:T(8,128)(2,1)}, u32[]{:S(2)}, u32[]{:S(2)}) collective-permute-start(bf16[128,1536]{1,0:T(8,128)(2,1)S(1)} %dynamic-slice_bitcast_fusion.1.feed.target), channel_id=1, source_target_pairs={{0,1},{1,2},{2,3},{3,0},{4,5},{5,6},{6,7},{7,4},{8,9},{9,10},{10,1... | collective-permute-start | bytes 1179656 | tf_op jit(solution)/shard_map/ppermute | solution.py:29
  32.8 20.2 %all-to-all-start = ((f32[64,8,128]{2,1,0:T(8,128)}), f32[64,8,128]{2,1,0:T(8,128)S(1)}, u32[]{:S(2)}, u32[]{:S(2)}) async-start(f32[64,8,128]{2,1,0:T(8,128)} %broadcast_in_dim.168), calls=%async_computation | async-start | bytes 524288 | tf_op jit(solution)/shard_map/all_to_all | solution.py:913
  41.9 84.1 %all-gather.6.cloned.1.call-start = ((), (), s32[]{:S(2)}) async-start(), calls=%async_computation.5 | async-start | bytes 2506752 | tf_op jit(solution)/shard_map/all_gather | solution.py:904
  72.6 105.8 %all-gather.8.cloned.1.call-start = ((), (), s32[]{:S(2)}) async-start(), calls=%async_computation.6 | async-start | bytes 3342336 | tf_op jit(solution)/shard_map/all_gather | solution.py:904
  72.7 8.3 %collective-permute-start.10 = (bf16[1536,1024]{1,0:T(8,128)(2,1)}, bf16[1536,1024]{1,0:T(8,128)(2,1)S(1)}, u32[]{:S(2)}, u32[]{:S(2)}) collective-permute-start(bf16[1536,1024]{1,0:T(8,128)(2,1)} %all-gather.4.cloned.1.call-done.own), channel_id=1, source_target_pairs={{0,64},{64,0},{1,65},{65,1},{2,66},{66,2},{3,67},{67,3},{4,68},{68... | collective-permute-start | bytes 9437192 | tf_op jit(solution)/shard_map/ppermute | solution.py:45
  109.9 10.2 %collective-permute-start.12 = (bf16[144,768]{1,0:T(8,128)(2,1)S(1)}, bf16[144,768]{1,0:T(8,128)(2,1)S(1)}, u32[]{:S(2)}, u32[]{:S(2)}) collective-permute-start(bf16[144,768]{1,0:T(8,128)(2,1)S(1)} %get-tuple-element.141), channel_id=1, source_target_pairs={{4,0},{8,4},{12,8},{0,12},{20,16},{24,20},{28,24},{16,28},{36,32},... | collective-permute-start | bytes 663560 | tf_op jit(solution)/shard_map/ppermute | solution.py:41
  109.9 11.0 %collective-permute-start.13 = (bf16[144,768]{1,0:T(8,128)(2,1)S(1)}, bf16[144,768]{1,0:T(8,128)(2,1)S(1)}, u32[]{:S(2)}, u32[]{:S(2)}) collective-permute-start(bf16[144,768]{1,0:T(8,128)(2,1)S(1)} %get-tuple-element.141), channel_id=1, source_target_pairs={{8,0},{12,4},{0,8},{4,12},{24,16},{28,20},{16,24},{20,28},{40,32},... | collective-permute-start | bytes 663560 | tf_op jit(solution)/shard_map/ppermute | solution.py:41
  110.0 16.0 %collective-permute-start.14 = (bf16[144,768]{1,0:T(8,128)(2,1)S(1)}, bf16[144,768]{1,0:T(8,128)(2,1)S(1)}, u32[]{:S(2)}, u32[]{:S(2)}) collective-permute-start(bf16[144,768]{1,0:T(8,128)(2,1)S(1)} %get-tuple-element.141), channel_id=1, source_target_pairs={{12,0},{0,4},{4,8},{8,12},{28,16},{16,20},{20,24},{24,28},{44,32},... | collective-permute-start | bytes 663560 | tf_op jit(solution)/shard_map/ppermute | solution.py:41
  111.4 18.1 %collective-permute-start.18 = (bf16[128,1536]{1,0:T(8,128)(2,1)S(1)}, bf16[128,1536]{1,0:T(8,128)(2,1)S(1)}, u32[]{:S(2)}, u32[]{:S(2)}) collective-permute-start(bf16[128,1536]{1,0:T(8,128)(2,1)S(1)} %dynamic-slice_bitcast_fusion.target.grad_new), channel_id=1, source_target_pairs={{0,3},{1,0},{2,1},{3,2},{4,7},{5,4},{6,5},{7,6},{8,11},{9,8},{10,9... | collective-permute-start | bytes 1179656 | tf_op jit(solution)/shard_map/ppermute | solution.py:29
  112.3 18.5 %collective-permute-start.19 = (bf16[128,1536]{1,0:T(8,128)(2,1)S(1)}, bf16[128,1536]{1,0:T(8,128)(2,1)S(1)}, u32[]{:S(2)}, u32[]{:S(2)}) collective-permute-start(bf16[128,1536]{1,0:T(8,128)(2,1)S(1)} %dynamic-slice_bitcast_fusion.target.grad_new), channel_id=1, source_target_pairs={{0,2},{1,3},{2,0},{3,1},{4,6},{5,7},{6,4},{7,5},{8,10},{9,11},{10,... | collective-permute-start | bytes 1179656 | tf_op jit(solution)/shard_map/ppermute | solution.py:29
  120.1 12.1 %collective-permute-start.20 = (bf16[128,1536]{1,0:T(8,128)(2,1)S(1)}, bf16[128,1536]{1,0:T(8,128)(2,1)S(1)}, u32[]{:S(2)}, u32[]{:S(2)}) collective-permute-start(bf16[128,1536]{1,0:T(8,128)(2,1)S(1)} %dynamic-slice_bitcast_fusion.target.grad_new), channel_id=1, source_target_pairs={{0,1},{1,2},{2,3},{3,0},{4,5},{5,6},{6,7},{7,4},{8,9},{9,10},{10,1... | collective-permute-start | bytes 1179656 | tf_op jit(solution)/shard_map/ppermute | solution.py:29
  126.0 18.9 %collective-permute-start.21 = (bf16[768,1536]{1,0:T(8,128)(2,1)}, bf16[768,1536]{1,0:T(8,128)(2,1)S(1)}, u32[]{:S(2)}, u32[]{:S(2)}) collective-permute-start(bf16[768,1536]{1,0:T(8,128)(2,1)} %all-gather.6.cloned.1.call-done), channel_id=1, source_target_pairs={{0,64},{64,0},{1,65},{65,1},{2,66},{66,2},{3,67},{67,3},{4,68},{68... | collective-permute-start | bytes 7077896 | tf_op jit(solution)/shard_map/ppermute | solution.py:45
  128.1 16.3 %collective-permute-start.15 = (bf16[144,768]{1,0:T(8,128)(2,1)S(1)}, bf16[144,768]{1,0:T(8,128)(2,1)S(1)}, u32[]{:S(2)}, u32[]{:S(2)}) collective-permute-start(bf16[144,768]{1,0:T(8,128)(2,1)S(1)} %maximum_maximum_fusion), channel_id=1, source_target_pairs={{0,48},{4,52},{8,56},{12,60},{1,49},{5,53},{9,57},{13,61},{2,50},{... | collective-permute-start | bytes 663560 | tf_op jit(solution)/shard_map/ppermute | solution.py:41
  129.5 8.9 %collective-permute-start.17 = (bf16[144,768]{1,0:T(8,128)(2,1)S(1)}, bf16[144,768]{1,0:T(8,128)(2,1)S(1)}, u32[]{:S(2)}, u32[]{:S(2)}) collective-permute-start(bf16[144,768]{1,0:T(8,128)(2,1)S(1)} %maximum_maximum_fusion), channel_id=1, source_target_pairs={{0,16},{4,20},{8,24},{12,28},{16,32},{20,36},{24,40},{28,44},{32,4... | collective-permute-start | bytes 663560 | tf_op jit(solution)/shard_map/ppermute | solution.py:41
  130.8 8.3 %collective-permute-start.16 = (bf16[144,768]{1,0:T(8,128)(2,1)S(1)}, bf16[144,768]{1,0:T(8,128)(2,1)S(1)}, u32[]{:S(2)}, u32[]{:S(2)}) collective-permute-start(bf16[144,768]{1,0:T(8,128)(2,1)S(1)} %maximum_maximum_fusion), channel_id=1, source_target_pairs={{0,32},{4,36},{8,40},{12,44},{16,48},{20,52},{24,56},{28,60},{1,33... | collective-permute-start | bytes 663560 | tf_op jit(solution)/shard_map/ppermute | solution.py:41
  151.9 9.8 %collective-permute-start.22 = (bf16[128,1664]{1,0:T(8,128)(2,1)S(1)}, bf16[128,1664]{1,0:T(8,128)(2,1)S(1)}, u32[]{:S(2)}, u32[]{:S(2)}) collective-permute-start(bf16[128,1664]{1,0:T(8,128)(2,1)S(1)} %get-tuple-element.149), channel_id=1, source_target_pairs={{0,1},{1,2},{2,3},{3,0},{4,5},{5,6},{6,7},{7,4},{8,9},{9,10},{10,1... | collective-permute-start | bytes 1277960 | tf_op jit(solution)/shard_map/ppermute | solution.py:29
  153.2 11.1 %collective-permute-start.23 = (bf16[128,1664]{1,0:T(8,128)(2,1)S(1)}, bf16[128,1664]{1,0:T(8,128)(2,1)S(1)}, u32[]{:S(2)}, u32[]{:S(2)}) collective-permute-start(bf16[128,1664]{1,0:T(8,128)(2,1)S(1)} %get-tuple-element.150), channel_id=1, source_target_pairs={{0,2},{1,3},{2,0},{3,1},{4,6},{5,7},{6,4},{7,5},{8,10},{9,11},{10,... | collective-permute-start | bytes 1277960 | tf_op jit(solution)/shard_map/ppermute | solution.py:29
  154.5 21.2 %collective-permute-start.24 = (bf16[128,1664]{1,0:T(8,128)(2,1)S(1)}, bf16[128,1664]{1,0:T(8,128)(2,1)S(1)}, u32[]{:S(2)}, u32[]{:S(2)}) collective-permute-start(bf16[128,1664]{1,0:T(8,128)(2,1)S(1)} %get-tuple-element.151), channel_id=1, source_target_pairs={{0,3},{1,0},{2,1},{3,2},{4,7},{5,4},{6,5},{7,6},{8,11},{9,8},{10,9... | collective-permute-start | bytes 1277960 | tf_op jit(solution)/shard_map/ppermute | solution.py:29
  178.4 22.3 %collective-permute-start.31 = (bf16[1536,1024]{1,0:T(8,128)(2,1)}, bf16[1536,1024]{1,0:T(8,128)(2,1)S(1)}, u32[]{:S(2)}, u32[]{:S(2)}) collective-permute-start(bf16[1536,1024]{1,0:T(8,128)(2,1)} %all-gather.8.cloned.1.call-done.own), channel_id=1, source_target_pairs={{0,64},{64,0},{1,65},{65,1},{2,66},{66,2},{3,67},{67,3},{4,68},{68... | collective-permute-start | bytes 9437192 | tf_op jit(solution)/shard_map/ppermute | solution.py:45
  178.8 20.4 %collective-permute-start.25 = (bf16[128,1536]{1,0:T(8,128)(2,1)}, bf16[128,1536]{1,0:T(8,128)(2,1)S(1)}, u32[]{:S(2)}, u32[]{:S(2)}) collective-permute-start(bf16[128,1536]{1,0:T(8,128)(2,1)} %copy-done.4), channel_id=1, source_target_pairs={{0,3},{1,0},{2,1},{3,2},{4,7},{5,4},{6,5},{7,6},{8,11},{9,8},{10,9... | collective-permute-start | bytes 1179656 | tf_op jit(solution)/shard_map/ppermute | solution.py:29
  178.8 20.4 %collective-permute-start.26 = (bf16[128,1536]{1,0:T(8,128)(2,1)}, bf16[128,1536]{1,0:T(8,128)(2,1)S(1)}, u32[]{:S(2)}, u32[]{:S(2)}) collective-permute-start(bf16[128,1536]{1,0:T(8,128)(2,1)} %copy-done.4), channel_id=1, source_target_pairs={{0,2},{1,3},{2,0},{3,1},{4,6},{5,7},{6,4},{7,5},{8,10},{9,11},{10,... | collective-permute-start | bytes 1179656 | tf_op jit(solution)/shard_map/ppermute | solution.py:29
  180.3 19.2 %collective-permute-start.27 = (bf16[128,1536]{1,0:T(8,128)(2,1)}, bf16[128,1536]{1,0:T(8,128)(2,1)S(1)}, u32[]{:S(2)}, u32[]{:S(2)}) collective-permute-start(bf16[128,1536]{1,0:T(8,128)(2,1)} %copy-done.4), channel_id=1, source_target_pairs={{0,1},{1,2},{2,3},{3,0},{4,5},{5,6},{6,7},{7,4},{8,9},{9,10},{10,1... | collective-permute-start | bytes 1179656 | tf_op jit(solution)/shard_map/ppermute | solution.py:29
  207.8 8.1 %collective-permute-start.32 = (bf16[8,1024]{1,0:T(8,128)(2,1)S(1)}, bf16[8,1024]{1,0:T(8,128)(2,1)S(1)}, u32[]{:S(2)}, u32[]{:S(2)}) collective-permute-start(bf16[8,1024]{1,0:T(8,128)(2,1)S(1)} %constant_dynamic-slice_fusion), channel_id=1, source_target_pairs={{0,4},{4,8},{8,12},{12,16},{16,20},{20,24},{24,28},{28,32},{32,36}... | collective-permute-start | bytes 49160 | tf_op jit(solution)/shard_map/ppermute | solution.py:948
  223.8 13.0 %collective-permute-start.35 = (bf16[144,768]{1,0:T(8,128)(2,1)S(1)}, bf16[144,768]{1,0:T(8,128)(2,1)S(1)}, u32[]{:S(2)}, u32[]{:S(2)}) collective-permute-start(bf16[144,768]{1,0:T(8,128)(2,1)S(1)} %get-tuple-element.164), channel_id=1, source_target_pairs={{12,0},{0,4},{4,8},{8,12},{28,16},{16,20},{20,24},{24,28},{44,32},... | collective-permute-start | bytes 663560 | tf_op jit(solution)/shard_map/ppermute | solution.py:41
  237.9 7.7 %collective-permute-start.38 = (bf16[144,768]{1,0:T(8,128)(2,1)S(1)}, bf16[144,768]{1,0:T(8,128)(2,1)S(1)}, u32[]{:S(2)}, u32[]{:S(2)}) collective-permute-start(bf16[144,768]{1,0:T(8,128)(2,1)S(1)} %maximum_maximum_fusion.1), channel_id=1, source_target_pairs={{0,16},{4,20},{8,24},{12,28},{16,32},{20,36},{24,40},{28,44},{32,4... | collective-permute-start | bytes 663560 | tf_op jit(solution)/shard_map/ppermute | solution.py:41
  239.2 13.7 %collective-permute-start.36 = (bf16[144,768]{1,0:T(8,128)(2,1)S(1)}, bf16[144,768]{1,0:T(8,128)(2,1)S(1)}, u32[]{:S(2)}, u32[]{:S(2)}) collective-permute-start(bf16[144,768]{1,0:T(8,128)(2,1)S(1)} %maximum_maximum_fusion.1), channel_id=1, source_target_pairs={{0,48},{4,52},{8,56},{12,60},{1,49},{5,53},{9,57},{13,61},{2,50},{... | collective-permute-start | bytes 663560 | tf_op jit(solution)/shard_map/ppermute | solution.py:41
  240.5 12.4 %collective-permute-start.37 = (bf16[144,768]{1,0:T(8,128)(2,1)S(1)}, bf16[144,768]{1,0:T(8,128)(2,1)S(1)}, u32[]{:S(2)}, u32[]{:S(2)}) collective-permute-start(bf16[144,768]{1,0:T(8,128)(2,1)S(1)} %maximum_maximum_fusion.1), channel_id=1, source_target_pairs={{0,32},{4,36},{8,40},{12,44},{16,48},{20,52},{24,56},{28,60},{1,33... | collective-permute-start | bytes 663560 | tf_op jit(solution)/shard_map/ppermute | solution.py:41
  258.0 13.1 %collective-permute-start.39 = (bf16[128,1664]{1,0:T(8,128)(2,1)S(1)}, bf16[128,1664]{1,0:T(8,128)(2,1)S(1)}, u32[]{:S(2)}, u32[]{:S(2)}) collective-permute-start(bf16[128,1664]{1,0:T(8,128)(2,1)S(1)} %get-tuple-element.168), channel_id=1, source_target_pairs={{0,1},{1,2},{2,3},{3,0},{4,5},{5,6},{6,7},{7,4},{8,9},{9,10},{10,1... | collective-permute-start | bytes 1277960 | tf_op jit(solution)/shard_map/ppermute | solution.py:29
  262.2 11.3 %collective-permute-start.40 = (bf16[128,1664]{1,0:T(8,128)(2,1)S(1)}, bf16[128,1664]{1,0:T(8,128)(2,1)S(1)}, u32[]{:S(2)}, u32[]{:S(2)}) collective-permute-start(bf16[128,1664]{1,0:T(8,128)(2,1)S(1)} %get-tuple-element.169), channel_id=1, source_target_pairs={{0,2},{1,3},{2,0},{3,1},{4,6},{5,7},{6,4},{7,5},{8,10},{9,11},{10,... | collective-permute-start | bytes 1277960 | tf_op jit(solution)/shard_map/ppermute | solution.py:29
  262.5 22.0 %collective-permute-start.41 = (bf16[128,1664]{1,0:T(8,128)(2,1)S(1)}, bf16[128,1664]{1,0:T(8,128)(2,1)S(1)}, u32[]{:S(2)}, u32[]{:S(2)}) collective-permute-start(bf16[128,1664]{1,0:T(8,128)(2,1)S(1)} %get-tuple-element.170), channel_id=1, source_target_pairs={{0,3},{1,0},{2,1},{3,2},{4,7},{5,4},{6,5},{7,6},{8,11},{9,8},{10,9... | collective-permute-start | bytes 1277960 | tf_op jit(solution)/shard_map/ppermute | solution.py:29
  307.1 12.1 %collective-permute-start.46 = (bf16[144,768]{1,0:T(8,128)(2,1)S(1)}, bf16[144,768]{1,0:T(8,128)(2,1)S(1)}, u32[]{:S(2)}, u32[]{:S(2)}) collective-permute-start(bf16[144,768]{1,0:T(8,128)(2,1)S(1)} %get-tuple-element.181), channel_id=1, source_target_pairs={{12,0},{0,4},{4,8},{8,12},{28,16},{16,20},{20,24},{24,28},{44,32},... | collective-permute-start | bytes 663560 | tf_op jit(solution)/shard_map/ppermute | solution.py:41
  307.1 12.1 %collective-permute-start.47 = (bf16[144,768]{1,0:T(8,128)(2,1)S(1)}, bf16[144,768]{1,0:T(8,128)(2,1)S(1)}, u32[]{:S(2)}, u32[]{:S(2)}) collective-permute-start(bf16[144,768]{1,0:T(8,128)(2,1)S(1)} %get-tuple-element.181), channel_id=1, source_target_pairs={{8,0},{12,4},{0,8},{4,12},{24,16},{28,20},{16,24},{20,28},{40,32},... | collective-permute-start | bytes 663560 | tf_op jit(solution)/shard_map/ppermute | solution.py:41
  307.1 12.2 %collective-permute-start.48 = (bf16[144,768]{1,0:T(8,128)(2,1)S(1)}, bf16[144,768]{1,0:T(8,128)(2,1)S(1)}, u32[]{:S(2)}, u32[]{:S(2)}) collective-permute-start(bf16[144,768]{1,0:T(8,128)(2,1)S(1)} %get-tuple-element.181), channel_id=1, source_target_pairs={{4,0},{8,4},{12,8},{0,12},{20,16},{24,20},{28,24},{16,28},{36,32},... | collective-permute-start | bytes 663560 | tf_op jit(solution)/shard_map/ppermute | solution.py:41
  316.1 61.2 %collective-permute-start.56 = (bf16[1536,768]{1,0:T(8,128)(2,1)}, bf16[1536,768]{1,0:T(8,128)(2,1)}, u32[]{:S(2)}, u32[]{:S(2)}) collective-permute-start(bf16[1536,768]{1,0:T(8,128)(2,1)} %get-tuple-element.193), channel_id=1, source_target_pairs={{0,64},{64,0},{1,65},{65,1},{2,66},{66,2},{3,67},{67,3},{4,68},{68... | collective-permute-start | bytes 7077896 | tf_op jit(solution)/shard_map/ppermute | solution.py:45
  322.6 7.8 %collective-permute-start.50 = (bf16[144,768]{1,0:T(8,128)(2,1)}, bf16[144,768]{1,0:T(8,128)(2,1)}, u32[]{:S(2)}, u32[]{:S(2)}) collective-permute-start(bf16[144,768]{1,0:T(8,128)(2,1)} %maximum_maximum_fusion.2), channel_id=1, source_target_pairs={{32,0},{36,4},{40,8},{44,12},{48,16},{52,20},{56,24},{60,28},{33,1... | collective-permute-start | bytes 663560 | tf_op jit(solution)/shard_map/ppermute | solution.py:41
  376.4 8.2 %collective-permute-start.54 = (bf16[128,1536]{1,0:T(8,128)(2,1)S(1)}, bf16[128,1536]{1,0:T(8,128)(2,1)S(1)}, u32[]{:S(2)}, u32[]{:S(2)}) collective-permute-start(bf16[128,1536]{1,0:T(8,128)(2,1)S(1)} %get-tuple-element.188), channel_id=1, source_target_pairs={{0,2},{1,3},{2,0},{3,1},{4,6},{5,7},{6,4},{7,5},{8,10},{9,11},{10,... | collective-permute-start | bytes 1179656 | tf_op jit(solution)/shard_map/ppermute | solution.py:29
  377.3 19.6 %collective-permute-start.55 = (bf16[128,1536]{1,0:T(8,128)(2,1)S(1)}, bf16[128,1536]{1,0:T(8,128)(2,1)S(1)}, u32[]{:S(2)}, u32[]{:S(2)}) collective-permute-start(bf16[128,1536]{1,0:T(8,128)(2,1)S(1)} %get-tuple-element.189), channel_id=1, source_target_pairs={{0,3},{1,0},{2,1},{3,2},{4,7},{5,4},{6,5},{7,6},{8,11},{9,8},{10,9... | collective-permute-start | bytes 1179656 | tf_op jit(solution)/shard_map/ppermute | solution.py:29
  397.6 46.0 %all-to-all-start.1 = ((bf16[16,96,768]{2,1,0:T(8,128)(2,1)}), bf16[16,96,768]{2,1,0:T(8,128)(2,1)}, u32[]{:S(2)}, u32[]{:S(2)}) async-start(bf16[16,96,768]{2,1,0:T(8,128)(2,1)} %bitcast.246), calls=%async_computation.1 | async-start | bytes 4718592 | tf_op jit(solution)/shard_map/all_to_all | solution.py:1034
  409.2 179.9 %reduce-scatter.2.cloned.1.call-start = ((), (), s32[]{:S(2)}) async-start(), calls=%async_computation.7 | async-start | bytes 4595712 | tf_op jit(solution)/shard_map/reduce_scatter | solution.py:1030
  417.2 29.1 %collective-permute-start.57 = (bf16[128,1664]{1,0:T(8,128)(2,1)}, bf16[128,1664]{1,0:T(8,128)(2,1)}, u32[]{:S(2)}, u32[]{:S(2)}) collective-permute-start(bf16[128,1664]{1,0:T(8,128)(2,1)} %constant_dynamic-update-slice_fusion.16), channel_id=1, source_target_pairs={{0,3},{1,0},{2,1},{3,2},{4,7},{5,4},{6,5},{7,6},{8,11},{9,8},{10,9... | collective-permute-start | bytes 1277960 | tf_op jit(solution)/shard_map/ppermute | solution.py:29
  417.2 29.1 %collective-permute-start.58 = (bf16[128,1664]{1,0:T(8,128)(2,1)}, bf16[128,1664]{1,0:T(8,128)(2,1)}, u32[]{:S(2)}, u32[]{:S(2)}) collective-permute-start(bf16[128,1664]{1,0:T(8,128)(2,1)} %constant_dynamic-update-slice_fusion.16), channel_id=1, source_target_pairs={{0,2},{1,3},{2,0},{3,1},{4,6},{5,7},{6,4},{7,5},{8,10},{9,11},{10,... | collective-permute-start | bytes 1277960 | tf_op jit(solution)/shard_map/ppermute | solution.py:29
  417.6 28.6 %collective-permute-start.59 = (bf16[128,1664]{1,0:T(8,128)(2,1)}, bf16[128,1664]{1,0:T(8,128)(2,1)}, u32[]{:S(2)}, u32[]{:S(2)}) collective-permute-start(bf16[128,1664]{1,0:T(8,128)(2,1)} %constant_dynamic-update-slice_fusion.16), channel_id=1, source_target_pairs={{0,1},{1,2},{2,3},{3,0},{4,5},{5,6},{6,7},{7,4},{8,9},{9,10},{10,1... | collective-permute-start | bytes 1277960 | tf_op jit(solution)/shard_map/ppermute | solution.py:29
  462.6 25.1 %collective-permute-start.70 = (bf16[1536,1408]{1,0:T(8,128)(2,1)S(1)}, bf16[1536,1408]{1,0:T(8,128)(2,1)S(1)}, u32[]{:S(2)}, u32[]{:S(2)}) collective-permute-start(bf16[1536,1408]{1,0:T(8,128)(2,1)S(1)} %pad_maximum_fusion), channel_id=1, source_target_pairs={{0,64},{64,0},{1,65},{65,1},{2,66},{66,2},{3,67},{67,3},{4,68},{68... | collective-permute-start | bytes 12976136 | tf_op jit(solution)/shard_map/ppermute | solution.py:45
  464.3 12.9 %collective-permute-start.60 = (bf16[144,768]{1,0:T(8,128)(2,1)S(1)}, bf16[144,768]{1,0:T(8,128)(2,1)S(1)}, u32[]{:S(2)}, u32[]{:S(2)}) collective-permute-start(bf16[144,768]{1,0:T(8,128)(2,1)S(1)} %get-tuple-element.216), channel_id=1, source_target_pairs={{12,0},{0,4},{4,8},{8,12},{28,16},{16,20},{20,24},{24,28},{44,32},... | collective-permute-start | bytes 663560 | tf_op jit(solution)/shard_map/ppermute | solution.py:41
  464.3 12.9 %collective-permute-start.61 = (bf16[144,768]{1,0:T(8,128)(2,1)S(1)}, bf16[144,768]{1,0:T(8,128)(2,1)S(1)}, u32[]{:S(2)}, u32[]{:S(2)}) collective-permute-start(bf16[144,768]{1,0:T(8,128)(2,1)S(1)} %get-tuple-element.216), channel_id=1, source_target_pairs={{8,0},{12,4},{0,8},{4,12},{24,16},{28,20},{16,24},{20,28},{40,32},... | collective-permute-start | bytes 663560 | tf_op jit(solution)/shard_map/ppermute | solution.py:41
  464.8 12.7 %collective-permute-start.62 = (bf16[144,768]{1,0:T(8,128)(2,1)S(1)}, bf16[144,768]{1,0:T(8,128)(2,1)S(1)}, u32[]{:S(2)}, u32[]{:S(2)}) collective-permute-start(bf16[144,768]{1,0:T(8,128)(2,1)S(1)} %get-tuple-element.216), channel_id=1, source_target_pairs={{4,0},{8,4},{12,8},{0,12},{20,16},{24,20},{28,24},{16,28},{36,32},... | collective-permute-start | bytes 663560 | tf_op jit(solution)/shard_map/ppermute | solution.py:41
  478.8 8.8 %collective-permute-start.65 = (bf16[144,768]{1,0:T(8,128)(2,1)}, bf16[144,768]{1,0:T(8,128)(2,1)S(1)}, u32[]{:S(2)}, u32[]{:S(2)}) collective-permute-start(bf16[144,768]{1,0:T(8,128)(2,1)} %maximum_maximum_fusion.3), channel_id=1, source_target_pairs={{16,0},{20,4},{24,8},{28,12},{32,16},{36,20},{40,24},{44,28},{48,3... | collective-permute-start | bytes 663560 | tf_op jit(solution)/shard_map/ppermute | solution.py:41
  480.1 11.9 %collective-permute-start.63 = (bf16[144,768]{1,0:T(8,128)(2,1)}, bf16[144,768]{1,0:T(8,128)(2,1)}, u32[]{:S(2)}, u32[]{:S(2)}) collective-permute-start(bf16[144,768]{1,0:T(8,128)(2,1)} %maximum_maximum_fusion.3), channel_id=1, source_target_pairs={{48,0},{52,4},{56,8},{60,12},{49,1},{53,5},{57,9},{61,13},{50,2},{... | collective-permute-start | bytes 663560 | tf_op jit(solution)/shard_map/ppermute | solution.py:41
  517.8 7.6 %collective-permute-start.66 = (f32[8,2048]{1,0:T(8,128)}, f32[8,2048]{1,0:T(8,128)}, u32[]{:S(2)}, u32[]{:S(2)}) collective-permute-start(f32[8,2048]{1,0:T(8,128)} %get-tuple-element.219), channel_id=1, source_target_pairs={{4,0},{8,4},{12,8},{16,12},{20,16},{24,20},{28,24},{32,28},{36,32}... | collective-permute-start | bytes 196616 | tf_op jit(solution)/shard_map/ppermute | solution.py:989
  543.9 42.3 %all-to-all-start.2 = ((bf16[16,96,640]{2,1,0:T(8,128)(2,1)}), bf16[16,96,640]{2,1,0:T(8,128)(2,1)}, u32[]{:S(2)}, u32[]{:S(2)}) async-start(bf16[16,96,640]{2,1,0:T(8,128)(2,1)} %bitcast.247), calls=%async_computation.2 | async-start | bytes 3932160 | tf_op jit(solution)/shard_map/all_to_all | solution.py:1034
  553.3 10.0 %collective-permute-start.67 = (bf16[128,1536]{1,0:T(8,128)(2,1)}, bf16[128,1536]{1,0:T(8,128)(2,1)S(1)}, u32[]{:S(2)}, u32[]{:S(2)}) collective-permute-start(bf16[128,1536]{1,0:T(8,128)(2,1)} %get-tuple-element.222), channel_id=1, source_target_pairs={{0,1},{1,2},{2,3},{3,0},{4,5},{5,6},{6,7},{7,4},{8,9},{9,10},{10,1... | collective-permute-start | bytes 1179656 | tf_op jit(solution)/shard_map/ppermute | solution.py:29
  553.3 11.6 %collective-permute-start.68 = (bf16[128,1536]{1,0:T(8,128)(2,1)}, bf16[128,1536]{1,0:T(8,128)(2,1)S(1)}, u32[]{:S(2)}, u32[]{:S(2)}) collective-permute-start(bf16[128,1536]{1,0:T(8,128)(2,1)} %get-tuple-element.223), channel_id=1, source_target_pairs={{0,2},{1,3},{2,0},{3,1},{4,6},{5,7},{6,4},{7,5},{8,10},{9,11},{10,... | collective-permute-start | bytes 1179656 | tf_op jit(solution)/shard_map/ppermute | solution.py:29
  553.6 21.0 %collective-permute-start.69 = (bf16[128,1536]{1,0:T(8,128)(2,1)S(1)}, bf16[128,1536]{1,0:T(8,128)(2,1)S(1)}, u32[]{:S(2)}, u32[]{:S(2)}) collective-permute-start(bf16[128,1536]{1,0:T(8,128)(2,1)S(1)} %copy-done.131), channel_id=1, source_target_pairs={{0,3},{1,0},{2,1},{3,2},{4,7},{5,4},{6,5},{7,6},{8,11},{9,8},{10,9... | collective-permute-start | bytes 1179656 | tf_op jit(solution)/shard_map/ppermute | solution.py:29
  554.8 23.1 %collective-permute-start.42 = (bf16[128,1536]{1,0:T(8,128)(2,1)S(1)}, bf16[128,1536]{1,0:T(8,128)(2,1)S(1)}, u32[]{:S(2)}, u32[]{:S(2)}) collective-permute-start(bf16[128,1536]{1,0:T(8,128)(2,1)S(1)} %broadcast_select_fusion.1), channel_id=1, source_target_pairs={{0,64},{64,0},{1,65},{65,1},{2,66},{66,2},{3,67},{67,3},{4,68},{68... | collective-permute-start | bytes 1179656 | tf_op jit(solution)/shard_map/ppermute | solution.py:45
  577.1 10.9 %collective-permute-start.71 = (bf16[128,1536]{1,0:T(8,128)(2,1)S(1)}, bf16[128,1536]{1,0:T(8,128)(2,1)S(1)}, u32[]{:S(2)}, u32[]{:S(2)}) collective-permute-start(bf16[128,1536]{1,0:T(8,128)(2,1)S(1)} %broadcast_select_fusion), channel_id=1, source_target_pairs={{0,64},{64,0},{1,65},{65,1},{2,66},{66,2},{3,67},{67,3},{4,68},{68... | collective-permute-start | bytes 1179656 | tf_op jit(solution)/shard_map/ppermute | solution.py:45
  590.0 19.6 %collective-permute-start.77 = (bf16[24,1536]{1,0:T(8,128)(2,1)S(1)}, bf16[24,1536]{1,0:T(8,128)(2,1)S(1)}, u32[]{:S(2)}, u32[]{:S(2)}) collective-permute-start(bf16[24,1536]{1,0:T(8,128)(2,1)S(1)} %bitcast.276), channel_id=1, source_target_pairs={{0,0},{1,16},{2,32},{3,48},{4,64},{5,80},{6,96},{7,112},{8,1},{9,1... | collective-permute-start | bytes 221192 | tf_op jit(solution)/shard_map/ppermute | solution.py:1125
  592.0 17.7 %collective-permute-start.78 = (bf16[24,1536]{1,0:T(8,128)(2,1)S(1)}, bf16[24,1536]{1,0:T(8,128)(2,1)S(1)}, u32[]{:S(2)}, u32[]{:S(2)}) collective-permute-start(bf16[24,1536]{1,0:T(8,128)(2,1)S(1)} %bitcast.277), channel_id=1, source_target_pairs={{0,64},{1,80},{2,96},{3,112},{4,0},{5,16},{6,32},{7,48},{8,65},{9,... | collective-permute-start | bytes 221192 | tf_op jit(solution)/shard_map/ppermute | solution.py:1126
  593.1 18.4 %collective-permute-start.73 = (bf16[24,2048]{1,0:T(8,128)(2,1)S(1)}, bf16[24,2048]{1,0:T(8,128)(2,1)S(1)}, u32[]{:S(2)}, u32[]{:S(2)}) collective-permute-start(bf16[24,2048]{1,0:T(8,128)(2,1)S(1)} %get-tuple-element.313), channel_id=1, source_target_pairs={{0,3},{1,0},{2,1},{3,2},{4,7},{5,4},{6,5},{7,6},{8,11},{9,8},{10,9... | collective-permute-start | bytes 294920 | tf_op jit(solution)/shard_map/ppermute | solution.py:29
  593.2 18.4 %collective-permute-start.74 = (bf16[24,2048]{1,0:T(8,128)(2,1)S(1)}, bf16[24,2048]{1,0:T(8,128)(2,1)S(1)}, u32[]{:S(2)}, u32[]{:S(2)}) collective-permute-start(bf16[24,2048]{1,0:T(8,128)(2,1)S(1)} %get-tuple-element.312), channel_id=1, source_target_pairs={{0,2},{1,3},{2,0},{3,1},{4,6},{5,7},{6,4},{7,5},{8,10},{9,11},{10,... | collective-permute-start | bytes 294920 | tf_op jit(solution)/shard_map/ppermute | solution.py:29
  599.2 12.4 %collective-permute-start.75 = (bf16[24,2048]{1,0:T(8,128)(2,1)S(1)}, bf16[24,2048]{1,0:T(8,128)(2,1)S(1)}, u32[]{:S(2)}, u32[]{:S(2)}) collective-permute-start(bf16[24,2048]{1,0:T(8,128)(2,1)S(1)} %get-tuple-element.310), channel_id=1, source_target_pairs={{0,1},{1,2},{2,3},{3,0},{4,5},{5,6},{6,7},{7,4},{8,9},{9,10},{10,1... | collective-permute-start | bytes 294920 | tf_op jit(solution)/shard_map/ppermute | solution.py:29
  (196 other events, 1883.0 us)
Sparse Core Ops, SparseCore 0:
  20.1 50.0 all-gather.3
  72.8 50.6 all-gather.5
  126.2 49.8 all-gather.7
  491.2 92.1 reduce-scatter.1

commit v3 on v2

--- a/solution.py
+++ b/solution.py
@@ -19,8 +19,8 @@
 PAIRS = 6
 EXTRA = 256
 ACT = GROUP + 2 * N
-SMALL_AT, SMALL = 19, 13
 WIDE = HALF + EXTRA + HALF
+SMALL_AT = 32
 VMEM = 24 * 1024 * 1024
 epsilon = 1e-05
 
@@ -106,6 +106,16 @@
     return jnp.concatenate([state.astype(bf16), high, low, fill], axis=0)
 
 
+def stored(shape, dtype):
+    return pltpu.HBM(shape, dtype)
+
+
+def far(pinned, *arrays):
+    if not pinned:
+        return list(arrays)
+    return [pltpu.with_memory_space_constraint(a, pltpu.HBM) for a in arrays]
+
+
 def dot(a, b):
     return jnp.dot(a.astype(bf16), b.astype(bf16), preferred_element_type=f32)
 
@@ -138,6 +148,12 @@
 
 def spread(values, j, first):
     return jnp.where(first, values[:, 2 * j : 2 * j + 1], values[:, 2 * j + 1 : 2 * j + 2])
+
+
+def apart(values, first):
+    return jnp.concatenate(
+        [jnp.where(first, values, 0.0), jnp.where(first, 0.0, values)], axis=0
+    ).astype(bf16)
 
 
 def step_parts(step, hp):
@@ -150,7 +166,7 @@
 
 def scan_kernel(
     place, conv_in, step, rim, taps, hp, skip, pre_out, mixed, query, run, starts, last, packed,
-    padded, act, state, carry
+    padded, act, state, carry, entered, weighted
 ):
     k = pl.program_id(0)
 
@@ -194,23 +210,26 @@
     first = lanes((PIECE, 128)) < 64
     first_row = lanes((1, 128)) < 64
     row16 = rows((16, 128))
+    entered[...] = dot(queries, state[...])
     for j in range(PAIRS):
         cols = slice(128 * j, 128 * j + 128)
         x = act[:, cols]
         scaled = x * spread(sizes, j, first)
-        y = jnp.zeros((PIECE, 128), f32)
-        for side in range(2):
-            h = 2 * j + side
+        weighted[:, cols] = (scaled * spread(to_end, j, first)).astype(bf16)
+        gaps = []
+        for h in (2 * j, 2 * j + 1):
             gap = jnp.exp(jnp.minimum(running[:, h : h + 1] - running_t[h : h + 1, :], 0.0))
-            mine = jnp.where(first if side == 0 else ~first, scaled, 0.0)
-            y = y + dot(gap * affinity, mine)
+            gaps.append(gap * affinity)
+        y = spread(from_start, j, first) * entered[:, cols] + dot(
+            jnp.concatenate(gaps, axis=1), apart(scaled, first)
+        )
+        mixed[:, cols] = y + skip[0:1, cols] * x
+    entered[...] = dot(keys_t, weighted[...])
+    for j in range(PAIRS):
+        cols = slice(128 * j, 128 * j + 128)
         before = state[:, cols]
-        starts[0, :, cols] = before
-        y = y + spread(from_start, j, first) * dot(queries, before)
-        mixed[:, cols] = y + skip[0:1, cols] * x
-        after = spread(whole, j, first_row) * before + dot(
-            keys_t, scaled * spread(to_end, j, first)
-        )
+        starts[0, :, cols] = before.astype(bf16)
+        after = spread(whole, j, first_row) * before + entered[:, cols]
         state[:, cols] = after
         last[:, cols] = after
         packed[0:N, cols] = after.astype(bf16)
@@ -225,8 +244,9 @@
     return lax.rem(k + 4 - place[0], 4)
 
 
-def scan_local(place, conv_in, step, rim, taps, hp, skip):
+def scan_local(place, conv_in, step, rim, taps, hp, skip, pinned):
     tokens = conv_in.shape[0]
+    kept = stored if pinned else jax.ShapeDtypeStruct
 
     def whole(shape):
         return pl.BlockSpec(shape, lambda k, place: (0,) * len(shape))
@@ -261,16 +281,18 @@
                 pltpu.VMEM((PIECE, ACT), f32),
                 pltpu.VMEM((N, GROUP), f32),
                 pltpu.VMEM((8, 128), f32),
+                pltpu.VMEM((PIECE, GROUP), f32),
+                pltpu.VMEM((PIECE, GROUP), bf16),
             ],
         ),
         out_shape=[
-            jax.ShapeDtypeStruct((tokens, ACT), f32),
+            kept((tokens, ACT), f32),
             jax.ShapeDtypeStruct((tokens, GROUP), f32),
             jax.ShapeDtypeStruct((tokens, N), bf16),
             jax.ShapeDtypeStruct((tokens, 128), f32),
-            jax.ShapeDtypeStruct((tokens // PIECE, N, GROUP), f32),
-            jax.ShapeDtypeStruct((N, GROUP), f32),
-            jax.ShapeDtypeStruct((N + 16, GROUP), bf16),
+            kept((tokens // PIECE, N, GROUP), bf16),
+            kept((N, GROUP), f32),
+            stored((N + 16, GROUP), bf16),
         ],
         compiler_params=pltpu.CompilerParams(vmem_limit_bytes=VMEM),
         cost_estimate=pl.CostEstimate(
@@ -294,11 +316,11 @@
     conv_in[:, GROUP:] = jnp.where(is_first, mine[:, HALF:edge], theirs[:, HALF:edge]).astype(bf16)
     slot = jnp.where(is_first, theirs[:, HALF : HALF + 128], mine[:, HALF + 128 : edge])
     step[...] = slot.astype(bf16).astype(f32)
-    gate[:, :HALF] = mine[:, edge:]
-    gate[:, HALF:] = theirs[:, edge:]
-
-
-def project(core, feed, gain, own, other):
+    gate[:, :HALF] = mine[:, edge:].astype(bf16)
+    gate[:, HALF:] = theirs[:, edge:].astype(bf16)
+
+
+def project(core, feed, gain, own, other, pinned):
     tokens = feed.shape[0]
 
     def whole(shape):
@@ -316,39 +338,46 @@
             out_specs=[piece(D), piece(ACT), piece(128), piece(GROUP)],
         ),
         out_shape=[
-            jax.ShapeDtypeStruct((tokens, D), bf16),
+            stored((tokens, D), bf16),
             jax.ShapeDtypeStruct((tokens, ACT), bf16),
             jax.ShapeDtypeStruct((tokens, 128), f32),
-            jax.ShapeDtypeStruct((tokens, GROUP), f32),
+            stored((tokens, GROUP), bf16),
         ],
         compiler_params=pltpu.CompilerParams(vmem_limit_bytes=VMEM),
         cost_estimate=pl.CostEstimate(
             flops=3_200_000_000, bytes_accessed=12_000_000, transcendentals=1000
         ),
         name="project",
-    )(core, feed, gain, own, other)
+    )(core, feed, gain, *far(pinned, own, other))
 
 
 def gate_kernel(
-    mixed, run, query, entering, gate, gain, out_own, out_other, mixed_out, sent0, sent1, sent2, sent3
+    mixed, run, query, entering, gate, gain, out_own, out_other, grad, mixed_out, sums0, sums1,
+    sums2, sums3, sent0, sent1, sent2, sent3, entered
 ):
     k = pl.program_id(0)
+    entered[...] = dot(query[...], entering[...])
+    inner = jnp.zeros((PIECE, 1), f32)
     decay = jnp.exp(run[...])
-    queries = query[...]
     first = lanes((PIECE, 128)) < 64
     total = jnp.zeros((PIECE, 1), f32)
     normed = []
     for j in range(PAIRS):
         cols = slice(128 * j, 128 * j + 128)
-        y = mixed[:, cols] + spread(decay, j, first) * dot(queries, entering[:, cols])
+        y = mixed[:, cols] + spread(decay, j, first) * entered[:, cols]
         mixed_out[:, cols] = y
-        pre = gate[:, cols]
+        pre = gate[:, cols].astype(f32)
         gated = y.astype(bf16).astype(f32) * (pre * jax.nn.sigmoid(pre))
         total = total + jnp.sum(gated * gated, axis=1, keepdims=True)
-        normed.append((gated * gain[0:1, cols]).astype(bf16))
+        scaled = gated * gain[0:1, cols]
+        inner = inner + jnp.sum(scaled * grad[:, cols], axis=1, keepdims=True)
+        normed.append(scaled.astype(bf16))
+    lane = lanes((PIECE, 128))
+    both = jnp.where(lane == 0, total, jnp.where(lane == 1, inner, 0.0)).T[0:8]
+    for sums in (sums0, sums1, sums2, sums3):
+        sums[...] = both
     part = dot(jnp.concatenate(normed[:3], axis=1), out_own[...])
     part = part + dot(jnp.concatenate(normed[3:], axis=1), out_other[...])
-    lane = lanes((PIECE, 128))
     high = total.astype(bf16).astype(f32)
     split = jnp.where(lane == 0, high, jnp.where(lane == 1, total - high, 0.0))
     for index, sent in enumerate((sent0, sent1, sent2, sent3)):
@@ -359,7 +388,7 @@
             sent[:, D:] = split.astype(sent.dtype)
 
 
-def gate_out(mixed, run, query, entering, gate, gain, out_own, out_other):
+def gate_out(mixed, run, query, entering, gate, gain, out_own, out_other, grad):
     tokens = mixed.shape[0]
 
     def whole(shape):
@@ -380,31 +409,74 @@
             whole((8, GROUP)),
             whole((HALF, D)),
             whole((HALF, D)),
+            piece(GROUP),
         ],
-        out_specs=[piece(GROUP)] + [whole((PIECE, D + 128))] * 4,
-        out_shape=[jax.ShapeDtypeStruct((tokens, GROUP), f32)]
-        + [jax.ShapeDtypeStruct((PIECE, D + 128), f32 if k == 0 else bf16) for k in range(4)],
+        out_specs=[piece(GROUP)]
+        + [pl.BlockSpec((8, PIECE), lambda k, by=by: (0, lax.rem(k + by, 4))) for by in range(4)]
+        + [whole((PIECE, D + 128))] * 4,
+        out_shape=[stored((tokens, GROUP), f32)]
+        + [stored((8, tokens), f32)] * 4
+        + [stored((PIECE, D + 128), f32 if k == 0 else bf16) for k in range(4)],
+        scratch_shapes=[pltpu.VMEM((PIECE, GROUP), f32)],
         compiler_params=pltpu.CompilerParams(vmem_limit_bytes=VMEM),
         cost_estimate=pl.CostEstimate(
             flops=1_300_000_000, bytes_accessed=9_000_000, transcendentals=400_000
         ),
         name="gate_out",
-    )(mixed, run, query, entering, gate, gain, out_own, out_other)
+    )(mixed, run, query, entering, gate, gain, out_own, out_other, grad)
+
+
+def scales_kernel(one, two, three, four, scale):
+    total = one[...] + two[...] + three[...] + four[...]
+    lane = lanes((PIECE, 128))
+    for k in range(total.shape[1] // PIECE):
+        block = total[:, PIECE * k : PIECE * k + PIECE]
+        columns = jnp.concatenate([block, jnp.zeros((120, PIECE), f32)], axis=0).T
+        s_out = lax.rsqrt(columns[:, 0:1] / DI + epsilon)
+        mean = s_out * columns[:, 1:2] / DI
+        scale[PIECE * k : PIECE * k + PIECE] = (
+            split_pair(s_out, lane, 0) + split_pair(mean, lane, 2)
+        ).astype(bf16)
+
+
+def scales(parts):
+    tokens = parts[0].shape[1]
+    return pl.pallas_call(
+        scales_kernel,
+        out_shape=jax.ShapeDtypeStruct((tokens, 128), bf16),
+        cost_estimate=pl.CostEstimate(
+            flops=1_000_000, bytes_accessed=200_000, transcendentals=1000
+        ),
+        name="scales",
+    )(*parts)
+
+
+def out_back_kernel(grad_new, out_own, out_other, product):
+    product[:, :HALF] = dot_nt(grad_new[...], out_own[...])
+    product[:, HALF:] = dot_nt(grad_new[...], out_other[...])
+
+
+def out_back(grad_new, out_own, out_other):
+    tokens = grad_new.shape[0]
+    return pl.pallas_call(
+        out_back_kernel,
+        out_shape=jax.ShapeDtypeStruct((tokens, GROUP), f32),
+        compiler_params=pltpu.CompilerParams(vmem_limit_bytes=VMEM),
+        cost_estimate=pl.CostEstimate(
+            flops=1_200_000_000, bytes_accessed=5_500_000, transcendentals=0
+        ),
+        name="out_back",
+    )(grad_new, out_own, out_other)
 
 
 def gate_back_kernel(
-    grad_new, out_own, out_other, gate, mixed, scale, run, query, gain, decay,
-    grad_scan, grad_gate, normed, packed, state, product
+    product, gate, mixed, scale, run, query, gain, decay, grad_scan, grad_gate, normed, packed, state
 ):
     k = pl.program_id(0)
 
     @pl.when(k == 0)
     def _():
         state[...] = jnp.zeros_like(state)
-        product[:, :HALF] = dot_nt(grad_new[...], out_own[...])
-        product[:, HALF:] = dot_nt(grad_new[...], out_other[...])
-
-    token = pl.ds(pl.multiple_of(k * PIECE, PIECE), PIECE)
     grown = jnp.exp(run[...])
     queries_t = query[...].astype(f32).T.astype(bf16)
     first = lanes((PIECE, 128)) < 64
@@ -413,8 +485,8 @@
     row16 = rows((16, 128))
     for j in range(PAIRS):
         cols = slice(128 * j, 128 * j + 128)
-        grad = product[token, cols]
-        pre = gate[:, cols]
+        grad = product[:, cols]
+        pre = gate[:, cols].astype(f32)
         sig = jax.nn.sigmoid(pre)
         out = mixed[:, cols].astype(bf16).astype(f32)
         unit = out * (pre * sig) * s_out
@@ -434,7 +506,7 @@
         ).astype(bf16)
 
 
-def gate_back(grad_new, out_own, out_other, gate, mixed, scale, run, query, gain, decay):
+def gate_back(product, gate, mixed, scale, run, query, gain, decay, pinned):
     tokens = mixed.shape[0]
 
     def whole(shape):
@@ -447,9 +519,7 @@
         gate_back_kernel,
         grid=(tokens // PIECE,),
         in_specs=[
-            whole((tokens, D)),
-            whole((HALF, D)),
-            whole((HALF, D)),
+            piece(GROUP),
             piece(GROUP),
             piece(GROUP),
             piece(128),
@@ -463,21 +533,21 @@
             jax.ShapeDtypeStruct((tokens, GROUP), bf16),
             jax.ShapeDtypeStruct((tokens, GROUP), bf16),
             jax.ShapeDtypeStruct((tokens, GROUP), bf16),
-            jax.ShapeDtypeStruct((N + 16, GROUP), bf16),
+            stored((N + 16, GROUP), bf16),
         ],
-        scratch_shapes=[pltpu.VMEM((N, GROUP), f32), pltpu.VMEM((tokens, GROUP), f32)],
+        scratch_shapes=[pltpu.VMEM((N, GROUP), f32)],
         compiler_params=pltpu.CompilerParams(vmem_limit_bytes=VMEM),
         cost_estimate=pl.CostEstimate(
-            flops=1_400_000_000, bytes_accessed=12_000_000, transcendentals=400_000
+            flops=120_000_000, bytes_accessed=8_000_000, transcendentals=400_000
         ),
         name="gate_back",
-    )(grad_new, out_own, out_other, gate, mixed, scale, run, query, gain, decay)
+    )(product, *far(pinned, gate, mixed), scale, *far(pinned, run, query), gain, decay)
 
 
 def scan_back_kernel(
     place, conv_in, pre_in, step, run, grad, grad_gate, mixed, starts, last, entering, leaving, rim,
-    taps, hp, skip, use_own, use_other, tail, rim_grad, grad_taps, grad_hp, act, delta, state, after,
-    skip_sum
+    taps, hp, skip, use_own, use_other, tail, rim_grad, laid, act, delta, state, after, skip_sum,
+    product, flows, weighted, ended, grad_taps, grad_hp, spots
 ):
     k = pl.program_id(0)
     count = pl.num_programs(0)
@@ -521,11 +591,7 @@
     affinity = jnp.where(upper, dot_nt(keys, queries), 0.0)
     running_t = running.T
     grad_affinity = jnp.zeros((PIECE, PIECE), f32)
-    grad_keys = jnp.zeros((PIECE, N), f32)
-    grad_queries = jnp.zeros((PIECE, N), f32)
-    inner_sum = jnp.zeros((PIECE, 128), f32)
-    outer_sum = jnp.zeros((PIECE, 128), f32)
-    bound = jnp.zeros((8, 128), f32)
+    product[...] = dot(keys, state[...])
     for j in range(PAIRS):
         cols = slice(128 * j, 128 * j + 128)
         x = act[:, cols]
@@ -534,30 +600,37 @@
         dm = grad[:, cols]
         dm32 = dm.astype(f32)
         to_end_j = spread(to_end, j, first)
-        back = state[:, cols]
-        z = to_end_j * dot(keys, back)
-        for side in range(2):
-            h = 2 * j + side
-            half = first if side == 0 else ~first
-            gap = jnp.exp(jnp.minimum(running_t[h : h + 1, :] - running[:, h : h + 1], 0.0))
-            mine = jnp.where(half, dm32, 0.0)
-            z = z + dot(gap * affinity, mine)
-            grad_affinity = grad_affinity + gap * dot_nt(jnp.where(half, scaled, 0.0), dm)
+        gaps = [
+            jnp.exp(jnp.minimum(running_t[h : h + 1, :] - running[:, h : h + 1], 0.0))
+            for h in (2 * j, 2 * j + 1)
+        ]
+        z = to_end_j * product[:, cols] + dot(
+            jnp.concatenate([gap * affinity for gap in gaps], axis=1), apart(dm32, first)
+        )
+        crossed = dot_nt(apart(scaled, first), dm)
+        grad_affinity = grad_affinity + gaps[0] * crossed[:PIECE] + gaps[1] * crossed[PIECE:]
         skip_j = skip[0:1, cols]
         delta[0:PIECE, cols] = sizes_j * z + skip_j * dm32
         skip_sum[0:1, cols] += jnp.sum(dm32 * x, axis=0, keepdims=True)
-        heads = (lanes((128, 128)) == 2 * j + (rows((128, 128)) >= 64)).astype(bf16)
-        inner_sum = inner_sum + dot_split(x * z, heads)
-        outer_sum = outer_sum + dot_split(dm32 * (mixed[:, cols] - skip_j * x), heads)
-        after_j = after[:, cols]
-        inside = jnp.sum(back * after_j, axis=0, keepdims=True)
-        bound = bound + dot_split(jnp.broadcast_to(inside, (8, 128)), heads)
-        before = spread(before_all, j, first_row) * entering[:, cols] + starts[0, :, cols]
-        after[:, cols] = before
-        weighted = spread(from_start, j, first) * dm32
-        grad_queries = grad_queries + dot_nt(weighted, before)
-        grad_keys = grad_keys + dot_nt(scaled * to_end_j, back)
-        state[:, cols] = spread(whole, j, first_row) * back + dot(queries_t, weighted)
+        flows[0:PIECE, cols] = x * z
+        flows[PIECE : 2 * PIECE, cols] = dm32 * (mixed[:, cols] - skip_j * x)
+        inside = jnp.sum(state[:, cols] * after[:, cols], axis=0, keepdims=True)
+        flows[2 * PIECE :, cols] = jnp.broadcast_to(inside, (16, 128))
+        after[:, cols] = spread(before_all, j, first_row) * entering[:, cols] + starts[
+            0, :, cols
+        ].astype(f32)
+        weighted[:, cols] = (spread(from_start, j, first) * dm32).astype(bf16)
+        ended[:, cols] = (scaled * to_end_j).astype(bf16)
+    heads = (lanes((GROUP, 128)) == lax.shift_right_logical(rows((GROUP, 128)), 6)).astype(bf16)
+    sums = dot_split(flows[...], heads)
+    inner_sum, outer_sum = sums[:PIECE], sums[PIECE : 2 * PIECE]
+    bound = sums[2 * PIECE :]
+    grad_queries = dot_nt(weighted[...], after[...])
+    grad_keys = dot_nt(ended[...], state[...])
+    product[...] = dot(queries_t, weighted[...])
+    for j in range(PAIRS):
+        cols = slice(128 * j, 128 * j + 128)
+        state[:, cols] = spread(whole, j, first_row) * state[:, cols] + product[:, cols]
     grad_affinity = jnp.where(upper, grad_affinity, 0.0)
     delta[0:PIECE, GROUP : GROUP + N] = grad_keys + dot(grad_affinity, queries)
     delta[0:PIECE, GROUP + N :] = grad_queries + dot(grad_affinity.T, keys)
@@ -642,11 +715,30 @@
                 rim_grad[:, WIDE + at : WIDE + at + 128] = jnp.where(is_first, 0.0, total)
         for side in range(2):
             rim_grad[:, WIDE * side + edge : WIDE * side + WIDE] = jnp.zeros((8, HALF), f32)
+        spots[...] = jnp.zeros_like(spots)
+        for j in range(PAIRS):
+            half = 2 * place[0] + (place[1] if j < 3 else 1 - place[1])
+            at = pl.ds(pl.multiple_of(half * HALF + 128 * (j % 3), 128), 128)
+            spots[:, at] = grad_taps[:, 128 * j : 128 * j + 128]
+        spots[:, DI : DI + 2 * N] = grad_taps[:, GROUP:]
+        lane = lanes((8, 128))
+        sums = grad_hp[...]
+        crossed = jnp.where(lane < 6, pltpu.roll(sums, 122, 1), pltpu.roll(sums, 6, 1))
+        sums = pltpu.roll(jnp.where(is_first, sums, crossed), SMALL_AT, 1)
+        sums = pltpu.roll(sums, 5, 0)
+        is_sum = (rows((8, 128)) >= 5) & (lane >= SMALL_AT) & (lane < SMALL_AT + HEADS)
+        is_tap = (rows((8, 128)) < 5) & (lane >= SMALL_AT) & (lane < SMALL_AT + 52)
+        sums = jnp.where(is_sum, sums, 0.0)
+        laid[...] = jnp.zeros_like(laid)
+        for d in range(64):
+            at = 52 * d // 128 * 128
+            window = pltpu.roll(spots[:, at : at + 256], (256 + SMALL_AT - 52 * d + at) % 256, 1)
+            laid[24 * d : 24 * d + 8] = jnp.where(is_tap, window[:, :128], sums)
 
 
 def scan_back(
     place, conv_in, pre, step, run, grad, grad_gate, mixed, starts, last, entering, leaving, rim,
-    taps, hp, skip
+    taps, hp, skip, pinned
 ):
     tokens = conv_in.shape[0]
     count = tokens // PIECE
@@ -684,8 +776,7 @@
                 piece(WIDE),
                 whole((8, 2 * WIDE)),
                 whole((8, 2 * WIDE)),
-                whole((8, ACT)),
-                whole((8, 128)),
+                whole((D, 128)),
             ],
             scratch_shapes=[
                 pltpu.VMEM((PIECE, ACT), f32),
@@ -693,6 +784,13 @@
                 pltpu.VMEM((N, GROUP), f32),
                 pltpu.VMEM((N, GROUP), f32),
                 pltpu.VMEM((8, GROUP), f32),
+                pltpu.VMEM((PIECE, GROUP), f32),
+                pltpu.VMEM((2 * PIECE + 16, GROUP), f32),
+                pltpu.VMEM((PIECE, GROUP), bf16),
+                pltpu.VMEM((PIECE, GROUP), bf16),
+                pltpu.VMEM((8, ACT), f32),
+                pltpu.VMEM((8, 128), f32),
+                pltpu.VMEM((8, DI + 2 * N + 128), f32),
             ],
         ),
         out_shape=[
@@ -700,16 +798,15 @@
             jax.ShapeDtypeStruct((tokens, WIDE), bf16),
             jax.ShapeDtypeStruct((8, 2 * WIDE), f32),
             jax.ShapeDtypeStruct((8, 2 * WIDE), f32),
-            jax.ShapeDtypeStruct((8, ACT), f32),
-            jax.ShapeDtypeStruct((8, 128), f32),
+            jax.ShapeDtypeStruct((D, 128), f32),
         ],
         compiler_params=pltpu.CompilerParams(vmem_limit_bytes=VMEM),
         cost_estimate=pl.CostEstimate(
             flops=2_000_000_000, bytes_accessed=9_000_000, transcendentals=2_500_000
         ),
         name="scan_back",
-    )(place, conv_in, pre, step, run, grad, grad_gate, mixed, starts, last, entering, leaving, rim,
-      taps, hp, skip)
+    )(place, *far(pinned, conv_in, pre, step, run), grad, grad_gate,
+      *far(pinned, mixed, starts, last, entering), leaving, rim, taps, hp, skip)
 
 
 def parts_kernel(use_own, use_other, own, other, sent0, sent1, sent2, sent3):
@@ -718,7 +815,7 @@
         sent[...] = part[PIECE * index : PIECE * index + PIECE].astype(sent.dtype)
 
 
-def project_back(use_own, use_other, own, other):
+def project_back(use_own, use_other, own, other, pinned):
     tokens = use_own.shape[0]
     width = 256
 
@@ -730,13 +827,13 @@
         grid=(D // width,),
         in_specs=[whole((tokens, WIDE))] * 2 + [pl.BlockSpec((width, WIDE), lambda k: (k, 0))] * 2,
         out_specs=[pl.BlockSpec((PIECE, width), lambda k: (0, k))] * 4,
-        out_shape=[jax.ShapeDtypeStruct((PIECE, D), f32 if k == 0 else bf16) for k in range(4)],
+        out_shape=[stored((PIECE, D), f32 if k == 0 else bf16) for k in range(4)],
         compiler_params=pltpu.CompilerParams(vmem_limit_bytes=VMEM),
         cost_estimate=pl.CostEstimate(
             flops=3_200_000_000, bytes_accessed=9_000_000, transcendentals=0
         ),
         name="project_back",
-    )(use_own, use_other, own, other)
+    )(use_own, use_other, *far(pinned, own, other))
 
 
 def early_kernel(normed, grad_gate, normed_out, grad_new, own, other, sums):
@@ -772,7 +869,7 @@
             whole((tokens, D)),
         ],
         out_specs=[pl.BlockSpec((HALF, GROUP), lambda i: (i, 0))] * 2,
-        out_shape=[jax.ShapeDtypeStruct((D, GROUP), bf16)] * 2,
+        out_shape=[stored((D, GROUP), bf16)] * 2,
         scratch_shapes=[pltpu.VMEM((2, HALF, D), f32)],
         compiler_params=pltpu.CompilerParams(vmem_limit_bytes=VMEM),
         cost_estimate=pl.CostEstimate(
@@ -780,6 +877,45 @@
         ),
         name="early_grads",
     )(normed, grad_gate, normed_out, grad_new)
+
+
+def inner_kernel(place, normed, use_own, use_other, slot, own, other):
+    is_first = place[1] == 0
+    for use, sent, holds in ((use_own, own, ~is_first), (use_other, other, is_first)):
+        block = dot_tn(normed[...], use[...])
+        sent[:, :HALF] = block[:, :HALF].astype(bf16)
+        middle = block[:, HALF : HALF + 128] + jnp.where(holds, slot[...], 0.0)
+        sent[:, HALF : HALF + 128] = middle.astype(bf16)
+        sent[:, HALF + 128 :] = block[:, HALF + 128 :].astype(bf16)
+
+
+def inner_grads(place, normed, use_own, use_other, slot):
+    tokens = normed.shape[0]
+    edge = HALF + EXTRA
+
+    def whole(shape):
+        return pl.BlockSpec(shape, lambda i, place: (0, 0))
+
+    return pl.pallas_call(
+        inner_kernel,
+        grid_spec=pltpu.PrefetchScalarGridSpec(
+            num_scalar_prefetch=1,
+            grid=(4,),
+            in_specs=[
+                pl.BlockSpec((tokens, HALF), lambda i, place: (0, i)),
+                whole((tokens, edge)),
+                whole((tokens, edge)),
+                pl.BlockSpec((HALF, 128), lambda i, place: (i, 0)),
+            ],
+            out_specs=[pl.BlockSpec((HALF, edge), lambda i, place: (i, 0))] * 2,
+        ),
+        out_shape=[stored((D, edge), bf16)] * 2,
+        compiler_params=pltpu.CompilerParams(vmem_limit_bytes=VMEM),
+        cost_estimate=pl.CostEstimate(
+            flops=2_000_000_000, bytes_accessed=7_000_000, transcendentals=0
+        ),
+        name="inner_grads",
+    )(place, normed, use_own, use_other, slot)
 
 
 def split_pair(values, lane, at):
@@ -803,7 +939,7 @@
     return pl.pallas_call(
         receive_kernel,
         out_shape=[
-            jax.ShapeDtypeStruct((PIECE, D), f32),
+            stored((PIECE, D), f32),
             jax.ShapeDtypeStruct((PIECE, D), bf16),
             jax.ShapeDtypeStruct((PIECE, 128), bf16),
         ],
@@ -940,33 +1076,35 @@
     return lax.optimization_barrier((values, anchor))[0]
 
 
-def layer_forward(core, head, feed, feed_all, target, weights, out_weights):
+def layer_forward(core, head, feed, feed_all, weights, out_weights, first):
     place = jnp.stack([head, core])
     own, other = weights["own"], weights["other"]
-    normed, conv_in, step, gate = project(core.reshape(1), feed_all, weights["gain_in"], own, other)
+    normed, conv_in, step, gate = project(core.reshape(1), feed_all, weights["gain_in"], own, other, first
+    )
     last_row = PIECE * lax.rem(7 - head, 4) + PIECE - 8
     rim = lax.ppermute(
         lax.dynamic_slice_in_dim(conv_in, last_row, 8, 0), "seq", [(i, i + 1) for i in range(15)]
     )
     pre, mixed0, query, run, starts, last, packed = scan_local(
-        place, conv_in, step, rim, weights["taps"], weights["hp"], weights["skip"]
+        place, conv_in, step, rim, weights["taps"], weights["hp"], weights["skip"], first
     )
     entering = carried(packed, -1)
-    entering, out_own, out_other = out_weights(packed, entering)
-    mixed, *sent = gate_out(
-        mixed0, run, query, entering, gate, weights["gain"], out_own, out_other
-    )
-    branch, result, scale = receive(scatter_head(sent), feed, target)
+    entering, out_own, out_other, product = out_weights(packed, entering)
+    mixed, *sums_and_sent = gate_out(
+        mixed0, run, query, entering, gate, weights["gain"], out_own, out_other,
+        mixed0 if product is None else product,
+    )
     kept = dict(
         feed=feed, normed=normed, gate=gate, conv_in=conv_in, rim=rim, step=step, pre=pre,
         mixed=mixed, query=query, run=run, starts=starts, last=last, entering=entering,
-        scale=scale, branch=branch, packed=packed, out_own=out_own, out_other=out_other,
-    )
-    return result, kept
+        packed=packed, out_own=out_own, out_other=out_other,
+    )
+    return sums_and_sent[:4], sums_and_sent[4:], kept
 
 
 def layer_backward(
-    core, head, incoming, gathered, scale, kept, below, weights, after_gate, before_receive
+    core, head, incoming, gathered, product, scale, kept, below, weights, after_gate, before_receive,
+    inner_first,
 ):
     place = jnp.stack([head, core])
     own, other = weights["own"], weights["other"]
@@ -975,51 +1113,37 @@
         (8, GROUP),
     )
     grad_scan, grad_gate, normed_out, packed = gate_back(
-        gathered, kept["out_own"], kept["out_other"], kept["gate"], kept["mixed"], scale,
-        kept["run"], kept["query"], weights["gain"], decay,
+        product, kept["gate"], kept["mixed"], scale, kept["run"], kept["query"], weights["gain"],
+        decay, not inner_first,
     )
     leaving = carried(packed, 1)
     normed = kept["normed"]
-    early, leaving = after_gate(early_grads(normed, grad_gate, normed_out, gathered), leaving)
-    use_own, use_other, tail, rim_grad, grad_taps, grad_hp = scan_back(
+    early, leaving = after_gate(
+        early_grads(normed, grad_gate, normed_out, gathered), packed, leaving
+    )
+    use_own, use_other, tail, rim_grad, slot = scan_back(
         place, kept["conv_in"], kept["pre"], kept["step"], kept["run"], grad_scan, grad_gate,
         kept["mixed"], kept["starts"], kept["last"], kept["entering"], leaving, kept["rim"],
-        weights["taps"], weights["hp"], weights["skip"],
+        weights["taps"], weights["hp"], weights["skip"], inner_first,
     )
     from_next = lax.ppermute(rim_grad, "seq", [(i + 1, i) for i in range(15)])
     last_row = PIECE * lax.rem(7 - head, 4) + PIECE - 8
     tail = (tail + from_next).astype(bf16)
     use_own = lax.dynamic_update_slice_in_dim(use_own, tail[:, :WIDE], last_row, 0)
     use_other = lax.dynamic_update_slice_in_dim(use_other, tail[:, WIDE:], last_row, 0)
-    sent = project_back(use_own, use_other, own, other)
-    edge = HALF + EXTRA
-    use_own, use_other = tied((use_own, use_other), sent[1])
-    small = small_columns(core, head, grad_taps, grad_hp)
-    small = jnp.pad(small, ((0, 0), (HALF + SMALL_AT, EXTRA - SMALL_AT - SMALL)))
-    grad_x = (
-        (dot_tn(normed, use_own[:, :edge]) + jnp.where(core == 1, small, 0.0)).astype(bf16),
-        (dot_tn(normed, use_other[:, :edge]) + jnp.where(core == 0, small, 0.0)).astype(bf16),
-    )
+    if inner_first:
+        grad_x = summed(*inner_grads(place, normed, use_own, use_other, slot))
+        use_own, use_other = tied((use_own, use_other), grad_x)
+        sent = project_back(use_own, use_other, own, other, inner_first)
+    else:
+        sent = project_back(use_own, use_other, own, other, inner_first)
     grad_feed, scale_below = receive_back(
-        before_receive(scatter_head(sent), grad_x), kept["feed"], incoming, weights["gain_in"], below["branch"],
+        before_receive(scatter_head(sent)), kept["feed"], incoming, weights["gain_in"], below["branch"],
         below["scale"],
     )
+    if not inner_first:
+        grad_x = inner_grads(place, normed, *tied((use_own, use_other), grad_feed), slot)
     return grad_feed, scale_below, grad_x, early
-
-
-def small_columns(core, head, grad_taps, grad_hp):
-    taps = grad_taps[:5]
-    full = jnp.zeros((5, DI), f32)
-    full = lax.dynamic_update_slice_in_dim(full, taps[:, :HALF], (2 * head + core) * HALF, 1)
-    full = lax.dynamic_update_slice_in_dim(
-        full, taps[:, HALF:GROUP], (2 * head + 1 - core) * HALF, 1
-    )
-    full = jnp.concatenate([full, taps[:, GROUP:]], axis=1)
-    full = full.reshape(5, 64, 52).transpose(1, 0, 2).reshape(64, 260)
-    first, second = grad_hp[:3, :6], grad_hp[:3, 6:HEADS]
-    sums = jnp.concatenate([pick(core, first, second), pick(core, second, first)], axis=1)
-    sums = jnp.broadcast_to(sums.reshape(1, 36), (64, 36))
-    return jnp.concatenate([full, sums, jnp.zeros((64, 16), f32)], axis=1).reshape(D, SMALL)
 
 
 def summed(own, other):
@@ -1071,46 +1195,59 @@
         later["out"] = (mine, swap(mine))
         grad_all = jnp.concatenate(gather_head(tied(grad_top, packed)), axis=0)
         entering, later["grad_all"] = lax.optimization_barrier((entering, grad_all))
-        return [entering] + [a[:HALF] for a in later["out"]]
+        return [entering] + [a[:HALF] for a in later["out"]] + [None]
 
     def out_second(packed, entering):
-        return [entering] + [a[HALF:] for a in later["out"]]
-
-    hidden, kept0 = layer_forward(core, head, tokens, feed_all, tokens, weights[0], out_first)
+        mine, theirs = [a[HALF:] for a in later["out"]]
+        later["product"] = out_back(tied(later["grad_all"], packed), mine, theirs)
+        return [entering, mine, theirs, later["product"]]
+
+    _, sent, kept0 = layer_forward(core, head, tokens, feed_all, weights[0], out_first, True)
+    branch, hidden, scale = receive(scatter_head(sent), tokens, tokens)
+    kept0.update(branch=branch, scale=scale)
     feed_all = jnp.concatenate(gather_head(hidden), axis=0)
     own1 = tied(own1, hidden)
     weights[1].update(own=own1, other=swap(own1))
-    result, kept1 = layer_forward(core, head, hidden, feed_all, grad_top, weights[1], out_second)
-    scale = jnp.concatenate(gather_head(kept1["scale"]), axis=0)
-
-    def after_gate1(values, leaving):
-        later["sum"] = summed(*values)
-        return later["sum"], leaving
-
-    def before_receive1(sent, grad_x):
-        return tied(sent, later["sum"])
+    sums, sent, kept1 = layer_forward(core, head, hidden, feed_all, weights[1], out_second, False)
+    sums = [sums[0]] + [from_head(sums[k], k) for k in (1, 3, 2)]
+    scale = scales(sums)
+
+    def after_gate1(values, packed, leaving):
+        _, result, _ = receive(scatter_head(tied(sent, packed)), hidden, hidden)
+        leaving, later["result"], values = lax.optimization_barrier(
+            (leaving, result, summed(*values))
+        )
+        return values, leaving
+
+    def before_receive1(sent):
+        return sent
 
     grad_hidden, scale, grad_x1, early1 = layer_backward(
-        core, head, grad_top, later["grad_all"], scale, kept1, kept0, weights[1], after_gate1, before_receive1
+        core, head, grad_top, later["grad_all"], later["product"], scale, kept1, kept0, weights[1],
+        after_gate1, before_receive1, False,
     )
     chunks = gather_head(jnp.concatenate([grad_hidden, scale], axis=1))
-    early1 = scatter_seq_now(tied(early1, grad_hidden))
-    chunks, grad_x1, early1 = lax.optimization_barrier((chunks, grad_x1, early1))
+    later["early"] = scatter_seq_now(tied(early1, grad_hidden))
+    chunks, grad_x1, later["early"] = lax.optimization_barrier((chunks, grad_x1, later["early"]))
     grad_all = jnp.concatenate([a[:, :D] for a in chunks], axis=0)
     scale = jnp.concatenate([a[:, D:] for a in chunks], axis=0)
 
-    def after_gate0(values, leaving):
+    def after_gate0(values, packed, leaving):
         values = [jnp.concatenate([grad_x1[i], values[i]], axis=1) for i in range(2)]
         later["sum"] = summed(*values)
         return scatter_seq(later["sum"]), leaving
 
-    def before_receive0(sent, grad_x):
+    def before_receive0(sent):
         return tied(sent, later["sum"])
 
+    product = out_back(grad_all, kept0["out_own"], kept0["out_other"])
     grad_feed, _, grad_x0, early0 = layer_backward(
-        core, head, grad_hidden, grad_all, scale, kept0, kept0, weights[0], after_gate0, before_receive0
-    )
-    x0 = scatter_seq_now(summed(*grad_x0))
+        core, head, grad_hidden, grad_all, product, scale, kept0, kept0, weights[0], after_gate0,
+        before_receive0, True,
+    )
+    early1 = later["early"]
+    x0 = scatter_seq_now(grad_x0)
+    result = later["result"]
     got = swap(pick(core, result, hidden))
     layer_out = jnp.stack([pick(core, hidden, got), pick(core, got, result)])
     got = swap(pick(core, grad_hidden, grad_feed))
@@ -1148,9 +1285,8 @@
         [turned_slot[:, :, 6:HEADS], turned_slot[:, :, :6]], axis=2
     )
     grad_step = jnp.concatenate([steps[g] for g in range(4)], axis=1)
-    small = slot[:, :, SMALL_AT : SMALL_AT + SMALL].reshape(4, 24 * SMALL)
-    taps = jnp.sum(small[:, :260], axis=0)
-    sums = small[:, 260:296].reshape(4, 3, HEADS).transpose(1, 0, 2).reshape(3, 48)
+    taps = jnp.sum(slot[:, :5, SMALL_AT : SMALL_AT + 52], axis=0)
+    sums = slot[:, 5:8, SMALL_AT : SMALL_AT + HEADS].transpose(1, 0, 2).reshape(3, 48)
     grad_output_gain = jnp.sum(grad_out * out_proj[0].astype(f32), axis=1) / output_gain[0].astype(
         f32
     )
@@ -1166,8 +1302,8 @@
         grad_gate_inner[None],
         grad_shared[None],
         grad_step[None],
-        taps[:208].reshape(1, 4, 52),
-        taps[208:260][None],
+        taps[None, :4],
+        taps[4:5],
         sums[0:1],
         sums[1:2],
         sums[2:3],

time: 638 us -> 606 us (0.950)
  local copies, waits for them, and re-layouts: 102 us -> 40.9 us
  Pallas kernels: 86.9 us -> 118 us
  waiting for transfers between devices: 231 us -> 250 us
  matrix products: 10.1 us -> 0 us
  starting transfers between devices: 138 us -> 128 us
    unnamed x384 -> x304, local copies, waits for them, and re-layouts: 67.3 us -> 16.3 us
    pallas_call x4 -> x9, Pallas kernels: 10.9 us -> 26.7 us  [the longest x2 9.97 us: inner_grads(): pl.pallas_call(inner_kernel, grid_spec=pltpu.PrefetchScalarGridSpec(num_s...]
    ppermute x24, waiting for transfers between devices: 57.6 us -> 70.1 us  [from_seq(): return lax.ppermute(a, 'seq', pairs)]
    ppermute x36, starting transfers between devices: 42.7 us -> 31.7 us  [from_head(): return lax.ppermute(a, 'head', [(i, (i - k) % 4) for i in range(4)])]
    dot_general x4 -> x0, matrix products: 10.1 us -> none  [dot_tn(): lax.dot_general(a.astype(bf16), b.astype(bf16), (((0,), (0,)), ((), ())),...]
    ppermute x12, waiting for transfers between devices: 4.38 us -> 11.6 us  [swap(): return lax.ppermute(a, 'section', [(0, 1), (1, 0)])]
    reshape x9 -> x0, local copies, waits for them, and re-layouts: 6.77 us -> none  [the longest x4 3.56 us: small_columns(): full = full.reshape(5, 64, 52).transpose(1, 0, 2).reshape(64, 260)]
  transfers between devices with their start and end apart: 86 -> 86, of which waited for: 51 -> 53; matrix products, arithmetic and copies ran while one was open for 10% -> 6% of each run, Pallas kernels for 9% -> 10%
where the time goes in v3:
time: 606 us; the launch traced here: 595 us
  waiting for transfers between devices  250 us (41%)
  starting transfers between devices  128 us (21%)
  Pallas kernels  118 us (19%)
  other arithmetic  41.2 us (7%)
  local copies, waits for them, and re-layouts  40.9 us (7%)
  between operations  16.9 us (3%)
    ppermute x36, waiting for transfers between devices, from_head(): return lax.ppermute(a, 'head', [(i, (i - k) % 4) for i in range(4)])  98.4 us
    ppermute x24, waiting for transfers between devices, from_seq(): return lax.ppermute(a, 'seq', pairs)  70.1 us
    ppermute x24, starting transfers between devices, from_seq(): return lax.ppermute(a, 'seq', pairs)  31.9 us
    ppermute x36, starting transfers between devices, from_head(): return lax.ppermute(a, 'head', [(i, (i - k) % 4) for i in range(4)])  31.7 us
    pallas_call x2, Pallas kernels, scan_back(): pl.pallas_call(scan_back_kernel, grid_spec=pltpu.PrefetchScalarGridSpec(n...  27.6 us
    all_to_all x2, waiting for transfers between devices, scatter_seq_now(): got = lax.all_to_all(a, 'seq', 0, 0, tiled=True).astype(f32)  21.3 us
    ppermute x12, starting transfers between devices, swap(): return lax.ppermute(a, 'section', [(0, 1), (1, 0)])  16.7 us
    unnamed x304, local copies, waits for them, and re-layouts  16.3 us
  transfers between devices with their start and end apart: 86, of which 53 were waited for; matrix products, arithmetic and copies ran while one was open for 6% of the time, Pallas kernels for 10%

profile of v3, /device:TPU:103, one launch (start us, length us, event | category | flops | bytes accessed | tf_op | source)
XLA Modules:
  0.0 595.3 jit_solution(9411220316261677659)
XLA Ops:
  20.0 5.9 collective-permute-start.9
  26.4 3.1 collective-permute-start.5
  32.1 11.0 %all-to-all-start = ((f32[64,8,128]{2,1,0:T(8,128)}), f32[64,8,128]{2,1,0:T(8,128)S(1)}, u32[]{:S(2)}, u32[]{:S(2)}) async-start(f32[64,8,128]{2,1,0:T(8,128)} %broadcast_in_dim.147), calls=%async_computation | async-start | bytes 524288 | tf_op jit(solution)/shard_map/all_to_all | solution.py:1049
  43.5 10.4 %all-to-all-done = f32[64,8,128]{2,1,0:T(8,128)S(1)} async-done(((f32[64,8,128]{2,1,0:T(8,128)}), f32[64,8,128]{2,1,0:T(8,128)S(1)}, u32[]{:S(2)}, u32[]{:S(2)}) %all-to-all-start) | async-done | bytes 262176 | tf_op jit(solution)/shard_map/all_to_all | solution.py:1049
  57.5 12.1 %all-gather.4.cloned.1.call-done.own = bf16[1536,1024]{1,0:T(8,128)(2,1)} async-done(((bf16[96,1024]{1,0:T(8,128)(2,1)}), bf16[1536,1024]{1,0:T(8,128)(2,1)}) %all-gather.4.cloned.1.call-update) | async-done | bytes 3145744 | tf_op jit(solution)/shard_map/all_gather | solution.py:1040
  80.5 7.7 %project.2 = (bf16[512,1536]{1,0:T(8,128)(2,1)}, bf16[512,1024]{1,0:T(8,128)(2,1)S(1)}, f32[512,128]{1,0:T(8,128)S(1)}, bf16[512,768]{1,0:T(8,128)(2,1)}) custom-call(s32[1]{0:T(128)} %bitcast.1.core, bf16[512,1536]{1,0:T(8,128)(2,1)S(1)} %pad_maximum_fusion.1.feed, f32[8,1536]{1,0:T(8,128)S(1)} %broadcast_in_dim.151.gain, ...), custom_call_target="tpu_custom_call" | custom-call | flops 3200000000 | bytes 12000000 | tf_op jit(solution)/shard_map/project/pallas_call | solution.py:332
  90.5 4.5 collective-permute-done.11.rim
  95.0 7.4 %scan_local.2 = (f32[512,1024]{1,0:T(8,128)}, f32[512,768]{1,0:T(8,128)S(1)}, bf16[512,128]{1,0:T(8,128)(2,1)S(1)}, f32[512,128]{1,0:T(8,128)S(1)}, bf16[4,128,7...) custom-call(s32[2]{0:T(128)S(1)} %pad_add_fusion.place, ...), custom_call_target="tpu_custom_call" | custom-call | flops 1000000000 | bytes 8000000 | tf_op jit(solution)/shard_map/scan_local/pallas_call | solution.py:257
  108.8 9.7 %collective-permute-done.14 = bf16[144,768]{1,0:T(8,128)(2,1)S(1)} collective-permute-done((bf16[144,768]{1,0:T(8,128)(2,1)}, bf16[144,768]{1,0:T(8,128)(2,1)S(1)}, u32[]{:S(2)}, u32[]{:S(2)}) %collective-permute-start.14) | collective-permute-done | bytes 221216 | tf_op jit(solution)/shard_map/ppermute | solution.py:41
  122.2 3.7 all-gather.6.cloned.1.call-done
  138.0 2.8 collective-permute-done.16
  140.8 7.3 %collective-permute-done.15 = bf16[144,768]{1,0:T(8,128)(2,1)S(1)} collective-permute-done((bf16[144,768]{1,0:T(8,128)(2,1)S(1)}, bf16[144,768]{1,0:T(8,128)(2,1)S(1)}, u32[]{:S(2)}, u32[]{:S(2)}) %collective-permute-start.15) | collective-permute-done | bytes 221216 | tf_op jit(solution)/shard_map/ppermute | solution.py:41
  151.3 5.7 gate_out.2
  159.4 8.9 %collective-permute-done.22.one = bf16[128,1664]{1,0:T(8,128)(2,1)S(1)} collective-permute-done((bf16[128,1664]{1,0:T(8,128)(2,1)}, bf16[128,1664]{1,0:T(8,128)(2,1)S(1)}, u32[]{:S(2)}, u32[]{:S(2)}) %collective-permute-start.22) | collective-permute-done | bytes 426016 | tf_op jit(solution)/shard_map/ppermute | solution.py:29
  168.3 2.7 collective-permute-done.23.two
  171.0 10.2 %collective-permute-done.24.three = bf16[128,1664]{1,0:T(8,128)(2,1)S(1)} collective-permute-done((bf16[128,1664]{1,0:T(8,128)(2,1)}, bf16[128,1664]{1,0:T(8,128)(2,1)S(1)}, u32[]{:S(2)}, u32[]{:S(2)}) %collective-permute-start.24) | collective-permute-done | bytes 426016 | tf_op jit(solution)/shard_map/ppermute | solution.py:29
  186.4 9.0 %collective-permute-done.27 = bf16[128,1536]{1,0:T(8,128)(2,1)S(1)} collective-permute-done((bf16[128,1536]{1,0:T(8,128)(2,1)S(1)}, bf16[128,1536]{1,0:T(8,128)(2,1)S(1)}, u32[]{:S(2)}, u32[]{:S(2)}) %collective-permute-start.27) | collective-permute-done | bytes 393248 | tf_op jit(solution)/shard_map/ppermute | solution.py:29
  197.0 9.0 %collective-permute-done.25 = bf16[128,1536]{1,0:T(8,128)(2,1)S(1)} collective-permute-done((bf16[128,1536]{1,0:T(8,128)(2,1)S(1)}, bf16[128,1536]{1,0:T(8,128)(2,1)S(1)}, u32[]{:S(2)}, u32[]{:S(2)}) %collective-permute-start.25) | collective-permute-done | bytes 393248 | tf_op jit(solution)/shard_map/ppermute | solution.py:29
  206.2 4.9 project.3
  213.4 4.3 collective-permute-done.32.rim
  217.7 7.1 %scan_local.3 = (f32[512,1024]{1,0:T(8,128)S(1)}, f32[512,768]{1,0:T(8,128)S(1)}, bf16[512,128]{1,0:T(8,128)(2,1)S(1)}, f32[512,128]{1,0:T(8,128)S(1)}, bf16[4,1...) custom-call(s32[2]{0:T(128)S(1)} %pad_add_fusion.place, ...), custom_call_target="tpu_custom_call" | custom-call | flops 1000000000 | bytes 8000000 | tf_op jit(solution)/shard_map/scan_local/pallas_call | solution.py:257
  225.0 2.6 collective-permute-start.33
  227.5 9.6 %collective-permute-done.35 = bf16[144,768]{1,0:T(8,128)(2,1)S(1)} collective-permute-done((bf16[144,768]{1,0:T(8,128)(2,1)}, bf16[144,768]{1,0:T(8,128)(2,1)S(1)}, u32[]{:S(2)}, u32[]{:S(2)}) %collective-permute-start.35) | collective-permute-done | bytes 221216 | tf_op jit(solution)/shard_map/ppermute | solution.py:41
  247.0 2.8 collective-permute-done.37
  249.8 4.9 collective-permute-done.36
  255.0 5.7 gate_out.3
  260.8 2.7 collective-permute-start.40
  264.9 3.0 collective-permute-done.41.four
  272.4 5.0 gate_back.2
  277.5 5.3 early_grads.2
  282.7 5.0 collective-permute-start.51
  287.7 2.9 collective-permute-start.44
  291.2 9.1 %collective-permute-done.44 = bf16[144,768]{1,0:T(8,128)(2,1)S(1)} collective-permute-done((bf16[144,768]{1,0:T(8,128)(2,1)}, bf16[144,768]{1,0:T(8,128)(2,1)S(1)}, u32[]{:S(2)}, u32[]{:S(2)}) %collective-permute-start.44) | collective-permute-done | bytes 221216 | tf_op jit(solution)/shard_map/ppermute | solution.py:41
  300.8 3.2 collective-permute-done.42
  308.8 3.0 collective-permute-start.46
  313.8 9.0 %collective-permute-done.50.three = bf16[128,1664]{1,0:T(8,128)(2,1)S(1)} collective-permute-done((bf16[128,1664]{1,0:T(8,128)(2,1)}, bf16[128,1664]{1,0:T(8,128)(2,1)S(1)}, u32[]{:S(2)}, u32[]{:S(2)}) %collective-permute-start.50) | collective-permute-done | bytes 426016 | tf_op jit(solution)/shard_map/ppermute | solution.py:29
  325.8 3.8 add_convert_fusion.1
  330.1 12.8 %scan_back.2 = (bf16[512,1024]{1,0:T(8,128)(2,1)S(1)}, bf16[512,1024]{1,0:T(8,128)(2,1)S(1)}, f32[8,2048]{1,0:T(8,128)S(1)}, f32[8,2048]{1,0:T(8,128)S(1)}, f32[1536,128]{1,0:T(8,128)S(1)}) custom-call(s32[2]{0:T(128)S(1)} %pad_add_fusion.place, bf16[512,1024]{1,0:T(8,128)(2,1)S(1)} %copy-done.33, f32[512,1024]{1,0:T(8,128)S(1)} %copy-done.28, ...), custom_call_target="tpu_custom_call" | custom-call | flops 2000000000 | bytes 9000000 | tf_op jit(solution)/shard_map/scan_back/pallas_call | solution.py:752
  347.9 5.2 project_back.2
  354.7 7.7 %collective-permute-done.54.one = bf16[128,1536]{1,0:T(8,128)(2,1)S(1)} collective-permute-done((bf16[128,1536]{1,0:T(8,128)(2,1)}, bf16[128,1536]{1,0:T(8,128)(2,1)S(1)}, u32[]{:S(2)}, u32[]{:S(2)}) %collective-permute-start.54) | collective-permute-done | bytes 393248 | tf_op jit(solution)/shard_map/ppermute | solution.py:29
  363.5 11.0 %collective-permute-done.56.three = bf16[128,1536]{1,0:T(8,128)(2,1)S(1)} collective-permute-done((bf16[128,1536]{1,0:T(8,128)(2,1)}, bf16[128,1536]{1,0:T(8,128)(2,1)S(1)}, u32[]{:S(2)}, u32[]{:S(2)}) %collective-permute-start.56) | collective-permute-done | bytes 393248 | tf_op jit(solution)/shard_map/ppermute | solution.py:29
  377.0 6.5 %all-to-all-start.1 = ((bf16[16,96,768]{2,1,0:T(8,128)(2,1)}), bf16[16,96,768]{2,1,0:T(8,128)(2,1)}, u32[]{:S(2)}, u32[]{:S(2)}) async-start(bf16[16,96,768]{2,1,0:T(8,128)(2,1)} %bitcast.237), calls=%async_computation.1 | async-start | bytes 4718592 | tf_op jit(solution)/shard_map/all_to_all | solution.py:1158
  391.6 5.0 inner_grads.2
  396.6 21.3 %all-to-all-done.1 = bf16[16,96,768]{2,1,0:T(8,128)(2,1)} async-done(((bf16[16,96,768]{2,1,0:T(8,128)(2,1)}), bf16[16,96,768]{2,1,0:T(8,128)(2,1)}, u32[]{:S(2)}, u32[]{:S(2)}) %all-to-all-start.1) | async-done | bytes 2359328 | tf_op jit(solution)/shard_map/all_to_all | solution.py:1158
  417.8 2.7 reduce_sum.80
  428.3 3.5 gate_back.3
  431.7 5.2 early_grads.3
  442.4 5.5 collective-permute-done.71
  447.9 2.7 add_convert_fusion
  450.6 3.9 collective-permute-done.60
  457.6 4.0 collective-permute-start.64
  464.0 7.6 %collective-permute-done.64 = bf16[144,768]{1,0:T(8,128)(2,1)S(1)} collective-permute-done((bf16[144,768]{1,0:T(8,128)(2,1)S(1)}, bf16[144,768]{1,0:T(8,128)(2,1)S(1)}, u32[]{:S(2)}, u32[]{:S(2)}) %collective-permute-start.64) | collective-permute-done | bytes 221216 | tf_op jit(solution)/shard_map/ppermute | solution.py:41
  474.0 14.8 %scan_back.3 = (bf16[512,1024]{1,0:T(8,128)(2,1)S(1)}, bf16[512,1024]{1,0:T(8,128)(2,1)S(1)}, f32[8,2048]{1,0:T(8,128)S(1)}, f32[8,2048]{1,0:T(8,128)S(1)}, f32[1536,128]{1,0:T(8,128)S(1)}) custom-call(s32[2]{0:T(128)S(1)} %pad_add_fusion.place, bf16[512,1024]{1,0:T(8,128)(2,1)} %copy-done.31, f32[512,1024]{1,0:T(8,128)} %get-tuple-element.199.pre_in, ...), custom_call_target="tpu_custom_call" | custom-call | flops 2000000000 | bytes 9000000 | tf_op jit(solution)/shard_map/scan_back/pallas_call | solution.py:752
  491.0 3.5 collective-permute-done.66
  494.6 5.0 inner_grads.3
  501.4 3.9 collective-permute-done.67
  505.3 3.9 add_convert_fusion.2
  509.3 9.2 %all-to-all-start.2 = ((bf16[16,96,640]{2,1,0:T(8,128)(2,1)}), bf16[16,96,640]{2,1,0:T(8,128)(2,1)}, u32[]{:S(2)}, u32[]{:S(2)}) async-start(bf16[16,96,640]{2,1,0:T(8,128)(2,1)} %bitcast.238), calls=%async_computation.2 | async-start | bytes 3932160 | tf_op jit(solution)/shard_map/all_to_all | solution.py:1158
  520.9 7.7 %project_back.3 = (f32[128,1536]{1,0:T(8,128)}, bf16[128,1536]{1,0:T(8,128)(2,1)}, bf16[128,1536]{1,0:T(8,128)(2,1)}, bf16[128,1536]{1,0:T(8,128)(2,1)}) custom-call(bf16[512,1024]{1,0:T(8,128)(2,1)S(1)} %copy-done.86, bf16[512,1024]{1,0:T(8,128)(2,1)S(1)} %copy-done.88, bf16[1536,1024]{1,0:T(8,128)(2,1)} %all-gather.4.cloned.1.call-done.own, ...), custom_call_target="tpu_custom_call" | custom-call | flops 3200000000 | bytes 9000000 | tf_op jit(solution)/shard_map/project_back/pallas_call | solution.py:825
  531.7 6.9 %collective-permute-done.68.one = bf16[128,1536]{1,0:T(8,128)(2,1)S(1)} collective-permute-done((bf16[128,1536]{1,0:T(8,128)(2,1)}, bf16[128,1536]{1,0:T(8,128)(2,1)S(1)}, u32[]{:S(2)}, u32[]{:S(2)}) %collective-permute-start.68) | collective-permute-done | bytes 393248 | tf_op jit(solution)/shard_map/ppermute | solution.py:29
  540.3 9.6 %collective-permute-done.70.three = bf16[128,1536]{1,0:T(8,128)(2,1)S(1)} collective-permute-done((bf16[128,1536]{1,0:T(8,128)(2,1)}, bf16[128,1536]{1,0:T(8,128)(2,1)S(1)}, u32[]{:S(2)}, u32[]{:S(2)}) %collective-permute-start.70) | collective-permute-done | bytes 393248 | tf_op jit(solution)/shard_map/ppermute | solution.py:29
  560.4 3.4 collective-permute-start.78
  564.9 4.2 collective-permute-start.74
  570.6 7.7 %collective-permute-done.77 = bf16[24,1536]{1,0:T(8,128)(2,1)S(1)} collective-permute-done((bf16[24,1536]{1,0:T(8,128)(2,1)S(1)}, bf16[24,1536]{1,0:T(8,128)(2,1)S(1)}, u32[]{:S(2)}, u32[]{:S(2)}) %collective-permute-start.77) | collective-permute-done | bytes 73760 | tf_op jit(solution)/shard_map/ppermute | solution.py:1262
  (645 shorter events, 169.3 us)
Async XLA Ops:
  7.2 62.4 %all-gather.4.cloned.1.call-start = ((), (), s32[]{:S(2)}) async-start(), calls=%async_computation.4 | async-start | bytes 3342336 | tf_op jit(solution)/shard_map/all_gather | solution.py:1040
  20.0 37.5 %collective-permute-start.9 = (bf16[48,1536]{1,0:T(8,128)(2,1)}, bf16[48,1536]{1,0:T(8,128)(2,1)}, u32[]{:S(2)}, u32[]{:S(2)}) collective-permute-start(bf16[48,1536]{1,0:T(8,128)(2,1)} %bitcast.44), channel_id=1, source_target_pairs={{0,0},{1,4},{2,8},{3,12},{4,16},{5,20},{6,24},{7,28},{8,64},{9,68}... | collective-permute-start | bytes 442376 | tf_op jit(solution)/shard_map/ppermute | solution.py:1174
  26.3 30.0 %collective-permute-start.6 = (bf16[128,1536]{1,0:T(8,128)(2,1)S(1)}, bf16[128,1536]{1,0:T(8,128)(2,1)S(1)}, u32[]{:S(2)}, u32[]{:S(2)}) collective-permute-start(bf16[128,1536]{1,0:T(8,128)(2,1)S(1)} %dynamic-slice_bitcast_fusion.1.feed.target), channel_id=1, source_target_pairs={{0,1},{1,2},{2,3},{3,0},{4,5},{5,6},{6,7},{7,4},{8,9},{9,10},{10,1... | collective-permute-start | bytes 1179656 | tf_op jit(solution)/shard_map/ppermute | solution.py:29
  26.4 30.0 %collective-permute-start.5 = (bf16[128,1536]{1,0:T(8,128)(2,1)S(1)}, bf16[128,1536]{1,0:T(8,128)(2,1)S(1)}, u32[]{:S(2)}, u32[]{:S(2)}) collective-permute-start(bf16[128,1536]{1,0:T(8,128)(2,1)S(1)} %dynamic-slice_bitcast_fusion.1.feed.target), channel_id=1, source_target_pairs={{0,2},{1,3},{2,0},{3,1},{4,6},{5,7},{6,4},{7,5},{8,10},{9,11},{10,... | collective-permute-start | bytes 1179656 | tf_op jit(solution)/shard_map/ppermute | solution.py:29
  29.5 26.9 %collective-permute-start.4 = (bf16[128,1536]{1,0:T(8,128)(2,1)S(1)}, bf16[128,1536]{1,0:T(8,128)(2,1)}, u32[]{:S(2)}, u32[]{:S(2)}) collective-permute-start(bf16[128,1536]{1,0:T(8,128)(2,1)S(1)} %dynamic-slice_bitcast_fusion.1.feed.target), channel_id=1, source_target_pairs={{0,3},{1,0},{2,1},{3,2},{4,7},{5,4},{6,5},{7,6},{8,11},{9,8},{10,9... | collective-permute-start | bytes 1179656 | tf_op jit(solution)/shard_map/ppermute | solution.py:29
  32.1 21.8 %all-to-all-start = ((f32[64,8,128]{2,1,0:T(8,128)}), f32[64,8,128]{2,1,0:T(8,128)S(1)}, u32[]{:S(2)}, u32[]{:S(2)}) async-start(f32[64,8,128]{2,1,0:T(8,128)} %broadcast_in_dim.147), calls=%async_computation | async-start | bytes 524288 | tf_op jit(solution)/shard_map/all_to_all | solution.py:1049
  43.1 82.8 %all-gather.6.cloned.1.call-start = ((), (), s32[]{:S(2)}) async-start(), calls=%async_computation.5 | async-start | bytes 2506752 | tf_op jit(solution)/shard_map/all_gather | solution.py:1040
  72.1 112.1 %all-gather.8.cloned.1.call-start = ((), (), s32[]{:S(2)}) async-start(), calls=%async_computation.6 | async-start | bytes 3342336 | tf_op jit(solution)/shard_map/all_gather | solution.py:1040
  102.5 16.1 %collective-permute-start.14 = (bf16[144,768]{1,0:T(8,128)(2,1)}, bf16[144,768]{1,0:T(8,128)(2,1)S(1)}, u32[]{:S(2)}, u32[]{:S(2)}) collective-permute-start(bf16[144,768]{1,0:T(8,128)(2,1)} %get-tuple-element.150), channel_id=1, source_target_pairs={{12,0},{0,4},{4,8},{8,12},{28,16},{16,20},{20,24},{24,28},{44,32},... | collective-permute-start | bytes 663560 | tf_op jit(solution)/shard_map/ppermute | solution.py:41
  102.5 16.6 %collective-permute-start.13 = (bf16[144,768]{1,0:T(8,128)(2,1)}, bf16[144,768]{1,0:T(8,128)(2,1)S(1)}, u32[]{:S(2)}, u32[]{:S(2)}) collective-permute-start(bf16[144,768]{1,0:T(8,128)(2,1)} %get-tuple-element.150), channel_id=1, source_target_pairs={{8,0},{12,4},{0,8},{4,12},{24,16},{28,20},{16,24},{20,28},{40,32},... | collective-permute-start | bytes 663560 | tf_op jit(solution)/shard_map/ppermute | solution.py:41
  102.6 18.9 %collective-permute-start.12 = (bf16[144,768]{1,0:T(8,128)(2,1)}, bf16[144,768]{1,0:T(8,128)(2,1)S(1)}, u32[]{:S(2)}, u32[]{:S(2)}) collective-permute-start(bf16[144,768]{1,0:T(8,128)(2,1)} %get-tuple-element.150), channel_id=1, source_target_pairs={{4,0},{8,4},{12,8},{0,12},{20,16},{24,20},{28,24},{16,28},{36,32},... | collective-permute-start | bytes 663560 | tf_op jit(solution)/shard_map/ppermute | solution.py:41
  106.2 24.1 %collective-permute-start.20 = (bf16[128,1536]{1,0:T(8,128)(2,1)S(1)}, bf16[128,1536]{1,0:T(8,128)(2,1)}, u32[]{:S(2)}, u32[]{:S(2)}) collective-permute-start(bf16[128,1536]{1,0:T(8,128)(2,1)S(1)} %dynamic-slice_bitcast_fusion.grad_new), channel_id=1, source_target_pairs={{0,1},{1,2},{2,3},{3,0},{4,5},{5,6},{6,7},{7,4},{8,9},{9,10},{10,1... | collective-permute-start | bytes 1179656 | tf_op jit(solution)/shard_map/ppermute | solution.py:29
  108.7 23.0 %collective-permute-start.19 = (bf16[128,1536]{1,0:T(8,128)(2,1)S(1)}, bf16[128,1536]{1,0:T(8,128)(2,1)}, u32[]{:S(2)}, u32[]{:S(2)}) collective-permute-start(bf16[128,1536]{1,0:T(8,128)(2,1)S(1)} %dynamic-slice_bitcast_fusion.grad_new), channel_id=1, source_target_pairs={{0,2},{1,3},{2,0},{3,1},{4,6},{5,7},{6,4},{7,5},{8,10},{9,11},{10,... | collective-permute-start | bytes 1179656 | tf_op jit(solution)/shard_map/ppermute | solution.py:29
  118.5 14.4 %collective-permute-start.18 = (bf16[128,1536]{1,0:T(8,128)(2,1)S(1)}, bf16[128,1536]{1,0:T(8,128)(2,1)}, u32[]{:S(2)}, u32[]{:S(2)}) collective-permute-start(bf16[128,1536]{1,0:T(8,128)(2,1)S(1)} %dynamic-slice_bitcast_fusion.grad_new), channel_id=1, source_target_pairs={{0,3},{1,0},{2,1},{3,2},{4,7},{5,4},{6,5},{7,6},{8,11},{9,8},{10,9... | collective-permute-start | bytes 1179656 | tf_op jit(solution)/shard_map/ppermute | solution.py:29
  125.9 23.7 %collective-permute-start.21 = (bf16[768,1536]{1,0:T(8,128)(2,1)}, bf16[768,1536]{1,0:T(8,128)(2,1)S(1)}, u32[]{:S(2)}, u32[]{:S(2)}) collective-permute-start(bf16[768,1536]{1,0:T(8,128)(2,1)} %all-gather.6.cloned.1.call-done), channel_id=1, source_target_pairs={{0,64},{64,0},{1,65},{65,1},{2,66},{66,2},{3,67},{67,3},{4,68},{68... | collective-permute-start | bytes 7077896 | tf_op jit(solution)/shard_map/ppermute | solution.py:45
  128.9 9.0 %collective-permute-start.17 = (bf16[144,768]{1,0:T(8,128)(2,1)S(1)}, bf16[144,768]{1,0:T(8,128)(2,1)S(1)}, u32[]{:S(2)}, u32[]{:S(2)}) collective-permute-start(bf16[144,768]{1,0:T(8,128)(2,1)S(1)} %maximum_maximum_fusion), channel_id=1, source_target_pairs={{0,16},{4,20},{8,24},{12,28},{16,32},{20,36},{24,40},{28,44},{32,4... | collective-permute-start | bytes 663560 | tf_op jit(solution)/shard_map/ppermute | solution.py:41
  130.4 10.4 %collective-permute-start.16 = (bf16[144,768]{1,0:T(8,128)(2,1)S(1)}, bf16[144,768]{1,0:T(8,128)(2,1)S(1)}, u32[]{:S(2)}, u32[]{:S(2)}) collective-permute-start(bf16[144,768]{1,0:T(8,128)(2,1)S(1)} %maximum_maximum_fusion), channel_id=1, source_target_pairs={{0,32},{4,36},{8,40},{12,44},{16,48},{20,52},{24,56},{28,60},{1,33... | collective-permute-start | bytes 663560 | tf_op jit(solution)/shard_map/ppermute | solution.py:41
  131.7 16.4 %collective-permute-start.15 = (bf16[144,768]{1,0:T(8,128)(2,1)S(1)}, bf16[144,768]{1,0:T(8,128)(2,1)S(1)}, u32[]{:S(2)}, u32[]{:S(2)}) collective-permute-start(bf16[144,768]{1,0:T(8,128)(2,1)S(1)} %maximum_maximum_fusion), channel_id=1, source_target_pairs={{0,48},{4,52},{8,56},{12,60},{1,49},{5,53},{9,57},{13,61},{2,50},{... | collective-permute-start | bytes 663560 | tf_op jit(solution)/shard_map/ppermute | solution.py:41
  157.0 11.3 %collective-permute-start.22 = (bf16[128,1664]{1,0:T(8,128)(2,1)}, bf16[128,1664]{1,0:T(8,128)(2,1)S(1)}, u32[]{:S(2)}, u32[]{:S(2)}) collective-permute-start(bf16[128,1664]{1,0:T(8,128)(2,1)} %get-tuple-element.158), channel_id=1, source_target_pairs={{0,1},{1,2},{2,3},{3,0},{4,5},{5,6},{6,7},{7,4},{8,9},{9,10},{10,1... | collective-permute-start | bytes 1277960 | tf_op jit(solution)/shard_map/ppermute | solution.py:29
  158.6 12.4 %collective-permute-start.23 = (bf16[128,1664]{1,0:T(8,128)(2,1)}, bf16[128,1664]{1,0:T(8,128)(2,1)S(1)}, u32[]{:S(2)}, u32[]{:S(2)}) collective-permute-start(bf16[128,1664]{1,0:T(8,128)(2,1)} %get-tuple-element.159), channel_id=1, source_target_pairs={{0,2},{1,3},{2,0},{3,1},{4,6},{5,7},{6,4},{7,5},{8,10},{9,11},{10,... | collective-permute-start | bytes 1277960 | tf_op jit(solution)/shard_map/ppermute | solution.py:29
  159.4 21.7 %collective-permute-start.24 = (bf16[128,1664]{1,0:T(8,128)(2,1)}, bf16[128,1664]{1,0:T(8,128)(2,1)S(1)}, u32[]{:S(2)}, u32[]{:S(2)}) collective-permute-start(bf16[128,1664]{1,0:T(8,128)(2,1)} %get-tuple-element.160), channel_id=1, source_target_pairs={{0,3},{1,0},{2,1},{3,2},{4,7},{5,4},{6,5},{7,6},{8,11},{9,8},{10,9... | collective-permute-start | bytes 1277960 | tf_op jit(solution)/shard_map/ppermute | solution.py:29
  184.2 21.9 %collective-permute-start.31 = (bf16[1536,1024]{1,0:T(8,128)(2,1)}, bf16[1536,1024]{1,0:T(8,128)(2,1)S(1)}, u32[]{:S(2)}, u32[]{:S(2)}) collective-permute-start(bf16[1536,1024]{1,0:T(8,128)(2,1)} %all-gather.8.cloned.1.call-done.own), channel_id=1, source_target_pairs={{0,64},{64,0},{1,65},{65,1},{2,66},{66,2},{3,67},{67,3},{4,68},{68... | collective-permute-start | bytes 9437192 | tf_op jit(solution)/shard_map/ppermute | solution.py:45
  184.7 10.7 %collective-permute-start.27 = (bf16[128,1536]{1,0:T(8,128)(2,1)S(1)}, bf16[128,1536]{1,0:T(8,128)(2,1)S(1)}, u32[]{:S(2)}, u32[]{:S(2)}) collective-permute-start(bf16[128,1536]{1,0:T(8,128)(2,1)S(1)} %get-tuple-element.161.feed.target), channel_id=1, source_target_pairs={{0,1},{1,2},{2,3},{3,0},{4,5},{5,6},{6,7},{7,4},{8,9},{9,10},{10,1... | collective-permute-start | bytes 1179656 | tf_op jit(solution)/shard_map/ppermute | solution.py:29
  185.1 12.0 %collective-permute-start.26 = (bf16[128,1536]{1,0:T(8,128)(2,1)S(1)}, bf16[128,1536]{1,0:T(8,128)(2,1)S(1)}, u32[]{:S(2)}, u32[]{:S(2)}) collective-permute-start(bf16[128,1536]{1,0:T(8,128)(2,1)S(1)} %get-tuple-element.161.feed.target), channel_id=1, source_target_pairs={{0,2},{1,3},{2,0},{3,1},{4,6},{5,7},{6,4},{7,5},{8,10},{9,11},{10,... | collective-permute-start | bytes 1179656 | tf_op jit(solution)/shard_map/ppermute | solution.py:29
  185.9 20.1 %collective-permute-start.25 = (bf16[128,1536]{1,0:T(8,128)(2,1)S(1)}, bf16[128,1536]{1,0:T(8,128)(2,1)S(1)}, u32[]{:S(2)}, u32[]{:S(2)}) collective-permute-start(bf16[128,1536]{1,0:T(8,128)(2,1)S(1)} %get-tuple-element.161.feed.target), channel_id=1, source_target_pairs={{0,3},{1,0},{2,1},{3,2},{4,7},{5,4},{6,5},{7,6},{8,11},{9,8},{10,9... | collective-permute-start | bytes 1179656 | tf_op jit(solution)/shard_map/ppermute | solution.py:29
  224.8 12.4 %collective-permute-start.35 = (bf16[144,768]{1,0:T(8,128)(2,1)}, bf16[144,768]{1,0:T(8,128)(2,1)S(1)}, u32[]{:S(2)}, u32[]{:S(2)}) collective-permute-start(bf16[144,768]{1,0:T(8,128)(2,1)} %get-tuple-element.171), channel_id=1, source_target_pairs={{12,0},{0,4},{4,8},{8,12},{28,16},{16,20},{20,24},{24,28},{44,32},... | collective-permute-start | bytes 663560 | tf_op jit(solution)/shard_map/ppermute | solution.py:41
  224.9 12.3 %collective-permute-start.34 = (bf16[144,768]{1,0:T(8,128)(2,1)}, bf16[144,768]{1,0:T(8,128)(2,1)S(1)}, u32[]{:S(2)}, u32[]{:S(2)}) collective-permute-start(bf16[144,768]{1,0:T(8,128)(2,1)} %get-tuple-element.171), channel_id=1, source_target_pairs={{8,0},{12,4},{0,8},{4,12},{24,16},{28,20},{16,24},{20,28},{40,32},... | collective-permute-start | bytes 663560 | tf_op jit(solution)/shard_map/ppermute | solution.py:41
  225.0 12.4 %collective-permute-start.33 = (bf16[144,768]{1,0:T(8,128)(2,1)}, bf16[144,768]{1,0:T(8,128)(2,1)S(1)}, u32[]{:S(2)}, u32[]{:S(2)}) collective-permute-start(bf16[144,768]{1,0:T(8,128)(2,1)} %get-tuple-element.171), channel_id=1, source_target_pairs={{4,0},{8,4},{12,8},{0,12},{20,16},{24,20},{28,24},{16,28},{36,32},... | collective-permute-start | bytes 663560 | tf_op jit(solution)/shard_map/ppermute | solution.py:41
  244.7 9.9 %collective-permute-start.36 = (bf16[144,768]{1,0:T(8,128)(2,1)S(1)}, bf16[144,768]{1,0:T(8,128)(2,1)S(1)}, u32[]{:S(2)}, u32[]{:S(2)}) collective-permute-start(bf16[144,768]{1,0:T(8,128)(2,1)S(1)} %maximum_maximum_fusion.1), channel_id=1, source_target_pairs={{0,48},{4,52},{8,56},{12,60},{1,49},{5,53},{9,57},{13,61},{2,50},{... | collective-permute-start | bytes 663560 | tf_op jit(solution)/shard_map/ppermute | solution.py:41
  282.7 43.0 %collective-permute-start.51 = (bf16[1536,768]{1,0:T(8,128)(2,1)}, bf16[1536,768]{1,0:T(8,128)(2,1)}, u32[]{:S(2)}, u32[]{:S(2)}) collective-permute-start(bf16[1536,768]{1,0:T(8,128)(2,1)} %get-tuple-element.197), channel_id=1, source_target_pairs={{0,64},{64,0},{1,65},{65,1},{2,66},{66,2},{3,67},{67,3},{4,68},{68... | collective-permute-start | bytes 7077896 | tf_op jit(solution)/shard_map/ppermute | solution.py:45
  287.7 12.6 %collective-permute-start.44 = (bf16[144,768]{1,0:T(8,128)(2,1)}, bf16[144,768]{1,0:T(8,128)(2,1)S(1)}, u32[]{:S(2)}, u32[]{:S(2)}) collective-permute-start(bf16[144,768]{1,0:T(8,128)(2,1)} %get-tuple-element.183), channel_id=1, source_target_pairs={{4,0},{8,4},{12,8},{0,12},{20,16},{24,20},{28,24},{16,28},{36,32},... | collective-permute-start | bytes 663560 | tf_op jit(solution)/shard_map/ppermute | solution.py:41
  290.6 9.7 %collective-permute-start.43 = (bf16[144,768]{1,0:T(8,128)(2,1)}, bf16[144,768]{1,0:T(8,128)(2,1)}, u32[]{:S(2)}, u32[]{:S(2)}) collective-permute-start(bf16[144,768]{1,0:T(8,128)(2,1)} %get-tuple-element.183), channel_id=1, source_target_pairs={{8,0},{12,4},{0,8},{4,12},{24,16},{28,20},{16,24},{20,28},{40,32},... | collective-permute-start | bytes 663560 | tf_op jit(solution)/shard_map/ppermute | solution.py:41
  290.6 13.4 %collective-permute-start.42 = (bf16[144,768]{1,0:T(8,128)(2,1)}, bf16[144,768]{1,0:T(8,128)(2,1)}, u32[]{:S(2)}, u32[]{:S(2)}) collective-permute-start(bf16[144,768]{1,0:T(8,128)(2,1)} %get-tuple-element.183), channel_id=1, source_target_pairs={{12,0},{0,4},{4,8},{8,12},{28,16},{16,20},{20,24},{24,28},{44,32},... | collective-permute-start | bytes 663560 | tf_op jit(solution)/shard_map/ppermute | solution.py:41
  291.2 17.6 %collective-permute-start.48 = (bf16[128,1664]{1,0:T(8,128)(2,1)}, bf16[128,1664]{1,0:T(8,128)(2,1)S(1)}, u32[]{:S(2)}, u32[]{:S(2)}) collective-permute-start(bf16[128,1664]{1,0:T(8,128)(2,1)} %get-tuple-element.189), channel_id=1, source_target_pairs={{0,1},{1,2},{2,3},{3,0},{4,5},{5,6},{6,7},{7,4},{8,9},{9,10},{10,1... | collective-permute-start | bytes 1277960 | tf_op jit(solution)/shard_map/ppermute | solution.py:29
  300.3 12.1 %collective-permute-start.49 = (bf16[128,1664]{1,0:T(8,128)(2,1)}, bf16[128,1664]{1,0:T(8,128)(2,1)S(1)}, u32[]{:S(2)}, u32[]{:S(2)}) collective-permute-start(bf16[128,1664]{1,0:T(8,128)(2,1)} %get-tuple-element.190), channel_id=1, source_target_pairs={{0,2},{1,3},{2,0},{3,1},{4,6},{5,7},{6,4},{7,5},{8,10},{9,11},{10,... | collective-permute-start | bytes 1277960 | tf_op jit(solution)/shard_map/ppermute | solution.py:29
  300.3 22.5 %collective-permute-start.50 = (bf16[128,1664]{1,0:T(8,128)(2,1)}, bf16[128,1664]{1,0:T(8,128)(2,1)S(1)}, u32[]{:S(2)}, u32[]{:S(2)}) collective-permute-start(bf16[128,1664]{1,0:T(8,128)(2,1)} %get-tuple-element.191), channel_id=1, source_target_pairs={{0,3},{1,0},{2,1},{3,2},{4,7},{5,4},{6,5},{7,6},{8,11},{9,8},{10,9... | collective-permute-start | bytes 1277960 | tf_op jit(solution)/shard_map/ppermute | solution.py:29
  307.4 16.8 %collective-permute-start.47 = (bf16[144,768]{1,0:T(8,128)(2,1)S(1)}, bf16[144,768]{1,0:T(8,128)(2,1)S(1)}, u32[]{:S(2)}, u32[]{:S(2)}) collective-permute-start(bf16[144,768]{1,0:T(8,128)(2,1)S(1)} %maximum_maximum_fusion.2), channel_id=1, source_target_pairs={{16,0},{20,4},{24,8},{28,12},{32,16},{36,20},{40,24},{44,28},{48,3... | collective-permute-start | bytes 663560 | tf_op jit(solution)/shard_map/ppermute | solution.py:41
  308.8 15.3 %collective-permute-start.46 = (bf16[144,768]{1,0:T(8,128)(2,1)S(1)}, bf16[144,768]{1,0:T(8,128)(2,1)S(1)}, u32[]{:S(2)}, u32[]{:S(2)}) collective-permute-start(bf16[144,768]{1,0:T(8,128)(2,1)S(1)} %maximum_maximum_fusion.2), channel_id=1, source_target_pairs={{32,0},{36,4},{40,8},{44,12},{48,16},{52,20},{56,24},{60,28},{33,1... | collective-permute-start | bytes 663560 | tf_op jit(solution)/shard_map/ppermute | solution.py:41
  312.5 11.7 %collective-permute-start.45 = (bf16[144,768]{1,0:T(8,128)(2,1)S(1)}, bf16[144,768]{1,0:T(8,128)(2,1)S(1)}, u32[]{:S(2)}, u32[]{:S(2)}) collective-permute-start(bf16[144,768]{1,0:T(8,128)(2,1)S(1)} %maximum_maximum_fusion.2), channel_id=1, source_target_pairs={{48,0},{52,4},{56,8},{60,12},{49,1},{53,5},{57,9},{61,13},{50,2},{... | collective-permute-start | bytes 663560 | tf_op jit(solution)/shard_map/ppermute | solution.py:41
  353.2 9.2 %collective-permute-start.54 = (bf16[128,1536]{1,0:T(8,128)(2,1)}, bf16[128,1536]{1,0:T(8,128)(2,1)S(1)}, u32[]{:S(2)}, u32[]{:S(2)}) collective-permute-start(bf16[128,1536]{1,0:T(8,128)(2,1)} %get-tuple-element.210), channel_id=1, source_target_pairs={{0,1},{1,2},{2,3},{3,0},{4,5},{5,6},{6,7},{7,4},{8,9},{9,10},{10,1... | collective-permute-start | bytes 1179656 | tf_op jit(solution)/shard_map/ppermute | solution.py:29
  353.3 10.2 %collective-permute-start.55 = (bf16[128,1536]{1,0:T(8,128)(2,1)}, bf16[128,1536]{1,0:T(8,128)(2,1)S(1)}, u32[]{:S(2)}, u32[]{:S(2)}) collective-permute-start(bf16[128,1536]{1,0:T(8,128)(2,1)} %get-tuple-element.211), channel_id=1, source_target_pairs={{0,2},{1,3},{2,0},{3,1},{4,6},{5,7},{6,4},{7,5},{8,10},{9,11},{10,... | collective-permute-start | bytes 1179656 | tf_op jit(solution)/shard_map/ppermute | solution.py:29
  353.5 21.1 %collective-permute-start.56 = (bf16[128,1536]{1,0:T(8,128)(2,1)}, bf16[128,1536]{1,0:T(8,128)(2,1)S(1)}, u32[]{:S(2)}, u32[]{:S(2)}) collective-permute-start(bf16[128,1536]{1,0:T(8,128)(2,1)} %get-tuple-element.212), channel_id=1, source_target_pairs={{0,3},{1,0},{2,1},{3,2},{4,7},{5,4},{6,5},{7,6},{8,11},{9,8},{10,9... | collective-permute-start | bytes 1179656 | tf_op jit(solution)/shard_map/ppermute | solution.py:29
  377.0 40.8 %all-to-all-start.1 = ((bf16[16,96,768]{2,1,0:T(8,128)(2,1)}), bf16[16,96,768]{2,1,0:T(8,128)(2,1)}, u32[]{:S(2)}, u32[]{:S(2)}) async-start(bf16[16,96,768]{2,1,0:T(8,128)(2,1)} %bitcast.237), calls=%async_computation.1 | async-start | bytes 4718592 | tf_op jit(solution)/shard_map/all_to_all | solution.py:1158
  383.5 173.4 %reduce-scatter.2.cloned.1.call-start = ((), (), s32[]{:S(2)}) async-start(), calls=%async_computation.7 | async-start | bytes 4595712 | tf_op jit(solution)/shard_map/reduce_scatter | solution.py:1154
  384.9 35.6 %collective-permute-start.57 = (bf16[128,1664]{1,0:T(8,128)(2,1)}, bf16[128,1664]{1,0:T(8,128)(2,1)S(1)}, u32[]{:S(2)}, u32[]{:S(2)}) collective-permute-start(bf16[128,1664]{1,0:T(8,128)(2,1)} %constant_dynamic-update-slice_fusion.16), channel_id=1, source_target_pairs={{0,3},{1,0},{2,1},{3,2},{4,7},{5,4},{6,5},{7,6},{8,11},{9,8},{10,9... | collective-permute-start | bytes 1277960 | tf_op jit(solution)/shard_map/ppermute | solution.py:29
  384.9 35.6 %collective-permute-start.58 = (bf16[128,1664]{1,0:T(8,128)(2,1)}, bf16[128,1664]{1,0:T(8,128)(2,1)}, u32[]{:S(2)}, u32[]{:S(2)}) collective-permute-start(bf16[128,1664]{1,0:T(8,128)(2,1)} %constant_dynamic-update-slice_fusion.16), channel_id=1, source_target_pairs={{0,2},{1,3},{2,0},{3,1},{4,6},{5,7},{6,4},{7,5},{8,10},{9,11},{10,... | collective-permute-start | bytes 1277960 | tf_op jit(solution)/shard_map/ppermute | solution.py:29
  385.5 35.1 %collective-permute-start.59 = (bf16[128,1664]{1,0:T(8,128)(2,1)}, bf16[128,1664]{1,0:T(8,128)(2,1)}, u32[]{:S(2)}, u32[]{:S(2)}) collective-permute-start(bf16[128,1664]{1,0:T(8,128)(2,1)} %constant_dynamic-update-slice_fusion.16), channel_id=1, source_target_pairs={{0,1},{1,2},{2,3},{3,0},{4,5},{5,6},{6,7},{7,4},{8,9},{9,10},{10,1... | collective-permute-start | bytes 1277960 | tf_op jit(solution)/shard_map/ppermute | solution.py:29
  439.2 8.7 %collective-permute-start.71 = (bf16[1536,1408]{1,0:T(8,128)(2,1)S(1)}, bf16[1536,1408]{1,0:T(8,128)(2,1)S(1)}, u32[]{:S(2)}, u32[]{:S(2)}) collective-permute-start(bf16[1536,1408]{1,0:T(8,128)(2,1)S(1)} %pad_maximum_fusion), channel_id=1, source_target_pairs={{0,64},{64,0},{1,65},{65,1},{2,66},{66,2},{3,67},{67,3},{4,68},{68... | collective-permute-start | bytes 12976136 | tf_op jit(solution)/shard_map/ppermute | solution.py:45
  440.9 9.7 %collective-permute-start.62 = (bf16[144,768]{1,0:T(8,128)(2,1)S(1)}, bf16[144,768]{1,0:T(8,128)(2,1)S(1)}, u32[]{:S(2)}, u32[]{:S(2)}) collective-permute-start(bf16[144,768]{1,0:T(8,128)(2,1)S(1)} %copy-done.116), channel_id=1, source_target_pairs={{4,0},{8,4},{12,8},{0,12},{20,16},{24,20},{28,24},{16,28},{36,32},... | collective-permute-start | bytes 663560 | tf_op jit(solution)/shard_map/ppermute | solution.py:41
  440.9 9.7 %collective-permute-start.61 = (bf16[144,768]{1,0:T(8,128)(2,1)S(1)}, bf16[144,768]{1,0:T(8,128)(2,1)S(1)}, u32[]{:S(2)}, u32[]{:S(2)}) collective-permute-start(bf16[144,768]{1,0:T(8,128)(2,1)S(1)} %copy-done.116), channel_id=1, source_target_pairs={{8,0},{12,4},{0,8},{4,12},{24,16},{28,20},{16,24},{20,28},{40,32},... | collective-permute-start | bytes 663560 | tf_op jit(solution)/shard_map/ppermute | solution.py:41
  440.9 13.6 %collective-permute-start.60 = (bf16[144,768]{1,0:T(8,128)(2,1)S(1)}, bf16[144,768]{1,0:T(8,128)(2,1)S(1)}, u32[]{:S(2)}, u32[]{:S(2)}) collective-permute-start(bf16[144,768]{1,0:T(8,128)(2,1)S(1)} %copy-done.116), channel_id=1, source_target_pairs={{12,0},{0,4},{4,8},{8,12},{28,16},{16,20},{20,24},{24,28},{44,32},... | collective-permute-start | bytes 663560 | tf_op jit(solution)/shard_map/ppermute | solution.py:41
  455.1 9.0 %collective-permute-start.65 = (bf16[144,768]{1,0:T(8,128)(2,1)S(1)}, bf16[144,768]{1,0:T(8,128)(2,1)S(1)}, u32[]{:S(2)}, u32[]{:S(2)}) collective-permute-start(bf16[144,768]{1,0:T(8,128)(2,1)S(1)} %maximum_maximum_fusion.3), channel_id=1, source_target_pairs={{16,0},{20,4},{24,8},{28,12},{32,16},{36,20},{40,24},{44,28},{48,3... | collective-permute-start | bytes 663560 | tf_op jit(solution)/shard_map/ppermute | solution.py:41
  457.6 14.1 %collective-permute-start.64 = (bf16[144,768]{1,0:T(8,128)(2,1)S(1)}, bf16[144,768]{1,0:T(8,128)(2,1)S(1)}, u32[]{:S(2)}, u32[]{:S(2)}) collective-permute-start(bf16[144,768]{1,0:T(8,128)(2,1)S(1)} %maximum_maximum_fusion.3), channel_id=1, source_target_pairs={{32,0},{36,4},{40,8},{44,12},{48,16},{52,20},{56,24},{60,28},{33,1... | collective-permute-start | bytes 663560 | tf_op jit(solution)/shard_map/ppermute | solution.py:41
  461.6 12.0 %collective-permute-start.63 = (bf16[144,768]{1,0:T(8,128)(2,1)S(1)}, bf16[144,768]{1,0:T(8,128)(2,1)S(1)}, u32[]{:S(2)}, u32[]{:S(2)}) collective-permute-start(bf16[144,768]{1,0:T(8,128)(2,1)S(1)} %maximum_maximum_fusion.3), channel_id=1, source_target_pairs={{48,0},{52,4},{56,8},{60,12},{49,1},{53,5},{57,9},{61,13},{50,2},{... | collective-permute-start | bytes 663560 | tf_op jit(solution)/shard_map/ppermute | solution.py:41
  509.3 44.8 %all-to-all-start.2 = ((bf16[16,96,640]{2,1,0:T(8,128)(2,1)}), bf16[16,96,640]{2,1,0:T(8,128)(2,1)}, u32[]{:S(2)}, u32[]{:S(2)}) async-start(bf16[16,96,640]{2,1,0:T(8,128)(2,1)} %bitcast.238), calls=%async_computation.2 | async-start | bytes 3932160 | tf_op jit(solution)/shard_map/all_to_all | solution.py:1158
  528.6 10.0 %collective-permute-start.68 = (bf16[128,1536]{1,0:T(8,128)(2,1)}, bf16[128,1536]{1,0:T(8,128)(2,1)S(1)}, u32[]{:S(2)}, u32[]{:S(2)}) collective-permute-start(bf16[128,1536]{1,0:T(8,128)(2,1)} %get-tuple-element.245), channel_id=1, source_target_pairs={{0,1},{1,2},{2,3},{3,0},{4,5},{5,6},{6,7},{7,4},{8,9},{9,10},{10,1... | collective-permute-start | bytes 1179656 | tf_op jit(solution)/shard_map/ppermute | solution.py:29
  528.6 11.6 %collective-permute-start.69 = (bf16[128,1536]{1,0:T(8,128)(2,1)}, bf16[128,1536]{1,0:T(8,128)(2,1)S(1)}, u32[]{:S(2)}, u32[]{:S(2)}) collective-permute-start(bf16[128,1536]{1,0:T(8,128)(2,1)} %get-tuple-element.246), channel_id=1, source_target_pairs={{0,2},{1,3},{2,0},{3,1},{4,6},{5,7},{6,4},{7,5},{8,10},{9,11},{10,... | collective-permute-start | bytes 1179656 | tf_op jit(solution)/shard_map/ppermute | solution.py:29
  528.7 21.2 %collective-permute-start.70 = (bf16[128,1536]{1,0:T(8,128)(2,1)}, bf16[128,1536]{1,0:T(8,128)(2,1)S(1)}, u32[]{:S(2)}, u32[]{:S(2)}) collective-permute-start(bf16[128,1536]{1,0:T(8,128)(2,1)} %get-tuple-element.247), channel_id=1, source_target_pairs={{0,3},{1,0},{2,1},{3,2},{4,7},{5,4},{6,5},{7,6},{8,11},{9,8},{10,9... | collective-permute-start | bytes 1179656 | tf_op jit(solution)/shard_map/ppermute | solution.py:29
  530.2 22.8 %collective-permute-start.52 = (bf16[128,1536]{1,0:T(8,128)(2,1)S(1)}, bf16[128,1536]{1,0:T(8,128)(2,1)S(1)}, u32[]{:S(2)}, u32[]{:S(2)}) collective-permute-start(bf16[128,1536]{1,0:T(8,128)(2,1)S(1)} %broadcast_select_fusion.1), channel_id=1, source_target_pairs={{0,64},{64,0},{1,65},{65,1},{2,66},{66,2},{3,67},{67,3},{4,68},{68... | collective-permute-start | bytes 1179656 | tf_op jit(solution)/shard_map/ppermute | solution.py:45
  557.9 20.3 %collective-permute-start.77 = (bf16[24,1536]{1,0:T(8,128)(2,1)S(1)}, bf16[24,1536]{1,0:T(8,128)(2,1)S(1)}, u32[]{:S(2)}, u32[]{:S(2)}) collective-permute-start(bf16[24,1536]{1,0:T(8,128)(2,1)S(1)} %bitcast.265), channel_id=1, source_target_pairs={{0,0},{1,16},{2,32},{3,48},{4,64},{5,80},{6,96},{7,112},{8,1},{9,1... | collective-permute-start | bytes 221192 | tf_op jit(solution)/shard_map/ppermute | solution.py:1262
  560.4 17.8 %collective-permute-start.78 = (bf16[24,1536]{1,0:T(8,128)(2,1)S(1)}, bf16[24,1536]{1,0:T(8,128)(2,1)S(1)}, u32[]{:S(2)}, u32[]{:S(2)}) collective-permute-start(bf16[24,1536]{1,0:T(8,128)(2,1)S(1)} %bitcast.266), channel_id=1, source_target_pairs={{0,64},{1,80},{2,96},{3,112},{4,0},{5,16},{6,32},{7,48},{8,65},{9,... | collective-permute-start | bytes 221192 | tf_op jit(solution)/shard_map/ppermute | solution.py:1263
  564.8 15.3 %collective-permute-start.73 = (bf16[24,2048]{1,0:T(8,128)(2,1)S(1)}, bf16[24,2048]{1,0:T(8,128)(2,1)S(1)}, u32[]{:S(2)}, u32[]{:S(2)}) collective-permute-start(bf16[24,2048]{1,0:T(8,128)(2,1)S(1)} %get-tuple-element.331), channel_id=1, source_target_pairs={{0,3},{1,0},{2,1},{3,2},{4,7},{5,4},{6,5},{7,6},{8,11},{9,8},{10,9... | collective-permute-start | bytes 294920 | tf_op jit(solution)/shard_map/ppermute | solution.py:29
  564.9 15.2 %collective-permute-start.74 = (bf16[24,2048]{1,0:T(8,128)(2,1)S(1)}, bf16[24,2048]{1,0:T(8,128)(2,1)S(1)}, u32[]{:S(2)}, u32[]{:S(2)}) collective-permute-start(bf16[24,2048]{1,0:T(8,128)(2,1)S(1)} %get-tuple-element.330), channel_id=1, source_target_pairs={{0,2},{1,3},{2,0},{3,1},{4,6},{5,7},{6,4},{7,5},{8,10},{9,11},{10,... | collective-permute-start | bytes 294920 | tf_op jit(solution)/shard_map/ppermute | solution.py:29
  569.1 11.1 %collective-permute-start.75 = (bf16[24,2048]{1,0:T(8,128)(2,1)S(1)}, bf16[24,2048]{1,0:T(8,128)(2,1)S(1)}, u32[]{:S(2)}, u32[]{:S(2)}) collective-permute-start(bf16[24,2048]{1,0:T(8,128)(2,1)S(1)} %get-tuple-element.328), channel_id=1, source_target_pairs={{0,1},{1,2},{2,3},{3,0},{4,5},{5,6},{6,7},{7,4},{8,9},{9,10},{10,1... | collective-permute-start | bytes 294920 | tf_op jit(solution)/shard_map/ppermute | solution.py:29
  (157 other events, 1802.0 us)
Sparse Core Ops, SparseCore 0:
  20.1 49.4 all-gather.3
  72.2 53.6 all-gather.5
  128.0 47.0 all-gather.7
  450.7 91.9 reduce-scatter.1

commit v4 on v3

--- a/solution.py
+++ b/solution.py
@@ -1118,9 +1118,11 @@
     )
     leaving = carried(packed, 1)
     normed = kept["normed"]
-    early, leaving = after_gate(
-        early_grads(normed, grad_gate, normed_out, gathered), packed, leaving
-    )
+    early_operands = (normed, grad_gate, normed_out, gathered)
+    if inner_first:
+        early, leaving = after_gate(early_grads(*early_operands), packed, leaving)
+    else:
+        _, leaving = after_gate(None, packed, leaving)
     use_own, use_other, tail, rim_grad, slot = scan_back(
         place, kept["conv_in"], kept["pre"], kept["step"], kept["run"], grad_scan, grad_gate,
         kept["mixed"], kept["starts"], kept["last"], kept["entering"], leaving, kept["rim"],
@@ -1137,8 +1139,11 @@
         sent = project_back(use_own, use_other, own, other, inner_first)
     else:
         sent = project_back(use_own, use_other, own, other, inner_first)
+    parts = before_receive(scatter_head(sent))
+    if not inner_first:
+        early = early_grads(*tied(early_operands, slot))
     grad_feed, scale_below = receive_back(
-        before_receive(scatter_head(sent)), kept["feed"], incoming, weights["gain_in"], below["branch"],
+        parts, kept["feed"], incoming, weights["gain_in"], below["branch"],
         below["scale"],
     )
     if not inner_first:
@@ -1199,11 +1204,15 @@
 
     def out_second(packed, entering):
         mine, theirs = [a[HALF:] for a in later["out"]]
-        later["product"] = out_back(tied(later["grad_all"], packed), mine, theirs)
         return [entering, mine, theirs, later["product"]]
 
     _, sent, kept0 = layer_forward(core, head, tokens, feed_all, weights[0], out_first, True)
-    branch, hidden, scale = receive(scatter_head(sent), tokens, tokens)
+    parts = scatter_head(sent)
+    later["product"] = out_back(
+        tied(later["grad_all"], sent[0]), later["out"][0][HALF:], later["out"][1][HALF:]
+    )
+    parts, later["product"] = lax.optimization_barrier((parts, later["product"]))
+    branch, hidden, scale = receive(parts, tokens, tokens)
     kept0.update(branch=branch, scale=scale)
     feed_all = jnp.concatenate(gather_head(hidden), axis=0)
     own1 = tied(own1, hidden)
@@ -1214,10 +1223,8 @@
 
     def after_gate1(values, packed, leaving):
         _, result, _ = receive(scatter_head(tied(sent, packed)), hidden, hidden)
-        leaving, later["result"], values = lax.optimization_barrier(
-            (leaving, result, summed(*values))
-        )
-        return values, leaving
+        leaving, later["result"] = lax.optimization_barrier((leaving, result))
+        return None, leaving
 
     def before_receive1(sent):
         return sent
@@ -1227,14 +1234,16 @@
         after_gate1, before_receive1, False,
     )
     chunks = gather_head(jnp.concatenate([grad_hidden, scale], axis=1))
-    later["early"] = scatter_seq_now(tied(early1, grad_hidden))
-    chunks, grad_x1, later["early"] = lax.optimization_barrier((chunks, grad_x1, later["early"]))
+    pieces1 = [(own, swap(other)) for own, other in (grad_x1, early1)]
+    chunks, pieces1 = lax.optimization_barrier((chunks, pieces1))
     grad_all = jnp.concatenate([a[:, :D] for a in chunks], axis=0)
     scale = jnp.concatenate([a[:, D:] for a in chunks], axis=0)
 
     def after_gate0(values, packed, leaving):
-        values = [jnp.concatenate([grad_x1[i], values[i]], axis=1) for i in range(2)]
-        later["sum"] = summed(*values)
+        both = [pieces1[0], (values[0], swap(values[1])), pieces1[1]]
+        later["sum"] = jnp.concatenate(
+            [(own.astype(f32) + got.astype(f32)).astype(bf16) for own, got in both], axis=1
+        )
         return scatter_seq(later["sum"]), leaving
 
     def before_receive0(sent):
@@ -1245,7 +1254,7 @@
         core, head, grad_hidden, grad_all, product, scale, kept0, kept0, weights[0], after_gate0,
         before_receive0, True,
     )
-    early1 = later["early"]
+    early0, early1 = early0[:, : edge + GROUP], early0[:, edge + GROUP :]
     x0 = scatter_seq_now(grad_x0)
     result = later["result"]
     got = swap(pick(core, result, hidden))
@@ -1253,10 +1262,16 @@
     got = swap(pick(core, grad_hidden, grad_feed))
     grad_in = jnp.stack([pick(core, grad_feed, got), pick(core, got, grad_hidden)])
 
+    both = jnp.concatenate(
+        [x0, early0[:, edge:WIDE], early0[:, :edge], early1[:, :HALF]], axis=1
+    ).reshape(4, 24, 2 * WIDE)
+    both = exchange_head(both, head)
+
     def out_rows(a):
         return a.reshape(4, 24, HALF).transpose(1, 0, 2).reshape(24, D)
 
     out0, out1 = out_rows(early0[:, WIDE:]), out_rows(early1[:, HALF:])
+    out0, out1 = tied((out0, out1), both)
     even = lax.rem(lax.axis_index("seq"), 2)
     rows_out = [
         lax.ppermute(pick(even, out0, out1), EVERY, out_back_pairs(0)),
@@ -1265,10 +1280,6 @@
     grad_out = jnp.concatenate(
         [pick(core, rows_out[0], rows_out[1]), pick(core, rows_out[1], rows_out[0])], axis=0
     ).astype(f32)
-    both = jnp.concatenate(
-        [x0, early0[:, edge:WIDE], early0[:, :edge], early1[:, :HALF]], axis=1
-    ).reshape(4, 24, 2 * WIDE)
-    both = exchange_head(both, head)
     first, second = both[:, :, :WIDE], both[:, :, WIDE:]
     mine = pick(core, first, second)
     theirs = swap(pick(core, second, first))

time: 606 us -> 596 us (0.983)
  waiting for transfers between devices: 250 us -> 239 us
  starting transfers between devices: 128 us -> 137 us
  other arithmetic: 41.2 us -> 32.9 us
    ppermute x36, starting transfers between devices: 31.7 us -> 44.1 us  [from_head(): return lax.ppermute(a, 'head', [(i, (i - k) % 4) for i in range(4)])]
    ppermute x36, waiting for transfers between devices: 98.4 us -> 86.9 us  [from_head(): return lax.ppermute(a, 'head', [(i, (i - k) % 4) for i in range(4)])]
    all_to_all x2 -> x1, waiting for transfers between devices: 21.3 us -> 12.4 us  [scatter_seq_now(): got = lax.all_to_all(a, 'seq', 0, 0, tiled=True).astype(f32)]
    ppermute x24, starting transfers between devices: 31.9 us -> 40.6 us  [from_seq(): return lax.ppermute(a, 'seq', pairs)]
    ppermute x24, waiting for transfers between devices: 70.1 us -> 77.7 us  [from_seq(): return lax.ppermute(a, 'seq', pairs)]
    all_to_all x2 -> x1, starting transfers between devices: 15.7 us -> 8.42 us  [scatter_seq_now(): got = lax.all_to_all(a, 'seq', 0, 0, tiled=True).astype(f32)]
    unnamed x304 -> x280, local copies, waits for them, and re-layouts: 16.3 us -> 23 us
    convert_element_type x3 -> x1, other arithmetic: 10.4 us -> 3.99 us  [summed(): return (own.astype(f32) + swap(other).astype(f32)).astype(bf16)]
  transfers between devices with their start and end apart: 86 -> 86, of which waited for: 53 -> 50; matrix products, arithmetic and copies ran while one was open for 6% -> 5% of each run, Pallas kernels for 10% -> 11%
where the time goes in v4:
time: 596 us; the launch traced here: 585 us
  waiting for transfers between devices  239 us (40%)
  starting transfers between devices  137 us (23%)
  Pallas kernels  119 us (20%)
  local copies, waits for them, and re-layouts  40.4 us (7%)
  other arithmetic  32.9 us (6%)
  between operations  16.7 us (3%)
    ppermute x36, waiting for transfers between devices, from_head(): return lax.ppermute(a, 'head', [(i, (i - k) % 4) for i in range(4)])  86.9 us
    ppermute x24, waiting for transfers between devices, from_seq(): return lax.ppermute(a, 'seq', pairs)  77.7 us
    ppermute x36, starting transfers between devices, from_head(): return lax.ppermute(a, 'head', [(i, (i - k) % 4) for i in range(4)])  44.1 us
    ppermute x24, starting transfers between devices, from_seq(): return lax.ppermute(a, 'seq', pairs)  40.6 us
    pallas_call x2, Pallas kernels, scan_back(): pl.pallas_call(scan_back_kernel, grid_spec=pltpu.PrefetchScalarGridSpec(n...  27.6 us
    unnamed x280, local copies, waits for them, and re-layouts  23 us
    all_gather x3, waiting for transfers between devices, gather_seq(): return lax.all_gather(a, 'seq', axis=0, tiled=True)  17.5 us
    ppermute x13, starting transfers between devices, swap(): return lax.ppermute(a, 'section', [(0, 1), (1, 0)])  15.3 us
  transfers between devices with their start and end apart: 86, of which 50 were waited for; matrix products, arithmetic and copies ran while one was open for 5% of the time, Pallas kernels for 11%

profile of v4, /device:TPU:103, one launch (start us, length us, event | category | flops | bytes accessed | tf_op | source)
XLA Modules:
  0.0 585.0 jit_solution(12915053533424086414)
XLA Ops:
  20.0 5.9 %collective-permute-start.9 = (bf16[48,1536]{1,0:T(8,128)(2,1)}, bf16[48,1536]{1,0:T(8,128)(2,1)}, u32[]{:S(2)}, u32[]{:S(2)}) collective-permute-start(bf16[48,1536]{1,0:T(8,128)(2,1)} %bitcast.44), channel_id=1, source_target_pairs={{0,0},{1,4},{2,8},{3,12},{4,16},{5,20},{6,24},{7,28},{8,64},{9,68}... | collective-permute-start | bytes 442376 | tf_op jit(solution)/shard_map/ppermute | solution.py:1179
  32.8 9.1 %all-to-all-start = ((f32[64,8,128]{2,1,0:T(8,128)}), f32[64,8,128]{2,1,0:T(8,128)S(1)}, u32[]{:S(2)}, u32[]{:S(2)}) async-start(f32[64,8,128]{2,1,0:T(8,128)} %broadcast_in_dim.147), calls=%async_computation | async-start | bytes 524288 | tf_op jit(solution)/shard_map/all_to_all | solution.py:1049
  42.3 10.7 %all-to-all-done = f32[64,8,128]{2,1,0:T(8,128)S(1)} async-done(((f32[64,8,128]{2,1,0:T(8,128)}), f32[64,8,128]{2,1,0:T(8,128)S(1)}, u32[]{:S(2)}, u32[]{:S(2)}) %all-to-all-start) | async-done | bytes 262176 | tf_op jit(solution)/shard_map/all_to_all | solution.py:1049
  56.6 13.6 %all-gather.4.cloned.1.call-done.own = bf16[1536,1024]{1,0:T(8,128)(2,1)} async-done(((bf16[96,1024]{1,0:T(8,128)(2,1)}), bf16[1536,1024]{1,0:T(8,128)(2,1)}) %all-gather.4.cloned.1.call-update) | async-done | bytes 3145744 | tf_op jit(solution)/shard_map/all_gather | solution.py:1040
  81.1 7.7 %project.2 = (bf16[512,1536]{1,0:T(8,128)(2,1)}, bf16[512,1024]{1,0:T(8,128)(2,1)S(1)}, f32[512,128]{1,0:T(8,128)S(1)}, bf16[512,768]{1,0:T(8,128)(2,1)}) custom-call(s32[1]{0:T(128)} %bitcast.1.core, bf16[512,1536]{1,0:T(8,128)(2,1)S(1)} %pad_maximum_fusion.1.feed, f32[8,1536]{1,0:T(8,128)S(1)} %broadcast_in_dim.151.gain, ...), custom_call_target="tpu_custom_call" | custom-call | flops 3200000000 | bytes 12000000 | tf_op jit(solution)/shard_map/project/pallas_call | solution.py:332
  91.1 4.5 collective-permute-done.11.rim
  95.6 7.4 %scan_local.2 = (f32[512,1024]{1,0:T(8,128)}, f32[512,768]{1,0:T(8,128)S(1)}, bf16[512,128]{1,0:T(8,128)(2,1)S(1)}, f32[512,128]{1,0:T(8,128)S(1)}, bf16[4,128,7...) custom-call(s32[2]{0:T(128)S(1)} %pad_add_fusion.place, ...), custom_call_target="tpu_custom_call" | custom-call | flops 1000000000 | bytes 8000000 | tf_op jit(solution)/shard_map/scan_local/pallas_call | solution.py:257
  106.4 2.8 collective-permute-start.19
  109.3 5.2 collective-permute-done.12
  116.4 5.3 collective-permute-done.14
  122.4 3.8 all-gather.6.cloned.1.call-done
  134.9 3.7 collective-permute-done.17
  138.6 2.8 collective-permute-done.16
  141.4 7.2 %collective-permute-done.15 = bf16[144,768]{1,0:T(8,128)(2,1)S(1)} collective-permute-done((bf16[144,768]{1,0:T(8,128)(2,1)S(1)}, bf16[144,768]{1,0:T(8,128)(2,1)S(1)}, u32[]{:S(2)}, u32[]{:S(2)}) %collective-permute-start.15) | collective-permute-done | bytes 221216 | tf_op jit(solution)/shard_map/ppermute | solution.py:41
  151.2 5.7 gate_out.2
  161.1 7.1 %collective-permute-done.22.one = bf16[128,1664]{1,0:T(8,128)(2,1)S(1)} collective-permute-done((bf16[128,1664]{1,0:T(8,128)(2,1)}, bf16[128,1664]{1,0:T(8,128)(2,1)S(1)}, u32[]{:S(2)}, u32[]{:S(2)}) %collective-permute-start.22) | collective-permute-done | bytes 426016 | tf_op jit(solution)/shard_map/ppermute | solution.py:29
  169.6 10.2 %collective-permute-done.24.three = bf16[128,1664]{1,0:T(8,128)(2,1)S(1)} collective-permute-done((bf16[128,1664]{1,0:T(8,128)(2,1)}, bf16[128,1664]{1,0:T(8,128)(2,1)S(1)}, u32[]{:S(2)}, u32[]{:S(2)}) %collective-permute-start.24) | collective-permute-done | bytes 426016 | tf_op jit(solution)/shard_map/ppermute | solution.py:29
  186.1 16.4 %collective-permute-done.25 = bf16[128,1536]{1,0:T(8,128)(2,1)S(1)} collective-permute-done((bf16[128,1536]{1,0:T(8,128)(2,1)S(1)}, bf16[128,1536]{1,0:T(8,128)(2,1)S(1)}, u32[]{:S(2)}, u32[]{:S(2)}) %collective-permute-start.25) | collective-permute-done | bytes 393248 | tf_op jit(solution)/shard_map/ppermute | solution.py:29
  204.9 4.9 project.3
  209.8 2.9 collective-permute-start.32
  212.7 3.7 collective-permute-done.32.rim
  216.4 7.1 %scan_local.3 = (f32[512,1024]{1,0:T(8,128)S(1)}, f32[512,768]{1,0:T(8,128)S(1)}, bf16[512,128]{1,0:T(8,128)(2,1)S(1)}, f32[512,128]{1,0:T(8,128)S(1)}, bf16[4,1...) custom-call(s32[2]{0:T(128)S(1)} %pad_add_fusion.place, ...), custom_call_target="tpu_custom_call" | custom-call | flops 1000000000 | bytes 8000000 | tf_op jit(solution)/shard_map/scan_local/pallas_call | solution.py:257
  227.3 3.5 collective-permute-done.33
  232.9 6.3 %collective-permute-done.35 = bf16[144,768]{1,0:T(8,128)(2,1)S(1)} collective-permute-done((bf16[144,768]{1,0:T(8,128)(2,1)}, bf16[144,768]{1,0:T(8,128)(2,1)S(1)}, u32[]{:S(2)}, u32[]{:S(2)}) %collective-permute-start.35) | collective-permute-done | bytes 221216 | tf_op jit(solution)/shard_map/ppermute | solution.py:41
  246.0 3.6 collective-permute-done.38
  249.6 2.8 collective-permute-done.37
  252.4 6.4 %collective-permute-done.36 = bf16[144,768]{1,0:T(8,128)(2,1)S(1)} collective-permute-done((bf16[144,768]{1,0:T(8,128)(2,1)S(1)}, bf16[144,768]{1,0:T(8,128)(2,1)S(1)}, u32[]{:S(2)}, u32[]{:S(2)}) %collective-permute-start.36) | collective-permute-done | bytes 221216 | tf_op jit(solution)/shard_map/ppermute | solution.py:41
  259.2 5.7 gate_out.3
  270.2 3.0 collective-permute-done.41.four
  277.6 4.9 gate_back.2
  289.6 7.9 %collective-permute-done.42 = bf16[144,768]{1,0:T(8,128)(2,1)S(1)} collective-permute-done((bf16[144,768]{1,0:T(8,128)(2,1)}, bf16[144,768]{1,0:T(8,128)(2,1)S(1)}, u32[]{:S(2)}, u32[]{:S(2)}) %collective-permute-start.42) | collective-permute-done | bytes 221216 | tf_op jit(solution)/shard_map/ppermute | solution.py:41
  302.5 3.0 collective-permute-start.46
  306.9 3.9 collective-permute-done.50.three
  318.9 12.7 %scan_back.2 = (bf16[512,1024]{1,0:T(8,128)(2,1)S(1)}, bf16[512,1024]{1,0:T(8,128)(2,1)S(1)}, f32[8,2048]{1,0:T(8,128)S(1)}, f32[8,2048]{1,0:T(8,128)S(1)}, f32[1536,128]{1,0:T(8,128)S(1)}) custom-call(s32[2]{0:T(128)S(1)} %pad_add_fusion.place, bf16[512,1024]{1,0:T(8,128)(2,1)S(1)} %copy-done.35, f32[512,1024]{1,0:T(8,128)S(1)} %copy-done.30, ...), custom_call_target="tpu_custom_call" | custom-call | flops 2000000000 | bytes 9000000 | tf_op jit(solution)/shard_map/scan_back/pallas_call | solution.py:752
  333.6 3.3 collective-permute-done.52
  336.9 5.3 project_back.2
  344.3 5.2 early_grads.2
  349.6 3.2 collective-permute-start.60
  352.8 10.6 %collective-permute-done.55.three = bf16[128,1536]{1,0:T(8,128)(2,1)S(1)} collective-permute-done((bf16[128,1536]{1,0:T(8,128)(2,1)}, bf16[128,1536]{1,0:T(8,128)(2,1)S(1)}, u32[]{:S(2)}, u32[]{:S(2)}) %collective-permute-start.55) | collective-permute-done | bytes 393248 | tf_op jit(solution)/shard_map/ppermute | solution.py:29
  364.1 5.0 inner_grads.2
  373.2 18.4 %collective-permute-done.56 = bf16[128,1664]{1,0:T(8,128)(2,1)S(1)} collective-permute-done((bf16[128,1664]{1,0:T(8,128)(2,1)S(1)}, bf16[128,1664]{1,0:T(8,128)(2,1)S(1)}, u32[]{:S(2)}, u32[]{:S(2)}) %collective-permute-start.56) | collective-permute-done | bytes 426016 | tf_op jit(solution)/shard_map/ppermute | solution.py:29
  395.2 3.5 gate_back.3
  398.6 5.2 early_grads.3
  406.2 3.2 collective-permute-done.72
  410.0 3.1 pad_maximum_fusion
  421.9 5.6 collective-permute-done.62
  428.0 5.0 collective-permute-start.66
  432.9 9.5 %collective-permute-start.65 = (bf16[144,768]{1,0:T(8,128)(2,1)S(1)}, bf16[144,768]{1,0:T(8,128)(2,1)S(1)}, u32[]{:S(2)}, u32[]{:S(2)}) collective-permute-start(bf16[144,768]{1,0:T(8,128)(2,1)S(1)} %maximum_maximum_fusion.3), channel_id=1, source_target_pairs={{32,0},{36,4},{40,8},{44,12},{48,16},{52,20},{56,24},{60,28},{33,1... | collective-permute-start | bytes 663560 | tf_op jit(solution)/shard_map/ppermute | solution.py:41
  443.8 7.4 %collective-permute-done.65 = bf16[144,768]{1,0:T(8,128)(2,1)S(1)} collective-permute-done((bf16[144,768]{1,0:T(8,128)(2,1)S(1)}, bf16[144,768]{1,0:T(8,128)(2,1)S(1)}, u32[]{:S(2)}, u32[]{:S(2)}) %collective-permute-start.65) | collective-permute-done | bytes 221216 | tf_op jit(solution)/shard_map/ppermute | solution.py:41
  451.2 5.0 collective-permute-done.64
  456.6 14.8 %scan_back.3 = (bf16[512,1024]{1,0:T(8,128)(2,1)S(1)}, bf16[512,1024]{1,0:T(8,128)(2,1)S(1)}, f32[8,2048]{1,0:T(8,128)S(1)}, f32[8,2048]{1,0:T(8,128)S(1)}, f32[1536,128]{1,0:T(8,128)S(1)}) custom-call(s32[2]{0:T(128)S(1)} %pad_add_fusion.place, bf16[512,1024]{1,0:T(8,128)(2,1)} %copy-done.33, f32[512,1024]{1,0:T(8,128)} %get-tuple-element.209.pre_in, ...), custom_call_target="tpu_custom_call" | custom-call | flops 2000000000 | bytes 9000000 | tf_op jit(solution)/shard_map/scan_back/pallas_call | solution.py:752
  473.7 3.8 collective-permute-done.67
  477.5 5.0 inner_grads.3
  484.9 3.9 collective-permute-done.68
  488.9 4.0 add_convert_fusion.3
  492.9 7.6 %project_back.3 = (f32[128,1536]{1,0:T(8,128)}, bf16[128,1536]{1,0:T(8,128)(2,1)}, bf16[128,1536]{1,0:T(8,128)(2,1)}, bf16[128,1536]{1,0:T(8,128)(2,1)}) custom-call(bf16[512,1024]{1,0:T(8,128)(2,1)S(1)} %get-tuple-element.259.use_own, bf16[512,1024]{1,0:T(8,128)(2,1)S(1)} %copy-done.87, bf16[1536,1024]{1,0:T(8,128)(2,1)} %all-gather.4.cloned.1.call-done.own, ...), custom_call_target="tpu_custom_call" | custom-call | flops 3200000000 | bytes 9000000 | tf_op jit(solution)/shard_map/project_back/pallas_call | solution.py:825
  500.5 3.8 collective-permute-start.69
  506.7 8.4 %all-to-all-start.1 = ((bf16[16,96,640]{2,1,0:T(8,128)(2,1)}), bf16[16,96,640]{2,1,0:T(8,128)(2,1)}, u32[]{:S(2)}, u32[]{:S(2)}) async-start(bf16[16,96,640]{2,1,0:T(8,128)(2,1)} %bitcast.236), calls=%async_computation.1 | async-start | bytes 3932160 | tf_op jit(solution)/shard_map/all_to_all | solution.py:1163
  515.1 6.1 %collective-permute-done.69.one = bf16[128,1536]{1,0:T(8,128)(2,1)S(1)} collective-permute-done((bf16[128,1536]{1,0:T(8,128)(2,1)}, bf16[128,1536]{1,0:T(8,128)(2,1)S(1)}, u32[]{:S(2)}, u32[]{:S(2)}) %collective-permute-start.69) | collective-permute-done | bytes 393248 | tf_op jit(solution)/shard_map/ppermute | solution.py:29
  521.2 4.0 collective-permute-done.71.three
  533.0 12.4 %all-to-all-done.1 = bf16[16,96,640]{2,1,0:T(8,128)(2,1)} async-done(((bf16[16,96,640]{2,1,0:T(8,128)(2,1)}), bf16[16,96,640]{2,1,0:T(8,128)(2,1)}, u32[]{:S(2)}, u32[]{:S(2)}) %all-to-all-start.1) | async-done | bytes 1966112 | tf_op jit(solution)/shard_map/all_to_all | solution.py:1163
  548.4 3.9 collective-permute-start.78
  555.6 3.0 collective-permute-start.75
  558.6 9.4 %collective-permute-done.78 = bf16[24,1536]{1,0:T(8,128)(2,1)S(1)} collective-permute-done((bf16[24,1536]{1,0:T(8,128)(2,1)S(1)}, bf16[24,1536]{1,0:T(8,128)(2,1)S(1)}, u32[]{:S(2)}, u32[]{:S(2)}) %collective-permute-start.78) | collective-permute-done | bytes 73760 | tf_op jit(solution)/shard_map/ppermute | solution.py:1277
  (621 shorter events, 168.3 us)
Async XLA Ops:
  7.2 63.0 %all-gather.4.cloned.1.call-start = ((), (), s32[]{:S(2)}) async-start(), calls=%async_computation.3 | async-start | bytes 3342336 | tf_op jit(solution)/shard_map/all_gather | solution.py:1040
  20.0 36.6 %collective-permute-start.9 = (bf16[48,1536]{1,0:T(8,128)(2,1)}, bf16[48,1536]{1,0:T(8,128)(2,1)}, u32[]{:S(2)}, u32[]{:S(2)}) collective-permute-start(bf16[48,1536]{1,0:T(8,128)(2,1)} %bitcast.44), channel_id=1, source_target_pairs={{0,0},{1,4},{2,8},{3,12},{4,16},{5,20},{6,24},{7,28},{8,64},{9,68}... | collective-permute-start | bytes 442376 | tf_op jit(solution)/shard_map/ppermute | solution.py:1179
  26.3 29.1 %collective-permute-start.4 = (bf16[128,1536]{1,0:T(8,128)(2,1)S(1)}, bf16[128,1536]{1,0:T(8,128)(2,1)S(1)}, u32[]{:S(2)}, u32[]{:S(2)}) collective-permute-start(bf16[128,1536]{1,0:T(8,128)(2,1)S(1)} %dynamic-slice_bitcast_fusion.1.feed.target), channel_id=1, source_target_pairs={{0,3},{1,0},{2,1},{3,2},{4,7},{5,4},{6,5},{7,6},{8,11},{9,8},{10,9... | collective-permute-start | bytes 1179656 | tf_op jit(solution)/shard_map/ppermute | solution.py:29
  27.7 27.7 %collective-permute-start.5 = (bf16[128,1536]{1,0:T(8,128)(2,1)S(1)}, bf16[128,1536]{1,0:T(8,128)(2,1)S(1)}, u32[]{:S(2)}, u32[]{:S(2)}) collective-permute-start(bf16[128,1536]{1,0:T(8,128)(2,1)S(1)} %dynamic-slice_bitcast_fusion.1.feed.target), channel_id=1, source_target_pairs={{0,2},{1,3},{2,0},{3,1},{4,6},{5,7},{6,4},{7,5},{8,10},{9,11},{10,... | collective-permute-start | bytes 1179656 | tf_op jit(solution)/shard_map/ppermute | solution.py:29
  27.7 27.7 %collective-permute-start.6 = (bf16[128,1536]{1,0:T(8,128)(2,1)S(1)}, bf16[128,1536]{1,0:T(8,128)(2,1)}, u32[]{:S(2)}, u32[]{:S(2)}) collective-permute-start(bf16[128,1536]{1,0:T(8,128)(2,1)S(1)} %dynamic-slice_bitcast_fusion.1.feed.target), channel_id=1, source_target_pairs={{0,1},{1,2},{2,3},{3,0},{4,5},{5,6},{6,7},{7,4},{8,9},{9,10},{10,1... | collective-permute-start | bytes 1179656 | tf_op jit(solution)/shard_map/ppermute | solution.py:29
  32.8 20.2 %all-to-all-start = ((f32[64,8,128]{2,1,0:T(8,128)}), f32[64,8,128]{2,1,0:T(8,128)S(1)}, u32[]{:S(2)}, u32[]{:S(2)}) async-start(f32[64,8,128]{2,1,0:T(8,128)} %broadcast_in_dim.147), calls=%async_computation | async-start | bytes 524288 | tf_op jit(solution)/shard_map/all_to_all | solution.py:1049
  41.9 84.3 %all-gather.6.cloned.1.call-start = ((), (), s32[]{:S(2)}) async-start(), calls=%async_computation.4 | async-start | bytes 2506752 | tf_op jit(solution)/shard_map/all_gather | solution.py:1040
  72.7 109.0 %all-gather.8.cloned.1.call-start = ((), (), s32[]{:S(2)}) async-start(), calls=%async_computation.5 | async-start | bytes 3342336 | tf_op jit(solution)/shard_map/all_gather | solution.py:1040
  72.7 8.3 %collective-permute-start.10 = (bf16[1536,1024]{1,0:T(8,128)(2,1)}, bf16[1536,1024]{1,0:T(8,128)(2,1)}, u32[]{:S(2)}, u32[]{:S(2)}) collective-permute-start(bf16[1536,1024]{1,0:T(8,128)(2,1)} %all-gather.4.cloned.1.call-done.own), channel_id=1, source_target_pairs={{0,64},{64,0},{1,65},{65,1},{2,66},{66,2},{3,67},{67,3},{4,68},{68... | collective-permute-start | bytes 9437192 | tf_op jit(solution)/shard_map/ppermute | solution.py:45
  81.1 466.2 %reduce-scatter.2.cloned.1.call-start = ((), (), s32[]{:S(2)}) async-start(), calls=%async_computation.6 | async-start | bytes 7102464 | tf_op jit(solution)/shard_map/reduce_scatter | solution.py:1159
  103.1 11.4 %collective-permute-start.12 = (bf16[144,768]{1,0:T(8,128)(2,1)}, bf16[144,768]{1,0:T(8,128)(2,1)S(1)}, u32[]{:S(2)}, u32[]{:S(2)}) collective-permute-start(bf16[144,768]{1,0:T(8,128)(2,1)} %get-tuple-element.160), channel_id=1, source_target_pairs={{4,0},{8,4},{12,8},{0,12},{20,16},{24,20},{28,24},{16,28},{36,32},... | collective-permute-start | bytes 663560 | tf_op jit(solution)/shard_map/ppermute | solution.py:41
  103.2 13.2 %collective-permute-start.13 = (bf16[144,768]{1,0:T(8,128)(2,1)}, bf16[144,768]{1,0:T(8,128)(2,1)S(1)}, u32[]{:S(2)}, u32[]{:S(2)}) collective-permute-start(bf16[144,768]{1,0:T(8,128)(2,1)} %get-tuple-element.160), channel_id=1, source_target_pairs={{8,0},{12,4},{0,8},{4,12},{24,16},{28,20},{16,24},{20,28},{40,32},... | collective-permute-start | bytes 663560 | tf_op jit(solution)/shard_map/ppermute | solution.py:41
  103.3 18.4 %collective-permute-start.14 = (bf16[144,768]{1,0:T(8,128)(2,1)}, bf16[144,768]{1,0:T(8,128)(2,1)S(1)}, u32[]{:S(2)}, u32[]{:S(2)}) collective-permute-start(bf16[144,768]{1,0:T(8,128)(2,1)} %get-tuple-element.160), channel_id=1, source_target_pairs={{12,0},{0,4},{4,8},{8,12},{28,16},{16,20},{20,24},{24,28},{44,32},... | collective-permute-start | bytes 663560 | tf_op jit(solution)/shard_map/ppermute | solution.py:41
  105.7 25.3 %collective-permute-start.18 = (bf16[128,1536]{1,0:T(8,128)(2,1)S(1)}, bf16[128,1536]{1,0:T(8,128)(2,1)}, u32[]{:S(2)}, u32[]{:S(2)}) collective-permute-start(bf16[128,1536]{1,0:T(8,128)(2,1)S(1)} %dynamic-slice_bitcast_fusion.grad_new), channel_id=1, source_target_pairs={{0,3},{1,0},{2,1},{3,2},{4,7},{5,4},{6,5},{7,6},{8,11},{9,8},{10,9... | collective-permute-start | bytes 1179656 | tf_op jit(solution)/shard_map/ppermute | solution.py:29
  106.4 25.8 %collective-permute-start.19 = (bf16[128,1536]{1,0:T(8,128)(2,1)S(1)}, bf16[128,1536]{1,0:T(8,128)(2,1)}, u32[]{:S(2)}, u32[]{:S(2)}) collective-permute-start(bf16[128,1536]{1,0:T(8,128)(2,1)S(1)} %dynamic-slice_bitcast_fusion.grad_new), channel_id=1, source_target_pairs={{0,2},{1,3},{2,0},{3,1},{4,6},{5,7},{6,4},{7,5},{8,10},{9,11},{10,... | collective-permute-start | bytes 1179656 | tf_op jit(solution)/shard_map/ppermute | solution.py:29
  114.5 19.0 %collective-permute-start.20 = (bf16[128,1536]{1,0:T(8,128)(2,1)S(1)}, bf16[128,1536]{1,0:T(8,128)(2,1)}, u32[]{:S(2)}, u32[]{:S(2)}) collective-permute-start(bf16[128,1536]{1,0:T(8,128)(2,1)S(1)} %dynamic-slice_bitcast_fusion.grad_new), channel_id=1, source_target_pairs={{0,1},{1,2},{2,3},{3,0},{4,5},{5,6},{6,7},{7,4},{8,9},{9,10},{10,1... | collective-permute-start | bytes 1179656 | tf_op jit(solution)/shard_map/ppermute | solution.py:29
  126.2 22.9 %collective-permute-start.21 = (bf16[768,1536]{1,0:T(8,128)(2,1)}, bf16[768,1536]{1,0:T(8,128)(2,1)S(1)}, u32[]{:S(2)}, u32[]{:S(2)}) collective-permute-start(bf16[768,1536]{1,0:T(8,128)(2,1)} %all-gather.6.cloned.1.call-done), channel_id=1, source_target_pairs={{0,64},{64,0},{1,65},{65,1},{2,66},{66,2},{3,67},{67,3},{4,68},{68... | collective-permute-start | bytes 7077896 | tf_op jit(solution)/shard_map/ppermute | solution.py:45
  129.5 9.1 %collective-permute-start.17 = (bf16[144,768]{1,0:T(8,128)(2,1)S(1)}, bf16[144,768]{1,0:T(8,128)(2,1)S(1)}, u32[]{:S(2)}, u32[]{:S(2)}) collective-permute-start(bf16[144,768]{1,0:T(8,128)(2,1)S(1)} %maximum_maximum_fusion), channel_id=1, source_target_pairs={{0,16},{4,20},{8,24},{12,28},{16,32},{20,36},{24,40},{28,44},{32,4... | collective-permute-start | bytes 663560 | tf_op jit(solution)/shard_map/ppermute | solution.py:41
  130.9 10.5 %collective-permute-start.16 = (bf16[144,768]{1,0:T(8,128)(2,1)S(1)}, bf16[144,768]{1,0:T(8,128)(2,1)S(1)}, u32[]{:S(2)}, u32[]{:S(2)}) collective-permute-start(bf16[144,768]{1,0:T(8,128)(2,1)S(1)} %maximum_maximum_fusion), channel_id=1, source_target_pairs={{0,32},{4,36},{8,40},{12,44},{16,48},{20,52},{24,56},{28,60},{1,33... | collective-permute-start | bytes 663560 | tf_op jit(solution)/shard_map/ppermute | solution.py:41
  132.3 16.3 %collective-permute-start.15 = (bf16[144,768]{1,0:T(8,128)(2,1)S(1)}, bf16[144,768]{1,0:T(8,128)(2,1)S(1)}, u32[]{:S(2)}, u32[]{:S(2)}) collective-permute-start(bf16[144,768]{1,0:T(8,128)(2,1)S(1)} %maximum_maximum_fusion), channel_id=1, source_target_pairs={{0,48},{4,52},{8,56},{12,60},{1,49},{5,53},{9,57},{13,61},{2,50},{... | collective-permute-start | bytes 663560 | tf_op jit(solution)/shard_map/ppermute | solution.py:41
  156.9 11.3 %collective-permute-start.22 = (bf16[128,1664]{1,0:T(8,128)(2,1)}, bf16[128,1664]{1,0:T(8,128)(2,1)S(1)}, u32[]{:S(2)}, u32[]{:S(2)}) collective-permute-start(bf16[128,1664]{1,0:T(8,128)(2,1)} %get-tuple-element.168), channel_id=1, source_target_pairs={{0,1},{1,2},{2,3},{3,0},{4,5},{5,6},{6,7},{7,4},{8,9},{9,10},{10,1... | collective-permute-start | bytes 1277960 | tf_op jit(solution)/shard_map/ppermute | solution.py:29
  157.2 12.4 %collective-permute-start.23 = (bf16[128,1664]{1,0:T(8,128)(2,1)}, bf16[128,1664]{1,0:T(8,128)(2,1)S(1)}, u32[]{:S(2)}, u32[]{:S(2)}) collective-permute-start(bf16[128,1664]{1,0:T(8,128)(2,1)} %get-tuple-element.169), channel_id=1, source_target_pairs={{0,2},{1,3},{2,0},{3,1},{4,6},{5,7},{6,4},{7,5},{8,10},{9,11},{10,... | collective-permute-start | bytes 1277960 | tf_op jit(solution)/shard_map/ppermute | solution.py:29
  159.3 20.5 %collective-permute-start.24 = (bf16[128,1664]{1,0:T(8,128)(2,1)}, bf16[128,1664]{1,0:T(8,128)(2,1)S(1)}, u32[]{:S(2)}, u32[]{:S(2)}) collective-permute-start(bf16[128,1664]{1,0:T(8,128)(2,1)} %get-tuple-element.170), channel_id=1, source_target_pairs={{0,3},{1,0},{2,1},{3,2},{4,7},{5,4},{6,5},{7,6},{8,11},{9,8},{10,9... | collective-permute-start | bytes 1277960 | tf_op jit(solution)/shard_map/ppermute | solution.py:29
  181.7 21.3 %collective-permute-start.31 = (bf16[1536,1024]{1,0:T(8,128)(2,1)}, bf16[1536,1024]{1,0:T(8,128)(2,1)S(1)}, u32[]{:S(2)}, u32[]{:S(2)}) collective-permute-start(bf16[1536,1024]{1,0:T(8,128)(2,1)} %all-gather.8.cloned.1.call-done.own), channel_id=1, source_target_pairs={{0,64},{64,0},{1,65},{65,1},{2,66},{66,2},{3,67},{67,3},{4,68},{68... | collective-permute-start | bytes 9437192 | tf_op jit(solution)/shard_map/ppermute | solution.py:45
  182.2 20.4 %collective-permute-start.25 = (bf16[128,1536]{1,0:T(8,128)(2,1)S(1)}, bf16[128,1536]{1,0:T(8,128)(2,1)S(1)}, u32[]{:S(2)}, u32[]{:S(2)}) collective-permute-start(bf16[128,1536]{1,0:T(8,128)(2,1)S(1)} %get-tuple-element.177.feed.target), channel_id=1, source_target_pairs={{0,3},{1,0},{2,1},{3,2},{4,7},{5,4},{6,5},{7,6},{8,11},{9,8},{10,9... | collective-permute-start | bytes 1179656 | tf_op jit(solution)/shard_map/ppermute | solution.py:29
  182.9 19.7 %collective-permute-start.26 = (bf16[128,1536]{1,0:T(8,128)(2,1)S(1)}, bf16[128,1536]{1,0:T(8,128)(2,1)S(1)}, u32[]{:S(2)}, u32[]{:S(2)}) collective-permute-start(bf16[128,1536]{1,0:T(8,128)(2,1)S(1)} %get-tuple-element.177.feed.target), channel_id=1, source_target_pairs={{0,2},{1,3},{2,0},{3,1},{4,6},{5,7},{6,4},{7,5},{8,10},{9,11},{10,... | collective-permute-start | bytes 1179656 | tf_op jit(solution)/shard_map/ppermute | solution.py:29
  184.0 18.8 %collective-permute-start.27 = (bf16[128,1536]{1,0:T(8,128)(2,1)S(1)}, bf16[128,1536]{1,0:T(8,128)(2,1)S(1)}, u32[]{:S(2)}, u32[]{:S(2)}) collective-permute-start(bf16[128,1536]{1,0:T(8,128)(2,1)S(1)} %get-tuple-element.177.feed.target), channel_id=1, source_target_pairs={{0,1},{1,2},{2,3},{3,0},{4,5},{5,6},{6,7},{7,4},{8,9},{9,10},{10,1... | collective-permute-start | bytes 1179656 | tf_op jit(solution)/shard_map/ppermute | solution.py:29
  226.4 12.8 %collective-permute-start.35 = (bf16[144,768]{1,0:T(8,128)(2,1)}, bf16[144,768]{1,0:T(8,128)(2,1)S(1)}, u32[]{:S(2)}, u32[]{:S(2)}) collective-permute-start(bf16[144,768]{1,0:T(8,128)(2,1)} %get-tuple-element.191), channel_id=1, source_target_pairs={{12,0},{0,4},{4,8},{8,12},{28,16},{16,20},{20,24},{24,28},{44,32},... | collective-permute-start | bytes 663560 | tf_op jit(solution)/shard_map/ppermute | solution.py:41
  242.1 7.5 %collective-permute-start.38 = (bf16[144,768]{1,0:T(8,128)(2,1)S(1)}, bf16[144,768]{1,0:T(8,128)(2,1)S(1)}, u32[]{:S(2)}, u32[]{:S(2)}) collective-permute-start(bf16[144,768]{1,0:T(8,128)(2,1)S(1)} %maximum_maximum_fusion.1), channel_id=1, source_target_pairs={{0,16},{4,20},{8,24},{12,28},{16,32},{20,36},{24,40},{28,44},{32,4... | collective-permute-start | bytes 663560 | tf_op jit(solution)/shard_map/ppermute | solution.py:41
  243.4 9.0 %collective-permute-start.37 = (bf16[144,768]{1,0:T(8,128)(2,1)S(1)}, bf16[144,768]{1,0:T(8,128)(2,1)S(1)}, u32[]{:S(2)}, u32[]{:S(2)}) collective-permute-start(bf16[144,768]{1,0:T(8,128)(2,1)S(1)} %maximum_maximum_fusion.1), channel_id=1, source_target_pairs={{0,32},{4,36},{8,40},{12,44},{16,48},{20,52},{24,56},{28,60},{1,33... | collective-permute-start | bytes 663560 | tf_op jit(solution)/shard_map/ppermute | solution.py:41
  244.7 14.1 %collective-permute-start.36 = (bf16[144,768]{1,0:T(8,128)(2,1)S(1)}, bf16[144,768]{1,0:T(8,128)(2,1)S(1)}, u32[]{:S(2)}, u32[]{:S(2)}) collective-permute-start(bf16[144,768]{1,0:T(8,128)(2,1)S(1)} %maximum_maximum_fusion.1), channel_id=1, source_target_pairs={{0,48},{4,52},{8,56},{12,60},{1,49},{5,53},{9,57},{13,61},{2,50},{... | collective-permute-start | bytes 663560 | tf_op jit(solution)/shard_map/ppermute | solution.py:41
  285.3 12.2 %collective-permute-start.42 = (bf16[144,768]{1,0:T(8,128)(2,1)}, bf16[144,768]{1,0:T(8,128)(2,1)S(1)}, u32[]{:S(2)}, u32[]{:S(2)}) collective-permute-start(bf16[144,768]{1,0:T(8,128)(2,1)} %get-tuple-element.198), channel_id=1, source_target_pairs={{12,0},{0,4},{4,8},{8,12},{28,16},{16,20},{20,24},{24,28},{44,32},... | collective-permute-start | bytes 663560 | tf_op jit(solution)/shard_map/ppermute | solution.py:41
  285.3 12.2 %collective-permute-start.43 = (bf16[144,768]{1,0:T(8,128)(2,1)}, bf16[144,768]{1,0:T(8,128)(2,1)S(1)}, u32[]{:S(2)}, u32[]{:S(2)}) collective-permute-start(bf16[144,768]{1,0:T(8,128)(2,1)} %get-tuple-element.198), channel_id=1, source_target_pairs={{8,0},{12,4},{0,8},{4,12},{24,16},{28,20},{16,24},{20,28},{40,32},... | collective-permute-start | bytes 663560 | tf_op jit(solution)/shard_map/ppermute | solution.py:41
  285.3 12.5 %collective-permute-start.44 = (bf16[144,768]{1,0:T(8,128)(2,1)}, bf16[144,768]{1,0:T(8,128)(2,1)S(1)}, u32[]{:S(2)}, u32[]{:S(2)}) collective-permute-start(bf16[144,768]{1,0:T(8,128)(2,1)} %get-tuple-element.198), channel_id=1, source_target_pairs={{4,0},{8,4},{12,8},{0,12},{20,16},{24,20},{28,24},{16,28},{36,32},... | collective-permute-start | bytes 663560 | tf_op jit(solution)/shard_map/ppermute | solution.py:41
  288.0 17.5 %collective-permute-start.48 = (bf16[128,1664]{1,0:T(8,128)(2,1)}, bf16[128,1664]{1,0:T(8,128)(2,1)S(1)}, u32[]{:S(2)}, u32[]{:S(2)}) collective-permute-start(bf16[128,1664]{1,0:T(8,128)(2,1)} %get-tuple-element.204), channel_id=1, source_target_pairs={{0,1},{1,2},{2,3},{3,0},{4,5},{5,6},{6,7},{7,4},{8,9},{9,10},{10,1... | collective-permute-start | bytes 1277960 | tf_op jit(solution)/shard_map/ppermute | solution.py:29
  289.3 17.6 %collective-permute-start.49 = (bf16[128,1664]{1,0:T(8,128)(2,1)}, bf16[128,1664]{1,0:T(8,128)(2,1)S(1)}, u32[]{:S(2)}, u32[]{:S(2)}) collective-permute-start(bf16[128,1664]{1,0:T(8,128)(2,1)} %get-tuple-element.205), channel_id=1, source_target_pairs={{0,2},{1,3},{2,0},{3,1},{4,6},{5,7},{6,4},{7,5},{8,10},{9,11},{10,... | collective-permute-start | bytes 1277960 | tf_op jit(solution)/shard_map/ppermute | solution.py:29
  297.5 13.4 %collective-permute-start.50 = (bf16[128,1664]{1,0:T(8,128)(2,1)}, bf16[128,1664]{1,0:T(8,128)(2,1)S(1)}, u32[]{:S(2)}, u32[]{:S(2)}) collective-permute-start(bf16[128,1664]{1,0:T(8,128)(2,1)} %get-tuple-element.206), channel_id=1, source_target_pairs={{0,3},{1,0},{2,1},{3,2},{4,7},{5,4},{6,5},{7,6},{8,11},{9,8},{10,9... | collective-permute-start | bytes 1277960 | tf_op jit(solution)/shard_map/ppermute | solution.py:29
  300.9 13.2 %collective-permute-start.47 = (bf16[144,768]{1,0:T(8,128)(2,1)S(1)}, bf16[144,768]{1,0:T(8,128)(2,1)S(1)}, u32[]{:S(2)}, u32[]{:S(2)}) collective-permute-start(bf16[144,768]{1,0:T(8,128)(2,1)S(1)} %maximum_maximum_fusion.2), channel_id=1, source_target_pairs={{16,0},{20,4},{24,8},{28,12},{32,16},{36,20},{40,24},{44,28},{48,3... | collective-permute-start | bytes 663560 | tf_op jit(solution)/shard_map/ppermute | solution.py:41
  302.5 11.6 %collective-permute-start.46 = (bf16[144,768]{1,0:T(8,128)(2,1)S(1)}, bf16[144,768]{1,0:T(8,128)(2,1)S(1)}, u32[]{:S(2)}, u32[]{:S(2)}) collective-permute-start(bf16[144,768]{1,0:T(8,128)(2,1)S(1)} %maximum_maximum_fusion.2), channel_id=1, source_target_pairs={{32,0},{36,4},{40,8},{44,12},{48,16},{52,20},{56,24},{60,28},{33,1... | collective-permute-start | bytes 663560 | tf_op jit(solution)/shard_map/ppermute | solution.py:41
  305.4 8.7 %collective-permute-start.45 = (bf16[144,768]{1,0:T(8,128)(2,1)S(1)}, bf16[144,768]{1,0:T(8,128)(2,1)S(1)}, u32[]{:S(2)}, u32[]{:S(2)}) collective-permute-start(bf16[144,768]{1,0:T(8,128)(2,1)S(1)} %maximum_maximum_fusion.2), channel_id=1, source_target_pairs={{48,0},{52,4},{56,8},{60,12},{49,1},{53,5},{57,9},{61,13},{50,2},{... | collective-permute-start | bytes 663560 | tf_op jit(solution)/shard_map/ppermute | solution.py:41
  342.2 10.6 %collective-permute-start.53 = (bf16[128,1536]{1,0:T(8,128)(2,1)}, bf16[128,1536]{1,0:T(8,128)(2,1)S(1)}, u32[]{:S(2)}, u32[]{:S(2)}) collective-permute-start(bf16[128,1536]{1,0:T(8,128)(2,1)} %get-tuple-element.221), channel_id=1, source_target_pairs={{0,1},{1,2},{2,3},{3,0},{4,5},{5,6},{6,7},{7,4},{8,9},{9,10},{10,1... | collective-permute-start | bytes 1179656 | tf_op jit(solution)/shard_map/ppermute | solution.py:29
  342.2 10.6 %collective-permute-start.54 = (bf16[128,1536]{1,0:T(8,128)(2,1)}, bf16[128,1536]{1,0:T(8,128)(2,1)S(1)}, u32[]{:S(2)}, u32[]{:S(2)}) collective-permute-start(bf16[128,1536]{1,0:T(8,128)(2,1)} %get-tuple-element.222), channel_id=1, source_target_pairs={{0,2},{1,3},{2,0},{3,1},{4,6},{5,7},{6,4},{7,5},{8,10},{9,11},{10,... | collective-permute-start | bytes 1179656 | tf_op jit(solution)/shard_map/ppermute | solution.py:29
  343.4 19.9 %collective-permute-start.55 = (bf16[128,1536]{1,0:T(8,128)(2,1)}, bf16[128,1536]{1,0:T(8,128)(2,1)S(1)}, u32[]{:S(2)}, u32[]{:S(2)}) collective-permute-start(bf16[128,1536]{1,0:T(8,128)(2,1)} %get-tuple-element.223), channel_id=1, source_target_pairs={{0,3},{1,0},{2,1},{3,2},{4,7},{5,4},{6,5},{7,6},{8,11},{9,8},{10,9... | collective-permute-start | bytes 1179656 | tf_op jit(solution)/shard_map/ppermute | solution.py:29
  349.6 42.3 %collective-permute-start.60 = (bf16[1536,768]{1,0:T(8,128)(2,1)}, bf16[1536,768]{1,0:T(8,128)(2,1)S(1)}, u32[]{:S(2)}, u32[]{:S(2)}) collective-permute-start(bf16[1536,768]{1,0:T(8,128)(2,1)} %get-tuple-element.240), channel_id=1, source_target_pairs={{0,64},{64,0},{1,65},{65,1},{2,66},{66,2},{3,67},{67,3},{4,68},{68... | collective-permute-start | bytes 7077896 | tf_op jit(solution)/shard_map/ppermute | solution.py:45
  369.1 22.8 %collective-permute-start.59 = (bf16[1536,640]{1,0:T(8,128)(2,1)}, bf16[1536,640]{1,0:T(8,128)(2,1)S(1)}, u32[]{:S(2)}, u32[]{:S(2)}) collective-permute-start(bf16[1536,640]{1,0:T(8,128)(2,1)} %get-tuple-element.233), channel_id=1, source_target_pairs={{0,64},{64,0},{1,65},{65,1},{2,66},{66,2},{3,67},{67,3},{4,68},{68... | collective-permute-start | bytes 5898248 | tf_op jit(solution)/shard_map/ppermute | solution.py:45
  369.7 21.9 %collective-permute-start.56 = (bf16[128,1664]{1,0:T(8,128)(2,1)S(1)}, bf16[128,1664]{1,0:T(8,128)(2,1)S(1)}, u32[]{:S(2)}, u32[]{:S(2)}) collective-permute-start(bf16[128,1664]{1,0:T(8,128)(2,1)S(1)} %constant_dynamic-update-slice_fusion.16), channel_id=1, source_target_pairs={{0,3},{1,0},{2,1},{3,2},{4,7},{5,4},{6,5},{7,6},{8,11},{9,8},{10,9... | collective-permute-start | bytes 1277960 | tf_op jit(solution)/shard_map/ppermute | solution.py:29
  369.8 21.8 %collective-permute-start.57 = (bf16[128,1664]{1,0:T(8,128)(2,1)S(1)}, bf16[128,1664]{1,0:T(8,128)(2,1)S(1)}, u32[]{:S(2)}, u32[]{:S(2)}) collective-permute-start(bf16[128,1664]{1,0:T(8,128)(2,1)S(1)} %constant_dynamic-update-slice_fusion.16), channel_id=1, source_target_pairs={{0,2},{1,3},{2,0},{3,1},{4,6},{5,7},{6,4},{7,5},{8,10},{9,11},{10,... | collective-permute-start | bytes 1277960 | tf_op jit(solution)/shard_map/ppermute | solution.py:29
  371.8 20.1 %collective-permute-start.58 = (bf16[128,1664]{1,0:T(8,128)(2,1)S(1)}, bf16[128,1664]{1,0:T(8,128)(2,1)S(1)}, u32[]{:S(2)}, u32[]{:S(2)}) collective-permute-start(bf16[128,1664]{1,0:T(8,128)(2,1)S(1)} %constant_dynamic-update-slice_fusion.16), channel_id=1, source_target_pairs={{0,1},{1,2},{2,3},{3,0},{4,5},{5,6},{6,7},{7,4},{8,9},{9,10},{10,1... | collective-permute-start | bytes 1277960 | tf_op jit(solution)/shard_map/ppermute | solution.py:29
  414.0 7.9 %collective-permute-start.61 = (bf16[144,768]{1,0:T(8,128)(2,1)S(1)}, bf16[144,768]{1,0:T(8,128)(2,1)S(1)}, u32[]{:S(2)}, u32[]{:S(2)}) collective-permute-start(bf16[144,768]{1,0:T(8,128)(2,1)S(1)} %copy-done.105), channel_id=1, source_target_pairs={{12,0},{0,4},{4,8},{8,12},{28,16},{16,20},{20,24},{24,28},{44,32},... | collective-permute-start | bytes 663560 | tf_op jit(solution)/shard_map/ppermute | solution.py:41
  415.4 12.0 %collective-permute-start.62 = (bf16[144,768]{1,0:T(8,128)(2,1)S(1)}, bf16[144,768]{1,0:T(8,128)(2,1)S(1)}, u32[]{:S(2)}, u32[]{:S(2)}) collective-permute-start(bf16[144,768]{1,0:T(8,128)(2,1)S(1)} %copy-done.105), channel_id=1, source_target_pairs={{8,0},{12,4},{0,8},{4,12},{24,16},{28,20},{16,24},{20,28},{40,32},... | collective-permute-start | bytes 663560 | tf_op jit(solution)/shard_map/ppermute | solution.py:41
  417.2 10.2 %collective-permute-start.63 = (bf16[144,768]{1,0:T(8,128)(2,1)S(1)}, bf16[144,768]{1,0:T(8,128)(2,1)S(1)}, u32[]{:S(2)}, u32[]{:S(2)}) collective-permute-start(bf16[144,768]{1,0:T(8,128)(2,1)S(1)} %copy-done.105), channel_id=1, source_target_pairs={{4,0},{8,4},{12,8},{0,12},{20,16},{24,20},{28,24},{16,28},{36,32},... | collective-permute-start | bytes 663560 | tf_op jit(solution)/shard_map/ppermute | solution.py:41
  428.0 15.8 %collective-permute-start.66 = (bf16[144,768]{1,0:T(8,128)(2,1)S(1)}, bf16[144,768]{1,0:T(8,128)(2,1)S(1)}, u32[]{:S(2)}, u32[]{:S(2)}) collective-permute-start(bf16[144,768]{1,0:T(8,128)(2,1)S(1)} %maximum_maximum_fusion.3), channel_id=1, source_target_pairs={{16,0},{20,4},{24,8},{28,12},{32,16},{36,20},{40,24},{44,28},{48,3... | collective-permute-start | bytes 663560 | tf_op jit(solution)/shard_map/ppermute | solution.py:41
  432.9 18.3 %collective-permute-start.65 = (bf16[144,768]{1,0:T(8,128)(2,1)S(1)}, bf16[144,768]{1,0:T(8,128)(2,1)S(1)}, u32[]{:S(2)}, u32[]{:S(2)}) collective-permute-start(bf16[144,768]{1,0:T(8,128)(2,1)S(1)} %maximum_maximum_fusion.3), channel_id=1, source_target_pairs={{32,0},{36,4},{40,8},{44,12},{48,16},{52,20},{56,24},{60,28},{33,1... | collective-permute-start | bytes 663560 | tf_op jit(solution)/shard_map/ppermute | solution.py:41
  442.4 13.9 %collective-permute-start.64 = (bf16[144,768]{1,0:T(8,128)(2,1)S(1)}, bf16[144,768]{1,0:T(8,128)(2,1)S(1)}, u32[]{:S(2)}, u32[]{:S(2)}) collective-permute-start(bf16[144,768]{1,0:T(8,128)(2,1)S(1)} %maximum_maximum_fusion.3), channel_id=1, source_target_pairs={{48,0},{52,4},{56,8},{60,12},{49,1},{53,5},{57,9},{61,13},{50,2},{... | collective-permute-start | bytes 663560 | tf_op jit(solution)/shard_map/ppermute | solution.py:41
  500.5 20.7 %collective-permute-start.69 = (bf16[128,1536]{1,0:T(8,128)(2,1)}, bf16[128,1536]{1,0:T(8,128)(2,1)S(1)}, u32[]{:S(2)}, u32[]{:S(2)}) collective-permute-start(bf16[128,1536]{1,0:T(8,128)(2,1)} %get-tuple-element.262), channel_id=1, source_target_pairs={{0,1},{1,2},{2,3},{3,0},{4,5},{5,6},{6,7},{7,4},{8,9},{9,10},{10,1... | collective-permute-start | bytes 1179656 | tf_op jit(solution)/shard_map/ppermute | solution.py:29
  504.3 16.9 %collective-permute-start.70 = (bf16[128,1536]{1,0:T(8,128)(2,1)}, bf16[128,1536]{1,0:T(8,128)(2,1)}, u32[]{:S(2)}, u32[]{:S(2)}) collective-permute-start(bf16[128,1536]{1,0:T(8,128)(2,1)} %get-tuple-element.263), channel_id=1, source_target_pairs={{0,2},{1,3},{2,0},{3,1},{4,6},{5,7},{6,4},{7,5},{8,10},{9,11},{10,... | collective-permute-start | bytes 1179656 | tf_op jit(solution)/shard_map/ppermute | solution.py:29
  504.3 20.8 %collective-permute-start.71 = (bf16[128,1536]{1,0:T(8,128)(2,1)}, bf16[128,1536]{1,0:T(8,128)(2,1)}, u32[]{:S(2)}, u32[]{:S(2)}) collective-permute-start(bf16[128,1536]{1,0:T(8,128)(2,1)} %get-tuple-element.264), channel_id=1, source_target_pairs={{0,3},{1,0},{2,1},{3,2},{4,7},{5,4},{6,5},{7,6},{8,11},{9,8},{10,9... | collective-permute-start | bytes 1179656 | tf_op jit(solution)/shard_map/ppermute | solution.py:29
  505.8 24.2 %collective-permute-start.51 = (bf16[128,1536]{1,0:T(8,128)(2,1)}, bf16[128,1536]{1,0:T(8,128)(2,1)}, u32[]{:S(2)}, u32[]{:S(2)}) collective-permute-start(bf16[128,1536]{1,0:T(8,128)(2,1)} %broadcast_select_fusion.1), channel_id=1, source_target_pairs={{0,64},{64,0},{1,65},{65,1},{2,66},{66,2},{3,67},{67,3},{4,68},{68... | collective-permute-start | bytes 1179656 | tf_op jit(solution)/shard_map/ppermute | solution.py:45
  506.7 38.8 %all-to-all-start.1 = ((bf16[16,96,640]{2,1,0:T(8,128)(2,1)}), bf16[16,96,640]{2,1,0:T(8,128)(2,1)}, u32[]{:S(2)}, u32[]{:S(2)}) async-start(bf16[16,96,640]{2,1,0:T(8,128)(2,1)} %bitcast.236), calls=%async_computation.1 | async-start | bytes 3932160 | tf_op jit(solution)/shard_map/all_to_all | solution.py:1163
  548.4 19.6 %collective-permute-start.78 = (bf16[24,1536]{1,0:T(8,128)(2,1)S(1)}, bf16[24,1536]{1,0:T(8,128)(2,1)S(1)}, u32[]{:S(2)}, u32[]{:S(2)}) collective-permute-start(bf16[24,1536]{1,0:T(8,128)(2,1)S(1)} %get-tuple-element.380), channel_id=1, source_target_pairs={{0,0},{1,16},{2,32},{3,48},{4,64},{5,80},{6,96},{7,112},{8,1},{9,1... | collective-permute-start | bytes 221192 | tf_op jit(solution)/shard_map/ppermute | solution.py:1277
  552.3 15.7 %collective-permute-start.79 = (bf16[24,1536]{1,0:T(8,128)(2,1)S(1)}, bf16[24,1536]{1,0:T(8,128)(2,1)S(1)}, u32[]{:S(2)}, u32[]{:S(2)}) collective-permute-start(bf16[24,1536]{1,0:T(8,128)(2,1)S(1)} %get-tuple-element.381), channel_id=1, source_target_pairs={{0,64},{1,80},{2,96},{3,112},{4,0},{5,16},{6,32},{7,48},{8,65},{9,... | collective-permute-start | bytes 221192 | tf_op jit(solution)/shard_map/ppermute | solution.py:1278
  553.4 16.4 %collective-permute-start.74 = (bf16[24,2048]{1,0:T(8,128)(2,1)S(1)}, bf16[24,2048]{1,0:T(8,128)(2,1)S(1)}, u32[]{:S(2)}, u32[]{:S(2)}) collective-permute-start(bf16[24,2048]{1,0:T(8,128)(2,1)S(1)} %get-tuple-element.353), channel_id=1, source_target_pairs={{0,3},{1,0},{2,1},{3,2},{4,7},{5,4},{6,5},{7,6},{8,11},{9,8},{10,9... | collective-permute-start | bytes 294920 | tf_op jit(solution)/shard_map/ppermute | solution.py:29
  555.6 14.2 %collective-permute-start.75 = (bf16[24,2048]{1,0:T(8,128)(2,1)S(1)}, bf16[24,2048]{1,0:T(8,128)(2,1)S(1)}, u32[]{:S(2)}, u32[]{:S(2)}) collective-permute-start(bf16[24,2048]{1,0:T(8,128)(2,1)S(1)} %get-tuple-element.352), channel_id=1, source_target_pairs={{0,2},{1,3},{2,0},{3,1},{4,6},{5,7},{6,4},{7,5},{8,10},{9,11},{10,... | collective-permute-start | bytes 294920 | tf_op jit(solution)/shard_map/ppermute | solution.py:29
  558.6 11.3 %collective-permute-start.76 = (bf16[24,2048]{1,0:T(8,128)(2,1)S(1)}, bf16[24,2048]{1,0:T(8,128)(2,1)S(1)}, u32[]{:S(2)}, u32[]{:S(2)}) collective-permute-start(bf16[24,2048]{1,0:T(8,128)(2,1)S(1)} %get-tuple-element.350), channel_id=1, source_target_pairs={{0,1},{1,2},{2,3},{3,0},{4,5},{5,6},{6,7},{7,4},{8,9},{9,10},{10,1... | collective-permute-start | bytes 294920 | tf_op jit(solution)/shard_map/ppermute | solution.py:29
  (144 other events, 1788.1 us)
Sparse Core Ops, SparseCore 0:
  20.1 50.0 all-gather.3
  72.8 53.3 all-gather.5
  128.4 48.1 all-gather.7
  413.2 90.8 reduce-scatter.1
